TPU v7x, 32 devices: a whole 2x2x4 slice. The times are simulated.
32 devices in a mesh: dp: 16 (over z, y, core), tp: 2 (over x).
Axes of the slice: x: 2, y: 2, z: 4, core: 2. Of those that a mesh axis runs over, the one named last changes fastest.
Arguments:
- layer_input: bfloat16 [16, 256, 2048], P('dp', 'tp'), may hold values from -6 to 6
- grad_out: bfloat16 [16, 256, 2048], P('dp', 'tp'), may hold values from -6 to 6
- lengths: int32 [16], P('dp'), may hold values from 1 to 256, 3072 in all
- resets: int32 [16, 256], P('dp', 'tp'), may hold values 0 or 1
- norm_gain: bfloat16 [2048], P(('dp', 'tp')), may hold values from 0.099609375 to 1.8984375
- w_x: bfloat16 [2048, 2560], P(('dp', 'tp')), may hold values from -0.125 to 0.125
- w_y: bfloat16 [2048, 2560], P(('dp', 'tp')), may hold values from -0.125 to 0.125
- conv_w: bfloat16 [4, 2560], P(None, ('dp', 'tp')), may hold values from -3 to 3
- conv_b: bfloat16 [2560], P(('dp', 'tp')), may hold values from -3 to 3
- gate_a_w: bfloat16 [2560, 256], P(('dp', 'tp')), may hold values from -0.375 to 0.375
- gate_a_b: bfloat16 [2560], P(('dp', 'tp')), may hold values from -3 to 3
- gate_i_w: bfloat16 [2560, 256], P(('dp', 'tp')), may hold values from -0.375 to 0.375
- gate_i_b: bfloat16 [2560], P(('dp', 'tp')), may hold values from -3 to 3
- decay_param: bfloat16 [2560], P(('dp', 'tp')), may hold values from 4.5 to 8
- w_out: bfloat16 [2560, 2048], P(('dp', 'tp')), may hold values from -0.5 to 0.5
- mlp_gain: bfloat16 [2048], P(('dp', 'tp')), may hold values from 0.099609375 to 1.8984375
- w_gate: bfloat16 [2048, 6144], P('dp', 'tp'), may hold values from -0.125 to 0.125
- w_up: bfloat16 [2048, 6144], P('dp', 'tp'), may hold values from -0.125 to 0.125
- w_down: bfloat16 [6144, 2048], P('tp', 'dp'), may hold values from -0.15625 to 0.15625
Outputs:
- layer_output: bfloat16 [16, 256, 2048], P('dp', 'tp')
- grad_x: float32 [16, 256, 2048], P('dp', 'tp')
- grad_norm_gain: float32 [2048], P(('dp', 'tp'))
- grad_w_x: float32 [2048, 2560], P(('dp', 'tp'))
- grad_w_y: float32 [2048, 2560], P(('dp', 'tp'))
- grad_conv_w: float32 [4, 2560], P(None, ('dp', 'tp'))
- grad_conv_b: float32 [2560], P(('dp', 'tp'))
- grad_gate_a_w: float32 [2560, 256], P(('dp', 'tp'))
- grad_gate_a_b: float32 [2560], P(('dp', 'tp'))
- grad_gate_i_w: float32 [2560, 256], P(('dp', 'tp'))
- grad_gate_i_b: float32 [2560], P(('dp', 'tp'))
- grad_decay: float32 [2560], P(('dp', 'tp'))
- grad_w_out: float32 [2560, 2048], P(('dp', 'tp'))
- grad_mlp_gain: float32 [2048], P(('dp', 'tp'))
- grad_w_gate: float32 [2048, 6144], P('dp', 'tp')
- grad_w_up: float32 [2048, 6144], P('dp', 'tp')
- grad_w_down: float32 [6144, 2048], P('tp', 'dp')
Inputs may be any that keep to these rules, and one draw needn't show every extreme that they name: `lengths`: some row has exactly 256. `resets`: position 0 of every row starts a segment in any case.
All inputs are finite; a program needn't handle non-finite values. No bound on the sum of `lengths` or of `resets` on one device may be relied on, other than what follows from the above.
Results may differ from a plain program's by a relative error of at most 0.017.
Values may be sent and summed in bfloat16 or wider, within the bound.
A program may use at most 384 MiB of HBM per device.

v0:
```python
import jax
import jax.numpy as jnp
from jax import lax
from jax.sharding import PartitionSpec as P

HEADS = 10
BLK = 256


epsilon = 1e-06


def passed_along(value, axis, steps):
    count = lax.axis_size(axis)
    initial, last = (max(0, -steps), min(count, count - steps))
    return lax.ppermute(value, axis, [(source, source + steps) for source in range(initial, last)])


def entering(value, axis, join, neutral, backward):
    count, mine = (lax.axis_size(axis), lax.axis_index(axis))
    pieces = jax.tree.map(lambda part: lax.all_gather(part, axis), value)
    if backward:
        pieces = jax.tree.map(lambda part: part[::-1], pieces)
        mine = count - 1 - mine
    running = jax.tree.map(
        lambda part, zero: jnp.full_like(part, 0) + jnp.asarray(zero, part.dtype), value, neutral
    )

    def turn(position, running):
        longer = join(running, jax.tree.map(lambda part: part[position], pieces))
        return jax.tree.map(lambda new, old: jnp.where(position < mine, new, old), longer, running)

    return lax.fori_loop(0, count - 1, turn, running)


def affine_pair(earlier, later):
    return (later[0] * earlier[0], later[0] * earlier[1] + later[1])


def rms_apply(values, gain):
    scaled = lax.rsqrt(jnp.mean(values * values, axis=-1, keepdims=True) + epsilon)
    return values * scaled * gain


def smooth_gate(values):
    return jax.nn.gelu(values, approximate=True)


def gated_mix(pre_gate, pre_up):
    return smooth_gate(pre_gate) * pre_up


def gate_section(pre_rate, pre_input, inputs, decay, bias_rate, bias_input, starts):
    rate = jax.nn.sigmoid(pre_rate + bias_rate)
    inject = jax.nn.sigmoid(pre_input + bias_input)
    log_decay = -8.0 * rate * jax.nn.softplus(-decay)
    factor = jnp.exp(log_decay) * (1.0 - starts)
    scale_in = jnp.where(starts > 0.5, 1.0, jnp.sqrt(-jnp.expm1(2.0 * log_decay)))
    return (factor, scale_in * inject * inputs)


def dot_inner(left, right):
    return lax.dot_general(
        left, right, (((1,), (1,)), ((), ())), preferred_element_type=jnp.float32
    )


def dot_outer(left, right):
    return lax.dot_general(
        left, right, (((0,), (0,)), ((), ())), preferred_element_type=jnp.float32
    )


def block_apply(values, weight):
    tokens = values.shape[0]
    blocks = weight.reshape(HEADS, BLK, BLK)
    result = jnp.einsum(
        "shi,hij->shj",
        values.reshape(tokens, HEADS, BLK),
        blocks,
        preferred_element_type=jnp.float32,
    )
    return result.reshape(tokens, HEADS * BLK)


def block_back(grads, weight):
    tokens = grads.shape[0]
    blocks = weight.reshape(HEADS, BLK, BLK)
    result = jnp.einsum(
        "shj,hij->shi",
        grads.reshape(tokens, HEADS, BLK),
        blocks,
        preferred_element_type=jnp.float32,
    )
    return result.reshape(tokens, HEADS * BLK)


def block_grad(values, grads):
    tokens = values.shape[0]
    result = jnp.einsum(
        "shi,shj->hij",
        values.reshape(tokens, HEADS, BLK),
        grads.reshape(tokens, HEADS, BLK),
        preferred_element_type=jnp.float32,
    )
    return result.reshape(HEADS * BLK, BLK)


def body(
    layer_input,
    grad_out,
    lengths,
    resets,
    norm_gain,
    w_x,
    w_y,
    conv_w,
    conv_b,
    gate_a_w,
    gate_a_b,
    gate_i_w,
    gate_i_b,
    decay_param,
    w_out,
    mlp_gain,
    w_gate,
    w_up,
    w_down,
):
    tokens = layer_input.shape[1]
    width = layer_input.shape[2]
    taps = conv_w.shape[0]
    rows_in = layer_input.reshape(tokens, width).astype(jnp.float32)
    place = lax.axis_index("tp") * tokens + jnp.arange(tokens, dtype=jnp.int32)
    starts = jnp.where((resets.reshape(tokens) > 0) | (place == 0), 1.0, 0.0).astype(jnp.float32)[
        :, None
    ]
    valid = (place < lengths[0]).astype(jnp.float32)[:, None]
    params = (
        lax.all_gather(norm_gain, ("dp", "tp"), axis=0, tiled=True),
        lax.all_gather(w_x, ("dp", "tp"), axis=0, tiled=True),
        lax.all_gather(w_y, ("dp", "tp"), axis=0, tiled=True),
        lax.all_gather(conv_w, ("dp", "tp"), axis=1, tiled=True),
        lax.all_gather(conv_b, ("dp", "tp"), axis=0, tiled=True),
        lax.all_gather(gate_a_w, ("dp", "tp"), axis=0, tiled=True),
        lax.all_gather(gate_a_b, ("dp", "tp"), axis=0, tiled=True),
        lax.all_gather(gate_i_w, ("dp", "tp"), axis=0, tiled=True),
        lax.all_gather(gate_i_b, ("dp", "tp"), axis=0, tiled=True),
        lax.all_gather(decay_param, ("dp", "tp"), axis=0, tiled=True),
        lax.all_gather(w_out, ("dp", "tp"), axis=0, tiled=True),
        lax.all_gather(mlp_gain, ("dp", "tp"), axis=0, tiled=True),
    )
    ff_weights = (
        lax.all_gather(w_gate, "dp", axis=0, tiled=True),
        lax.all_gather(w_up, "dp", axis=0, tiled=True),
        lax.all_gather(w_down, "dp", axis=1, tiled=True),
    )
    (
        gain_one,
        proj_x,
        proj_y,
        conv_taps,
        conv_bias,
        rate_w,
        rate_b,
        input_w,
        input_b,
        decay_full,
        proj_out,
        gain_two,
    ) = params
    gain_one_f = gain_one.astype(jnp.float32)
    gain_two_f = gain_two.astype(jnp.float32)
    taps_f = conv_taps.astype(jnp.float32)
    decay_f = decay_full.astype(jnp.float32)
    rate_bf = rate_b.astype(jnp.float32)
    input_bf = input_b.astype(jnp.float32)
    normed = rms_apply(rows_in, gain_one_f).astype(jnp.bfloat16)
    branch_x = jnp.dot(normed, proj_x, preferred_element_type=jnp.float32).astype(jnp.bfloat16)
    pre_y = jnp.dot(normed, proj_y, preferred_element_type=jnp.float32)
    branch_y = smooth_gate(pre_y)
    before = passed_along(branch_x[tokens - (taps - 1) :], "tp", 1)
    padded = jnp.concatenate([before, branch_x], axis=0).astype(jnp.float32)
    conv_sum = conv_bias.astype(jnp.float32) + jnp.zeros((tokens, branch_x.shape[1]), jnp.float32)
    for tap_index in range(taps):
        conv_sum = (
            conv_sum
            + taps_f[tap_index] * padded[taps - 1 - tap_index : taps - 1 - tap_index + tokens]
        )
    mixed = conv_sum.astype(jnp.bfloat16)
    mixed_f = mixed.astype(jnp.float32)
    pre_rate = block_apply(mixed, rate_w)
    pre_input = block_apply(mixed, input_w)
    factor, inject = gate_section(pre_rate, pre_input, mixed_f, decay_f, rate_bf, input_bf, starts)
    coefs, local_states = lax.associative_scan(affine_pair, (factor, inject), axis=0)
    unit = (jnp.ones_like(coefs[-1]), jnp.zeros_like(local_states[-1]))
    carried = entering((coefs[-1], local_states[-1]), "tp", affine_pair, unit, False)
    states = local_states + coefs * carried[1]
    gated = (states * branch_y).astype(jnp.bfloat16)
    first_sum = rows_in + jnp.dot(gated, proj_out, preferred_element_type=jnp.float32)
    normed_two = rms_apply(first_sum, gain_two_f).astype(jnp.bfloat16)
    ff_gate, ff_up, ff_down = ff_weights
    all_rows = lax.all_gather(normed_two, "tp", axis=0, tiled=True)
    pre_gate = jnp.dot(all_rows, ff_gate, preferred_element_type=jnp.float32)
    pre_up = jnp.dot(all_rows, ff_up, preferred_element_type=jnp.float32)
    hidden = gated_mix(pre_gate, pre_up).astype(jnp.bfloat16)
    ff_out = lax.psum_scatter(
        jnp.dot(hidden, ff_down, preferred_element_type=jnp.float32).astype(jnp.bfloat16),
        "tp",
        scatter_dimension=0,
        tiled=True,
    ).astype(jnp.float32)
    result = (first_sum + ff_out).astype(jnp.bfloat16).reshape(1, tokens, width)
    cotangent = grad_out.reshape(tokens, width).astype(jnp.float32) * valid
    back_gate, back_up, back_down = ff_weights
    grad_rows = lax.all_gather(cotangent.astype(jnp.bfloat16), "tp", axis=0, tiled=True)
    grad_hidden = dot_inner(grad_rows, back_down)
    mix_pull = jax.vjp(gated_mix, pre_gate, pre_up)[1]
    grad_gate_f, grad_up_f = mix_pull(grad_hidden)
    grad_gate_b = grad_gate_f.astype(jnp.bfloat16)
    grad_up_b = grad_up_f.astype(jnp.bfloat16)
    ff_cols = back_gate.shape[1]
    row_count = all_rows.shape[0]
    zero_block = jnp.zeros((row_count, ff_cols), jnp.bfloat16)
    left_pair = jnp.concatenate([all_rows, grad_rows], axis=0)
    right_pair = jnp.concatenate(
        [
            jnp.concatenate([grad_gate_b, grad_up_b, zero_block], axis=1),
            jnp.concatenate([zero_block, zero_block, hidden], axis=1),
        ],
        axis=0,
    )
    ff_grads = lax.psum_scatter(
        dot_outer(left_pair, right_pair), "dp", scatter_dimension=0, tiled=True
    )
    grad_normed_two = lax.psum_scatter(
        (dot_inner(grad_gate_b, back_gate) + dot_inner(grad_up_b, back_up)).astype(jnp.bfloat16),
        "tp",
        scatter_dimension=0,
        tiled=True,
    ).astype(jnp.float32)
    norm_pull = jax.vjp(rms_apply, first_sum, gain_two_f)[1]
    grad_first_norm, grad_gain_two = norm_pull(grad_normed_two)
    grad_first = cotangent + grad_first_norm
    back_proj_x = params[1]
    back_proj_y = params[2]
    back_taps = params[3].astype(jnp.float32)
    back_rate_w = params[5]
    back_input_w = params[7]
    back_proj_out = params[10]
    grad_branch = grad_first.astype(jnp.bfloat16)
    term_out = dot_outer(gated, grad_branch)
    grad_gated = dot_inner(grad_branch, back_proj_out)
    gelu_pull = jax.vjp(smooth_gate, pre_y)[1]
    grad_pre_y = gelu_pull(grad_gated * states)[0].astype(jnp.bfloat16)
    grad_states = grad_gated * branch_y
    shifted = jnp.concatenate([factor[1:], jnp.ones_like(factor[:1])], axis=0)
    flip_coef, flip_adj = lax.associative_scan(
        affine_pair, (jnp.flip(shifted, 0), jnp.flip(grad_states, 0)), axis=0
    )
    back_coef = jnp.flip(flip_coef, 0)
    back_adj = jnp.flip(flip_adj, 0)
    incoming = entering(
        (factor[0] * back_coef[0], factor[0] * back_adj[0]), "tp", affine_pair, unit, True
    )
    adjoint = back_adj + back_coef * incoming[1]
    previous = jnp.concatenate([carried[1][None, :], states[:-1]], axis=0)
    section_pull = jax.vjp(
        gate_section, pre_rate, pre_input, mixed_f, decay_f, rate_bf, input_bf, starts
    )[1]
    (
        grad_rate,
        grad_input,
        grad_mixed_direct,
        grad_decay,
        grad_rate_b,
        grad_input_b,
        unused_start,
    ) = section_pull((adjoint * previous, adjoint))
    grad_rate_b16 = grad_rate.astype(jnp.bfloat16)
    grad_input_b16 = grad_input.astype(jnp.bfloat16)
    term_rate_w = block_grad(mixed, grad_rate_b16)
    term_input_w = block_grad(mixed, grad_input_b16)
    grad_mixed = (
        grad_mixed_direct
        + block_back(grad_rate_b16, back_rate_w)
        + block_back(grad_input_b16, back_input_w)
    ).astype(jnp.bfloat16)
    after = passed_along(grad_mixed[: taps - 1], "tp", -1)
    grad_padded = jnp.concatenate([grad_mixed, after], axis=0).astype(jnp.float32)
    grad_mixed_f = grad_padded[:tokens]
    term_taps = jnp.stack(
        [
            jnp.sum(
                grad_mixed_f * padded[taps - 1 - tap_index : taps - 1 - tap_index + tokens], axis=0
            )
            for tap_index in range(taps)
        ],
        axis=0,
    )
    term_bias = jnp.sum(grad_mixed_f, axis=0)
    grad_branch_x = jnp.zeros_like(grad_mixed_f)
    for tap_index in range(taps):
        grad_branch_x = (
            grad_branch_x + back_taps[tap_index] * grad_padded[tap_index : tap_index + tokens]
        )
    grad_branch_x = grad_branch_x.astype(jnp.bfloat16)
    term_x = dot_outer(normed, grad_branch_x)
    term_y = dot_outer(normed, grad_pre_y)
    grad_normed = dot_inner(grad_branch_x, back_proj_x) + dot_inner(grad_pre_y, back_proj_y)
    first_pull = jax.vjp(rms_apply, rows_in, gain_one_f)[1]
    grad_in_norm, grad_gain_one = first_pull(grad_normed)
    grad_input_rows = (grad_first + grad_in_norm).reshape(1, tokens, width)
    summed = (
        lax.psum_scatter(grad_gain_one, ("dp", "tp"), scatter_dimension=0, tiled=True),
        lax.psum_scatter(term_x, ("dp", "tp"), scatter_dimension=0, tiled=True),
        lax.psum_scatter(term_y, ("dp", "tp"), scatter_dimension=0, tiled=True),
        lax.psum_scatter(term_taps, ("dp", "tp"), scatter_dimension=1, tiled=True),
        lax.psum_scatter(term_bias, ("dp", "tp"), scatter_dimension=0, tiled=True),
        lax.psum_scatter(term_rate_w, ("dp", "tp"), scatter_dimension=0, tiled=True),
        lax.psum_scatter(grad_rate_b, ("dp", "tp"), scatter_dimension=0, tiled=True),
        lax.psum_scatter(term_input_w, ("dp", "tp"), scatter_dimension=0, tiled=True),
        lax.psum_scatter(grad_input_b, ("dp", "tp"), scatter_dimension=0, tiled=True),
        lax.psum_scatter(grad_decay, ("dp", "tp"), scatter_dimension=0, tiled=True),
        lax.psum_scatter(term_out, ("dp", "tp"), scatter_dimension=0, tiled=True),
        lax.psum_scatter(grad_gain_two, ("dp", "tp"), scatter_dimension=0, tiled=True),
    )
    grad_ff_gate = ff_grads[:, :ff_cols]
    grad_ff_up = ff_grads[:, ff_cols : 2 * ff_cols]
    grad_ff_down = ff_grads[:, 2 * ff_cols :].T
    return (
        result,
        grad_input_rows,
        summed[0],
        summed[1],
        summed[2],
        summed[3],
        summed[4],
        summed[5],
        summed[6],
        summed[7],
        summed[8],
        summed[9],
        summed[10],
        summed[11],
        grad_ff_gate,
        grad_ff_up,
        grad_ff_down,
    )


def solution(mesh):
    return jax.shard_map(
        body,
        mesh=mesh,
        in_specs=(
            P("dp", "tp", None),
            P("dp", "tp", None),
            P("dp"),
            P("dp", "tp"),
            P(("dp", "tp")),
            P(("dp", "tp"), None),
            P(("dp", "tp"), None),
            P(None, ("dp", "tp")),
            P(("dp", "tp")),
            P(("dp", "tp"), None),
            P(("dp", "tp")),
            P(("dp", "tp"), None),
            P(("dp", "tp")),
            P(("dp", "tp")),
            P(("dp", "tp"), None),
            P(("dp", "tp")),
            P("dp", "tp"),
            P("dp", "tp"),
            P("tp", "dp"),
        ),
        out_specs=(
            P("dp", "tp", None),
            P("dp", "tp", None),
            P(("dp", "tp")),
            P(("dp", "tp"), None),
            P(("dp", "tp"), None),
            P(None, ("dp", "tp")),
            P(("dp", "tp")),
            P(("dp", "tp"), None),
            P(("dp", "tp")),
            P(("dp", "tp"), None),
            P(("dp", "tp")),
            P(("dp", "tp")),
            P(("dp", "tp"), None),
            P(("dp", "tp")),
            P("dp", "tp"),
            P("dp", "tp"),
            P("tp", "dp"),
        ),
        check_vma=False,
    )
```

profile of v0, /device:TPU:0, one launch (start us, length us, event | category | flops | bytes accessed | tf_op | source)
XLA Modules:
  0.0 3565.0 jit_solution(15136693648864097596)
XLA Ops:
  10.7 70.5 %all-gather = bf16[32,80,4]{1,2,0:T(4,128)(2,1)S(1)} all-gather(bf16[1,80,4]{1,2,0:T(4,128)(2,1)} %bitcast.127), channel_id=1, replica_groups=mesh['dp'=16,'tp'=2] {'dp','tp'}, dimensions={0}, use_global_device_ids=true | all-gather | bytes 21120 | tf_op jit(solution)/shard_map/all_gather | solution.py:143
  82.9 37.4 %all-reduce.72 = (bf16[2560]{0:T(1024)(128)(2,1)S(1)}, bf16[2048]{0:T(1024)(128)(2,1)S(1)}, bf16[2560]{0:T(1024)(128)(2,1)S(1)}, bf16[2560]{0:T(1024)(128)(2,1)S...) all-reduce(bf16[2560]{0:T(1024)(128)(2,1)S(1)} %dynamic-update-slic, ...), channel_id=1, replica_groups=mesh['dp'=16,'tp'=2] {'dp','tp'}, use_global_device_ids=true, to_apply=%add.62 | all-reduce | flops 14336 | bytes 57344
  121.2 5.6 convolution_convert_fusion
  126.8 4.3 collective-permute-start
  133.6 23.9 all-gather.18.cloned.1.call-done
  164.7 49.0 %all-gather.20.cloned.1.call-done = bf16[2560,256]{1,0:T(8,128)(2,1)} async-done(((bf16[80,256]{1,0:T(8,128)(2,1)}), bf16[2560,256]{1,0:T(8,128)(2,1)}) %all-gather.20.cloned.1.call-update) | async-done | bytes 1310736 | tf_op jit(solution)/shard_map/all_gather | solution.py:147
  222.3 4.9 exponential_multiply_fusion
  227.3 3.3 slice.517
  302.3 3.5 slice.516
  307.3 3.4 slice.565
  358.2 4.8 pad.188
  375.8 4.8 pad.187
  380.6 4.8 pad.202
  387.5 5.0 pad.201
  393.4 4.4 all-gather.2
  398.8 4.6 all-gather.1
  404.0 9.2 multiply_convert_fusion.2
  413.2 5.9 multiply_reduce_fusion.5
  424.9 17.1 all-gather.26.cloned.1.call-done
  442.0 103.1 %all-gather.28.cloned.1.call-done = bf16[2048,3072]{1,0:T(8,128)(2,1)} async-done(((bf16[128,3072]{1,0:T(8,128)(2,1)}), bf16[2048,3072]{1,0:T(8,128)(2,1)}) %all-gather.28.cloned.1.call-update) | async-done | bytes 12582928 | tf_op jit(solution)/shard_map/all_gather | solution.py:154
  545.1 9.9 fusion.121
  555.0 91.3 %all-gather.30.cloned.1.call-done = bf16[2048,3072]{1,0:T(8,128)(2,1)} async-done(((bf16[128,3072]{1,0:T(8,128)(2,1)}), bf16[2048,3072]{1,0:T(8,128)(2,1)}) %all-gather.30.cloned.1.call-update) | async-done | bytes 12582928 | tf_op jit(solution)/shard_map/all_gather | solution.py:155
  646.3 9.9 fusion.122
  656.3 11.7 all-gather.34.cloned.1.call-done
  668.0 106.0 %all-gather.32.cloned.1.call-done = bf16[3072,2048]{1,0:T(8,128)(2,1)} async-done(((bf16[3072,128]{1,0:T(8,128)(2,1)}), bf16[3072,2048]{1,0:T(8,128)(2,1)}) %all-gather.32.cloned.1.call-update) | async-done | bytes 12582928 | tf_op jit(solution)/shard_map/all_gather | solution.py:156
  774.0 11.4 multiply_convert_fusion
  785.4 7.6 fusion.123
  793.0 9.0 fusion.19
  802.1 9.8 convolution_convert_fusion.1
  814.7 3.5 slice.583
  818.2 3.3 slice.585
  823.7 9.9 slice.584
  833.6 9.8 slice.586
  843.4 6.3 slice.593
  855.0 9.9 fusion.29
  864.9 3.4 slice.589
  870.4 9.9 slice.590
  880.3 6.3 slice.588
  947.6 3.4 slice.637
  979.2 9.9 slice.638
  1004.6 4.9 pad.216
  1010.4 4.9 pad.229
  1023.7 10.8 rev.11
  1034.5 10.9 rev.12
  1045.4 4.4 all-gather.4
  1049.7 4.6 all-gather.3
  1054.5 5.6 fusion.101
  1070.3 4.8 multiply_reduce_fusion
  1086.6 4.0 add_convert_fusion
  1091.9 4.4 collective-permute-done.1
  1100.6 32.8 fusion.2
  1141.0 8.7 fusion.94
  1151.1 8.7 fusion.61
  1160.0 8.8 fusion.96
  1169.6 7.5 fusion.124
  1177.0 8.5 fusion.45
  1185.5 39.3 %all-reduce.71 = (f32[2048]{0:T(1024)S(1)}, f32[2560]{0:T(1024)S(1)}, f32[2560]{0:T(1024)S(1)}, f32[2560]{0:T(1024)S(1)}, f32[2560]{0:T(1024)S(1)}, /*index=5*/f32[2048]{0:T(1024)S(1)}) all-reduce(f32[2048]{0:T(1024)S(1)} %get-tuple-element.129, f32[2560]{0:T(1024)S(1)} %get-tuple-element.131, ...), channel_id=4, replica_groups=mesh['dp'=16,'tp'=2] {'dp','tp'}, use_global_device_ids=true, to_apply=%region_7.8.clone | all-reduce | flops 14336 | bytes 114688
  1234.5 703.4 %reduce-scatter.26.cloned.1.call-done = f32[128,9216]{1,0:T(8,128)} async-done(((f32[2048,9216]{1,0:T(8,128)}), f32[128,9216]{1,0:T(8,128)}) %reduce-scatter.26.cloned.1.call-update) | async-done | bytes 4718608 | tf_op jit(solution)/shard_map/reduce_scatter | solution.py:233
  1938.0 4.5 slice_bitcast_fusion
  1944.0 135.0 %reduce-scatter.20.cloned.1.call-done = f32[80,256]{1,0:T(8,128)} async-done(((f32[2560,256]{1,0:T(8,128)}), f32[80,256]{1,0:T(8,128)}) %reduce-scatter.20.cloned.1.call-update) | async-done | bytes 81936 | tf_op jit(solution)/shard_map/reduce_scatter | solution.py:320
  2079.0 137.6 %reduce-scatter.22.cloned.1.call-done = f32[80,256]{1,0:T(8,128)} async-done(((f32[2560,256]{1,0:T(8,128)}), f32[80,256]{1,0:T(8,128)}) %reduce-scatter.22.cloned.1.call-update) | async-done | bytes 81936 | tf_op jit(solution)/shard_map/reduce_scatter | solution.py:322
  2216.6 443.4 %reduce-scatter.18.cloned.1.call-done = f32[64,2560]{1,0:T(8,128)} async-done(((f32[2048,2560]{1,0:T(8,128)}), f32[64,2560]{1,0:T(8,128)}) %reduce-scatter.18.cloned.1.call-update) | async-done | bytes 655376 | tf_op jit(solution)/shard_map/reduce_scatter | solution.py:317
  2660.0 449.1 %reduce-scatter.24.cloned.1.call-done = f32[80,2048]{1,0:T(8,128)} async-done(((f32[2560,2048]{1,0:T(8,128)}), f32[80,2048]{1,0:T(8,128)}) %reduce-scatter.24.cloned.1.call-update) | async-done | bytes 655376 | tf_op jit(solution)/shard_map/reduce_scatter | solution.py:325
  3109.1 449.2 %reduce-scatter.16.cloned.1.call-done = f32[64,2560]{1,0:T(8,128)} async-done(((f32[2048,2560]{1,0:T(8,128)}), f32[64,2560]{1,0:T(8,128)}) %reduce-scatter.16.cloned.1.call-update) | async-done | bytes 655376 | tf_op jit(solution)/shard_map/reduce_scatter | solution.py:316
  (549 shorter events, 341.3 us)
Async XLA Ops:
  7.2 74.0 %copy-start = (bf16[1,128,2048]{2,1,0:T(8,128)(2,1)S(1)}, bf16[1,128,2048]{2,1,0:T(8,128)(2,1)}, u32[]{:S(2)}) copy-start(bf16[1,128,2048]{2,1,0:T(8,128)(2,1)} %param.19) | copy-start | bytes 1572868
  7.2 74.2 %copy-start.107 = (bf16[80]{0:T(256)(128)(2,1)S(1)}, bf16[80]{0:T(256)(128)(2,1)}, u32[]{:S(2)}) copy-start(bf16[80]{0:T(256)(128)(2,1)} %param.32) | copy-start | bytes 484
  7.2 74.4 %copy-start.108 = (bf16[80]{0:T(256)(128)(2,1)S(1)}, bf16[80]{0:T(256)(128)(2,1)}, u32[]{:S(2)}) copy-start(bf16[80]{0:T(256)(128)(2,1)} %param.27) | copy-start | bytes 484
  7.2 74.7 %copy-start.109 = (bf16[80]{0:T(256)(128)(2,1)S(1)}, bf16[80]{0:T(256)(128)(2,1)}, u32[]{:S(2)}) copy-start(bf16[80]{0:T(256)(128)(2,1)} %param.29) | copy-start | bytes 484
  7.2 74.9 %copy-start.110 = (bf16[80]{0:T(256)(128)(2,1)S(1)}, bf16[80]{0:T(256)(128)(2,1)}, u32[]{:S(2)}) copy-start(bf16[80]{0:T(256)(128)(2,1)} %param.31) | copy-start | bytes 484
  7.2 75.2 %copy-start.111 = (bf16[64]{0:T(256)(128)(2,1)S(1)}, bf16[64]{0:T(256)(128)(2,1)}, u32[]{:S(2)}) copy-start(bf16[64]{0:T(256)(128)(2,1)} %param.23) | copy-start | bytes 388
  7.3 75.4 %copy-start.112 = (bf16[64]{0:T(256)(128)(2,1)S(1)}, bf16[64]{0:T(256)(128)(2,1)}, u32[]{:S(2)}) copy-start(bf16[64]{0:T(256)(128)(2,1)} %param.34) | copy-start | bytes 388
  7.3 113.2 %copy-start.106 = (s32[1,128]{1,0:T(1,128)S(1)}, s32[1,128]{1,0:T(1,128)}, u32[]{:S(2)}) copy-start(s32[1,128]{1,0:T(1,128)} %param.22) | copy-start | bytes 1540
  7.3 113.9 %all-gather.16.cloned.1.call-start = ((), (), s32[]{:S(2)}) async-start(), calls=%async_computation.9 | async-start | bytes 10813440 | tf_op jit(solution)/shard_map/all_gather | solution.py:141
  8.0 149.5 %all-gather.18.cloned.1.call-start = ((), (), s32[]{:S(2)}) async-start(), calls=%async_computation.10 | async-start | bytes 1351680 | tf_op jit(solution)/shard_map/all_gather | solution.py:145
  8.8 205.0 %all-gather.20.cloned.1.call-start = ((), (), s32[]{:S(2)}) async-start(), calls=%async_computation.11 | async-start | bytes 1351680 | tf_op jit(solution)/shard_map/all_gather | solution.py:147
  9.5 394.5 %all-gather.22.cloned.1.call-start = ((), (), s32[]{:S(2)}) async-start(), calls=%async_computation.12 | async-start | bytes 10813440 | tf_op jit(solution)/shard_map/all_gather | solution.py:142
  10.1 403.1 %all-gather.24.cloned.1.call-start = ((), (), s32[]{:S(2)}) async-start(), calls=%async_computation.13 | async-start | bytes 10813440 | tf_op jit(solution)/shard_map/all_gather | solution.py:150
  10.7 431.4 %all-gather.26.cloned.1.call-start = ((), (), s32[]{:S(2)}) async-start(), calls=%async_computation.14 | async-start | bytes 1572864 | tf_op jit(solution)/shard_map/all_gather | solution.py:203
  81.4 45.4 %copy-start.104 = (f32[128]{0:T(128)}, f32[128]{0:T(128)S(1)}, u32[]{:S(2)}) copy-start(f32[128]{0:T(128)S(1)} %fusion.51) | copy-start | bytes 1540
  120.5 101.7 %copy-start.100 = (pred[128]{0:T(512)(128)(4,1)}, pred[128]{0:T(512)(128)(4,1)S(1)}, u32[]{:S(2)}) copy-start(pred[128]{0:T(512)(128)(4,1)S(1)} %get-tuple-element.156) | copy-start | bytes 388
  120.6 101.7 %copy-start.102 = (f32[128]{0:T(128)}, f32[128]{0:T(128)S(1)}, u32[]{:S(2)}) copy-start(f32[128]{0:T(128)S(1)} %broadcast_subtract_fusion) | copy-start | bytes 1540
  121.2 101.0 %copy-start.64 = (f32[2560]{0:T(1024)}, f32[2560]{0:T(1024)S(1)}, u32[]{:S(2)}) copy-start(f32[2560]{0:T(1024)S(1)} %get-tuple-element.234) | copy-start | bytes 30724
  126.8 5.6 collective-permute-start
  131.3 91.0 %copy-start.50 = (f32[2560]{0:T(1024)}, f32[2560]{0:T(1024)S(1)}, u32[]{:S(2)}) copy-start(f32[2560]{0:T(1024)S(1)} %get-tuple-element.132) | copy-start | bytes 30724
  131.3 91.0 %copy-start.52 = (f32[2560]{0:T(1024)}, f32[2560]{0:T(1024)S(1)}, u32[]{:S(2)}) copy-start(f32[2560]{0:T(1024)S(1)} %get-tuple-element.133) | copy-start | bytes 30724
  131.3 91.0 %copy-start.54 = (f32[2560]{0:T(1024)}, f32[2560]{0:T(1024)S(1)}, u32[]{:S(2)}) copy-start(f32[2560]{0:T(1024)S(1)} %get-tuple-element.134) | copy-start | bytes 30724
  131.3 91.0 %copy-start.56 = (f32[2560]{0:T(1024)}, f32[2560]{0:T(1024)S(1)}, u32[]{:S(2)}) copy-start(f32[2560]{0:T(1024)S(1)} %get-tuple-element.135) | copy-start | bytes 30724
  131.3 91.0 %copy-start.62 = (f32[2560]{0:T(1024)}, f32[2560]{0:T(1024)S(1)}, u32[]{:S(2)}) copy-start(f32[2560]{0:T(1024)S(1)} %convert_element_type.112) | copy-start | bytes 30724
  131.3 91.0 %copy-start.48 = (f32[2560]{0:T(1024)}, f32[2560]{0:T(1024)S(1)}, u32[]{:S(2)}) copy-start(f32[2560]{0:T(1024)S(1)} %convert_element_type.119) | copy-start | bytes 30724
  131.4 91.0 %copy-start.60 = (f32[2560]{0:T(1024)}, f32[2560]{0:T(1024)S(1)}, u32[]{:S(2)}) copy-start(f32[2560]{0:T(1024)S(1)} %convert_element_type.121) | copy-start | bytes 30724
  133.6 26.6 copy-start.3
  302.2 11.4 copy-start.75
  302.2 11.4 copy-start.76
  302.2 11.4 copy-start.77
  302.2 11.4 copy-start.78
  302.2 11.5 copy-start.66
  302.3 11.5 copy-start.67
  387.5 16.5 copy-start.44
  387.5 16.5 copy-start.80
  421.1 124.0 %all-gather.28.cloned.1.call-start = ((), (), s32[]{:S(2)}) async-start(), calls=%async_computation.15 | async-start | bytes 13369344 | tf_op jit(solution)/shard_map/all_gather | solution.py:154
  421.8 224.5 %all-gather.30.cloned.1.call-start = ((), (), s32[]{:S(2)}) async-start(), calls=%async_computation.16 | async-start | bytes 13369344 | tf_op jit(solution)/shard_map/all_gather | solution.py:155
  422.6 245.4 %all-gather.34.cloned.1.call-start = ((), (), s32[]{:S(2)}) async-start(), calls=%async_computation.19 | async-start | bytes 1572864 | tf_op jit(solution)/shard_map/all_gather | solution.py:216
  424.2 349.7 %all-gather.32.cloned.1.call-start = ((), (), s32[]{:S(2)}) async-start(), calls=%async_computation.17 | async-start | bytes 13369344 | tf_op jit(solution)/shard_map/all_gather | solution.py:156
  424.8 424.9 %reduce-scatter.14.cloned.1.call-start = ((), (), s32[]{:S(2)}) async-start(), calls=%async_computation.20 | async-start | bytes 1572864 | tf_op jit(solution)/shard_map/reduce_scatter | solution.py:236
  802.1 50.0 %reduce-scatter.12.cloned.1.call-start = ((), (), s32[]{:S(2)}) async-start(), calls=%async_computation.18 | async-start | bytes 1572864 | tf_op jit(solution)/shard_map/reduce_scatter | solution.py:207
  812.0 421.1 %reduce-scatter.28.cloned.1.call-start = ((), (), s32[]{:S(2)}) async-start(), calls=%async_computation.27 | async-start | bytes 1351680
  941.9 10.6 copy-start.88
  941.9 10.7 copy-start.74
  941.9 10.8 copy-start.85
  941.9 10.8 copy-start.86
  979.2 12.7 copy-start.95
  1034.4 19.9 copy-start.49
  1034.4 19.9 copy-start.51
  1034.4 19.9 copy-start.53
  1034.4 20.0 copy-start.55
  1034.4 20.0 copy-start.57
  1034.5 20.0 copy-start.61
  1034.5 20.0 copy-start.63
  1034.5 20.0 copy-start.65
  1034.5 20.0 copy-start.101
  1090.6 5.7 collective-permute-start.1
  1099.4 838.5 %reduce-scatter.26.cloned.1.call-start = ((), (), s32[]{:S(2)}) async-start(), calls=%async_computation.26 | async-start | bytes 80216064 | tf_op jit(solution)/shard_map/reduce_scatter | solution.py:233
  1133.4 945.6 %reduce-scatter.20.cloned.1.call-start = ((), (), s32[]{:S(2)}) async-start(), calls=%async_computation.23 | async-start | bytes 2703360 | tf_op jit(solution)/shard_map/reduce_scatter | solution.py:320
  1136.7 1079.9 %reduce-scatter.22.cloned.1.call-start = ((), (), s32[]{:S(2)}) async-start(), calls=%async_computation.24 | async-start | bytes 2703360 | tf_op jit(solution)/shard_map/reduce_scatter | solution.py:322
  1139.8 1520.2 %reduce-scatter.18.cloned.1.call-start = ((), (), s32[]{:S(2)}) async-start(), calls=%async_computation.22 | async-start | bytes 21626880 | tf_op jit(solution)/shard_map/reduce_scatter | solution.py:317
  1149.7 1959.4 %reduce-scatter.24.cloned.1.call-start = ((), (), s32[]{:S(2)}) async-start(), calls=%async_computation.25 | async-start | bytes 21626880 | tf_op jit(solution)/shard_map/reduce_scatter | solution.py:325
  1159.8 2398.5 %reduce-scatter.16.cloned.1.call-start = ((), (), s32[]{:S(2)}) async-start(), calls=%async_computation.21 | async-start | bytes 21626880 | tf_op jit(solution)/shard_map/reduce_scatter | solution.py:316
  1177.0 51.3 %copy-start.105 = (f32[128]{0:T(128)S(1)}, f32[128]{0:T(128)}, u32[]{:S(2)}) copy-start(f32[128]{0:T(128)} %copy-done.104) | copy-start | bytes 1540
  (70 other events, 267.0 us)
Sparse Core Ops, SparseCore 0:
  11.0 89.4 all-gather.15
  103.3 54.1 all-gather.17
  160.3 53.3 all-gather.19
  216.5 85.7 all-gather.21
  305.0 85.2 all-gather.23
  421.2 20.7 all-gather.25
  444.3 100.7 all-gather.27
  547.4 98.9 all-gather.29
  648.5 19.4 all-gather.33
  670.0 103.9 all-gather.31
  802.2 18.4 reduce-scatter.13
  822.9 20.3 reduce-scatter.11
  1099.5 133.5 reduce-scatter.27
  1237.8 700.1 reduce-scatter.25
  1940.7 138.3 reduce-scatter.19
  2081.7 134.8 reduce-scatter.21
  2219.4 440.5 reduce-scatter.17
  2662.7 446.3 reduce-scatter.23
  3112.0 446.3 reduce-scatter.15
where the time goes:
time: 3580 us; the launch traced here: 3570 us
  waiting for transfers between devices  2730 us (76%)
  local copies, waits for them, and re-layouts  348 us (10%)
  matrix products  179 us (5%)
  blocking collectives  165 us (5%)
  other arithmetic  117 us (3%)
    reduce_scatter x1, waiting for transfers between devices, body(): lax.psum_scatter(dot_outer(left_pair, right_pair), 'dp', scatter_dimensio...  703 us
    reduce_scatter x1, waiting for transfers between devices, body(): lax.psum_scatter(term_x, ('dp', 'tp'), scatter_dimension=0, tiled=True)  449 us
    reduce_scatter x1, waiting for transfers between devices, body(): lax.psum_scatter(term_out, ('dp', 'tp'), scatter_dimension=0, tiled=True)  449 us
    reduce_scatter x1, waiting for transfers between devices, body(): lax.psum_scatter(term_y, ('dp', 'tp'), scatter_dimension=0, tiled=True)  443 us
    reduce_scatter x1, waiting for transfers between devices, body(): lax.psum_scatter(term_input_w, ('dp', 'tp'), scatter_dimension=0, tiled=T...  138 us
    reduce_scatter x1, waiting for transfers between devices, body(): lax.psum_scatter(term_rate_w, ('dp', 'tp'), scatter_dimension=0, tiled=True)  135 us
    slice x49, local copies, waits for them, and re-layouts, body(): lax.associative_scan(affine_pair, (jnp.flip(shifted, 0), jnp.flip(grad_st...  120 us
    all_gather x1, waiting for transfers between devices, body(): lax.all_gather(w_down, 'dp', axis=1, tiled=True)  106 us
  transfers between devices with their start and end apart: 21, of which 16 were waited for; matrix products, arithmetic and copies ran while one was open for 10% of the time, Pallas kernels for 0%

commit v1 on v0

v1 whole, which is shorter than its diff:
```python
import functools

import jax
import jax.numpy as jnp
from jax import lax
from jax.experimental import pallas as pl
from jax.experimental.pallas import tpu as pltpu
from jax.sharding import PartitionSpec as P

BLK = 256
PAD = 16
WIDE = 512
EPS = 1e-06
MESH = pl.DeviceIdType.MESH
F32 = jnp.float32
BF16 = jnp.bfloat16


def chip_at(pos, n):
    back = pos // (n // 2)
    return (1 - back) * (2 * pos) + back * (2 * (n - 1 - pos) + 1)


def place_of(chip, n):
    odd = chip % 2
    return (1 - odd) * (chip // 2) + odd * (n - 1 - chip // 2)


def gather_kernel(
    n,
    wx, wy, wo, gs, wg, wu, wd, rows_in, cot, starts,
    o_xy, o_out, o_gs, o_gu, o_d, o_rows, o_cot, o_starts,
    local_sem, pair_send, pair_recv, ring_send, ring_recv, x_send, x_recv,
):
    dp, x = lax.axis_index("dp"), lax.axis_index("tp")
    chip, core = dp // 2, dp % 2
    other = 1 - core
    pos = place_of(chip, n)
    half = n // 2
    nxt = (chip_at((pos + 1) % n, n) * 2 + core, x)
    prv = (chip_at((pos + n - 1) % n, n) * 2 + core, x)
    sib = (chip * 2 + other, x)
    across = (dp, 1 - x)
    barrier = pltpu.get_barrier_semaphore()
    for device in (nxt, prv, sib, across):
        pl.semaphore_signal(barrier, inc=1, device_id=device, device_id_type=MESH)
    pl.semaphore_wait(barrier, 4)

    def cols(width, which):
        return pl.ds(pl.multiple_of(which * width, 128), width)

    taken = {"l": 0, "p": 0, "r": 0, "x": 0}

    def local(src, dst):
        copy = pltpu.make_async_copy(src, dst, local_sem.at[taken["l"]])
        taken["l"] += 1
        copy.start()
        return copy

    def remote(kind, src, dst, device):
        sends, recvs = {"p": (pair_send, pair_recv), "r": (ring_send, ring_recv), "x": (x_send, x_recv)}[kind]
        i = taken[kind]
        taken[kind] += 1
        copy = pltpu.make_async_remote_copy(
            src_ref=src, dst_ref=dst, send_sem=sends.at[i], recv_sem=recvs.at[i],
            device_id=device, device_id_type=MESH,
        )
        copy.start()
        return copy

    rhalf = wx.shape[1] // 2
    dhalf = wo.shape[1] // 2
    fhalf = wg.shape[1] // 2
    parts = [
        (wx, rhalf, lambda: o_xy.at[chip, core, x, :, pl.ds(0, rhalf)]),
        (wy, rhalf, lambda: o_xy.at[chip, core, x, :, pl.ds(rhalf, rhalf)]),
        (wo, dhalf, lambda: o_out.at[chip, core, x]),
        (wg, fhalf, lambda: o_gu.at[chip, core, :, pl.ds(0, fhalf)]),
        (wu, fhalf, lambda: o_gu.at[chip, core, :, pl.ds(fhalf, fhalf)]),
        (wd, fhalf, lambda: o_d.at[chip, core]),
    ]
    pair, mine = [], []
    for src, width, slot in parts[:3]:
        pair.append(remote("p", src.at[:, cols(width, other)], slot(), sib))
    for src, width, slot in parts[:3]:
        mine.append(local(src.at[:, cols(width, core)], slot()))
    mine.append(local(gs, o_gs.at[core, chip, x]))
    for src, width, slot in parts[3:]:
        pair.append(remote("p", src.at[:, cols(width, other)], slot(), sib))
    for src, width, slot in parts[3:]:
        mine.append(local(src.at[:, cols(width, core)], slot()))
    late = [
        remote("p", rows_in, o_rows.at[1], sib),
        remote("p", starts, o_starts.at[1], sib),
        remote("p", cot, o_cot.at[2], sib),
    ]
    plain = [local(rows_in, o_rows.at[0]), local(starts, o_starts.at[0]), local(cot, o_cot.at[0])]
    cot_x = remote("x", cot, o_cot.at[1], across)

    def rec_block(chip_id):
        return [o_xy.at[chip_id, :, x], o_out.at[chip_id, :, x], o_gs.at[core, chip_id, x]]

    def rec_half(chip_id, which):
        piece = [o_xy.at[chip_id, which, x], o_out.at[chip_id, which, x]]
        return piece + ([o_gs.at[core, chip_id, x]] if which == 0 else [])

    def ff_block(chip_id):
        return [o_gu.at[chip_id], o_d.at[chip_id]]

    def ff_half(chip_id, which):
        return [o_gu.at[chip_id, which], o_d.at[chip_id, which]]

    def send_all(kind, refs, device):
        return [remote(kind, ref, ref, device) for ref in refs]

    for copy in pair[:3]:
        copy.wait_recv()
    for copy in mine[:4]:
        copy.wait()
    sends, arrivals_x = [], []

    def step(block, piece, s, first):
        ahead = chip_at((pos + n - (s - 1)) % n, n)
        behind = chip_at((pos + s - 1) % n, n)
        if s < half:
            f = send_all("r", block(ahead), nxt)
            b = send_all("r", block(behind), prv)
        else:
            f = send_all("r", piece(ahead, 0), nxt)
            b = send_all("r", piece(behind, 1), prv)
        if first:
            arrivals_x.extend(send_all("x", block(ahead), across))
        return f, b

    f, b = step(rec_block, rec_half, 1, True)
    for s in range(2, half + 1):
        for copy in f + b:
            copy.wait_recv()
        sends.extend(f + b)
        ahead = chip_at((pos + n - (s - 1)) % n, n)
        behind = chip_at((pos + s - 1) % n, n)
        f, b = step(rec_block, rec_half, s, False)
        arrivals_x.extend(send_all("x", rec_block(ahead), across))
        arrivals_x.extend(send_all("x", rec_block(behind), across))
    rec_last = f + b
    for copy in pair[3:]:
        copy.wait_recv()
    for copy in mine[4:]:
        copy.wait()
    f, b = step(ff_block, ff_half, 1, False)
    for copy in rec_last:
        copy.wait_recv()
    sends.extend(rec_last)
    arrivals_x.extend(send_all("x", rec_block(chip_at((pos + half) % n, n)), across))
    cot_x.wait_recv()
    last_cot = remote("p", o_cot.at[1], o_cot.at[3], sib)
    for s in range(2, half + 1):
        for copy in f + b:
            copy.wait_recv()
        sends.extend(f + b)
        f, b = step(ff_block, ff_half, s, False)
    for copy in arrivals_x:
        copy.wait_recv()
    swap = remote("p", o_gs.at[core], o_gs.at[core], sib)
    for copy in f + b:
        copy.wait_recv()
    sends.extend(f + b)
    swap.wait_recv()
    last_cot.wait_recv()
    for copy in late:
        copy.wait_recv()
    for copy in plain:
        copy.wait()
    for copy in pair + late + [cot_x, last_cot, swap] + sends + arrivals_x:
        copy.wait_send()


def gather_weights(n, wx, wy, wo, gs, wg, wu, wd, rows_in, cot, starts):
    r, d, f = wx.shape[1], wo.shape[1], wg.shape[1]
    half = n // 2
    tokens = rows_in.shape[0]
    shapes = [
        jax.ShapeDtypeStruct((n, 2, 2, wx.shape[0], r), BF16),
        jax.ShapeDtypeStruct((n, 2, 2, wo.shape[0], d // 2), BF16),
        jax.ShapeDtypeStruct((2, n, 2) + gs.shape, BF16),
        jax.ShapeDtypeStruct((n, 2, wg.shape[0], f), BF16),
        jax.ShapeDtypeStruct((n, 2, wg.shape[0], f // 2), BF16),
        jax.ShapeDtypeStruct((2, tokens, d), BF16),
        jax.ShapeDtypeStruct((4, tokens, d), BF16),
        jax.ShapeDtypeStruct((2,) + starts.shape, F32),
    ]
    pairs, ring, over = 11, half * 10 - 1, 3 * n + 1
    dma = pltpu.SemaphoreType.DMA
    result = pl.pallas_call(
        functools.partial(gather_kernel, n),
        out_shape=shapes,
        in_specs=[pl.BlockSpec(memory_space=pl.ANY)] * 10,
        out_specs=[pl.BlockSpec(memory_space=pl.ANY)] * 8,
        scratch_shapes=[
            dma((10,)), dma((pairs,)), dma((pairs,)), dma((ring,)), dma((ring,)), dma((over,)), dma((over,)),
        ],
        compiler_params=pltpu.CompilerParams(collective_id=0, has_side_effects=True),
        name="gather_weights",
    )(wx, wy, wo, gs, wg, wu, wd, rows_in, cot, starts)
    return result


def minus_expm1(v):
    series = jnp.ones_like(v)
    for k in range(9, 1, -1):
        series = 1.0 + series * v * (1.0 / k)
    return jnp.where(v > -0.5, -v * series, 1.0 - jnp.exp(v))


def gates_of(u, weights, cp, start):
    tokens = u.shape[0] * u.shape[1]
    flat = u.reshape(tokens, BLK)
    z = jnp.dot(flat, weights, preferred_element_type=F32)
    r = jax.nn.sigmoid(z[:, :BLK] + cp[5:6]).reshape(u.shape)
    ig = jax.nn.sigmoid(z[:, BLK:] + cp[6:7]).reshape(u.shape)
    la = -8.0 * r * cp[7:8][None]
    decayed = jnp.exp(la)
    rest = minus_expm1(2.0 * la)
    return r, ig, decayed, rest


def recurrence_kernel(xb, halo, weights, cp, starts, u_ref, a_ref, h_ref, c_ref, b_ref):
    rows, length = xb.shape[0], xb.shape[1]
    p = cp[...]
    us = []
    for row in range(rows):
        padded = jnp.concatenate([halo[row], xb[row].astype(F32)], axis=0)
        total = p[4:5] + p[0:1] * padded[8 : 8 + length]
        for k in range(1, 4):
            total = total + p[k : k + 1] * padded[8 - k : 8 - k + length]
        us.append(total.astype(BF16))
    u = jnp.stack(us)
    u_ref[...] = u
    start = starts[...]
    start = jnp.concatenate([start, start], axis=2)
    r, ig, decayed, rest = gates_of(u, weights[...], p, start)
    a_ref[...] = decayed * (1.0 - start)
    b_ref[...] = jnp.where(start > 0.5, 1.0, jnp.sqrt(rest)) * ig * u.astype(F32)

    def eight(i, carry):
        at = pl.ds(pl.multiple_of(i * 8, 8), 8)
        out = []
        for row in range(rows):
            h, c = carry[row]
            a, b = a_ref[row, at, :], b_ref[row, at, :]
            hs, cs = [], []
            for j in range(8):
                h = a[j : j + 1] * h + b[j : j + 1]
                c = a[j : j + 1] * c
                hs.append(h)
                cs.append(c)
            h_ref[row, at, :] = jnp.concatenate(hs, axis=0)
            c_ref[row, at, :] = jnp.concatenate(cs, axis=0)
            out.append((h, c))
        return tuple(out)

    zero, one = jnp.zeros((1, BLK), F32), jnp.ones((1, BLK), F32)
    lax.fori_loop(0, length // 8, eight, ((zero, one),) * rows)


def recurrence(xb, halo, weights, cp, starts):
    rows, length, channels = xb.shape
    wide = pl.BlockSpec((rows, length, BLK), lambda h: (0, 0, h))
    return pl.pallas_call(
        recurrence_kernel,
        grid=(channels // BLK,),
        in_specs=[
            wide,
            pl.BlockSpec((rows, 8, BLK), lambda h: (0, 0, h)),
            pl.BlockSpec((BLK, 2 * BLK), lambda h: (h, 0)),
            pl.BlockSpec((cp.shape[0], BLK), lambda h: (0, h)),
            pl.BlockSpec(starts.shape, lambda h: (0, 0, 0)),
        ],
        out_specs=[wide] * 4,
        out_shape=[jax.ShapeDtypeStruct(xb.shape, BF16)] + [jax.ShapeDtypeStruct(xb.shape, F32)] * 3,
        scratch_shapes=[pltpu.VMEM((rows, length, BLK), F32)],
        compiler_params=pltpu.CompilerParams(vmem_limit_bytes=40 << 20),
        cost_estimate=pl.CostEstimate(flops=4 * 10**8, bytes_accessed=6 * 10**6, transcendentals=2 * 10**6),
        name="recurrence",
    )(xb, halo, weights, cp, starts)


def gelu_parts(v):
    inner = 0.7978845608028654 * (v + 0.044715 * v * v * v)
    t = jnp.tanh(inner)
    value = 0.5 * v * (1.0 + t)
    slope = 0.5 * (1.0 + t) + 0.5 * v * (1.0 - t * t) * 0.7978845608028654 * (1.0 + 3.0 * 0.044715 * v * v)
    return value, slope


def adjoint_kernel(do, h_ref, y_ref, a_ref, dy_ref, lam_ref, c_ref, dh_ref):
    rows, length = do.shape[0], do.shape[1]
    value, slope = gelu_parts(y_ref[...])
    dy_ref[...] = (do[...] * h_ref[...] * slope).astype(BF16)
    dh_ref[...] = do[...] * value

    def eight(step, carry):
        i = length // 8 - 1 - step
        at = pl.ds(pl.multiple_of(i * 8, 8), 8)
        out = []
        for row in range(rows):
            ahead, c = carry[row]
            a, d = a_ref[row, at, :], dh_ref[row, at, :]
            ls, cs = [None] * 8, [None] * 8
            for j in range(7, -1, -1):
                lam = d[j : j + 1] + ahead
                ls[j], cs[j] = lam, c
                ahead = a[j : j + 1] * lam
                c = a[j : j + 1] * c
            lam_ref[row, at, :] = jnp.concatenate(ls, axis=0)
            c_ref[row, at, :] = jnp.concatenate(cs, axis=0)
            out.append((ahead, c))
        return tuple(out)

    zero, one = jnp.zeros((1, BLK), F32), jnp.ones((1, BLK), F32)
    lax.fori_loop(0, length // 8, eight, ((zero, one),) * rows)


def adjoint(do, h, ypre, a):
    rows, length, channels = do.shape
    wide = pl.BlockSpec((rows, length, BLK), lambda i: (0, 0, i))
    return pl.pallas_call(
        adjoint_kernel,
        grid=(channels // BLK,),
        in_specs=[wide] * 4,
        out_specs=[wide] * 3,
        out_shape=[jax.ShapeDtypeStruct(do.shape, BF16)] + [jax.ShapeDtypeStruct(do.shape, F32)] * 2,
        scratch_shapes=[pltpu.VMEM((rows, length, BLK), F32)],
        compiler_params=pltpu.CompilerParams(vmem_limit_bytes=40 << 20),
        cost_estimate=pl.CostEstimate(flops=10**7, bytes_accessed=9 * 10**6, transcendentals=10**6),
        name="adjoint",
    )(do, h, ypre, a)


def gates_back_kernel(lam_ref, c_ref, inc, h_ref, h_in, u_ref, weights, cp, starts, du_ref, dw_ref, sums_ref):
    rows, length = u_ref.shape[0], u_ref.shape[1]
    tokens = rows * length
    p = cp[...]
    u = u_ref[...]
    uf = u.astype(F32)
    start = starts[...]
    start = jnp.concatenate([start, start], axis=2)
    w = weights[...]
    r, ig, decayed, rest = gates_of(u, w, p, start)
    mult = jnp.where(start > 0.5, 1.0, jnp.sqrt(rest))
    lam = lam_ref[...] + c_ref[...] * inc[...]
    before = jnp.stack([jnp.concatenate([h_in[row], h_ref[row][: length - 1]], axis=0) for row in range(rows)])
    keep = 1.0 - start
    d_la = lam * before * decayed * keep - jnp.where(
        start > 0.5, 0.0, lam * ig * uf * decayed * decayed * lax.rsqrt(jnp.where(start > 0.5, 1.0, rest))
    )
    dpa = d_la * (-8.0 * p[7:8][None]) * r * (1.0 - r)
    direct = lam * mult
    dpi = direct * uf * ig * (1.0 - ig)
    d_decay = d_la * (8.0 * p[8:9][None]) * r
    dz = jnp.concatenate(
        [dpa.reshape(tokens, BLK).astype(BF16), dpi.reshape(tokens, BLK).astype(BF16)], axis=1
    )
    back = lax.dot_general(dz, w, (((1,), (1,)), ((), ())), preferred_element_type=F32)
    du_ref[...] = (direct * ig + back.reshape(u.shape)).astype(BF16)
    dw_ref[...] = lax.dot_general(
        u.reshape(tokens, BLK), dz, (((0,), (0,)), ((), ())), preferred_element_type=F32
    )
    zero = jnp.zeros((5, BLK), F32)
    sums_ref[...] = jnp.concatenate(
        [jnp.sum(v.reshape(tokens, BLK), axis=0, keepdims=True) for v in (dpa, dpi, d_decay)] + [zero], axis=0
    )


def gates_back(lam, coef, inc, h, h_in, u, weights, cp, starts):
    rows, length, channels = u.shape
    wide = pl.BlockSpec((rows, length, BLK), lambda i: (0, 0, i))
    line = pl.BlockSpec((rows, 1, BLK), lambda i: (0, 0, i))
    square = pl.BlockSpec((BLK, 2 * BLK), lambda i: (i, 0))
    return pl.pallas_call(
        gates_back_kernel,
        grid=(channels // BLK,),
        in_specs=[
            wide, wide, line, wide, line, wide, square,
            pl.BlockSpec((cp.shape[0], BLK), lambda i: (0, i)),
            pl.BlockSpec(starts.shape, lambda i: (0, 0, 0)),
        ],
        out_specs=[wide, square, pl.BlockSpec((8, BLK), lambda i: (0, i))],
        out_shape=[
            jax.ShapeDtypeStruct(u.shape, BF16),
            jax.ShapeDtypeStruct((channels, 2 * BLK), F32),
            jax.ShapeDtypeStruct((8, channels), F32),
        ],
        compiler_params=pltpu.CompilerParams(vmem_limit_bytes=40 << 20),
        cost_estimate=pl.CostEstimate(flops=12 * 10**8, bytes_accessed=9 * 10**6, transcendentals=2 * 10**6),
        name="gates_back",
    )(lam, coef, inc, h, h_in, u, weights, cp, starts)


def nt(left, right):
    return lax.dot_general(left, right, (((1,), (1,)), ((), ())), preferred_element_type=F32)


def nn(left, right):
    return jnp.dot(left, right, preferred_element_type=F32)


def body(
    dp_size,
    layer_input, grad_out, lengths, resets, norm_gain, w_x, w_y, conv_w, conv_b, gate_a_w, gate_a_b,
    gate_i_w, gate_i_b, decay_param, w_out, mlp_gain, w_gate, w_up, w_down,
):
    n = dp_size // 2
    half = n // 2
    dp, x = lax.axis_index("dp"), lax.axis_index("tp")
    chip, core = dp // 2, dp % 2
    pos = place_of(chip, n)
    tokens, width = layer_input.shape[1], layer_input.shape[2]
    rec = w_x.shape[1]
    rh = rec // 2
    taps = conv_w.shape[0]
    own = rec // (2 * dp_size)
    own_d = width // (2 * dp_size)

    ring = [chip_at(i, n) for i in range(n)]
    up = [(ring[i] * 2 + c, ring[(i + 1) % n] * 2 + c) for i in range(n) for c in range(2)]
    down = [(b, a) for a, b in up]
    pairs = [(d, d + 1 - 2 * (d % 2)) for d in range(dp_size)]

    def sibling(v):
        return lax.ppermute(v, "dp", pairs)

    def across(v):
        return lax.ppermute(v, "tp", [(0, 1), (1, 0)])

    def swapped(v):
        return jnp.concatenate([v[1:], v[:1]], axis=0)

    def by_core(mine, theirs, axis):
        return jnp.where(
            core == 0, jnp.concatenate([mine, theirs], axis), jnp.concatenate([theirs, mine], axis)
        )

    rows_own = layer_input.reshape(tokens, width)
    place = x * tokens + jnp.arange(tokens, dtype=jnp.int32)
    starts = jnp.where((resets.reshape(tokens) > 0) | (place == 0), 1.0, 0.0).astype(F32)
    starts = jnp.broadcast_to(starts[:, None], (tokens, 128))
    valid = (place < lengths[0]).astype(F32)[:, None]
    cot = grad_out.reshape(tokens, width).astype(F32) * valid

    small = jnp.concatenate(
        [norm_gain, mlp_gain, conv_w.reshape(-1), conv_b, gate_a_b, gate_i_b, decay_param]
    )
    small = jnp.pad(small, (0, PAD * WIDE - small.shape[0])).reshape(PAD, WIDE)
    gs = jnp.concatenate([jnp.concatenate([gate_a_w, gate_i_w], axis=1), small], axis=0)
    w_xy, w_o, all_gs, w_gu, w_d, rows_two, cot_all, starts_two = gather_weights(
        n, w_x, w_y, w_out, gs, w_gate, w_up, w_down.T, rows_own, cot.astype(BF16), starts
    )
    w_xy = w_xy.reshape(width, rec)
    w_o = w_o.reshape(rec, width // 2)
    w_gu = w_gu.reshape(width, w_gate.shape[1])
    w_d = w_d.reshape(width, w_gate.shape[1] // 2)
    cot_all = cot_all.reshape(4 * tokens, width)

    vectors = all_gs[:, :, :, own:].transpose(1, 0, 2, 3, 4).reshape(2 * dp_size, PAD * WIDE)
    gain_one = vectors[:, :own_d].reshape(width).astype(F32)
    gain_two = vectors[:, own_d : 2 * own_d].reshape(width).astype(F32)
    lines = vectors[:, 2 * own_d : 2 * own_d + (taps + 4) * own].reshape(2 * dp_size, taps + 4, own)
    lines = lax.dynamic_slice_in_dim(lines, core * dp_size, dp_size, 0)
    lines = lines.transpose(1, 0, 2).reshape(taps + 4, rh).astype(F32)
    decay = lines[taps + 3 :]
    cp = jnp.concatenate(
        [lines[: taps + 3], jax.nn.softplus(-decay), jax.nn.sigmoid(-decay), jnp.zeros((7, rh), F32)], axis=0
    )
    gates = lax.dynamic_slice_in_dim(all_gs[:, :, :, :own], core * half, half, 1)
    gates = gates.transpose(1, 0, 2, 3, 4).reshape(rh, WIDE)

    rows_f = rows_two.astype(F32)
    rs1 = lax.rsqrt(jnp.mean(rows_f * rows_f, axis=-1, keepdims=True) + EPS)
    n1 = (rows_f * rs1 * gain_one).astype(BF16).reshape(2 * tokens, width)
    xy = nn(n1, w_xy)
    xb = xy[:, :rh].astype(BF16).reshape(2, tokens, rh)
    ypre = xy[:, rh:].reshape(2, tokens, rh)
    before = lax.ppermute(xb[:, tokens - (taps - 1) :], "tp", [(0, 1)])
    halo = jnp.concatenate([jnp.zeros((2, 8 - (taps - 1), rh), F32), before.astype(F32)], axis=1)
    u, a, h_local, coef = recurrence(xb, halo, gates, cp, starts_two)
    h_in = lax.ppermute(h_local[:, tokens - 1 :], "tp", [(0, 1)])
    h = h_local + coef * h_in
    ybr, _ = gelu_parts(ypre)
    o = (h * ybr).astype(BF16)
    o_sib = swapped(sibling(o))
    o_full = by_core(o, o_sib, 2).reshape(2 * tokens, rec)
    part = nn(o_full, w_o).reshape(2, tokens, width // 2)
    x1 = rows_own.astype(F32) + by_core(part[0], sibling(part[1]), 1)
    rs2 = lax.rsqrt(jnp.mean(x1 * x1, axis=-1, keepdims=True) + EPS)
    n2 = (x1 * rs2 * gain_two).astype(BF16)
    two = jnp.concatenate([n2, across(n2)], axis=0)
    n2_all = jnp.concatenate([two, sibling(two)], axis=0)

    fh = w_d.shape[1]
    gu = nn(n2_all, w_gu)
    gate, upv = gu[:, :fh], gu[:, fh:]
    act, slope = gelu_parts(gate)
    hidden = (act * upv).astype(BF16)
    d_hidden = nn(cot_all, w_d)
    d_gu = jnp.concatenate([(d_hidden * upv * slope).astype(BF16), (d_hidden * act).astype(BF16)], axis=1)

    def gathered_sum(partial):
        partial = partial.astype(BF16)
        kept = partial[: 2 * tokens].astype(F32) + sibling(partial[2 * tokens :]).astype(F32)
        kept = kept.astype(BF16)
        return kept[:tokens].astype(F32) + across(kept[tokens:]).astype(F32)

    d_n2 = gathered_sum(nt(d_gu, w_gu))

    def chip_rel(k):
        return chip_at((pos + k) % n, n)

    def ring_sum(product):
        def way(perm, sign, far):
            out = {}
            for which in (0, 1):
                first = half if which == far else half - 1
                got = None
                for k in range(first, 0, -1):
                    term = product(chip_rel((sign * k) % n), which)
                    send = term if got is None else term + got.astype(F32)
                    got = lax.ppermute(send.astype(BF16), "dp", perm)
                out[which] = got
            return out

        f, b = way(up, 1, 0), way(down, -1, 1)
        return [product(chip, w) + f[w].astype(F32) + b[w].astype(F32) for w in (0, 1)]

    def pick(array, chip_id, which):
        other = core + which - 2 * core * which
        index = (chip_id, other) + (0,) * (array.ndim - 2)
        return lax.dynamic_slice(array, index, (1, 1) + array.shape[2:]).reshape(array.shape[2:])

    cot_t = cot_all.T.reshape(n, 2, width // dp_size, 4 * tokens)
    n2_t = n2_all.T.reshape(n, 2, width // dp_size, 4 * tokens)
    sum_d = ring_sum(lambda chip_id, which: nn(pick(cot_t, chip_id, which), hidden))
    sum_gu = ring_sum(lambda chip_id, which: nn(pick(n2_t, chip_id, which), d_gu))
    ff_out = gathered_sum(nt(hidden, w_d))
    result = (x1 + ff_out).astype(BF16).reshape(1, tokens, width)

    q2 = gain_two * d_n2
    d_gain_two = jnp.sum(d_n2 * x1 * rs2, axis=0)
    d_x1 = cot + rs2 * q2 - x1 * (rs2 * rs2 * rs2) * jnp.mean(x1 * q2, axis=-1, keepdims=True)
    dbr = d_x1.astype(BF16)
    dbr_mine = lax.dynamic_slice_in_dim(dbr, core * (width // 2), width // 2, 1)
    dbr_theirs = lax.dynamic_slice_in_dim(dbr, (1 - core) * (width // 2), width // 2, 1)
    dbr_half = jnp.concatenate([dbr_mine, sibling(dbr_theirs)], axis=0)
    do_part = nt(dbr_half, w_o)
    do_mine = lax.dynamic_slice_in_dim(do_part, core * rh, rh, 1).reshape(2, tokens, rh)
    do_theirs = lax.dynamic_slice_in_dim(do_part, (1 - core) * rh, rh, 1).reshape(2, tokens, rh)
    do = do_mine + swapped(sibling(do_theirs))

    d_ypre, lam_local, coef_back = adjoint(do, h, ypre, a)
    inc = lax.ppermute(a[:, :1] * lam_local[:, :1], "tp", [(1, 0)])
    du, d_gates, sums = gates_back(lam_local, coef_back, inc, h, h_in, u, gates, cp, starts_two)
    after = lax.ppermute(du[:, : taps - 1], "tp", [(1, 0)])
    du_pad = jnp.concatenate([du, after], axis=1).astype(F32)
    xb_pad = jnp.concatenate([before, xb], axis=1).astype(F32)
    d_taps = jnp.stack(
        [jnp.sum(du_pad[:, :tokens] * xb_pad[:, taps - 1 - k : taps - 1 - k + tokens], axis=(0, 1)) for k in range(taps)]
    )
    d_bias = jnp.sum(du_pad[:, :tokens], axis=(0, 1))[None]
    d_xb = sum(cp[k] * du_pad[:, k : k + tokens] for k in range(taps)).astype(BF16)
    d_xy = jnp.concatenate([d_xb, d_ypre], axis=2).reshape(2 * tokens, rec)
    d_n1_part = nt(d_xy, w_xy).reshape(2, tokens, width)
    d_n1 = d_n1_part[0] + sibling(d_n1_part[1])
    q1 = gain_one * d_n1
    own_f, own_rs = rows_f[0], rs1[0]
    d_gain_one = jnp.sum(d_n1 * own_f * own_rs, axis=0)
    grad_x = d_x1 + own_rs * q1 - own_f * (own_rs * own_rs * own_rs) * jnp.mean(own_f * q1, axis=-1, keepdims=True)

    def plane(array, which):
        return lax.dynamic_index_in_dim(array, which, 2, keepdims=False)

    def both(mine, axis):
        return jnp.concatenate([mine, across(mine)], axis)

    def plane_rows(values, rows):
        grouped = values.T.reshape(n, 2, 2, rows, 2 * tokens)
        return jnp.concatenate([plane(grouped, x), across(plane(grouped, 1 - x))], axis=3)

    o_t = plane_rows(o_full, own)
    dbr_x = both(dbr_half, 0)
    sum_out = ring_sum(lambda chip_id, which: nn(pick(o_t, chip_id, which), dbr_x))
    n1_t = plane_rows(n1, own_d)
    d_xy_x = both(d_xy, 0)
    sum_xy = ring_sum(lambda chip_id, which: nn(pick(n1_t, chip_id, which), d_xy_x))

    def placed(part):
        zero = jnp.zeros_like(part)
        return by_core_rows(part, zero)

    def by_core_rows(mine, theirs):
        return jnp.where(
            core == 0, jnp.concatenate([mine, theirs], 0), jnp.concatenate([theirs, mine], 0)
        )

    g = d_gates.reshape(half, 2, 2, own, WIDE)
    g = plane(g, x) + across(plane(g, 1 - x).astype(BF16)).astype(F32)
    g_mine = lax.dynamic_index_in_dim(g, core, 1, keepdims=False)
    g_theirs = lax.dynamic_index_in_dim(g, 1 - core, 1, keepdims=False)
    g_lane = by_core_rows(g_mine, sibling(g_theirs))

    lines_back = jnp.concatenate([d_taps, d_bias, sums[:3]], axis=0)
    lines_back = lines_back.reshape(taps + 4, half, 2, 2, own).transpose(1, 2, 3, 0, 4)
    lines_back = placed(lines_back.reshape(half, 2, 2, (taps + 4) * own))
    gains = jnp.concatenate([d_gain_one.reshape(n, 2, 2, own_d), d_gain_two.reshape(n, 2, 2, own_d)], axis=3)
    vec = jnp.concatenate([gains, lines_back], axis=3)
    vec = jnp.pad(vec, ((0, 0), (0, 0), (0, 0), (0, -vec.shape[3] % 128)))
    vec = plane(vec, x) + across(plane(vec, 1 - x))
    vec = lax.dynamic_index_in_dim(vec, core, 1, keepdims=False) + sibling(
        lax.dynamic_index_in_dim(vec, 1 - core, 1, keepdims=False)
    )

    def lane_sum(array):
        def at(chip_id):
            return lax.dynamic_index_in_dim(array, chip_id, 0, keepdims=False)

        total = at(chip)
        for perm, sign, first in ((up, 1, half), (down, -1, half - 1)):
            got = None
            for k in range(first, 0, -1):
                term = at(chip_rel((sign * k) % n))
                send = term if got is None else term + got.astype(F32)
                got = lax.ppermute(send, "dp", perm)
            total = total + got
        return total

    sum_gates = lane_sum(g_lane)
    sum_vec = lane_sum(vec)

    def whole(halves, axis):
        return by_core(halves[0], sibling(halves[1]), axis)

    gu0, gu1 = sum_gu
    grad_gate = whole((gu0[:, :fh], gu1[:, :fh]), 1)
    grad_up = whole((gu0[:, fh:], gu1[:, fh:]), 1)
    grad_down = whole(sum_d, 1).T
    grad_w_x = whole((sum_xy[0][:, :rh], sum_xy[1][:, :rh]), 1)
    grad_w_y = whole((sum_xy[0][:, rh:], sum_xy[1][:, rh:]), 1)
    grad_w_out = whole(sum_out, 1)
    tail = sum_vec[2 * own_d : 2 * own_d + (taps + 4) * own].reshape(taps + 4, own)
    return (
        result,
        grad_x.reshape(1, tokens, width),
        sum_vec[:own_d],
        grad_w_x,
        grad_w_y,
        tail[:taps],
        tail[taps],
        sum_gates[:, :BLK],
        tail[taps + 1],
        sum_gates[:, BLK:],
        tail[taps + 2],
        tail[taps + 3],
        grad_w_out,
        sum_vec[own_d : 2 * own_d],
        grad_gate,
        grad_up,
        grad_down,
    )


def solution(mesh):
    every = ("dp", "tp")
    return jax.shard_map(
        functools.partial(body, mesh.shape["dp"]),
        mesh=mesh,
        in_specs=(
            P("dp", "tp", None),
            P("dp", "tp", None),
            P("dp"),
            P("dp", "tp"),
            P(every),
            P(every, None),
            P(every, None),
            P(None, every),
            P(every),
            P(every, None),
            P(every),
            P(every, None),
            P(every),
            P(every),
            P(every, None),
            P(every),
            P("dp", "tp"),
            P("dp", "tp"),
            P("tp", "dp"),
        ),
        out_specs=(
            P("dp", "tp", None),
            P("dp", "tp", None),
            P(every),
            P(every, None),
            P(every, None),
            P(None, every),
            P(every),
            P(every, None),
            P(every),
            P(every, None),
            P(every),
            P(every),
            P(every, None),
            P(every),
            P("dp", "tp"),
            P("dp", "tp"),
            P("tp", "dp"),
        ),
        check_vma=False,
    )
```

time: 3580 us -> 911 us (0.25)
  waiting for transfers between devices: 2730 us -> 247 us
  Pallas kernels: 0 us -> 306 us
  local copies, waits for them, and re-layouts: 348 us -> 59.9 us
  blocking collectives: 165 us -> 0 us
  starting transfers between devices: 6.93 us -> 90.7 us
  other arithmetic: 117 us -> 53 us
  matrix products: 179 us -> 140 us
    reduce_scatter x8 -> x0, waiting for transfers between devices: 2320 us -> none  [the longest x1 703 us: body(): lax.psum_scatter(dot_outer(left_pair, right_pair), 'dp', scatter_dimensio...]
    all_gather x10 -> x0, waiting for transfers between devices: 402 us -> none  [the longest x1 106 us: body(): lax.all_gather(w_down, 'dp', axis=1, tiled=True)]
    pallas_call x0 -> x4, Pallas kernels: none -> 306 us  [the longest x1 288 us: gather_weights(): pl.pallas_call(functools.partial(gather_kernel, n), out_shape=shapes, in_...]
    ppermute x2 -> x99, waiting for transfers between devices: 4.85 us -> 247 us  [the longest x56 151 us: way(): got = lax.ppermute(send.astype(BF16), 'dp', perm)]
    slice x97 -> x27, local copies, waits for them, and re-layouts: 197 us -> 13.8 us  [the longest x2 2.54 us: body(): grad_up = whole((gu0[:, fh:], gu1[:, fh:]), 1)]
    all_gather x5 -> x0, blocking collectives: 88.4 us -> none  [the longest x1 70.5 us: body(): lax.all_gather(conv_w, ('dp', 'tp'), axis=1, tiled=True)]
    ppermute x2 -> x99, starting transfers between devices: 5.6 us -> 90.7 us  [the longest x56 56.7 us: way(): got = lax.ppermute(send.astype(BF16), 'dp', perm)]
    pad x48 -> x1, local copies, waits for them, and re-layouts: 79 us -> 0.01 us  [body(): small = jnp.pad(small, (0, PAD * WIDE - small.shape[0])).reshape(PAD, WIDE)]
  transfers between devices with their start and end apart: 21 -> 99, of which waited for: 16 -> 42; matrix products, arithmetic and copies ran while one was open for 10% -> 23% of each run, Pallas kernels for 0% -> 1%
where the time goes in v1:
time: 911 us; the launch traced here: 900 us
  Pallas kernels  306 us (34%)
  waiting for transfers between devices  247 us (27%)
  matrix products  140 us (15%)
  starting transfers between devices  90.7 us (10%)
  local copies, waits for them, and re-layouts  59.9 us (7%)
  other arithmetic  53 us (6%)
    pallas_call x1, Pallas kernels, gather_weights(): pl.pallas_call(functools.partial(gather_kernel, n), out_shape=shapes, in_...  288 us
    ppermute x56, waiting for transfers between devices, way(): got = lax.ppermute(send.astype(BF16), 'dp', perm)  151 us
    dot_general x68, matrix products, nn(): return jnp.dot(left, right, preferred_element_type=F32)  121 us
    ppermute x9, waiting for transfers between devices, across(): return lax.ppermute(v, 'tp', [(0, 1), (1, 0)])  71.3 us
    ppermute x56, starting transfers between devices, way(): got = lax.ppermute(send.astype(BF16), 'dp', perm)  56.7 us
    dot_general x4, matrix products, nt(): lax.dot_general(left, right, (((1,), (1,)), ((), ())), preferred_element_...  18.8 us
  transfers between devices with their start and end apart: 99, of which 42 were waited for; matrix products, arithmetic and copies ran while one was open for 23% of the time, Pallas kernels for 1%

profile of v1, /device:TPU:0, one launch (start us, length us, event | category | flops | bytes accessed | tf_op | source)
XLA Modules:
  0.0 900.4 jit_solution(12482808546137049879)
XLA Ops:
  2.0 2.3 copy.39
  5.1 4.1 concatenate.144
  12.6 288.0 %gather_weights.1 = (bf16[8,2,2,64,2560]{4,3,2,1,0:T(8,128)(2,1)}, bf16[8,2,2,80,1024]{4,3,2,1,0:T(8,128)(2,1)}, bf16[2,8,2,96,512]{4,3,2,1,0:T(8,128)(2,1)}, bf...) custom-call(bf16[64,2560]{1,0:T(8,128)(2,1)} %wx.1, ...), custom_call_target="tpu_custom_call" | custom-call | tf_op jit(solution)/shard_map/gather_weights/pallas_call | solution.py:194
  302.9 6.0 fusion.388
  311.1 4.3 collective-permute-start
  319.6 6.9 recurrence.1
  339.8 4.5 fusion.389
  350.7 2.4 collective-permute-start.4
  353.1 12.3 %collective-permute-done.4 = bf16[128,2048]{1,0:T(8,128)(2,1)S(1)} collective-permute-done((bf16[128,2048]{1,0:T(8,128)(2,1)S(1)}, bf16[128,2048]{1,0:T(8,128)(2,1)S(1)}, u32[]{:S(2)}, u32[]{:S(2)}) %collective-permute-start.4) | collective-permute-done | bytes 524320 | tf_op jit(solution)/shard_map/ppermute | solution.py:434
  366.6 2.5 copy.48
  369.1 2.3 dynamic-slice_bitcast_fusion.5
  373.1 2.8 convert_element_type.476
  375.9 3.9 copy.65
  387.3 9.9 %fusion.52 = f32[512,3072]{1,0:T(8,128)S(1)} fusion(bf16[2048,3072]{1,0:T(8,128)(2,1)} %bitcast.450, bf16[256,2048]{1,0:T(8,128)(2,1)} %collective-permute-done.5, bf16[128,2048]{1,0:T(8,128)(2,1)S(1)} %copy-done.40, bf16[128,2048]{1,0:T(8,128)(2,1)S(1)} %copy-done.24), kind=kOutput, calls=%fused_computation.218 | convolution fusion | flops 6448742400 | bytes 20971520 | tf_op jit(solution)/shard_map/dot_general | solution.py:405
  397.3 6.5 fusion.18
  403.8 2.3 fusion.88
  408.3 2.2 fusion.70
  410.5 2.2 fusion.63
  414.8 2.2 fusion.72
  418.3 2.9 fusion.51
  421.2 3.9 copy.67
  425.1 2.7 convolution_convert_fusion.3
  435.0 3.7 convolution_convert_fusion.9
  438.7 10.6 %convolution_convert_fusion.8 = bf16[512,2048]{1,0:T(8,128)(2,1)S(1)} fusion(bf16[2048,3072]{1,0:T(8,128)(2,1)} %bitcast.451, bf16[512,1536]{1,0:T(8,128)(2,1)} %get-tuple-element.117, bf16[512,1536]{1,0:T(8,128)(2,1)S(1)} %copy-done.73), kind=kOutput, calls=%fused_computation.108 | convolution fusion | flops 6449790976 | bytes 17825792 | tf_op jit(solution)/shard_map/dot_general | solution.py:401
  455.5 5.8 collective-permute-done.84
  464.2 5.6 collective-permute-done.91
  472.6 21.7 %collective-permute-done.85 = bf16[128,1536]{1,0:T(8,128)(2,1)S(1)} collective-permute-done((bf16[128,1536]{1,0:T(8,128)(2,1)S(1)}, bf16[128,1536]{1,0:T(8,128)(2,1)S(1)}, u32[]{:S(2)}, u32[]{:S(2)}) %collective-permute-start.85) | collective-permute-done | bytes 393248 | tf_op jit(solution)/shard_map/ppermute | solution.py:528
  495.0 9.7 %collective-permute-done.89 = bf16[128,1536]{1,0:T(8,128)(2,1)S(1)} collective-permute-done((bf16[128,1536]{1,0:T(8,128)(2,1)S(1)}, bf16[128,1536]{1,0:T(8,128)(2,1)S(1)}, u32[]{:S(2)}, u32[]{:S(2)}) %collective-permute-start.89) | collective-permute-done | bytes 393248 | tf_op jit(solution)/shard_map/ppermute | solution.py:528
  510.0 21.0 %collective-permute-done.92 = bf16[128,1536]{1,0:T(8,128)(2,1)S(1)} collective-permute-done((bf16[128,1536]{1,0:T(8,128)(2,1)S(1)}, bf16[128,1536]{1,0:T(8,128)(2,1)S(1)}, u32[]{:S(2)}, u32[]{:S(2)}) %collective-permute-start.92) | collective-permute-done | bytes 393248 | tf_op jit(solution)/shard_map/ppermute | solution.py:528
  534.9 8.5 collective-permute-done.95
  548.6 6.8 collective-permute-done.86
  559.2 13.1 %collective-permute-done.69 = bf16[128,3072]{1,0:T(8,128)(2,1)S(1)} collective-permute-done((bf16[128,3072]{1,0:T(8,128)(2,1)S(1)}, bf16[128,3072]{1,0:T(8,128)(2,1)S(1)}, u32[]{:S(2)}, u32[]{:S(2)}) %collective-permute-start.69) | collective-permute-done | bytes 786464 | tf_op jit(solution)/shard_map/ppermute | solution.py:528
  576.8 7.2 collective-permute-done.9
  585.2 2.7 collective-permute-done.76
  590.1 5.0 collective-permute-done.7
  596.3 3.7 fusion.375
  600.1 6.4 collective-permute-done.79
  607.7 2.3 add_convert_fusion.3
  613.2 5.3 collective-permute-done.93
  619.2 2.9 collective-permute-done.97
  628.6 9.1 %collective-permute-done.52 = bf16[256,1024]{1,0:T(8,128)(2,1)S(1)} collective-permute-done((bf16[256,1024]{1,0:T(8,128)(2,1)S(1)}, bf16[256,1024]{1,0:T(8,128)(2,1)S(1)}, u32[]{:S(2)}, u32[]{:S(2)}) %collective-permute-start.52) | collective-permute-done | bytes 524320 | tf_op jit(solution)/shard_map/ppermute | solution.py:434
  645.4 2.4 add_convert_fusion.9
  648.5 2.4 add_convert_fusion.2
  653.5 3.0 copy.66
  681.1 3.4 collective-permute-done.65
  687.7 3.2 collective-permute-done.56
  694.8 3.2 collective-permute-done.66
  704.8 4.7 adjoint.1
  709.6 15.7 %collective-permute-done.71 = bf16[128,3072]{1,0:T(8,128)(2,1)S(1)} collective-permute-done((bf16[128,3072]{1,0:T(8,128)(2,1)S(1)}, bf16[128,3072]{1,0:T(8,128)(2,1)S(1)}, u32[]{:S(2)}, u32[]{:S(2)}) %collective-permute-start.71) | collective-permute-done | bytes 786464 | tf_op jit(solution)/shard_map/ppermute | solution.py:528
  728.0 2.8 collective-permute-done.12.inc
  730.9 6.6 gates_back.1
  739.3 4.1 collective-permute-done.13
  745.7 2.9 fusion.390
  754.6 2.3 maximum_select_fusion.8
  761.4 10.9 %collective-permute-done.42 = bf16[4,2,80,512]{3,2,1,0:T(8,128)(2,1)} collective-permute-done((bf16[4,2,80,512]{3,2,1,0:T(8,128)(2,1)S(1)}, bf16[4,2,80,512]{3,2,1,0:T(8,128)(2,1)}, u32[]{:S(2)}, u32[]{:S(2)}) %collective-permute-start.42) | collective-permute-done | bytes 655392 | tf_op jit(solution)/shard_map/ppermute | solution.py:434
  773.6 26.8 %collective-permute-done.15 = f32[8,2,768]{2,1,0:T(2,128)S(1)} collective-permute-done((f32[8,2,768]{2,1,0:T(2,128)S(1)}, f32[8,2,768]{2,1,0:T(2,128)S(1)}, u32[]{:S(2)}, u32[]{:S(2)}) %collective-permute-start.15) | collective-permute-done | bytes 49184 | tf_op jit(solution)/shard_map/ppermute | solution.py:434
  802.8 2.8 maximum_select_fusion.1
  807.8 2.7 maximum_select_fusion
  816.1 2.6 subtract_bitcast_fusion
  824.5 2.5 convolution_convert_fusion.7
  837.2 4.2 collective-permute-done.45
  856.6 6.1 collective-permute-done.49
  876.8 6.7 collective-permute-done.38
  890.1 2.4 collective-permute-done.39
  (541 shorter events, 244.3 us)
Async XLA Ops:
  350.7 14.7 %collective-permute-start.4 = (bf16[128,2048]{1,0:T(8,128)(2,1)S(1)}, bf16[128,2048]{1,0:T(8,128)(2,1)S(1)}, u32[]{:S(2)}, u32[]{:S(2)}) collective-permute-start(bf16[128,2048]{1,0:T(8,128)(2,1)S(1)} %multiply_convert_fusion.3), channel_id=1, source_target_pairs={{0,1},{1,0},{2,3},{3,2},{4,5},{5,4},{6,7},{7,6},{8,9},{9,8},{10,11... | collective-permute-start | bytes 1572872 | tf_op jit(solution)/shard_map/ppermute | solution.py:434
  366.6 20.7 %collective-permute-start.5 = (bf16[256,2048]{1,0:T(8,128)(2,1)}, bf16[256,2048]{1,0:T(8,128)(2,1)}, u32[]{:S(2)}, u32[]{:S(2)}) collective-permute-start(bf16[256,2048]{1,0:T(8,128)(2,1)} %pad_maximum_fusion.4), channel_id=1, source_target_pairs={{0,2},{2,0},{4,6},{6,4},{8,10},{10,8},{12,14},{14,12},{16,18},{18,... | collective-permute-start | bytes 3145736 | tf_op jit(solution)/shard_map/ppermute | solution.py:431
  371.3 453.1 %collective-permute-start.24 = (bf16[8,2,64,256]{3,2,1,0:T(8,128)(2,1)}, bf16[8,2,64,256]{3,2,1,0:T(8,128)(2,1)}, u32[]{:S(2)}, u32[]{:S(2)}) collective-permute-start(bf16[8,2,64,256]{3,2,1,0:T(8,128)(2,1)} %get-tuple-element.136), channel_id=1, source_target_pairs={{0,1},{1,0},{2,3},{3,2},{4,5},{5,4},{6,7},{7,6},{8,9},{9,8},{10,11... | collective-permute-start | bytes 1572872 | tf_op jit(solution)/shard_map/ppermute | solution.py:434
  387.0 240.7 %collective-permute-start.51 = (bf16[8,2,80,256]{3,2,1,0:T(8,128)(2,1)}, bf16[8,2,80,256]{3,2,1,0:T(8,128)(2,1)}, u32[]{:S(2)}, u32[]{:S(2)}) collective-permute-start(bf16[8,2,80,256]{3,2,1,0:T(8,128)(2,1)} %get-tuple-element.126), channel_id=1, source_target_pairs={{0,1},{1,0},{2,3},{3,2},{4,5},{5,4},{6,7},{7,6},{8,9},{9,8},{10,11... | collective-permute-start | bytes 1966088 | tf_op jit(solution)/shard_map/ppermute | solution.py:434
  449.3 12.0 %collective-permute-start.84 = (bf16[128,1536]{1,0:T(8,128)(2,1)S(1)}, bf16[128,1536]{1,0:T(8,128)(2,1)S(1)}, u32[]{:S(2)}, u32[]{:S(2)}) collective-permute-start(bf16[128,1536]{1,0:T(8,128)(2,1)S(1)} %convolution_convert_fusion.13), channel_id=1, source_target_pairs={{0,8},{2,10},{8,16},{10,18},{16,24},{18,26},{24,28},{26,30},{28,20... | collective-permute-start | bytes 1179656 | tf_op jit(solution)/shard_map/ppermute | solution.py:528
  451.0 11.4 %collective-permute-start.88 = (bf16[128,1536]{1,0:T(8,128)(2,1)S(1)}, bf16[128,1536]{1,0:T(8,128)(2,1)S(1)}, u32[]{:S(2)}, u32[]{:S(2)}) collective-permute-start(bf16[128,1536]{1,0:T(8,128)(2,1)S(1)} %convolution_convert_fusion.12), channel_id=1, source_target_pairs={{8,0},{10,2},{16,8},{18,10},{24,16},{26,18},{28,24},{30,26},{20,28... | collective-permute-start | bytes 1179656 | tf_op jit(solution)/shard_map/ppermute | solution.py:528
  451.8 17.9 %collective-permute-start.91 = (bf16[128,1536]{1,0:T(8,128)(2,1)S(1)}, bf16[128,1536]{1,0:T(8,128)(2,1)S(1)}, u32[]{:S(2)}, u32[]{:S(2)}) collective-permute-start(bf16[128,1536]{1,0:T(8,128)(2,1)S(1)} %convolution_convert_fusion.11), channel_id=1, source_target_pairs={{0,8},{2,10},{8,16},{10,18},{16,24},{18,26},{24,28},{26,30},{28,20... | collective-permute-start | bytes 1179656 | tf_op jit(solution)/shard_map/ppermute | solution.py:528
  462.4 44.4 %collective-permute-start.68 = (bf16[128,3072]{1,0:T(8,128)(2,1)S(1)}, bf16[128,3072]{1,0:T(8,128)(2,1)S(1)}, u32[]{:S(2)}, u32[]{:S(2)}) collective-permute-start(bf16[128,3072]{1,0:T(8,128)(2,1)S(1)} %convolution_convert_fusion.3), channel_id=1, source_target_pairs={{0,8},{2,10},{8,16},{10,18},{16,24},{18,26},{24,28},{26,30},{28,20... | collective-permute-start | bytes 2359304 | tf_op jit(solution)/shard_map/ppermute | solution.py:528
  469.8 24.5 %collective-permute-start.85 = (bf16[128,1536]{1,0:T(8,128)(2,1)S(1)}, bf16[128,1536]{1,0:T(8,128)(2,1)S(1)}, u32[]{:S(2)}, u32[]{:S(2)}) collective-permute-start(bf16[128,1536]{1,0:T(8,128)(2,1)S(1)} %add_convert_fusion.22), channel_id=1, source_target_pairs={{0,8},{2,10},{8,16},{10,18},{16,24},{18,26},{24,28},{26,30},{28,20... | collective-permute-start | bytes 1179656 | tf_op jit(solution)/shard_map/ppermute | solution.py:528
  471.4 36.8 %collective-permute-start.72 = (bf16[128,3072]{1,0:T(8,128)(2,1)S(1)}, bf16[128,3072]{1,0:T(8,128)(2,1)S(1)}, u32[]{:S(2)}, u32[]{:S(2)}) collective-permute-start(bf16[128,3072]{1,0:T(8,128)(2,1)S(1)} %convolution_convert_fusion.2), channel_id=1, source_target_pairs={{8,0},{10,2},{16,8},{18,10},{24,16},{26,18},{28,24},{30,26},{20,28... | collective-permute-start | bytes 2359304 | tf_op jit(solution)/shard_map/ppermute | solution.py:528
  494.3 10.4 %collective-permute-start.89 = (bf16[128,1536]{1,0:T(8,128)(2,1)S(1)}, bf16[128,1536]{1,0:T(8,128)(2,1)S(1)}, u32[]{:S(2)}, u32[]{:S(2)}) collective-permute-start(bf16[128,1536]{1,0:T(8,128)(2,1)S(1)} %add_convert_fusion.19), channel_id=1, source_target_pairs={{8,0},{10,2},{16,8},{18,10},{24,16},{26,18},{28,24},{30,26},{20,28... | collective-permute-start | bytes 1179656 | tf_op jit(solution)/shard_map/ppermute | solution.py:528
  504.7 27.2 %collective-permute-start.75 = (bf16[128,3072]{1,0:T(8,128)(2,1)S(1)}, bf16[128,3072]{1,0:T(8,128)(2,1)S(1)}, u32[]{:S(2)}, u32[]{:S(2)}) collective-permute-start(bf16[128,3072]{1,0:T(8,128)(2,1)S(1)} %convolution_convert_fusion.1), channel_id=1, source_target_pairs={{0,8},{2,10},{8,16},{10,18},{16,24},{18,26},{24,28},{26,30},{28,20... | collective-permute-start | bytes 2359304 | tf_op jit(solution)/shard_map/ppermute | solution.py:528
  506.8 24.3 %collective-permute-start.92 = (bf16[128,1536]{1,0:T(8,128)(2,1)S(1)}, bf16[128,1536]{1,0:T(8,128)(2,1)S(1)}, u32[]{:S(2)}, u32[]{:S(2)}) collective-permute-start(bf16[128,1536]{1,0:T(8,128)(2,1)S(1)} %add_convert_fusion.17), channel_id=1, source_target_pairs={{0,8},{2,10},{8,16},{10,18},{16,24},{18,26},{24,28},{26,30},{28,20... | collective-permute-start | bytes 1179656 | tf_op jit(solution)/shard_map/ppermute | solution.py:528
  508.2 24.9 %collective-permute-start.78 = (bf16[128,3072]{1,0:T(8,128)(2,1)S(1)}, bf16[128,3072]{1,0:T(8,128)(2,1)S(1)}, u32[]{:S(2)}, u32[]{:S(2)}) collective-permute-start(bf16[128,3072]{1,0:T(8,128)(2,1)S(1)} %convolution_convert_fusion), channel_id=1, source_target_pairs={{8,0},{10,2},{16,8},{18,10},{24,16},{26,18},{28,24},{30,26},{20,28... | collective-permute-start | bytes 2359304 | tf_op jit(solution)/shard_map/ppermute | solution.py:528
  531.1 13.6 %collective-permute-start.6 = (bf16[256,2048]{1,0:T(8,128)(2,1)S(1)}, bf16[256,2048]{1,0:T(8,128)(2,1)S(1)}, u32[]{:S(2)}, u32[]{:S(2)}) collective-permute-start(bf16[256,2048]{1,0:T(8,128)(2,1)S(1)} %slice.311), channel_id=1, source_target_pairs={{0,2},{2,0},{4,6},{6,4},{8,10},{10,8},{12,14},{14,12},{16,18},{18,... | collective-permute-start | bytes 3145736 | tf_op jit(solution)/shard_map/ppermute | solution.py:431
  531.9 11.5 %collective-permute-start.95 = (bf16[128,1536]{1,0:T(8,128)(2,1)S(1)}, bf16[128,1536]{1,0:T(8,128)(2,1)S(1)}, u32[]{:S(2)}, u32[]{:S(2)}) collective-permute-start(bf16[128,1536]{1,0:T(8,128)(2,1)S(1)} %add_convert_fusion.15), channel_id=1, source_target_pairs={{8,0},{10,2},{16,8},{18,10},{24,16},{26,18},{28,24},{30,26},{20,28... | collective-permute-start | bytes 1179656 | tf_op jit(solution)/shard_map/ppermute | solution.py:528
  533.1 13.8 %collective-permute-start.8 = (bf16[256,2048]{1,0:T(8,128)(2,1)S(1)}, bf16[256,2048]{1,0:T(8,128)(2,1)S(1)}, u32[]{:S(2)}, u32[]{:S(2)}) collective-permute-start(bf16[256,2048]{1,0:T(8,128)(2,1)S(1)} %slice.315), channel_id=1, source_target_pairs={{0,2},{2,0},{4,6},{6,4},{8,10},{10,8},{12,14},{14,12},{16,18},{18,... | collective-permute-start | bytes 3145736 | tf_op jit(solution)/shard_map/ppermute | solution.py:431
  543.4 12.0 %collective-permute-start.86 = (bf16[128,1536]{1,0:T(8,128)(2,1)S(1)}, bf16[128,1536]{1,0:T(8,128)(2,1)S(1)}, u32[]{:S(2)}, u32[]{:S(2)}) collective-permute-start(bf16[128,1536]{1,0:T(8,128)(2,1)S(1)} %add_convert_fusion.21), channel_id=1, source_target_pairs={{0,8},{2,10},{8,16},{10,18},{16,24},{18,26},{24,28},{26,30},{28,20... | collective-permute-start | bytes 1179656 | tf_op jit(solution)/shard_map/ppermute | solution.py:528
  544.7 12.2 %collective-permute-start.96 = (bf16[128,1536]{1,0:T(8,128)(2,1)S(1)}, bf16[128,1536]{1,0:T(8,128)(2,1)S(1)}, u32[]{:S(2)}, u32[]{:S(2)}) collective-permute-start(bf16[128,1536]{1,0:T(8,128)(2,1)S(1)} %add_convert_fusion.14), channel_id=1, source_target_pairs={{8,0},{10,2},{16,8},{18,10},{24,16},{26,18},{28,24},{30,26},{20,28... | collective-permute-start | bytes 1179656 | tf_op jit(solution)/shard_map/ppermute | solution.py:528
  547.0 25.3 %collective-permute-start.69 = (bf16[128,3072]{1,0:T(8,128)(2,1)S(1)}, bf16[128,3072]{1,0:T(8,128)(2,1)S(1)}, u32[]{:S(2)}, u32[]{:S(2)}) collective-permute-start(bf16[128,3072]{1,0:T(8,128)(2,1)S(1)} %add_convert_fusion.11), channel_id=1, source_target_pairs={{0,8},{2,10},{8,16},{10,18},{16,24},{18,26},{24,28},{26,30},{28,20... | collective-permute-start | bytes 2359304 | tf_op jit(solution)/shard_map/ppermute | solution.py:528
  555.4 19.0 %collective-permute-start.73 = (bf16[128,3072]{1,0:T(8,128)(2,1)S(1)}, bf16[128,3072]{1,0:T(8,128)(2,1)S(1)}, u32[]{:S(2)}, u32[]{:S(2)}) collective-permute-start(bf16[128,3072]{1,0:T(8,128)(2,1)S(1)} %add_convert_fusion.8), channel_id=1, source_target_pairs={{8,0},{10,2},{16,8},{18,10},{24,16},{26,18},{28,24},{30,26},{20,28... | collective-permute-start | bytes 2359304 | tf_op jit(solution)/shard_map/ppermute | solution.py:528
  556.9 30.9 %collective-permute-start.76 = (bf16[128,3072]{1,0:T(8,128)(2,1)S(1)}, bf16[128,3072]{1,0:T(8,128)(2,1)S(1)}, u32[]{:S(2)}, u32[]{:S(2)}) collective-permute-start(bf16[128,3072]{1,0:T(8,128)(2,1)S(1)} %add_convert_fusion.6), channel_id=1, source_target_pairs={{0,8},{2,10},{8,16},{10,18},{16,24},{18,26},{24,28},{26,30},{28,20... | collective-permute-start | bytes 2359304 | tf_op jit(solution)/shard_map/ppermute | solution.py:528
  572.3 11.8 %collective-permute-start.9 = (bf16[128,2048]{1,0:T(8,128)(2,1)S(1)}, bf16[128,2048]{1,0:T(8,128)(2,1)S(1)}, u32[]{:S(2)}, u32[]{:S(2)}) collective-permute-start(bf16[128,2048]{1,0:T(8,128)(2,1)S(1)} %slice.317), channel_id=1, source_target_pairs={{0,1},{1,0},{2,3},{3,2},{4,5},{5,4},{6,7},{7,6},{8,9},{9,8},{10,11... | collective-permute-start | bytes 1572872 | tf_op jit(solution)/shard_map/ppermute | solution.py:434
  574.5 35.5 %collective-permute-start.90 = (bf16[128,1536]{1,0:T(8,128)(2,1)}, bf16[128,1536]{1,0:T(8,128)(2,1)}, u32[]{:S(2)}, u32[]{:S(2)}) collective-permute-start(bf16[128,1536]{1,0:T(8,128)(2,1)} %add_convert_fusion.18), channel_id=1, source_target_pairs={{8,0},{10,2},{16,8},{18,10},{24,16},{26,18},{28,24},{30,26},{20,28... | collective-permute-start | bytes 1179656 | tf_op jit(solution)/shard_map/ppermute | solution.py:528
  584.1 11.0 %collective-permute-start.7 = (bf16[128,2048]{1,0:T(8,128)(2,1)}, bf16[128,2048]{1,0:T(8,128)(2,1)}, u32[]{:S(2)}, u32[]{:S(2)}) collective-permute-start(bf16[128,2048]{1,0:T(8,128)(2,1)} %slice.313), channel_id=1, source_target_pairs={{0,1},{1,0},{2,3},{3,2},{4,5},{5,4},{6,7},{7,6},{8,9},{9,8},{10,11... | collective-permute-start | bytes 1572872 | tf_op jit(solution)/shard_map/ppermute | solution.py:434
  587.9 18.6 %collective-permute-start.79 = (bf16[128,3072]{1,0:T(8,128)(2,1)}, bf16[128,3072]{1,0:T(8,128)(2,1)}, u32[]{:S(2)}, u32[]{:S(2)}) collective-permute-start(bf16[128,3072]{1,0:T(8,128)(2,1)} %add_convert_fusion.4), channel_id=1, source_target_pairs={{8,0},{10,2},{16,8},{18,10},{24,16},{26,18},{28,24},{30,26},{20,28... | collective-permute-start | bytes 2359304 | tf_op jit(solution)/shard_map/ppermute | solution.py:528
  595.0 15.8 %collective-permute-start.87 = (bf16[128,1536]{1,0:T(8,128)(2,1)}, bf16[128,1536]{1,0:T(8,128)(2,1)S(1)}, u32[]{:S(2)}, u32[]{:S(2)}) collective-permute-start(bf16[128,1536]{1,0:T(8,128)(2,1)} %add_convert_fusion.20), channel_id=1, source_target_pairs={{0,8},{2,10},{8,16},{10,18},{16,24},{18,26},{24,28},{26,30},{28,20... | collective-permute-start | bytes 1179656 | tf_op jit(solution)/shard_map/ppermute | solution.py:528
  606.5 12.1 %collective-permute-start.93 = (bf16[128,1536]{1,0:T(8,128)(2,1)S(1)}, bf16[128,1536]{1,0:T(8,128)(2,1)S(1)}, u32[]{:S(2)}, u32[]{:S(2)}) collective-permute-start(bf16[128,1536]{1,0:T(8,128)(2,1)S(1)} %copy-done.51), channel_id=1, source_target_pairs={{0,8},{2,10},{8,16},{10,18},{16,24},{18,26},{24,28},{26,30},{28,20... | collective-permute-start | bytes 1179656 | tf_op jit(solution)/shard_map/ppermute | solution.py:528
  610.0 12.1 %collective-permute-start.97 = (bf16[128,1536]{1,0:T(8,128)(2,1)S(1)}, bf16[128,1536]{1,0:T(8,128)(2,1)S(1)}, u32[]{:S(2)}, u32[]{:S(2)}) collective-permute-start(bf16[128,1536]{1,0:T(8,128)(2,1)S(1)} %copy-done.52), channel_id=1, source_target_pairs={{8,0},{10,2},{16,8},{18,10},{24,16},{26,18},{28,24},{30,26},{20,28... | collective-permute-start | bytes 1179656 | tf_op jit(solution)/shard_map/ppermute | solution.py:528
  610.9 34.1 %collective-permute-start.70 = (bf16[128,3072]{1,0:T(8,128)(2,1)S(1)}, bf16[128,3072]{1,0:T(8,128)(2,1)S(1)}, u32[]{:S(2)}, u32[]{:S(2)}) collective-permute-start(bf16[128,3072]{1,0:T(8,128)(2,1)S(1)} %copy-done.69), channel_id=1, source_target_pairs={{0,8},{2,10},{8,16},{10,18},{16,24},{18,26},{24,28},{26,30},{28,20... | collective-permute-start | bytes 2359304 | tf_op jit(solution)/shard_map/ppermute | solution.py:528
  618.5 29.3 %collective-permute-start.80 = (bf16[128,3072]{1,0:T(8,128)(2,1)S(1)}, bf16[128,3072]{1,0:T(8,128)(2,1)S(1)}, u32[]{:S(2)}, u32[]{:S(2)}) collective-permute-start(bf16[128,3072]{1,0:T(8,128)(2,1)S(1)} %add_convert_fusion.3), channel_id=1, source_target_pairs={{8,0},{10,2},{16,8},{18,10},{24,16},{26,18},{28,24},{30,26},{20,28... | collective-permute-start | bytes 2359304 | tf_op jit(solution)/shard_map/ppermute | solution.py:528
  623.7 14.0 %collective-permute-start.52 = (bf16[256,1024]{1,0:T(8,128)(2,1)S(1)}, bf16[256,1024]{1,0:T(8,128)(2,1)S(1)}, u32[]{:S(2)}, u32[]{:S(2)}) collective-permute-start(bf16[256,1024]{1,0:T(8,128)(2,1)S(1)} %pad_maximum_fusion.8), channel_id=1, source_target_pairs={{0,1},{1,0},{2,3},{3,2},{4,5},{5,4},{6,7},{7,6},{8,9},{9,8},{10,11... | collective-permute-start | bytes 1572872 | tf_op jit(solution)/shard_map/ppermute | solution.py:434
  627.8 81.7 %collective-permute-start.74 = (bf16[128,3072]{1,0:T(8,128)(2,1)}, bf16[128,3072]{1,0:T(8,128)(2,1)}, u32[]{:S(2)}, u32[]{:S(2)}) collective-permute-start(bf16[128,3072]{1,0:T(8,128)(2,1)} %add_convert_fusion.7), channel_id=1, source_target_pairs={{8,0},{10,2},{16,8},{18,10},{24,16},{26,18},{28,24},{30,26},{20,28... | collective-permute-start | bytes 2359304 | tf_op jit(solution)/shard_map/ppermute | solution.py:528
  637.7 13.2 %collective-permute-start.98 = (f32[128,1536]{1,0:T(8,128)S(1)}, f32[128,1536]{1,0:T(8,128)S(1)}, u32[]{:S(2)}, u32[]{:S(2)}) collective-permute-start(f32[128,1536]{1,0:T(8,128)S(1)} %convert_add_fusion.3), channel_id=1, source_target_pairs={{0,2},{2,0},{4,6},{6,4},{8,10},{10,8},{12,14},{14,12},{16,18},{18,... | collective-permute-start | bytes 2359304 | tf_op jit(solution)/shard_map/ppermute | solution.py:431
  644.9 55.3 %collective-permute-start.11 = (f32[2,128,1280]{2,1,0:T(8,128)}, f32[2,128,1280]{2,1,0:T(8,128)}, u32[]{:S(2)}, u32[]{:S(2)}) collective-permute-start(f32[2,128,1280]{2,1,0:T(8,128)} %bitcast.22), channel_id=1, source_target_pairs={{0,2},{2,0},{4,6},{6,4},{8,10},{10,8},{12,14},{14,12},{16,18},{18,... | collective-permute-start | bytes 3932168 | tf_op jit(solution)/shard_map/ppermute | solution.py:431
  675.7 10.6 %collective-permute-start.59 = (bf16[80,1024]{1,0:T(8,128)(2,1)S(1)}, bf16[80,1024]{1,0:T(8,128)(2,1)S(1)}, u32[]{:S(2)}, u32[]{:S(2)}) collective-permute-start(bf16[80,1024]{1,0:T(8,128)(2,1)S(1)} %fusion.39), channel_id=1, source_target_pairs={{8,0},{10,2},{16,8},{18,10},{24,16},{26,18},{28,24},{30,26},{20,28... | collective-permute-start | bytes 491528 | tf_op jit(solution)/shard_map/ppermute | solution.py:528
  694.5 44.5 %collective-permute-start.77 = (bf16[128,3072]{1,0:T(8,128)(2,1)S(1)}, bf16[128,3072]{1,0:T(8,128)(2,1)S(1)}, u32[]{:S(2)}, u32[]{:S(2)}) collective-permute-start(bf16[128,3072]{1,0:T(8,128)(2,1)S(1)} %copy-done.67), channel_id=1, source_target_pairs={{0,8},{2,10},{8,16},{10,18},{16,24},{18,26},{24,28},{26,30},{28,20... | collective-permute-start | bytes 2359304 | tf_op jit(solution)/shard_map/ppermute | solution.py:528
  698.0 27.3 %collective-permute-start.71 = (bf16[128,3072]{1,0:T(8,128)(2,1)S(1)}, bf16[128,3072]{1,0:T(8,128)(2,1)S(1)}, u32[]{:S(2)}, u32[]{:S(2)}) collective-permute-start(bf16[128,3072]{1,0:T(8,128)(2,1)S(1)} %copy-done.68), channel_id=1, source_target_pairs={{0,8},{2,10},{8,16},{10,18},{16,24},{18,26},{24,28},{26,30},{28,20... | collective-permute-start | bytes 2359304 | tf_op jit(solution)/shard_map/ppermute | solution.py:528
  700.2 38.8 %collective-permute-start.81 = (bf16[128,3072]{1,0:T(8,128)(2,1)}, bf16[128,3072]{1,0:T(8,128)(2,1)S(1)}, u32[]{:S(2)}, u32[]{:S(2)}) collective-permute-start(bf16[128,3072]{1,0:T(8,128)(2,1)} %add_convert_fusion.2), channel_id=1, source_target_pairs={{8,0},{10,2},{16,8},{18,10},{24,16},{26,18},{28,24},{30,26},{20,28... | collective-permute-start | bytes 2359304 | tf_op jit(solution)/shard_map/ppermute | solution.py:528
  709.5 45.0 %collective-permute-start.67 = (f32[80,1024]{1,0:T(8,128)}, f32[80,1024]{1,0:T(8,128)}, u32[]{:S(2)}, u32[]{:S(2)}) collective-permute-start(f32[80,1024]{1,0:T(8,128)} %fusion.34), channel_id=1, source_target_pairs={{0,2},{2,0},{4,6},{6,4},{8,10},{10,8},{12,14},{14,12},{16,18},{18,... | collective-permute-start | bytes 983048 | tf_op jit(solution)/shard_map/ppermute | solution.py:431
  752.8 49.3 %collective-permute-start.83 = (f32[128,1536]{1,0:T(8,128)}, f32[128,1536]{1,0:T(8,128)}, u32[]{:S(2)}, u32[]{:S(2)}) collective-permute-start(f32[128,1536]{1,0:T(8,128)} %get-tuple-element.123), channel_id=1, source_target_pairs={{0,2},{2,0},{4,6},{6,4},{8,10},{10,8},{12,14},{14,12},{16,18},{18,... | collective-permute-start | bytes 2359304 | tf_op jit(solution)/shard_map/ppermute | solution.py:431
  752.8 54.3 %collective-permute-start.82 = (f32[128,1536]{1,0:T(8,128)}, f32[128,1536]{1,0:T(8,128)}, u32[]{:S(2)}, u32[]{:S(2)}) collective-permute-start(f32[128,1536]{1,0:T(8,128)} %get-tuple-element.124), channel_id=1, source_target_pairs={{0,2},{2,0},{4,6},{6,4},{8,10},{10,8},{12,14},{14,12},{16,18},{18,... | collective-permute-start | bytes 2359304 | tf_op jit(solution)/shard_map/ppermute | solution.py:431
  754.6 17.8 %collective-permute-start.42 = (bf16[4,2,80,512]{3,2,1,0:T(8,128)(2,1)S(1)}, bf16[4,2,80,512]{3,2,1,0:T(8,128)(2,1)}, u32[]{:S(2)}, u32[]{:S(2)}) collective-permute-start(bf16[4,2,80,512]{3,2,1,0:T(8,128)(2,1)S(1)} %fusion.53), channel_id=1, source_target_pairs={{0,1},{1,0},{2,3},{3,2},{4,5},{5,4},{6,7},{7,6},{8,9},{9,8},{10,11... | collective-permute-start | bytes 1966088 | tf_op jit(solution)/shard_map/ppermute | solution.py:434
  756.9 67.5 %collective-permute-start.25 = (bf16[256,2560]{1,0:T(8,128)(2,1)}, bf16[256,2560]{1,0:T(8,128)(2,1)}, u32[]{:S(2)}, u32[]{:S(2)}) collective-permute-start(bf16[256,2560]{1,0:T(8,128)(2,1)} %bitcast.426), channel_id=1, source_target_pairs={{0,1},{1,0},{2,3},{3,2},{4,5},{5,4},{6,7},{7,6},{8,9},{9,8},{10,11... | collective-permute-start | bytes 3932168 | tf_op jit(solution)/shard_map/ppermute | solution.py:434
  772.3 28.1 %collective-permute-start.15 = (f32[8,2,768]{2,1,0:T(2,128)S(1)}, f32[8,2,768]{2,1,0:T(2,128)S(1)}, u32[]{:S(2)}, u32[]{:S(2)}) collective-permute-start(f32[8,2,768]{2,1,0:T(2,128)S(1)} %bitcast.447), channel_id=1, source_target_pairs={{0,1},{1,0},{2,3},{3,2},{4,5},{5,4},{6,7},{7,6},{8,9},{9,8},{10,11... | collective-permute-start | bytes 147464 | tf_op jit(solution)/shard_map/ppermute | solution.py:434
  801.8 19.1 %collective-permute-start.43 = (f32[4,80,512]{2,1,0:T(8,128)S(1)}, f32[4,80,512]{2,1,0:T(8,128)}, u32[]{:S(2)}, u32[]{:S(2)}) collective-permute-start(f32[4,80,512]{2,1,0:T(8,128)S(1)} %get-tuple-element.133), channel_id=1, source_target_pairs={{0,2},{2,0},{4,6},{6,4},{8,10},{10,8},{12,14},{14,12},{16,18},{18,... | collective-permute-start | bytes 1966088 | tf_op jit(solution)/shard_map/ppermute | solution.py:431
  823.5 27.9 %collective-permute-start.48 = (f32[80,512]{1,0:T(8,128)S(1)}, f32[80,512]{1,0:T(8,128)S(1)}, u32[]{:S(2)}, u32[]{:S(2)}) collective-permute-start(f32[80,512]{1,0:T(8,128)S(1)} %get-tuple-element.131), channel_id=1, source_target_pairs={{8,0},{10,2},{16,8},{18,10},{24,16},{26,18},{28,24},{30,26},{20,28... | collective-permute-start | bytes 491528 | tf_op jit(solution)/shard_map/ppermute | solution.py:631
  826.9 15.5 %collective-permute-start.26 = (bf16[64,2560]{1,0:T(8,128)(2,1)S(1)}, bf16[64,2560]{1,0:T(8,128)(2,1)S(1)}, u32[]{:S(2)}, u32[]{:S(2)}) collective-permute-start(bf16[64,2560]{1,0:T(8,128)(2,1)S(1)} %convolution_convert_fusion.7), channel_id=1, source_target_pairs={{0,8},{2,10},{8,16},{10,18},{16,24},{18,26},{24,28},{26,30},{28,20... | collective-permute-start | bytes 983048 | tf_op jit(solution)/shard_map/ppermute | solution.py:528
  830.2 15.2 %collective-permute-start.30 = (bf16[64,2560]{1,0:T(8,128)(2,1)S(1)}, bf16[64,2560]{1,0:T(8,128)(2,1)S(1)}, u32[]{:S(2)}, u32[]{:S(2)}) collective-permute-start(bf16[64,2560]{1,0:T(8,128)(2,1)S(1)} %convolution_convert_fusion.6), channel_id=1, source_target_pairs={{8,0},{10,2},{16,8},{18,10},{24,16},{26,18},{28,24},{30,26},{20,28... | collective-permute-start | bytes 983048 | tf_op jit(solution)/shard_map/ppermute | solution.py:528
  831.3 10.1 %collective-permute-start.45 = (f32[80,512]{1,0:T(8,128)S(1)}, f32[80,512]{1,0:T(8,128)S(1)}, u32[]{:S(2)}, u32[]{:S(2)}) collective-permute-start(f32[80,512]{1,0:T(8,128)S(1)} %bitcast_add_fusion.3), channel_id=1, source_target_pairs={{0,8},{2,10},{8,16},{10,18},{16,24},{18,26},{24,28},{26,30},{28,20... | collective-permute-start | bytes 491528 | tf_op jit(solution)/shard_map/ppermute | solution.py:631
  834.3 14.2 %collective-permute-start.33 = (bf16[64,2560]{1,0:T(8,128)(2,1)S(1)}, bf16[64,2560]{1,0:T(8,128)(2,1)S(1)}, u32[]{:S(2)}, u32[]{:S(2)}) collective-permute-start(bf16[64,2560]{1,0:T(8,128)(2,1)S(1)} %convolution_convert_fusion.5), channel_id=1, source_target_pairs={{0,8},{2,10},{8,16},{10,18},{16,24},{18,26},{24,28},{26,30},{28,20... | collective-permute-start | bytes 983048 | tf_op jit(solution)/shard_map/ppermute | solution.py:528
  841.4 12.2 %collective-permute-start.36 = (bf16[64,2560]{1,0:T(8,128)(2,1)S(1)}, bf16[64,2560]{1,0:T(8,128)(2,1)S(1)}, u32[]{:S(2)}, u32[]{:S(2)}) collective-permute-start(bf16[64,2560]{1,0:T(8,128)(2,1)S(1)} %convolution_convert_fusion.4), channel_id=1, source_target_pairs={{8,0},{10,2},{16,8},{18,10},{24,16},{26,18},{28,24},{30,26},{20,28... | collective-permute-start | bytes 983048 | tf_op jit(solution)/shard_map/ppermute | solution.py:528
  842.4 10.0 %collective-permute-start.46 = (f32[80,512]{1,0:T(8,128)S(1)}, f32[80,512]{1,0:T(8,128)S(1)}, u32[]{:S(2)}, u32[]{:S(2)}) collective-permute-start(f32[80,512]{1,0:T(8,128)S(1)} %bitcast_add_fusion.4), channel_id=1, source_target_pairs={{0,8},{2,10},{8,16},{10,18},{16,24},{18,26},{24,28},{26,30},{28,20... | collective-permute-start | bytes 491528 | tf_op jit(solution)/shard_map/ppermute | solution.py:631
  845.4 18.3 %collective-permute-start.27 = (bf16[64,2560]{1,0:T(8,128)(2,1)S(1)}, bf16[64,2560]{1,0:T(8,128)(2,1)S(1)}, u32[]{:S(2)}, u32[]{:S(2)}) collective-permute-start(bf16[64,2560]{1,0:T(8,128)(2,1)S(1)} %fusion.4), channel_id=1, source_target_pairs={{0,8},{2,10},{8,16},{10,18},{16,24},{18,26},{24,28},{26,30},{28,20... | collective-permute-start | bytes 983048 | tf_op jit(solution)/shard_map/ppermute | solution.py:528
  848.4 18.2 %collective-permute-start.31 = (bf16[64,2560]{1,0:T(8,128)(2,1)S(1)}, bf16[64,2560]{1,0:T(8,128)(2,1)S(1)}, u32[]{:S(2)}, u32[]{:S(2)}) collective-permute-start(bf16[64,2560]{1,0:T(8,128)(2,1)S(1)} %fusion.6), channel_id=1, source_target_pairs={{8,0},{10,2},{16,8},{18,10},{24,16},{26,18},{28,24},{30,26},{20,28... | collective-permute-start | bytes 983048 | tf_op jit(solution)/shard_map/ppermute | solution.py:528
  851.4 21.3 %collective-permute-start.34 = (bf16[64,2560]{1,0:T(8,128)(2,1)S(1)}, bf16[64,2560]{1,0:T(8,128)(2,1)S(1)}, u32[]{:S(2)}, u32[]{:S(2)}) collective-permute-start(bf16[64,2560]{1,0:T(8,128)(2,1)S(1)} %fusion.8), channel_id=1, source_target_pairs={{0,8},{2,10},{8,16},{10,18},{16,24},{18,26},{24,28},{26,30},{28,20... | collective-permute-start | bytes 983048 | tf_op jit(solution)/shard_map/ppermute | solution.py:528
  852.5 10.1 %collective-permute-start.49 = (f32[80,512]{1,0:T(8,128)S(1)}, f32[80,512]{1,0:T(8,128)S(1)}, u32[]{:S(2)}, u32[]{:S(2)}) collective-permute-start(f32[80,512]{1,0:T(8,128)S(1)} %get-tuple-element.129), channel_id=1, source_target_pairs={{8,0},{10,2},{16,8},{18,10},{24,16},{26,18},{28,24},{30,26},{20,28... | collective-permute-start | bytes 491528 | tf_op jit(solution)/shard_map/ppermute | solution.py:631
  855.5 14.2 %collective-permute-start.37 = (bf16[64,2560]{1,0:T(8,128)(2,1)S(1)}, bf16[64,2560]{1,0:T(8,128)(2,1)S(1)}, u32[]{:S(2)}, u32[]{:S(2)}) collective-permute-start(bf16[64,2560]{1,0:T(8,128)(2,1)S(1)} %fusion.11), channel_id=1, source_target_pairs={{8,0},{10,2},{16,8},{18,10},{24,16},{26,18},{28,24},{30,26},{20,28... | collective-permute-start | bytes 983048 | tf_op jit(solution)/shard_map/ppermute | solution.py:528
  862.7 13.0 %collective-permute-start.47 = (f32[80,512]{1,0:T(8,128)S(1)}, f32[80,512]{1,0:T(8,128)S(1)}, u32[]{:S(2)}, u32[]{:S(2)}) collective-permute-start(f32[80,512]{1,0:T(8,128)S(1)} %get-tuple-element.128), channel_id=1, source_target_pairs={{0,8},{2,10},{8,16},{10,18},{16,24},{18,26},{24,28},{26,30},{28,20... | collective-permute-start | bytes 491528 | tf_op jit(solution)/shard_map/ppermute | solution.py:631
  863.7 13.0 %collective-permute-start.50 = (f32[80,512]{1,0:T(8,128)S(1)}, f32[80,512]{1,0:T(8,128)S(1)}, u32[]{:S(2)}, u32[]{:S(2)}) collective-permute-start(f32[80,512]{1,0:T(8,128)S(1)} %bitcast_add_fusion.2), channel_id=1, source_target_pairs={{8,0},{10,2},{16,8},{18,10},{24,16},{26,18},{28,24},{30,26},{20,28... | collective-permute-start | bytes 491528 | tf_op jit(solution)/shard_map/ppermute | solution.py:631
  866.7 20.5 %collective-permute-start.28 = (bf16[64,2560]{1,0:T(8,128)(2,1)S(1)}, bf16[64,2560]{1,0:T(8,128)(2,1)S(1)}, u32[]{:S(2)}, u32[]{:S(2)}) collective-permute-start(bf16[64,2560]{1,0:T(8,128)(2,1)S(1)} %fusion.3), channel_id=1, source_target_pairs={{0,8},{2,10},{8,16},{10,18},{16,24},{18,26},{24,28},{26,30},{28,20... | collective-permute-start | bytes 983048 | tf_op jit(solution)/shard_map/ppermute | solution.py:528
  869.7 25.4 %collective-permute-start.32 = (bf16[64,2560]{1,0:T(8,128)(2,1)S(1)}, bf16[64,2560]{1,0:T(8,128)(2,1)S(1)}, u32[]{:S(2)}, u32[]{:S(2)}) collective-permute-start(bf16[64,2560]{1,0:T(8,128)(2,1)S(1)} %fusion.5), channel_id=1, source_target_pairs={{8,0},{10,2},{16,8},{18,10},{24,16},{26,18},{28,24},{30,26},{20,28... | collective-permute-start | bytes 983048 | tf_op jit(solution)/shard_map/ppermute | solution.py:528
  872.7 10.8 %collective-permute-start.38 = (bf16[64,2560]{1,0:T(8,128)(2,1)S(1)}, bf16[64,2560]{1,0:T(8,128)(2,1)S(1)}, u32[]{:S(2)}, u32[]{:S(2)}) collective-permute-start(bf16[64,2560]{1,0:T(8,128)(2,1)S(1)} %fusion.10), channel_id=1, source_target_pairs={{8,0},{10,2},{16,8},{18,10},{24,16},{26,18},{28,24},{30,26},{20,28... | collective-permute-start | bytes 983048 | tf_op jit(solution)/shard_map/ppermute | solution.py:528
  875.6 14.5 %collective-permute-start.35 = (bf16[64,2560]{1,0:T(8,128)(2,1)S(1)}, bf16[64,2560]{1,0:T(8,128)(2,1)S(1)}, u32[]{:S(2)}, u32[]{:S(2)}) collective-permute-start(bf16[64,2560]{1,0:T(8,128)(2,1)S(1)} %fusion.7), channel_id=1, source_target_pairs={{0,8},{2,10},{8,16},{10,18},{16,24},{18,26},{24,28},{26,30},{28,20... | collective-permute-start | bytes 983048 | tf_op jit(solution)/shard_map/ppermute | solution.py:528
  (123 other events, 1023.3 us)

commit v2 on v1

--- a/solution.py
+++ b/solution.py
@@ -26,11 +26,48 @@
     return (1 - odd) * (chip // 2) + odd * (n - 1 - chip // 2)
 
 
+def heads_first(chip, core, n):
+    return (chip + n - core * (n // 2)) % n
+
+
+class Copies:
+    def __init__(self, local, sends, recvs):
+        self.local, self.sends, self.recvs = local, sends, recvs
+        self.locals_used = self.used = 0
+
+    def stay(self, src, dst):
+        copy = pltpu.make_async_copy(src, dst, self.local.at[self.locals_used])
+        self.locals_used += 1
+        copy.start()
+        return copy
+
+    def send(self, src, dst, device):
+        copy = pltpu.make_async_remote_copy(
+            src_ref=src, dst_ref=dst, send_sem=self.sends.at[self.used], recv_sem=self.recvs.at[self.used],
+            device_id=device, device_id_type=MESH,
+        )
+        self.used += 1
+        copy.start()
+        return copy
+
+
+def greet(devices):
+    barrier = pltpu.get_barrier_semaphore()
+    for device in devices:
+        pl.semaphore_signal(barrier, inc=1, device_id=device, device_id_type=MESH)
+    pl.semaphore_wait(barrier, len(devices))
+
+
+def half_cols(ref, which):
+    width = ref.shape[1] // 2
+    return ref.at[:, pl.ds(pl.multiple_of(which * width, 128), width)]
+
+
 def gather_kernel(
     n,
     wx, wy, wo, gs, wg, wu, wd, rows_in, cot, starts,
     o_xy, o_out, o_gs, o_gu, o_d, o_rows, o_cot, o_starts,
-    local_sem, pair_send, pair_recv, ring_send, ring_recv, x_send, x_recv,
+    local_sem, send_sem, recv_sem,
 ):
     dp, x = lax.axis_index("dp"), lax.axis_index("tp")
     chip, core = dp // 2, dp % 2
@@ -40,169 +77,317 @@
     nxt = (chip_at((pos + 1) % n, n) * 2 + core, x)
     prv = (chip_at((pos + n - 1) % n, n) * 2 + core, x)
     sib = (chip * 2 + other, x)
-    across = (dp, 1 - x)
-    barrier = pltpu.get_barrier_semaphore()
-    for device in (nxt, prv, sib, across):
-        pl.semaphore_signal(barrier, inc=1, device_id=device, device_id_type=MESH)
-    pl.semaphore_wait(barrier, 4)
-
-    def cols(width, which):
-        return pl.ds(pl.multiple_of(which * width, 128), width)
-
-    taken = {"l": 0, "p": 0, "r": 0, "x": 0}
-
-    def local(src, dst):
-        copy = pltpu.make_async_copy(src, dst, local_sem.at[taken["l"]])
-        taken["l"] += 1
-        copy.start()
-        return copy
-
-    def remote(kind, src, dst, device):
-        sends, recvs = {"p": (pair_send, pair_recv), "r": (ring_send, ring_recv), "x": (x_send, x_recv)}[kind]
-        i = taken[kind]
-        taken[kind] += 1
-        copy = pltpu.make_async_remote_copy(
-            src_ref=src, dst_ref=dst, send_sem=sends.at[i], recv_sem=recvs.at[i],
-            device_id=device, device_id_type=MESH,
-        )
-        copy.start()
-        return copy
+    over = (dp, 1 - x)
+    greet([nxt, prv, sib, over])
+    copies = Copies(local_sem, send_sem, recv_sem)
+    send, stay = copies.send, copies.stay
+
+    def by_heads(chip_id, which):
+        return heads_first(chip_id, which, n)
 
     rhalf = wx.shape[1] // 2
-    dhalf = wo.shape[1] // 2
     fhalf = wg.shape[1] // 2
-    parts = [
-        (wx, rhalf, lambda: o_xy.at[chip, core, x, :, pl.ds(0, rhalf)]),
-        (wy, rhalf, lambda: o_xy.at[chip, core, x, :, pl.ds(rhalf, rhalf)]),
-        (wo, dhalf, lambda: o_out.at[chip, core, x]),
-        (wg, fhalf, lambda: o_gu.at[chip, core, :, pl.ds(0, fhalf)]),
-        (wu, fhalf, lambda: o_gu.at[chip, core, :, pl.ds(fhalf, fhalf)]),
-        (wd, fhalf, lambda: o_d.at[chip, core]),
+    rec_parts = [
+        (wx, o_xy.at[chip, core, x, :, pl.ds(0, rhalf)]),
+        (wy, o_xy.at[chip, core, x, :, pl.ds(rhalf, rhalf)]),
     ]
-    pair, mine = [], []
-    for src, width, slot in parts[:3]:
-        pair.append(remote("p", src.at[:, cols(width, other)], slot(), sib))
-    for src, width, slot in parts[:3]:
-        mine.append(local(src.at[:, cols(width, core)], slot()))
-    mine.append(local(gs, o_gs.at[core, chip, x]))
-    for src, width, slot in parts[3:]:
-        pair.append(remote("p", src.at[:, cols(width, other)], slot(), sib))
-    for src, width, slot in parts[3:]:
-        mine.append(local(src.at[:, cols(width, core)], slot()))
-    late = [
-        remote("p", rows_in, o_rows.at[1], sib),
-        remote("p", starts, o_starts.at[1], sib),
-        remote("p", cot, o_cot.at[2], sib),
+    ff_parts = [
+        (wg, o_gu.at[chip, core, :, pl.ds(0, fhalf)]),
+        (wu, o_gu.at[chip, core, :, pl.ds(fhalf, fhalf)]),
+        (wd, o_d.at[core]),
     ]
-    plain = [local(rows_in, o_rows.at[0]), local(starts, o_starts.at[0]), local(cot, o_cot.at[0])]
-    cot_x = remote("x", cot, o_cot.at[1], across)
+    pair = [send(half_cols(src, other), slot, sib) for src, slot in rec_parts]
+    pair.append(send(half_cols(wo, other), o_out.at[by_heads(chip, other), core, x], sib))
+    mine = [stay(half_cols(src, core), slot) for src, slot in rec_parts] + [stay(gs, o_gs.at[core, chip, x])]
+    mine.append(stay(half_cols(wo, core), o_out.at[by_heads(chip, core), core, x]))
+    late = [send(half_cols(src, other), slot, sib) for src, slot in ff_parts]
+    plain = [stay(half_cols(src, core), slot) for src, slot in ff_parts]
+    late += [send(rows_in, o_rows.at[1], sib), send(starts, o_starts.at[1], sib), send(cot, o_cot.at[2], sib)]
+    plain += [stay(rows_in, o_rows.at[0]), stay(starts, o_starts.at[0]), stay(cot, o_cot.at[0])]
 
     def rec_block(chip_id):
-        return [o_xy.at[chip_id, :, x], o_out.at[chip_id, :, x], o_gs.at[core, chip_id, x]]
-
-    def rec_half(chip_id, which):
-        piece = [o_xy.at[chip_id, which, x], o_out.at[chip_id, which, x]]
-        return piece + ([o_gs.at[core, chip_id, x]] if which == 0 else [])
+        return [o_xy.at[chip_id, :, x], o_out.at[by_heads(chip_id, core), :, x], o_gs.at[core, chip_id, x]]
+
+    def rec_piece(chip_id, which):
+        refs = [o_xy.at[chip_id, which, x], o_out.at[by_heads(chip_id, core), which, x]]
+        return refs + ([o_gs.at[core, chip_id, x]] if which == 0 else [])
 
     def ff_block(chip_id):
-        return [o_gu.at[chip_id], o_d.at[chip_id]]
-
-    def ff_half(chip_id, which):
-        return [o_gu.at[chip_id, which], o_d.at[chip_id, which]]
-
-    def send_all(kind, refs, device):
-        return [remote(kind, ref, ref, device) for ref in refs]
-
-    for copy in pair[:3]:
-        copy.wait_recv()
-    for copy in mine[:4]:
-        copy.wait()
-    sends, arrivals_x = [], []
-
-    def step(block, piece, s, first):
+        return [o_gu.at[chip_id]]
+
+    def ff_piece(chip_id, which):
+        return [o_gu.at[chip_id, which]]
+
+    def send_all(refs, device):
+        return [send(ref, ref, device) for ref in refs]
+
+    def hop(s, block, piece):
         ahead = chip_at((pos + n - (s - 1)) % n, n)
         behind = chip_at((pos + s - 1) % n, n)
         if s < half:
-            f = send_all("r", block(ahead), nxt)
-            b = send_all("r", block(behind), prv)
-        else:
-            f = send_all("r", piece(ahead, 0), nxt)
-            b = send_all("r", piece(behind, 1), prv)
-        if first:
-            arrivals_x.extend(send_all("x", block(ahead), across))
-        return f, b
-
-    f, b = step(rec_block, rec_half, 1, True)
-    for s in range(2, half + 1):
-        for copy in f + b:
+            return send_all(block(ahead), nxt) + send_all(block(behind), prv)
+        return send_all(piece(ahead, 0), nxt) + send_all(piece(behind, 1), prv)
+
+    for copy in pair:
+        copy.wait_recv()
+    for copy in mine:
+        copy.wait()
+    done, crossed, moving = [], send_all(rec_block(chip), over), []
+    for s in range(1, half + 1):
+        for copy in moving:
             copy.wait_recv()
-        sends.extend(f + b)
-        ahead = chip_at((pos + n - (s - 1)) % n, n)
-        behind = chip_at((pos + s - 1) % n, n)
-        f, b = step(rec_block, rec_half, s, False)
-        arrivals_x.extend(send_all("x", rec_block(ahead), across))
-        arrivals_x.extend(send_all("x", rec_block(behind), across))
-    rec_last = f + b
-    for copy in pair[3:]:
-        copy.wait_recv()
-    for copy in mine[4:]:
-        copy.wait()
-    f, b = step(ff_block, ff_half, 1, False)
-    for copy in rec_last:
-        copy.wait_recv()
-    sends.extend(rec_last)
-    arrivals_x.extend(send_all("x", rec_block(chip_at((pos + half) % n, n)), across))
-    cot_x.wait_recv()
-    last_cot = remote("p", o_cot.at[1], o_cot.at[3], sib)
-    for s in range(2, half + 1):
-        for copy in f + b:
-            copy.wait_recv()
-        sends.extend(f + b)
-        f, b = step(ff_block, ff_half, s, False)
-    for copy in arrivals_x:
-        copy.wait_recv()
-    swap = remote("p", o_gs.at[core], o_gs.at[core], sib)
-    for copy in f + b:
-        copy.wait_recv()
-    sends.extend(f + b)
-    swap.wait_recv()
-    last_cot.wait_recv()
+        done.extend(moving)
+        moving = hop(s, rec_block, rec_piece)
+        if s > 1:
+            crossed.extend(send_all(rec_block(chip_at((pos + n - (s - 1)) % n, n)), over))
+            crossed.extend(send_all(rec_block(chip_at((pos + s - 1) % n, n)), over))
+    last_rec = moving
     for copy in late:
         copy.wait_recv()
     for copy in plain:
         copy.wait()
-    for copy in pair + late + [cot_x, last_cot, swap] + sends + arrivals_x:
+    moving = hop(1, ff_block, ff_piece)
+    for copy in last_rec:
+        copy.wait_recv()
+    done.extend(last_rec)
+    crossed.extend(send_all(rec_block(chip_at((pos + half) % n, n)), over))
+    cot_over = send(cot, o_cot.at[1], over)
+    for s in range(2, half + 1):
+        for copy in moving:
+            copy.wait_recv()
+        done.extend(moving)
+        moving = hop(s, ff_block, ff_piece)
+    for copy in crossed:
+        copy.wait_recv()
+    swap = send(o_gs.at[core], o_gs.at[core], sib)
+    cot_over.wait_recv()
+    last = send(o_cot.at[1], o_cot.at[3], sib)
+    for copy in moving:
+        copy.wait_recv()
+    done.extend(moving)
+    swap.wait_recv()
+    last.wait_recv()
+    for copy in pair + late + done + crossed + [cot_over, swap, last]:
         copy.wait_send()
 
 
 def gather_weights(n, wx, wy, wo, gs, wg, wu, wd, rows_in, cot, starts):
-    r, d, f = wx.shape[1], wo.shape[1], wg.shape[1]
-    half = n // 2
+    r, d, (rows_f, f) = wx.shape[1], wo.shape[1], wg.shape
     tokens = rows_in.shape[0]
     shapes = [
         jax.ShapeDtypeStruct((n, 2, 2, wx.shape[0], r), BF16),
         jax.ShapeDtypeStruct((n, 2, 2, wo.shape[0], d // 2), BF16),
         jax.ShapeDtypeStruct((2, n, 2) + gs.shape, BF16),
-        jax.ShapeDtypeStruct((n, 2, wg.shape[0], f), BF16),
-        jax.ShapeDtypeStruct((n, 2, wg.shape[0], f // 2), BF16),
+        jax.ShapeDtypeStruct((n, 2, rows_f, f), BF16),
+        jax.ShapeDtypeStruct((2, rows_f, f // 2), BF16),
         jax.ShapeDtypeStruct((2, tokens, d), BF16),
         jax.ShapeDtypeStruct((4, tokens, d), BF16),
         jax.ShapeDtypeStruct((2,) + starts.shape, F32),
     ]
-    pairs, ring, over = 11, half * 10 - 1, 3 * n + 1
+    count = 9 + (3 * n - 1) + n + 3 * n + 3
     dma = pltpu.SemaphoreType.DMA
-    result = pl.pallas_call(
+    return pl.pallas_call(
         functools.partial(gather_kernel, n),
         out_shape=shapes,
-        in_specs=[pl.BlockSpec(memory_space=pl.ANY)] * 10,
+        in_specs=[pl.BlockSpec(memory_space=pltpu.VMEM)] * 10,
         out_specs=[pl.BlockSpec(memory_space=pl.ANY)] * 8,
-        scratch_shapes=[
-            dma((10,)), dma((pairs,)), dma((pairs,)), dma((ring,)), dma((ring,)), dma((over,)), dma((over,)),
-        ],
-        compiler_params=pltpu.CompilerParams(collective_id=0, has_side_effects=True),
+        scratch_shapes=[dma((10,)), dma((count,)), dma((count,))],
+        compiler_params=pltpu.CompilerParams(
+            collective_id=0, has_side_effects=True, vmem_limit_bytes=24 << 20
+        ),
         name="gather_weights",
     )(wx, wy, wo, gs, wg, wu, wd, rows_in, cot, starts)
-    return result
+
+
+def scatter_kernel(
+    n,
+    c_x, c_y, c_out, c_g, c_v,
+    g_x, g_y, g_out, g_gates, g_vec,
+    r_x, r_y, r_out, r_g, r_v, s_x, s_y, s_out,
+    send_sem, recv_sem,
+):
+    dp, x = lax.axis_index("dp"), lax.axis_index("tp")
+    chip, core = dp // 2, dp % 2
+    pos = place_of(chip, n)
+    half = n // 2
+    nxt = (chip_at((pos + 1) % n, n) * 2 + core, x)
+    prv = (chip_at((pos + n - 1) % n, n) * 2 + core, x)
+    sib = (dp + 1 - 2 * core, x)
+    greet([nxt, prv, sib])
+    copies = Copies(None, send_sem, recv_sem)
+
+    pieces = []
+    for part in (0, 1):
+        for terms, slots, first in ((c_out, r_out, core), (c_y, r_y, 0), (c_x, r_x, 0)):
+            pieces.append((
+                lambda c, terms=terms, part=part, first=first: terms.at[heads_first(c, first, n), part],
+                lambda w, k, slots=slots, part=part: slots.at[part, w, k],
+                part,
+            ))
+    pieces.append((lambda c: c_g.at[c], lambda w, k: r_g.at[w, k], 0))
+    pieces.append((lambda c: c_v.at[c], lambda w, k: r_v.at[w, k], 1))
+
+    def add(a, b):
+        return a[...].astype(F32) + b[...].astype(F32)
+
+    sent, coming = [], {}
+    for k in range(half, -1, -1):
+        for i, (term, slot, far) in enumerate(pieces):
+            for way, (device, sign) in enumerate(((nxt, 1), (prv, n - 1))):
+                first = half if way == far else half - 1
+                if k > first or k == 0:
+                    continue
+                source = term(chip_at((pos + sign * k) % n, n))
+                if k < first:
+                    coming[i, way].wait_recv()
+                    got = slot(way, k)
+                    got[...] = add(got, source).astype(got.dtype)
+                    source = got
+                copy = copies.send(source, slot(way, k - 1), device)
+                coming[i, way] = copy
+                sent.append(copy)
+
+    def total(i):
+        term, slot, _ = pieces[i]
+        for way in (0, 1):
+            coming[i, way].wait_recv()
+        return add(term(chip), slot(0, 0)) + slot(1, 0)[...].astype(F32)
+
+    def cols(ref):
+        width = ref.shape[1] // 2
+        return pl.ds(pl.multiple_of(core * width, 128), width)
+
+    results = ((g_out, s_out), (g_y, s_y), (g_x, s_x))
+    for part in (0, 1):
+        sums = [total(3 * part + i) for i in range(3)]
+
+        @pl.when(core == part)
+        def _():
+            for value, (ref, _) in zip(sums, results):
+                ref[:, cols(ref)] = value
+
+        @pl.when(core != part)
+        def _():
+            for value, (_, ref) in zip(sums, results):
+                ref[...] = value
+
+    final = [copies.send(src, ref.at[:, cols(ref)], sib) for ref, src in results]
+    g_gates[...] = total(6)
+    g_vec[...] = total(7)
+    for copy in final:
+        copy.wait_recv()
+    for copy in sent + final:
+        copy.wait_send()
+
+
+def scatter_sums(n, c_x, c_y, c_out, c_g, c_v):
+    _, _, rows_d, rhalf = c_x.shape
+    _, _, rows_r, dhalf = c_out.shape
+    half = n // 2
+    count = 8 * (2 * half - 1) + 3
+    dma = pltpu.SemaphoreType.DMA
+    vmem = pl.BlockSpec(memory_space=pltpu.VMEM)
+    return pl.pallas_call(
+        functools.partial(scatter_kernel, n),
+        out_shape=[
+            jax.ShapeDtypeStruct((rows_d, 2 * rhalf), F32),
+            jax.ShapeDtypeStruct((rows_d, 2 * rhalf), F32),
+            jax.ShapeDtypeStruct((rows_r, 2 * dhalf), F32),
+            jax.ShapeDtypeStruct(c_g.shape[1:], F32),
+            jax.ShapeDtypeStruct(c_v.shape[1:], F32),
+        ],
+        in_specs=[vmem] * 5,
+        out_specs=[vmem] * 5,
+        scratch_shapes=[
+            pltpu.VMEM((2, 2, half, rows_d, rhalf), BF16),
+            pltpu.VMEM((2, 2, half, rows_d, rhalf), BF16),
+            pltpu.VMEM((2, 2, half, rows_r, dhalf), BF16),
+            pltpu.VMEM((2, half) + c_g.shape[1:], BF16),
+            pltpu.VMEM((2, half) + c_v.shape[1:], F32),
+            pltpu.VMEM((rows_d, rhalf), F32),
+            pltpu.VMEM((rows_d, rhalf), F32),
+            pltpu.VMEM((rows_r, dhalf), F32),
+            dma((count,)), dma((count,)),
+        ],
+        compiler_params=pltpu.CompilerParams(
+            collective_id=1, has_side_effects=True, vmem_limit_bytes=56 << 20
+        ),
+        name="scatter_sums",
+    )(c_x, c_y, c_out, c_g, c_v)
+
+
+def project_kernel(steps, rows, gain, w, n1_ref, x_ref, y_ref):
+    i = pl.program_id(0)
+
+    @pl.when(i == 0)
+    def _():
+        values = rows[...].astype(F32)
+        scale = lax.rsqrt(jnp.mean(values * values, axis=-1, keepdims=True) + EPS)
+        n1_ref[...] = (values * scale * gain[...]).astype(BF16).reshape(n1_ref.shape)
+
+    result = jnp.dot(n1_ref[...], w[...], preferred_element_type=F32).reshape(y_ref.shape)
+
+    @pl.when(i < steps)
+    def _():
+        x_ref[...] = result.astype(BF16)
+
+    @pl.when(i >= steps)
+    def _():
+        y_ref[...] = result
+
+
+def project(rows, gain, w):
+    _, tokens, width = rows.shape
+    rh = w.shape[1] // 2
+    steps = rh // BLK
+    return pl.pallas_call(
+        functools.partial(project_kernel, steps),
+        grid=(2 * steps,),
+        in_specs=[
+            pl.BlockSpec(rows.shape, lambda i: (0, 0, 0)),
+            pl.BlockSpec((1, width), lambda i: (0, 0)),
+            pl.BlockSpec((width, BLK), lambda i: (0, i)),
+        ],
+        out_specs=[
+            pl.BlockSpec((2 * tokens, width), lambda i: (0, 0)),
+            pl.BlockSpec((2, tokens, BLK), lambda i: (0, 0, jnp.minimum(i, steps - 1))),
+            pl.BlockSpec((2, tokens, BLK), lambda i: (0, 0, jnp.maximum(i - steps, 0))),
+        ],
+        out_shape=[
+            jax.ShapeDtypeStruct((2 * tokens, width), BF16),
+            jax.ShapeDtypeStruct((2, tokens, rh), BF16),
+            jax.ShapeDtypeStruct((2, tokens, rh), F32),
+        ],
+        compiler_params=pltpu.CompilerParams(vmem_limit_bytes=40 << 20),
+        cost_estimate=pl.CostEstimate(flops=27 * 10**8, bytes_accessed=15 * 10**6, transcendentals=0),
+        name="project",
+    )(rows, gain, w)
+
+
+def project_out_kernel(o, o_sib, w, mine_ref, theirs_ref):
+    rh = o.shape[2]
+    for row, ref in ((0, mine_ref), (1, theirs_ref)):
+        ref[...] = jnp.dot(o[row], w[:rh], preferred_element_type=F32) + jnp.dot(
+            o_sib[1 - row], w[rh:], preferred_element_type=F32
+        )
+
+
+def project_out(o, o_sib, w):
+    _, tokens, rh = o.shape
+    cols = w.shape[1]
+    tile = min(BLK, cols)
+    whole = pl.BlockSpec(o.shape, lambda i: (0, 0, 0))
+    part = pl.BlockSpec((tokens, tile), lambda i: (0, i))
+    return pl.pallas_call(
+        project_out_kernel,
+        grid=(cols // tile,),
+        in_specs=[whole, whole, pl.BlockSpec((2 * rh, tile), lambda i: (0, i))],
+        out_specs=[part, part],
+        out_shape=[jax.ShapeDtypeStruct((tokens, cols), F32)] * 2,
+        compiler_params=pltpu.CompilerParams(vmem_limit_bytes=40 << 20),
+        cost_estimate=pl.CostEstimate(flops=14 * 10**8, bytes_accessed=8 * 10**6, transcendentals=0),
+        name="project_out",
+    )(o, o_sib, w)
 
 
 def minus_expm1(v):
@@ -425,6 +610,7 @@
     ring = [chip_at(i, n) for i in range(n)]
     up = [(ring[i] * 2 + c, ring[(i + 1) % n] * 2 + c) for i in range(n) for c in range(2)]
     down = [(b, a) for a, b in up]
+    lanes = [[chip_id * 2 + c for chip_id in ring] for c in range(2)]
     pairs = [(d, d + 1 - 2 * (d % 2)) for d in range(dp_size)]
 
     def sibling(v):
@@ -440,6 +626,20 @@
         return jnp.where(
             core == 0, jnp.concatenate([mine, theirs], axis), jnp.concatenate([theirs, mine], axis)
         )
+
+    def ring_order(array, axis):
+        size = array.shape[axis] // n
+        return jnp.concatenate([lax.slice_in_dim(array, i * size, (i + 1) * size, axis=axis) for i in ring], axis)
+
+    def chip_order(array, axis):
+        size = array.shape[axis] // n
+        return jnp.concatenate(
+            [lax.slice_in_dim(array, ring.index(i) * size, (ring.index(i) + 1) * size, axis=axis) for i in range(n)],
+            axis,
+        )
+
+    def after(value, *others):
+        return lax.optimization_barrier((value,) + others)[0]
 
     rows_own = layer_input.reshape(tokens, width)
     place = x * tokens + jnp.arange(tokens, dtype=jnp.int32)
@@ -453,13 +653,18 @@
     )
     small = jnp.pad(small, (0, PAD * WIDE - small.shape[0])).reshape(PAD, WIDE)
     gs = jnp.concatenate([jnp.concatenate([gate_a_w, gate_i_w], axis=1), small], axis=0)
-    w_xy, w_o, all_gs, w_gu, w_d, rows_two, cot_all, starts_two = gather_weights(
-        n, w_x, w_y, w_out, gs, w_gate, w_up, w_down.T, rows_own, cot.astype(BF16), starts
-    )
+    w_xy, w_o, all_gs, w_gu, d_block, rows_two, cot_all, starts_two = gather_weights(
+        n, w_x, w_y, w_out, gs, w_gate, w_up, w_down.T, rows_own, ring_order(cot.astype(BF16), 1), starts
+    )
+    w_d = lax.all_gather(
+        d_block.reshape(-1, d_block.shape[2]), "dp", axis=0, tiled=True, axis_index_groups=lanes
+    )
+    w_gu = w_gu.reshape(width, w_gate.shape[1])
     w_xy = w_xy.reshape(width, rec)
     w_o = w_o.reshape(rec, width // 2)
-    w_gu = w_gu.reshape(width, w_gate.shape[1])
-    w_d = w_d.reshape(width, w_gate.shape[1] // 2)
+    def lane_sum(array):
+        return lax.psum_scatter(array, "dp", scatter_dimension=0, tiled=True, axis_index_groups=lanes)
+
     cot_all = cot_all.reshape(4 * tokens, width)
 
     vectors = all_gs[:, :, :, own:].transpose(1, 0, 2, 3, 4).reshape(2 * dp_size, PAD * WIDE)
@@ -475,12 +680,7 @@
     gates = lax.dynamic_slice_in_dim(all_gs[:, :, :, :own], core * half, half, 1)
     gates = gates.transpose(1, 0, 2, 3, 4).reshape(rh, WIDE)
 
-    rows_f = rows_two.astype(F32)
-    rs1 = lax.rsqrt(jnp.mean(rows_f * rows_f, axis=-1, keepdims=True) + EPS)
-    n1 = (rows_f * rs1 * gain_one).astype(BF16).reshape(2 * tokens, width)
-    xy = nn(n1, w_xy)
-    xb = xy[:, :rh].astype(BF16).reshape(2, tokens, rh)
-    ypre = xy[:, rh:].reshape(2, tokens, rh)
+    n1, xb, ypre = project(rows_two, gain_one[None], w_xy)
     before = lax.ppermute(xb[:, tokens - (taps - 1) :], "tp", [(0, 1)])
     halo = jnp.concatenate([jnp.zeros((2, 8 - (taps - 1), rh), F32), before.astype(F32)], axis=1)
     u, a, h_local, coef = recurrence(xb, halo, gates, cp, starts_two)
@@ -488,61 +688,54 @@
     h = h_local + coef * h_in
     ybr, _ = gelu_parts(ypre)
     o = (h * ybr).astype(BF16)
-    o_sib = swapped(sibling(o))
-    o_full = by_core(o, o_sib, 2).reshape(2 * tokens, rec)
-    part = nn(o_full, w_o).reshape(2, tokens, width // 2)
-    x1 = rows_own.astype(F32) + by_core(part[0], sibling(part[1]), 1)
+    o_sib = sibling(o)
+    part_mine, part_theirs = project_out(o, o_sib, w_o)
+    x1 = rows_own.astype(F32) + by_core(part_mine, sibling(part_theirs), 1)
     rs2 = lax.rsqrt(jnp.mean(x1 * x1, axis=-1, keepdims=True) + EPS)
     n2 = (x1 * rs2 * gain_two).astype(BF16)
-    two = jnp.concatenate([n2, across(n2)], axis=0)
+    def plane(array, which):
+        return lax.dynamic_index_in_dim(array, which, 2, keepdims=False)
+
+    def both(mine, axis):
+        return jnp.concatenate([mine, across(mine)], axis)
+
+    n2_x = across(n2)
+
+    def plane_rows(values, rows):
+        grouped = after(values, n2_x).T.reshape(n, 2, 2, rows, 2 * tokens)
+        return plane(grouped, x), plane(grouped, 1 - x)
+
+    o_here, o_send = plane_rows(jnp.concatenate([o, swapped(o_sib)], axis=2).reshape(2 * tokens, rec), own)
+    n1_here, n1_send = plane_rows(n1, own_d)
+    two = jnp.concatenate([n2, n2_x], axis=0)
     n2_all = jnp.concatenate([two, sibling(two)], axis=0)
+    o_t = jnp.concatenate([o_here, across(o_send)], axis=3).reshape(rh, 4 * tokens)
+    n1_t = jnp.concatenate([n1_here, across(n1_send)], axis=3).reshape(width // 2, 4 * tokens)
 
     fh = w_d.shape[1]
     gu = nn(n2_all, w_gu)
     gate, upv = gu[:, :fh], gu[:, fh:]
     act, slope = gelu_parts(gate)
     hidden = (act * upv).astype(BF16)
-    d_hidden = nn(cot_all, w_d)
+
+    def tn(left, right):
+        return lax.dot_general(left, right, (((0,), (0,)), ((), ())), preferred_element_type=F32)
+
+    part_d = tn(cot_all, hidden).astype(BF16)
+    sum_d = lane_sum(part_d)
+    d_hidden = nn(after(cot_all, part_d), w_d)
     d_gu = jnp.concatenate([(d_hidden * upv * slope).astype(BF16), (d_hidden * act).astype(BF16)], axis=1)
 
-    def gathered_sum(partial):
-        partial = partial.astype(BF16)
-        kept = partial[: 2 * tokens].astype(F32) + sibling(partial[2 * tokens :]).astype(F32)
-        kept = kept.astype(BF16)
-        return kept[:tokens].astype(F32) + across(kept[tokens:]).astype(F32)
-
-    d_n2 = gathered_sum(nt(d_gu, w_gu))
-
-    def chip_rel(k):
-        return chip_at((pos + k) % n, n)
-
-    def ring_sum(product):
-        def way(perm, sign, far):
-            out = {}
-            for which in (0, 1):
-                first = half if which == far else half - 1
-                got = None
-                for k in range(first, 0, -1):
-                    term = product(chip_rel((sign * k) % n), which)
-                    send = term if got is None else term + got.astype(F32)
-                    got = lax.ppermute(send.astype(BF16), "dp", perm)
-                out[which] = got
-            return out
-
-        f, b = way(up, 1, 0), way(down, -1, 1)
-        return [product(chip, w) + f[w].astype(F32) + b[w].astype(F32) for w in (0, 1)]
-
-    def pick(array, chip_id, which):
-        other = core + which - 2 * core * which
-        index = (chip_id, other) + (0,) * (array.ndim - 2)
-        return lax.dynamic_slice(array, index, (1, 1) + array.shape[2:]).reshape(array.shape[2:])
-
-    cot_t = cot_all.T.reshape(n, 2, width // dp_size, 4 * tokens)
-    n2_t = n2_all.T.reshape(n, 2, width // dp_size, 4 * tokens)
-    sum_d = ring_sum(lambda chip_id, which: nn(pick(cot_t, chip_id, which), hidden))
-    sum_gu = ring_sum(lambda chip_id, which: nn(pick(n2_t, chip_id, which), d_gu))
-    ff_out = gathered_sum(nt(hidden, w_d))
-    result = (x1 + ff_out).astype(BF16).reshape(1, tokens, width)
+    def pair_sum(partial):
+        return (partial[: 2 * tokens].astype(F32) + sibling(partial[2 * tokens :]).astype(F32)).astype(BF16)
+
+    d_n2_pair = pair_sum(nt(d_gu, w_gu).astype(BF16))
+    d_n2_send = d_n2_pair[tokens:]
+    d_n2 = d_n2_pair[:tokens].astype(F32) + across(d_n2_send).astype(F32)
+    part_gu = tn(ring_order(n2_all, 1), after(d_gu, d_n2_send)).astype(BF16)
+    sum_gu = lane_sum(part_gu)
+    ff_pair = pair_sum(nt(after(hidden, part_gu), w_d).astype(BF16))
+    ff_out = ff_pair[:tokens].astype(F32) + across(ff_pair[tokens:]).astype(F32)
 
     q2 = gain_two * d_n2
     d_gain_two = jnp.sum(d_n2 * x1 * rs2, axis=0)
@@ -552,15 +745,15 @@
     dbr_theirs = lax.dynamic_slice_in_dim(dbr, (1 - core) * (width // 2), width // 2, 1)
     dbr_half = jnp.concatenate([dbr_mine, sibling(dbr_theirs)], axis=0)
     do_part = nt(dbr_half, w_o)
-    do_mine = lax.dynamic_slice_in_dim(do_part, core * rh, rh, 1).reshape(2, tokens, rh)
-    do_theirs = lax.dynamic_slice_in_dim(do_part, (1 - core) * rh, rh, 1).reshape(2, tokens, rh)
-    do = do_mine + swapped(sibling(do_theirs))
+    do = do_part[:, :rh].reshape(2, tokens, rh) + swapped(sibling(do_part[:, rh:].reshape(2, tokens, rh)))
+    dbr_x = across(dbr_half)
 
     d_ypre, lam_local, coef_back = adjoint(do, h, ypre, a)
+    d_ypre_x = both(d_ypre.reshape(2 * tokens, rh), 0)
     inc = lax.ppermute(a[:, :1] * lam_local[:, :1], "tp", [(1, 0)])
     du, d_gates, sums = gates_back(lam_local, coef_back, inc, h, h_in, u, gates, cp, starts_two)
-    after = lax.ppermute(du[:, : taps - 1], "tp", [(1, 0)])
-    du_pad = jnp.concatenate([du, after], axis=1).astype(F32)
+    du_next = lax.ppermute(du[:, : taps - 1], "tp", [(1, 0)])
+    du_pad = jnp.concatenate([du, du_next], axis=1).astype(F32)
     xb_pad = jnp.concatenate([before, xb], axis=1).astype(F32)
     d_taps = jnp.stack(
         [jnp.sum(du_pad[:, :tokens] * xb_pad[:, taps - 1 - k : taps - 1 - k + tokens], axis=(0, 1)) for k in range(taps)]
@@ -568,29 +761,18 @@
     d_bias = jnp.sum(du_pad[:, :tokens], axis=(0, 1))[None]
     d_xb = sum(cp[k] * du_pad[:, k : k + tokens] for k in range(taps)).astype(BF16)
     d_xy = jnp.concatenate([d_xb, d_ypre], axis=2).reshape(2 * tokens, rec)
+    result = (after(x1, d_xb) + chip_order(ff_out, 1)).astype(BF16).reshape(1, tokens, width)
     d_n1_part = nt(d_xy, w_xy).reshape(2, tokens, width)
     d_n1 = d_n1_part[0] + sibling(d_n1_part[1])
     q1 = gain_one * d_n1
-    own_f, own_rs = rows_f[0], rs1[0]
+    own_f = rows_own.astype(F32)
+    own_rs = lax.rsqrt(jnp.mean(own_f * own_f, axis=-1, keepdims=True) + EPS)
     d_gain_one = jnp.sum(d_n1 * own_f * own_rs, axis=0)
     grad_x = d_x1 + own_rs * q1 - own_f * (own_rs * own_rs * own_rs) * jnp.mean(own_f * q1, axis=-1, keepdims=True)
 
-    def plane(array, which):
-        return lax.dynamic_index_in_dim(array, which, 2, keepdims=False)
-
-    def both(mine, axis):
-        return jnp.concatenate([mine, across(mine)], axis)
-
-    def plane_rows(values, rows):
-        grouped = values.T.reshape(n, 2, 2, rows, 2 * tokens)
-        return jnp.concatenate([plane(grouped, x), across(plane(grouped, 1 - x))], axis=3)
-
-    o_t = plane_rows(o_full, own)
-    dbr_x = both(dbr_half, 0)
-    sum_out = ring_sum(lambda chip_id, which: nn(pick(o_t, chip_id, which), dbr_x))
-    n1_t = plane_rows(n1, own_d)
-    d_xy_x = both(d_xy, 0)
-    sum_xy = ring_sum(lambda chip_id, which: nn(pick(n1_t, chip_id, which), d_xy_x))
+    c_out = nn(after(o_t, d_xb), jnp.concatenate([dbr_half, dbr_x], axis=0)).astype(BF16).reshape(n, 2, own, width // 2)
+    c_x = nn(n1_t, both(d_xb.reshape(2 * tokens, rh), 0)).astype(BF16).reshape(n, 2, own_d, rh)
+    c_y = nn(n1_t, d_ypre_x).astype(BF16).reshape(n, 2, own_d, rh)
 
     def placed(part):
         zero = jnp.zeros_like(part)
@@ -618,33 +800,25 @@
         lax.dynamic_index_in_dim(vec, 1 - core, 1, keepdims=False)
     )
 
-    def lane_sum(array):
-        def at(chip_id):
-            return lax.dynamic_index_in_dim(array, chip_id, 0, keepdims=False)
-
-        total = at(chip)
-        for perm, sign, first in ((up, 1, half), (down, -1, half - 1)):
-            got = None
-            for k in range(first, 0, -1):
-                term = at(chip_rel((sign * k) % n))
-                send = term if got is None else term + got.astype(F32)
-                got = lax.ppermute(send, "dp", perm)
-            total = total + got
-        return total
-
-    sum_gates = lane_sum(g_lane)
-    sum_vec = lane_sum(vec)
-
-    def whole(halves, axis):
-        return by_core(halves[0], sibling(halves[1]), axis)
-
-    gu0, gu1 = sum_gu
-    grad_gate = whole((gu0[:, :fh], gu1[:, :fh]), 1)
-    grad_up = whole((gu0[:, fh:], gu1[:, fh:]), 1)
-    grad_down = whole(sum_d, 1).T
-    grad_w_x = whole((sum_xy[0][:, :rh], sum_xy[1][:, :rh]), 1)
-    grad_w_y = whole((sum_xy[0][:, rh:], sum_xy[1][:, rh:]), 1)
-    grad_w_out = whole(sum_out, 1)
+    vec = jnp.pad(vec, ((0, 0), (0, -vec.shape[1] % 1024))).reshape(n, -1, 128)
+    def whole(block):
+        rows = block.shape[0] // 2
+        block = block.reshape(2, rows, block.shape[1])
+        mine = lax.dynamic_index_in_dim(block, core, 0, keepdims=False)
+        theirs = lax.dynamic_index_in_dim(block, 1 - core, 0, keepdims=False)
+        return mine, sibling(theirs)
+
+    def halves(pair):
+        return by_core(pair[0], pair[1], 1).astype(F32)
+
+    grad_down = halves(whole(sum_d)).T
+    grad_w_x, grad_w_y, grad_w_out, sum_gates, sum_vec = scatter_sums(
+        n, after(c_x, grad_down, result, grad_x), c_y, c_out, g_lane.astype(BF16), vec
+    )
+    sum_vec = sum_vec.reshape(-1)
+    gu_mine, gu_theirs = whole(sum_gu)
+    grad_gate = halves((gu_mine[:, :fh], gu_theirs[:, :fh]))
+    grad_up = halves((gu_mine[:, fh:], gu_theirs[:, fh:]))
     tail = sum_vec[2 * own_d : 2 * own_d + (taps + 4) * own].reshape(taps + 4, own)
     return (
         result,

time: 911 us -> 641 us (0.70)
  waiting for transfers between devices: 247 us -> 70.7 us
  starting transfers between devices: 90.7 us -> 23 us
  matrix products: 140 us -> 74.5 us
  Pallas kernels: 306 us -> 335 us
  local copies, waits for them, and re-layouts: 59.9 us -> 73 us
  between operations: 3.62 us -> 16.4 us
  other arithmetic: 53 us -> 42.5 us
    ppermute x71 -> x1, waiting for transfers between devices: 167 us -> 2.5 us  [body(): du_next = lax.ppermute(du[:, :taps - 1], 'tp', [(1, 0)])]
    pallas_call x0 -> x3, Pallas kernels: none -> 101 us  [the longest x1 91 us: scatter_sums(): pl.pallas_call(functools.partial(scatter_kernel, n), out_shape=[jax.Shape...]
    dot_general x68 -> x5, matrix products: 121 us -> 33.6 us  [nn(): return jnp.dot(left, right, preferred_element_type=F32)]
    pallas_call x1, Pallas kernels: 288 us -> 216 us  [gather_weights(): pl.pallas_call(functools.partial(gather_kernel, n), out_shape=shapes, in_...]
    ppermute x71 -> x1, starting transfers between devices: 72.4 us -> 1.6 us  [body(): du_next = lax.ppermute(du[:, :taps - 1], 'tp', [(1, 0)])]
    unnamed x182 -> x211, local copies, waits for them, and re-layouts: 13.9 us -> 41.6 us
    dot_general x0 -> x2, matrix products: none -> 16.8 us  [tn(): lax.dot_general(left, right, (((0,), (0,)), ((), ())), preferred_element_...]
    ppermute x9 -> x10, waiting for transfers between devices: 71.3 us -> 58.5 us  [across(): return lax.ppermute(v, 'tp', [(0, 1), (1, 0)])]
  transfers between devices with their start and end apart: 99 -> 29, of which waited for: 42 -> 11; matrix products, arithmetic and copies ran while one was open for 23% -> 23% of each run, Pallas kernels for 1% -> 19%
where the time goes in v2:
time: 641 us; the launch traced here: 635 us
  Pallas kernels  335 us (52%)
  matrix products  74.5 us (12%)
  local copies, waits for them, and re-layouts  73 us (11%)
  waiting for transfers between devices  70.7 us (11%)
  other arithmetic  42.5 us (7%)
  starting transfers between devices  23 us (4%)
  between operations  16.4 us (3%)
    pallas_call x1, Pallas kernels, gather_weights(): pl.pallas_call(functools.partial(gather_kernel, n), out_shape=shapes, in_...  216 us
    pallas_call x1, Pallas kernels, scatter_sums(): pl.pallas_call(functools.partial(scatter_kernel, n), out_shape=[jax.Shape...  91 us
    ppermute x10, waiting for transfers between devices, across(): return lax.ppermute(v, 'tp', [(0, 1), (1, 0)])  58.5 us
    unnamed x211, local copies, waits for them, and re-layouts  41.6 us
    dot_general x5, matrix products, nn(): return jnp.dot(left, right, preferred_element_type=F32)  33.6 us
    dot_general x4, matrix products, nt(): lax.dot_general(left, right, (((1,), (1,)), ((), ())), preferred_element_...  24.1 us
    dot_general x2, matrix products, tn(): lax.dot_general(left, right, (((0,), (0,)), ((), ())), preferred_element_...  16.8 us
    ppermute x10, starting transfers between devices, across(): return lax.ppermute(v, 'tp', [(0, 1), (1, 0)])  14.2 us
  transfers between devices with their start and end apart: 29, of which 11 were waited for; matrix products, arithmetic and copies ran while one was open for 23% of the time, Pallas kernels for 19%

profile of v2, /device:TPU:0, one launch (start us, length us, event | category | flops | bytes accessed | tf_op | source)
XLA Modules:
  0.0 635.1 jit_solution(7208114127192306246)
XLA Ops:
  9.5 1.4 copy.46
  15.5 215.5 %gather_weights.1 = (bf16[8,2,2,64,2560]{4,3,2,1,0:T(8,128)(2,1)S(1)}, bf16[8,2,2,80,1024]{4,3,2,1,0:T(8,128)(2,1)S(1)}, bf16[2,8,2,96,512]{4,3,2,1,0:T(8,128)(2...) custom-call(bf16[64,2560]{1,0:T(8,128)(2,1)S(1)} %copy-done.25, ...), custom_call_target="tpu_custom_call" | custom-call | tf_op jit(solution)/shard_map/gather_weights/pallas_call | solution.py:189
  231.1 3.8 copy-done
  234.9 2.4 copy-done.4
  237.3 1.7 copy-done.10
  240.0 1.4 copy-done.31
  243.6 4.2 copy-done.1
  247.9 6.1 project.1
  256.1 2.4 collective-permute-start
  258.5 3.7 slice.270
  262.9 1.5 dynamic-slice_bitcast_fusion
  264.7 6.9 %recurrence.1 = (bf16[2,128,1280]{2,1,0:T(8,128)(2,1)S(1)}, f32[2,128,1280]{2,1,0:T(8,128)S(1)}, f32[2,128,1280]{2,1,0:T(8,128)S(1)}, f32[2,128,1280]{2,1,0:T(8,128)S(1)}) custom-call(bf16[2,128,1280]{2,1,0:T(8,128)(2,1)S(1)} %get-tuple-element.56.xb, f32[2,8,1280]{2,1,0:T(8,128)S(1)} %pad_convert_fusion.halo, bf16[1280,512]{1,0:T(8,128)(2,1)S(1)} %bitcast.130, ...), custom_call_target="tpu_custom_call" | custom-call | flops 400000000 | bytes 6000000 | tf_op jit(solution)/shard_map/recurrence/pallas_call | solution.py:454
  272.4 1.5 collective-permute-start.1
  275.7 2.1 collective-permute-done.2.o_sib
  277.8 3.5 project_out.1
  282.3 2.0 collective-permute-done.3
  284.4 1.9 multiply_reduce_fusion.2
  287.0 2.4 collective-permute-start.4
  289.4 12.2 %collective-permute-done.4 = bf16[128,2048]{1,0:T(8,128)(2,1)S(1)} collective-permute-done((bf16[128,2048]{1,0:T(8,128)(2,1)S(1)}, bf16[128,2048]{1,0:T(8,128)(2,1)S(1)}, u32[]{:S(2)}, u32[]{:S(2)}) %collective-permute-start.4) | collective-permute-done | bytes 524320 | tf_op jit(solution)/shard_map/ppermute | solution.py:620
  301.8 2.6 collective-permute-done.5
  304.4 9.7 %fusion.52 = f32[512,3072]{1,0:T(8,128)S(1)} fusion(bf16[2048,3072]{1,0:T(8,128)(2,1)} %bitcast.168, bf16[256,2048]{1,0:T(8,128)(2,1)S(1)} %collective-permute-done.5, bf16[128,2048]{1,0:T(8,128)(2,1)S(1)} %collective-permute-done.4, bf16[128,2048]{1,0:T(8,128)(2,1)S(1)} %multiply_convert_fusion.2), kind=kOutput, calls=%fused_computation.186 | convolution fusion | flops 6448742400 | bytes 20971520 | tf_op jit(solution)/shard_map/dot_general | solution.py:590
  315.2 1.7 copy-done.44
  318.1 5.5 convolution_convert_fusion.1
  323.7 1.8 maximum_dynamic-update-slice_fusion.5
  326.3 1.6 pad_maximum_fusion.1
  327.8 10.9 %fusion.6 = (bf16[512,1536]{1,0:T(8,128)(2,1)S(1)}, bf16[512,1536]{1,0:T(8,128)(2,1)S(1)}) fusion(f32[512,3072]{1,0:T(8,128)} %copy-done.44, bf16[512,2048]{1,0:T(8,128)(2,1)} %bitcast.137, bf16[2048,1536]{1,0:T(8,128)(2,1)} %all-gather.2.cloned.1.call-done), kind=kOutput, calls=%fused_computation.13 | convolution fusion | flops 3239313408 | bytes 17825792 | tf_op jit(solution)/shard_map/dot_general | solution.py:590
  338.7 10.2 %convolution_convert_fusion.5 = bf16[512,2048]{1,0:T(8,128)(2,1)S(1)} fusion(bf16[2048,3072]{1,0:T(8,128)(2,1)} %bitcast.169, bf16[512,1536]{1,0:T(8,128)(2,1)S(1)} %get-tuple-element.145, bf16[512,1536]{1,0:T(8,128)(2,1)S(1)} %get-tuple-element.144), kind=kOutput, calls=%fused_computation.17 | convolution fusion | flops 6449790976 | bytes 17825792 | tf_op jit(solution)/shard_map/dot_general | solution.py:586
  351.1 1.9 slice_dynamic-update-slice_fusion
  358.0 11.3 %convolution_convert_fusion = bf16[2048,3072]{1,0:T(8,128)(2,1)} fusion(bf16[512,2048]{1,0:T(8,128)(2,1)} %maximum_dynamic-update-slice_fusion, bf16[512,3072]{1,0:T(8,128)(2,1)S(1)} %pad_maximum_fusion), kind=kOutput, calls=%fused_computation | convolution fusion | flops 6448742400 | bytes 17825792 | tf_op jit(solution)/shard_map/dot_general | solution.py:722
  372.1 2.3 maximum_convert_fusion.1
  376.2 2.5 copy.53
  378.7 2.4 constant_dynamic-slice_fusion.8
  381.2 1.7 collective-permute-start.19
  384.8 1.7 collective-permute-start.7
  386.5 6.6 %convolution_convert_fusion.6 = bf16[512,2048]{1,0:T(8,128)(2,1)S(1)} fusion(bf16[512,1536]{1,0:T(8,128)(2,1)S(1)} %copy-done.52, bf16[2048,1536]{1,0:T(8,128)(2,1)} %all-gather.2.cloned.1.call-done), kind=kOutput, calls=%fused_computation.18 | convolution fusion | flops 3222274048 | bytes 9961472 | tf_op jit(solution)/shard_map/dot_general | solution.py:586
  394.3 26.3 %collective-permute-done.7 = bf16[128,2048]{1,0:T(8,128)(2,1)S(1)} collective-permute-done((bf16[128,2048]{1,0:T(8,128)(2,1)S(1)}, bf16[128,2048]{1,0:T(8,128)(2,1)S(1)}, u32[]{:S(2)}, u32[]{:S(2)}) %collective-permute-start.7) | collective-permute-done | bytes 524320 | tf_op jit(solution)/shard_map/ppermute | solution.py:620
  421.1 1.5 fusion.53
  423.3 2.2 pad_maximum_fusion.3
  426.3 4.3 fusion.51
  430.7 1.6 add_convert_fusion
  432.4 1.8 collective-permute-start.13
  436.0 11.2 %collective-permute-done.13 = bf16[128,2048]{1,0:T(8,128)(2,1)S(1)} collective-permute-done((bf16[128,2048]{1,0:T(8,128)(2,1)S(1)}, bf16[128,2048]{1,0:T(8,128)(2,1)S(1)}, u32[]{:S(2)}, u32[]{:S(2)}) %collective-permute-start.13) | collective-permute-done | bytes 524320 | tf_op jit(solution)/shard_map/ppermute | solution.py:620
  449.2 5.3 adjoint.1
  455.9 2.7 collective-permute-start.18
  458.6 1.7 collective-permute-done.10.inc
  460.3 6.6 %gates_back.1 = (bf16[2,128,1280]{2,1,0:T(8,128)(2,1)S(1)}, f32[1280,512]{1,0:T(8,128)S(1)}, f32[8,1280]{1,0:T(8,128)S(1)}) custom-call(f32[2,128,1280]{2,1,0:T(8,128)S(1)} %get-tuple-element.69.lam_ref, f32[2,128,1280]{2,1,0:T(8,128)S(1)} %get-tuple-element.70.c_ref, f32[2,1,1280]{2,1,0:T(1,128)S(1)} %collective-permute-done.10.inc, ...), custom_call_target="tpu_custom_call" | custom-call | flops 1200000000 | bytes 9000000 | tf_op jit(solution)/shard_map/gates_back/pallas_call | solution.py:565
  467.0 1.6 collective-permute-start.11
  469.7 2.7 collective-permute-start.21
  472.4 2.5 collective-permute-done.11
  476.1 5.2 fusion.13
  481.3 1.4 pad_maximum_fusion.2
  482.7 2.9 fusion.62
  489.3 4.2 convolution_convert_fusion.2
  495.7 4.5 convolution_convert_fusion.3
  500.2 5.0 collective-permute-done.16
  505.2 4.5 convolution_convert_fusion.4
  510.6 1.6 fusion.33
  512.9 3.8 collective-permute-done.23
  519.5 2.9 fusion.30
  524.5 91.0 %scatter_sums.1 = (f32[64,2560]{1,0:T(8,128)}, f32[64,2560]{1,0:T(8,128)}, f32[80,2048]{1,0:T(8,128)}, f32[80,512]{1,0:T(8,128)}, f32[8,128]{1,0:T(8,128)}) custom-call(bf16[8,2,64,1280]{3,2,1,0:T(8,128)(2,1)} %bitcast.146, bf16[8,2,64,1280]{3,2,1,0:T(8,128)(2,1)} %bitcast.145, bf16[8,2,80,1024]{3,2,1,0:T(8,128)(2,1)} %bitcast.144, ...), custom_call_target="tpu_custom_call" | custom-call | tf_op jit(solution)/shard_map/scatter_sums/pallas_call | solution.py:290
  616.8 1.5 constant_dynamic-slice_fusion.1
  619.2 1.3 fusion.61
  622.6 1.6 copy.59
  624.2 1.6 copy.60
  (353 shorter events, 62.6 us)
Async XLA Ops:
  7.3 320.5 %all-gather.2.cloned.1.call-start = ((), (), s32[]{:S(2)}) async-start(), calls=%async_computation.2 | async-start | bytes 7077888 | tf_op jit(solution)/shard_map/all_gather | solution.py:659
  241.3 12.6 %copy-start.28 = (f32[2,128,128]{2,1,0:T(8,128)}, f32[2,128,128]{2,1,0:T(8,128)S(1)}, u32[]{:S(2)}) copy-start(f32[2,128,128]{2,1,0:T(8,128)S(1)} %get-tuple-element.57.starts) | copy-start | bytes 393220
  241.4 275.5 %reduce-scatter.3.cloned.1.call-start = ((), (), s32[]{:S(2)}) async-start(), calls=%async_computation.3 | async-start | bytes 7077888 | tf_op jit(solution)/shard_map/reduce_scatter | solution.py:666
  256.1 8.6 %copy-start.20 = (bf16[2,128,1280]{2,1,0:T(8,128)(2,1)}, bf16[2,128,1280]{2,1,0:T(8,128)(2,1)S(1)}, u32[]{:S(2)}) copy-start(bf16[2,128,1280]{2,1,0:T(8,128)(2,1)S(1)} %get-tuple-element.56.xb) | copy-start | bytes 1966084
  256.1 8.5 %collective-permute-start = (bf16[2,3,1280]{2,1,0:T(4,128)(2,1)S(1)}, bf16[2,3,1280]{2,1,0:T(4,128)(2,1)S(1)}, u32[]{:S(2)}, u32[]{:S(2)}) collective-permute-start(bf16[2,3,1280]{2,1,0:T(4,128)(2,1)S(1)} %slice.269), channel_id=1, source_target_pairs={{0,1},{2,3},{4,5},{6,7},{8,9},{10,11},{12,13},{14,15},{16,17},{18,... | collective-permute-start | bytes 46088 | tf_op jit(solution)/shard_map/ppermute | solution.py:684
  264.4 13.4 %slice-start.3 = ((s8[5242880]{0:T(1024)(128)(4,1)}), s8[4194304]{0:T(1024)(128)(4,1)S(1)}, s32[]{:S(2)}) async-start(s8[5242880]{0:T(1024)(128)(4,1)} %bitcast.127), calls=%async_computation.8 | async-start | bytes 8388608
  264.6 11.1 %copy-start.8 = (bf16[4,2,2,80,512]{4,3,2,1,0:T(8,128)(2,1)}, bf16[4,2,2,80,512]{4,3,2,1,0:T(8,128)(2,1)S(1)}, u32[]{:S(2)}) copy-start(bf16[4,2,2,80,512]{4,3,2,1,0:T(8,128)(2,1)S(1)} %copy.48) | copy-start | bytes 3932164
  264.6 10.5 %copy-start.6 = (f32[2,128,1280]{2,1,0:T(8,128)S(1)}, f32[2,128,1280]{2,1,0:T(8,128)}, u32[]{:S(2)}) copy-start(f32[2,128,1280]{2,1,0:T(8,128)} %copy-done.5) | copy-start | bytes 3932164
  264.7 13.2 %slice-start.4 = ((s8[5242880]{0:T(1024)(128)(4,1)}), s8[1048576]{0:T(1024)(128)(4,1)S(1)}, s32[]{:S(2)}) async-start(s8[5242880]{0:T(1024)(128)(4,1)} %bitcast.127), calls=%async_computation.9 | async-start | bytes 2097152
  272.4 2.7 collective-permute-start.1
  275.7 2.2 collective-permute-start.2
  277.8 4.4 copy-start.67
  282.1 2.3 collective-permute-start.3
  286.3 18.1 %copy-start.39 = (f32[128,2048]{1,0:T(8,128)}, f32[128,2048]{1,0:T(8,128)S(1)}, u32[]{:S(2)}) copy-start(f32[128,2048]{1,0:T(8,128)S(1)} %get-tuple-element.73) | copy-start | bytes 3145732
  286.9 27.2 %copy-start.74 = (f32[128]{0:T(128)}, f32[128]{0:T(128)S(1)}, u32[]{:S(2)}) copy-start(f32[128]{0:T(128)S(1)} %get-tuple-element.187) | copy-start | bytes 1540
  287.0 14.6 %collective-permute-start.4 = (bf16[128,2048]{1,0:T(8,128)(2,1)S(1)}, bf16[128,2048]{1,0:T(8,128)(2,1)S(1)}, u32[]{:S(2)}, u32[]{:S(2)}) collective-permute-start(bf16[128,2048]{1,0:T(8,128)(2,1)S(1)} %multiply_convert_fusion.2), channel_id=1, source_target_pairs={{0,1},{1,0},{2,3},{3,2},{4,5},{5,4},{6,7},{7,6},{8,9},{9,8},{10,11... | collective-permute-start | bytes 1572872 | tf_op jit(solution)/shard_map/ppermute | solution.py:620
  301.6 12.5 %copy-start.36 = (bf16[128,2048]{1,0:T(8,128)(2,1)}, bf16[128,2048]{1,0:T(8,128)(2,1)S(1)}, u32[]{:S(2)}) copy-start(bf16[128,2048]{1,0:T(8,128)(2,1)S(1)} %collective-permute-done.4) | copy-start | bytes 1572868
  301.7 2.7 collective-permute-start.5
  304.4 9.7 %copy-start.33 = (bf16[256,2048]{1,0:T(8,128)(2,1)}, bf16[256,2048]{1,0:T(8,128)(2,1)S(1)}, u32[]{:S(2)}) copy-start(bf16[256,2048]{1,0:T(8,128)(2,1)S(1)} %collective-permute-done.5) | copy-start | bytes 3145732
  323.7 293.1 %reduce-scatter.5.cloned.1.call-start = ((), (), s32[]{:S(2)}) async-start(), calls=%async_computation.4 | async-start | bytes 14155776 | tf_op jit(solution)/shard_map/reduce_scatter | solution.py:666
  349.0 6.7 %collective-permute-start.6 = (bf16[256,2048]{1,0:T(8,128)(2,1)S(1)}, bf16[256,2048]{1,0:T(8,128)(2,1)S(1)}, u32[]{:S(2)}, u32[]{:S(2)}) collective-permute-start(bf16[256,2048]{1,0:T(8,128)(2,1)S(1)} %slice.355), channel_id=1, source_target_pairs={{0,2},{2,0},{4,6},{6,4},{8,10},{10,8},{12,14},{14,12},{16,18},{18,... | collective-permute-start | bytes 3145736 | tf_op jit(solution)/shard_map/ppermute | solution.py:617
  376.2 6.7 %copy-start.16 = (bf16[256,2048]{1,0:T(8,128)(2,1)S(1)}, bf16[256,2048]{1,0:T(8,128)(2,1)}, u32[]{:S(2)}) copy-start(bf16[256,2048]{1,0:T(8,128)(2,1)} %copy-done.15) | copy-start | bytes 3145732
  381.2 42.1 %collective-permute-start.19 = (bf16[8,2,80,256]{3,2,1,0:T(8,128)(2,1)}, bf16[8,2,80,256]{3,2,1,0:T(8,128)(2,1)}, u32[]{:S(2)}, u32[]{:S(2)}) collective-permute-start(bf16[8,2,80,256]{3,2,1,0:T(8,128)(2,1)} %get-tuple-element.152), channel_id=1, source_target_pairs={{0,1},{1,0},{2,3},{3,2},{4,5},{5,4},{6,7},{7,6},{8,9},{9,8},{10,11... | collective-permute-start | bytes 1966088 | tf_op jit(solution)/shard_map/ppermute | solution.py:620
  384.5 111.2 %collective-permute-start.15 = (bf16[8,2,64,256]{3,2,1,0:T(8,128)(2,1)}, bf16[8,2,64,256]{3,2,1,0:T(8,128)(2,1)}, u32[]{:S(2)}, u32[]{:S(2)}) collective-permute-start(bf16[8,2,64,256]{3,2,1,0:T(8,128)(2,1)} %get-tuple-element.156), channel_id=1, source_target_pairs={{0,1},{1,0},{2,3},{3,2},{4,5},{5,4},{6,7},{7,6},{8,9},{9,8},{10,11... | collective-permute-start | bytes 1572872 | tf_op jit(solution)/shard_map/ppermute | solution.py:620
  384.8 35.8 %collective-permute-start.7 = (bf16[128,2048]{1,0:T(8,128)(2,1)S(1)}, bf16[128,2048]{1,0:T(8,128)(2,1)S(1)}, u32[]{:S(2)}, u32[]{:S(2)}) collective-permute-start(bf16[128,2048]{1,0:T(8,128)(2,1)S(1)} %copy-done.61), channel_id=1, source_target_pairs={{0,1},{1,0},{2,3},{3,2},{4,5},{5,4},{6,7},{7,6},{8,9},{9,8},{10,11... | collective-permute-start | bytes 1572872 | tf_op jit(solution)/shard_map/ppermute | solution.py:620
  386.5 34.0 %copy-start.75 = (f32[128]{0:T(128)S(1)}, f32[128]{0:T(128)}, u32[]{:S(2)}) copy-start(f32[128]{0:T(128)} %copy-done.74) | copy-start | bytes 1540
  393.2 27.8 %copy-start.48 = (bf16[512,2048]{1,0:T(8,128)(2,1)}, bf16[512,2048]{1,0:T(8,128)(2,1)S(1)}, u32[]{:S(2)}) copy-start(bf16[512,2048]{1,0:T(8,128)(2,1)S(1)} %convolution_convert_fusion.6) | copy-start | bytes 6291460
  393.2 27.4 %copy-start.40 = (f32[128,2048]{1,0:T(8,128)S(1)}, f32[128,2048]{1,0:T(8,128)}, u32[]{:S(2)}) copy-start(f32[128,2048]{1,0:T(8,128)} %copy-done.39) | copy-start | bytes 3145732
  393.2 27.4 %copy-start.43 = (bf16[256,2048]{1,0:T(8,128)(2,1)S(1)}, bf16[256,2048]{1,0:T(8,128)(2,1)}, u32[]{:S(2)}) copy-start(bf16[256,2048]{1,0:T(8,128)(2,1)} %copy-done.42) | copy-start | bytes 3145732
  393.2 27.8 %copy-start.50 = (bf16[1,128,2048]{2,1,0:T(8,128)(2,1)S(1)}, bf16[1,128,2048]{2,1,0:T(8,128)(2,1)}, u32[]{:S(2)}) copy-start(bf16[1,128,2048]{2,1,0:T(8,128)(2,1)} %param.20) | copy-start | bytes 1572868
  393.2 27.8 %copy-start.77 = (f32[128]{0:T(128)S(1)}, f32[128]{0:T(128)}, u32[]{:S(2)}) copy-start(f32[128]{0:T(128)} %copy-done.76) | copy-start | bytes 1540
  393.2 27.8 %copy-start.86 = (f32[128]{0:T(128)S(1)}, f32[128]{0:T(128)}, u32[]{:S(2)}) copy-start(f32[128]{0:T(128)} %get-tuple-element.186) | copy-start | bytes 1540
  394.3 36.4 %collective-permute-start.12 = (bf16[256,2048]{1,0:T(8,128)(2,1)}, bf16[256,2048]{1,0:T(8,128)(2,1)}, u32[]{:S(2)}, u32[]{:S(2)}) collective-permute-start(bf16[256,2048]{1,0:T(8,128)(2,1)} %slice.371), channel_id=1, source_target_pairs={{0,2},{2,0},{4,6},{6,4},{8,10},{10,8},{12,14},{14,12},{16,18},{18,... | collective-permute-start | bytes 3145736 | tf_op jit(solution)/shard_map/ppermute | solution.py:617
  423.3 2.3 collective-permute-start.8
  426.3 4.4 copy-start.49
  432.4 14.8 %collective-permute-start.13 = (bf16[128,2048]{1,0:T(8,128)(2,1)S(1)}, bf16[128,2048]{1,0:T(8,128)(2,1)S(1)}, u32[]{:S(2)}, u32[]{:S(2)}) collective-permute-start(bf16[128,2048]{1,0:T(8,128)(2,1)S(1)} %slice.373), channel_id=1, source_target_pairs={{0,1},{1,0},{2,3},{3,2},{4,5},{5,4},{6,7},{7,6},{8,9},{9,8},{10,11... | collective-permute-start | bytes 1572872 | tf_op jit(solution)/shard_map/ppermute | solution.py:620
  434.4 13.0 %collective-permute-start.9 = (f32[2,128,1280]{2,1,0:T(8,128)S(1)}, f32[2,128,1280]{2,1,0:T(8,128)S(1)}, u32[]{:S(2)}, u32[]{:S(2)}) collective-permute-start(f32[2,128,1280]{2,1,0:T(8,128)S(1)} %bitcast.151), channel_id=1, source_target_pairs={{0,2},{2,0},{4,6},{6,4},{8,10},{10,8},{12,14},{14,12},{16,18},{18,... | collective-permute-start | bytes 3932168 | tf_op jit(solution)/shard_map/ppermute | solution.py:617
  435.5 53.7 %collective-permute-start.20 = (bf16[256,1024]{1,0:T(8,128)(2,1)}, bf16[256,1024]{1,0:T(8,128)(2,1)}, u32[]{:S(2)}, u32[]{:S(2)}) collective-permute-start(bf16[256,1024]{1,0:T(8,128)(2,1)} %pad_maximum_fusion.8), channel_id=1, source_target_pairs={{0,1},{1,0},{2,3},{3,2},{4,5},{5,4},{6,7},{7,6},{8,9},{9,8},{10,11... | collective-permute-start | bytes 1572872 | tf_op jit(solution)/shard_map/ppermute | solution.py:620
  449.2 11.0 %copy-start.9 = (bf16[4,2,2,80,512]{4,3,2,1,0:T(8,128)(2,1)S(1)}, bf16[4,2,2,80,512]{4,3,2,1,0:T(8,128)(2,1)}, u32[]{:S(2)}) copy-start(bf16[4,2,2,80,512]{4,3,2,1,0:T(8,128)(2,1)} %copy-done.8) | copy-start | bytes 3932164
  449.2 11.0 %copy-start.23 = (bf16[2,128,1280]{2,1,0:T(8,128)(2,1)S(1)}, bf16[2,128,1280]{2,1,0:T(8,128)(2,1)}, u32[]{:S(2)}) copy-start(bf16[2,128,1280]{2,1,0:T(8,128)(2,1)} %copy-done.22) | copy-start | bytes 1966084
  449.2 11.0 %copy-start.30 = (f32[2,128,128]{2,1,0:T(8,128)S(1)}, f32[2,128,128]{2,1,0:T(8,128)}, u32[]{:S(2)}) copy-start(f32[2,128,128]{2,1,0:T(8,128)} %copy-done.28) | copy-start | bytes 393220
  454.6 5.7 collective-permute-start.10
  455.9 11.0 %copy-start.53 = (f32[128,2048]{1,0:T(8,128)}, f32[128,2048]{1,0:T(8,128)S(1)}, u32[]{:S(2)}) copy-start(f32[128,2048]{1,0:T(8,128)S(1)} %slice_dynamic-update-slice_fusion.1) | copy-start | bytes 3145732
  455.9 39.8 %collective-permute-start.18 = (bf16[256,1280]{1,0:T(8,128)(2,1)}, bf16[256,1280]{1,0:T(8,128)(2,1)}, u32[]{:S(2)}, u32[]{:S(2)}) collective-permute-start(bf16[256,1280]{1,0:T(8,128)(2,1)} %bitcast.30), channel_id=1, source_target_pairs={{0,1},{1,0},{2,3},{3,2},{4,5},{5,4},{6,7},{7,6},{8,9},{9,8},{10,11... | collective-permute-start | bytes 1966088 | tf_op jit(solution)/shard_map/ppermute | solution.py:620
  460.3 22.4 %slice-start = ((s8[10485760]{0:T(1024)(128)(4,1)}), s8[2097152]{0:T(1024)(128)(4,1)S(1)}, s32[]{:S(2)}) async-start(s8[10485760]{0:T(1024)(128)(4,1)} %bitcast.122), calls=%async_computation.5 | async-start | bytes 4194304
  466.9 9.2 %copy-start.70 = (f32[1280]{0:T(1024)S(1)}, f32[1280]{0:T(1024)}, u32[]{:S(2)}) copy-start(f32[1280]{0:T(1024)} %mul.332) | copy-start | bytes 15364
  466.9 9.2 %copy-start.71 = (f32[1280]{0:T(1024)S(1)}, f32[1280]{0:T(1024)}, u32[]{:S(2)}) copy-start(f32[1280]{0:T(1024)} %mul.371) | copy-start | bytes 15364
  467.0 9.2 %copy-start.72 = (f32[1280]{0:T(1024)S(1)}, f32[1280]{0:T(1024)}, u32[]{:S(2)}) copy-start(f32[1280]{0:T(1024)} %mul.374) | copy-start | bytes 15364
  467.0 9.2 %copy-start.73 = (f32[1280]{0:T(1024)S(1)}, f32[1280]{0:T(1024)}, u32[]{:S(2)}) copy-start(f32[1280]{0:T(1024)} %mul.377) | copy-start | bytes 15364
  467.0 7.9 %collective-permute-start.11 = (bf16[2,3,1280]{2,1,0:T(4,128)(2,1)S(1)}, bf16[2,3,1280]{2,1,0:T(4,128)(2,1)S(1)}, u32[]{:S(2)}, u32[]{:S(2)}) collective-permute-start(bf16[2,3,1280]{2,1,0:T(4,128)(2,1)S(1)} %slice.290), channel_id=1, source_target_pairs={{1,0},{3,2},{5,4},{7,6},{9,8},{11,10},{13,12},{15,14},{17,16},{19,... | collective-permute-start | bytes 46088 | tf_op jit(solution)/shard_map/ppermute | solution.py:755
  469.7 13.0 %slice-start.1 = ((s8[10485760]{0:T(1024)(128)(4,1)}), s8[4194304]{0:T(1024)(128)(4,1)S(1)}, s32[]{:S(2)}) async-start(s8[10485760]{0:T(1024)(128)(4,1)} %bitcast.122), calls=%async_computation.6 | async-start | bytes 8388608
  469.7 24.5 %collective-permute-start.21 = (bf16[4,2,80,512]{3,2,0,1:T(8,128)(2,1)}, bf16[4,2,80,512]{3,2,0,1:T(8,128)(2,1)}, u32[]{:S(2)}, u32[]{:S(2)}) collective-permute-start(bf16[4,2,80,512]{3,2,0,1:T(8,128)(2,1)} %fusion.45), channel_id=1, source_target_pairs={{0,1},{1,0},{2,3},{3,2},{4,5},{5,4},{6,7},{7,6},{8,9},{9,8},{10,11... | collective-permute-start | bytes 1966088 | tf_op jit(solution)/shard_map/ppermute | solution.py:620
  476.1 6.6 %slice-start.2 = ((s8[10485760]{0:T(1024)(128)(4,1)}), s8[4194304]{0:T(1024)(128)(4,1)S(1)}, s32[]{:S(2)}) async-start(s8[10485760]{0:T(1024)(128)(4,1)} %bitcast.122), calls=%async_computation.7 | async-start | bytes 8388608
  486.7 23.9 %collective-permute-start.14 = (f32[128,2048]{1,0:T(8,128)}, f32[128,2048]{1,0:T(8,128)}, u32[]{:S(2)}, u32[]{:S(2)}) collective-permute-start(f32[128,2048]{1,0:T(8,128)} %slice.382), channel_id=1, source_target_pairs={{0,2},{2,0},{4,6},{6,4},{8,10},{10,8},{12,14},{14,12},{16,18},{18,... | collective-permute-start | bytes 3145736 | tf_op jit(solution)/shard_map/ppermute | solution.py:617
  489.2 5.0 copy-start.12
  489.2 16.0 %collective-permute-start.16 = (bf16[256,1280]{1,0:T(8,128)(2,1)}, bf16[256,1280]{1,0:T(8,128)(2,1)}, u32[]{:S(2)}, u32[]{:S(2)}) collective-permute-start(bf16[256,1280]{1,0:T(8,128)(2,1)} %bitcast.24), channel_id=1, source_target_pairs={{0,1},{1,0},{2,3},{3,2},{4,5},{5,4},{6,7},{7,6},{8,9},{9,8},{10,11... | collective-permute-start | bytes 1966088 | tf_op jit(solution)/shard_map/ppermute | solution.py:620
  495.6 14.1 %collective-permute-start.22 = (bf16[4,80,512]{2,1,0:T(8,128)(2,1)S(1)}, bf16[4,80,512]{2,1,0:T(8,128)(2,1)S(1)}, u32[]{:S(2)}, u32[]{:S(2)}) collective-permute-start(bf16[4,80,512]{2,1,0:T(8,128)(2,1)S(1)} %get-tuple-element.164), channel_id=1, source_target_pairs={{0,2},{2,0},{4,6},{6,4},{8,10},{10,8},{12,14},{14,12},{16,18},{18,... | collective-permute-start | bytes 983048 | tf_op jit(solution)/shard_map/ppermute | solution.py:617
  500.2 10.5 %copy-start.3 = (bf16[1,128,2048]{2,1,0:T(8,128)(2,1)S(1)}, bf16[1,128,2048]{2,1,0:T(8,128)(2,1)}, u32[]{:S(2)}) copy-start(bf16[1,128,2048]{2,1,0:T(8,128)(2,1)} %param.19) | copy-start | bytes 1572868
  500.2 10.5 %copy-start.46 = (f32[256,2048]{1,0:T(8,128)S(1)}, f32[256,2048]{1,0:T(8,128)}, u32[]{:S(2)}) copy-start(f32[256,2048]{1,0:T(8,128)} %copy-done.45) | copy-start | bytes 6291460
  512.2 7.3 %copy-start.79 = (f32[128]{0:T(128)S(1)}, f32[128]{0:T(128)}, u32[]{:S(2)}) copy-start(f32[128]{0:T(128)} %get-tuple-element.184) | copy-start | bytes 1540
  512.5 4.2 collective-permute-start.23
  516.8 5.5 collective-permute-start.24
  519.0 4.2 collective-permute-start.17
  618.7 3.6 collective-permute-start.25
  (58 other events, 140.3 us)
Sparse Core Ops, SparseCore 0:
  241.5 65.7 all-gather.1
  323.8 67.4 reduce-scatter.2
  393.5 127.9 reduce-scatter.4

commit v3 on v2

--- a/solution.py
+++ b/solution.py
@@ -582,6 +582,453 @@
     )(lam, coef, inc, h, h_in, u, weights, cp, starts)
 
 
+def log1p_small(e):
+    series = jnp.ones_like(e) * (1.0 / 14)
+    for k in range(13, 0, -1):
+        series = 1.0 / k - e * series
+    return jnp.where(e < 0.25, e * series, jnp.log(1.0 + e))
+
+
+def front_kernel(n, *refs):
+    (
+        wx, wy, wo, gs, wg, wu, wd, rows_in, cot, starts, spread_r, pick_r, spread_d, pick_d,
+        o_xy, o_out, o_gates, o_cp, o_gains, o_gu, o_d, o_cot, o_starts, o_ypre, o_u, o_a, o_h, o_hin, o_xb, o_before,
+        o_x1, o_n2, o_n1t, o_ot, o_hidden, o_gate, o_up, o_pd,
+        v_xy, v_out, v_gs, v_gates, v_rows, v_cot, v_starts, v_cp, v_gains, v_n1, v_n1t, v_xb, v_ypre, v_halo, v_u, v_a,
+        v_b, v_h, v_c, v_carry, v_o, v_osib, v_ot, v_part, v_theirs, v_psib, v_x1, v_n2, v_w, v_hidden, v_gu, v_pd,
+        local_sem, send_sem, recv_sem, load_sem, store_sem, pd_sem,
+    ) = refs
+    dp, x = lax.axis_index("dp"), lax.axis_index("tp")
+    chip, core = dp // 2, dp % 2
+    other = 1 - core
+    pos = place_of(chip, n)
+    half = n // 2
+    nxt = (chip_at((pos + 1) % n, n) * 2 + core, x)
+    prv = (chip_at((pos + n - 1) % n, n) * 2 + core, x)
+    sib = (chip * 2 + other, x)
+    over = (dp, 1 - x)
+    greet([nxt, prv, sib, over])
+    copies = Copies(local_sem, send_sem, recv_sem)
+    send, stay = copies.send, copies.stay
+    tokens, width = rows_in.shape
+    rec = wx.shape[1]
+    rh = rec // 2
+    own, own_d = wo.shape[0], wx.shape[0]
+    fh = wg.shape[1] // 2
+    kept, every = [], []
+
+    def put(src, dst):
+        kept.append(stay(src, dst))
+
+    def give(src, dst, device):
+        copy = send(src, dst, device)
+        every.append(copy)
+        return copy
+
+    def land(group):
+        for copy in group:
+            copy.wait_recv()
+
+    parts = [(wx, v_xy.at[chip, core, x, :, pl.ds(0, rh)]), (wy, v_xy.at[chip, core, x, :, pl.ds(rh, rh)])]
+    pair = [give(half_cols(src, other), slot, sib) for src, slot in parts]
+    pair.append(give(half_cols(wo, other), v_out.at[heads_first(chip, other, n), core, x], sib))
+    mine = [stay(half_cols(src, core), slot) for src, slot in parts]
+    mine.append(stay(half_cols(wo, core), v_out.at[heads_first(chip, core, n), core, x]))
+    mine.append(stay(gs, v_gs.at[core, chip, x]))
+    parts = [
+        (wg, o_gu.at[chip, core, :, pl.ds(0, fh)]),
+        (wu, o_gu.at[chip, core, :, pl.ds(fh, fh)]),
+        (wd, o_d.at[pos, core]),
+    ]
+    late = [give(half_cols(src, other), slot, sib) for src, slot in parts]
+    plain = [stay(half_cols(src, core), slot) for src, slot in parts]
+    late += [give(rows_in, v_rows.at[1], sib), give(starts, v_starts.at[1], sib), give(cot, v_cot.at[2], sib)]
+    plain += [stay(rows_in, v_rows.at[0]), stay(starts, v_starts.at[0]), stay(cot, v_cot.at[0])]
+
+    def rec_block(place):
+        c = chip_at(place, n)
+        return [v_xy.at[c, :, x], v_out.at[heads_first(c, core, n), :, x], v_gs.at[core, c, x]]
+
+    def rec_piece(place, which):
+        c = chip_at(place, n)
+        refs = [v_xy.at[c, which, x], v_out.at[heads_first(c, core, n), which, x]]
+        return refs + ([v_gs.at[core, c, x]] if which == 0 else [])
+
+    def gu_block(place):
+        return [o_gu.at[chip_at(place, n)]]
+
+    def gu_piece(place, which):
+        return [o_gu.at[chip_at(place, n), which]]
+
+    def d_block(place):
+        return [o_d.at[place]]
+
+    def d_piece(place, which):
+        return [o_d.at[place, which]]
+
+    def give_all(group, device):
+        return [give(ref, ref, device) for ref in group]
+
+    def hop(s, block, piece):
+        ahead, behind = (pos + n - (s - 1)) % n, (pos + s - 1) % n
+        if s < half:
+            return give_all(block(ahead), nxt) + give_all(block(behind), prv)
+        return give_all(piece(ahead, 0), nxt) + give_all(piece(behind, 1), prv)
+
+    land(pair)
+    for copy in mine:
+        copy.wait()
+    crossed, moving = give_all(rec_block(pos), over), []
+    for s in range(1, half + 1):
+        land(moving)
+        moving = hop(s, rec_block, rec_piece)
+        if s > 1:
+            crossed += give_all(rec_block((pos + n - (s - 1)) % n), over)
+            crossed += give_all(rec_block((pos + s - 1) % n), over)
+    land(late)
+    for copy in plain:
+        copy.wait()
+    gu = hop(1, gu_block, gu_piece)
+    land(moving)
+    crossed += give_all(rec_block((pos + half) % n), over)
+    swap = [give(v_gs.at[core, :, x], v_gs.at[core, :, x], sib)]
+    put(v_starts, o_starts)
+    for s in range(2, half + 1):
+        land(gu)
+        gu = hop(s, gu_block, gu_piece)
+    down = hop(1, d_block, d_piece)
+    land(crossed)
+    swap.append(give(v_gs.at[core, :, 1 - x], v_gs.at[core, :, 1 - x], sib))
+    put(v_xy, o_xy)
+    put(v_out, o_out)
+    land(swap)
+
+    small = v_gs[:, :, :, own : own + PAD, :128].reshape(4 * n * PAD, 128)
+    spread = jnp.dot(small, spread_r[...], preferred_element_type=F32).reshape(4 * n, PAD, rh)
+    lines = jnp.sum(spread[:, :8] * pick_r[...][:, None, :], axis=0)
+    decay = lines[7:8]
+    e = jnp.exp(-jnp.abs(decay))
+    v_cp[0:8, :] = lines
+    v_cp[7:8, :] = jnp.maximum(-decay, 0.0) + log1p_small(e)
+    v_cp[8:16, :] = jnp.broadcast_to(jax.nn.sigmoid(-decay), (8, rh))
+    for i in range(width // WIDE):
+        at = pl.ds(i * WIDE, WIDE)
+        wide = jnp.dot(small, spread_d[:, at], preferred_element_type=F32).reshape(4 * n, PAD, WIDE)
+        v_gains[:, at] = jnp.sum(wide[:, 8:] * pick_d[:, at][:, None, :], axis=0)
+    for i in range(2 * n):
+        v_gates[i * own : (i + 1) * own, :] = v_gs[(i // 2) % 2, core * half + i // 4, i % 2, 0:own, :]
+    put(v_cp, o_cp)
+    put(v_gains, o_gains)
+    put(v_gates, o_gates)
+
+    values = v_rows[...].astype(F32)
+    scale = lax.rsqrt(jnp.mean(values * values, axis=-1, keepdims=True) + EPS)
+    v_n1[...] = (values * scale * v_gains[0:1, :]).astype(BF16).reshape(2 * tokens, width)
+
+    def project_x(i, _):
+        at = pl.ds(pl.multiple_of(i * BLK, BLK), BLK)
+        w = v_xy[:, :, :, :, at].reshape(width, BLK)
+        v_xb[:, :, at] = jnp.dot(v_n1[...], w, preferred_element_type=F32).astype(BF16).reshape(2, tokens, BLK)
+        return 0
+
+    def project_y(i, _):
+        at = pl.ds(pl.multiple_of(i * BLK, BLK), BLK)
+        w = v_xy[:, :, :, :, pl.ds(pl.multiple_of(rh + i * BLK, BLK), BLK)].reshape(width, BLK)
+        v_ypre[:, :, at] = jnp.dot(v_n1[...], w, preferred_element_type=F32).reshape(2, tokens, BLK)
+        return 0
+
+    lax.fori_loop(0, rh // BLK, project_x, 0)
+    halo = give(v_xb.at[:, pl.ds(tokens - 16, 16)], v_halo, over)
+    put(v_xb, o_xb)
+    lax.fori_loop(0, rh // BLK, project_y, 0)
+    put(v_ypre, o_ypre)
+    chips_n = BLK // (4 * own_d)
+
+    def turn_n1(i, _):
+        at = pl.ds(pl.multiple_of(i * BLK, BLK), BLK)
+        turned = v_n1[:, at].astype(F32).T.astype(BF16)
+        v_n1t[pl.ds(i * chips_n, chips_n)] = turned.reshape(chips_n, 2, 2, own_d, 2 * tokens)
+        return 0
+
+    lax.fori_loop(0, width // BLK, turn_n1, 0)
+    halo.wait_recv()
+    v_halo[...] = jnp.where(x == 0, jnp.zeros_like(v_halo), v_halo[...])
+    put(v_halo, o_before)
+    n1_over = give(v_n1t.at[:, :, 1 - x], o_n1t.at[:, :, :, pl.ds(2 * tokens, 2 * tokens)], over)
+    put(v_n1t.at[:, :, x], o_n1t.at[:, :, :, pl.ds(0, 2 * tokens)])
+
+    def head(i, _):
+        at = pl.ds(pl.multiple_of(i * BLK, BLK), BLK)
+        p = v_cp[:, at]
+        us = []
+        for row in range(2):
+            padded = jnp.concatenate([v_halo[row, :, at].astype(F32)[8:], v_xb[row, :, at].astype(F32)], axis=0)
+            total = p[4:5] + p[0:1] * padded[8 : 8 + tokens]
+            for k in range(1, 4):
+                total = total + p[k : k + 1] * padded[8 - k : 8 - k + tokens]
+            us.append(total.astype(BF16))
+        u = jnp.stack(us)
+        v_u[:, :, at] = u
+        start = v_starts[...]
+        start = jnp.concatenate([start, start], axis=2)
+        _, ig, decayed, rest = gates_of(u, v_gates[at, :], p, start)
+        v_a[:, :, at] = decayed * (1.0 - start)
+        v_b[...] = jnp.where(start > 0.5, 1.0, jnp.sqrt(rest)) * ig * u.astype(F32)
+
+        def eight(j, carry):
+            rows8 = pl.ds(pl.multiple_of(j * 8, 8), 8)
+            out = []
+            for row in range(2):
+                h, c = carry[row]
+                a, b = v_a[row, rows8, at], v_b[row, rows8, :]
+                hs, cs = [], []
+                for k in range(8):
+                    h = a[k : k + 1] * h + b[k : k + 1]
+                    c = a[k : k + 1] * c
+                    hs.append(h)
+                    cs.append(c)
+                v_h[row, rows8, at] = jnp.concatenate(hs, axis=0)
+                v_c[row, rows8, at] = jnp.concatenate(cs, axis=0)
+                out.append((h, c))
+            return tuple(out)
+
+        zero, one = jnp.zeros((1, BLK), F32), jnp.ones((1, BLK), F32)
+        lax.fori_loop(0, tokens // 8, eight, ((zero, one),) * 2)
+        return 0
+
+    lax.fori_loop(0, rh // BLK, head, 0)
+    carry = give(v_h.at[:, pl.ds(tokens - 8, 8)], v_carry, over)
+    put(v_u, o_u)
+    put(v_a, o_a)
+    carry.wait_recv()
+    carry.wait_send()
+    cot_over = give(v_cot.at[0], v_cot.at[1], over)
+    v_carry[...] = jnp.where(x == 0, jnp.zeros_like(v_carry), v_carry[...])
+    put(v_carry, o_hin)
+
+    def output(i, _):
+        at = pl.ds(pl.multiple_of(i * BLK, BLK), BLK)
+        h = v_h[:, :, at] + v_c[:, :, at] * v_carry[:, 7:8, at]
+        v_h[:, :, at] = h
+        value, _ = gelu_parts(v_ypre[:, :, at])
+        v_o[:, :, at] = (h * value).astype(BF16)
+        return 0
+
+    lax.fori_loop(0, rh // BLK, output, 0)
+    o_pair = give(v_o, v_osib, sib)
+    put(v_h, o_h)
+    land(gu)
+    land(down)
+    down = hop(2, d_block, d_piece)
+    o_pair.wait_recv()
+
+    def project_row(row, ref):
+        def tile(i, _):
+            at = pl.ds(pl.multiple_of(i * BLK, BLK), BLK)
+            w0 = v_out[0:half, :, :, :, at].reshape(rh, BLK)
+            w1 = v_out[half:n, :, :, :, at].reshape(rh, BLK)
+            ref[:, at] = jnp.dot(v_o[row], w0, preferred_element_type=F32) + jnp.dot(
+                v_osib[1 - row], w1, preferred_element_type=F32
+            )
+            return 0
+
+        lax.fori_loop(0, width // 2 // BLK, tile, 0)
+
+    project_row(1, v_theirs)
+    x1_pair = give(v_theirs, v_psib, sib)
+    project_row(0, v_part)
+    x1_pair.wait_recv()
+    at_mine = pl.ds(pl.multiple_of(core * (width // 2), 128), width // 2)
+    at_theirs = pl.ds(pl.multiple_of(other * (width // 2), 128), width // 2)
+    v_x1[:, at_mine] = rows_in[:, at_mine].astype(F32) + v_part[...]
+    v_x1[:, at_theirs] = rows_in[:, at_theirs].astype(F32) + v_psib[...]
+    put(v_x1, o_x1)
+    x1 = v_x1[...]
+    scale = lax.rsqrt(jnp.mean(x1 * x1, axis=-1, keepdims=True) + EPS)
+    v_n2[0] = (x1 * scale * v_gains[1:2, :]).astype(BF16)
+    n2_over = give(v_n2.at[0], v_n2.at[1], over)
+    n2_pair = give(v_n2.at[0], v_n2.at[2], sib)
+
+    chips_o = 640 // (4 * own)
+
+    def turn_o(i, _):
+        at = pl.ds(pl.multiple_of(i * 640, 128), 640)
+        here = v_o[:, :, at].astype(F32).reshape(2 * tokens, 640).T.astype(BF16)
+        v_ot[pl.ds(i * chips_o, chips_o)] = here.reshape(chips_o, 2, 2, own, 2 * tokens)
+        there = jnp.concatenate([v_osib[1, :, at], v_osib[0, :, at]], axis=0).astype(F32).T.astype(BF16)
+        v_ot[pl.ds(half + i * chips_o, chips_o)] = there.reshape(chips_o, 2, 2, own, 2 * tokens)
+        return 0
+
+    lax.fori_loop(0, rh // 640, turn_o, 0)
+    cot_over.wait_recv()
+    cot_last = give(v_cot.at[1], v_cot.at[3], sib)
+    o_over = give(v_ot.at[:, :, 1 - x], o_ot.at[:, :, :, pl.ds(2 * tokens, 2 * tokens)], over)
+    put(v_ot.at[:, :, x], o_ot.at[:, :, :, pl.ds(0, 2 * tokens)])
+
+    tile = 128
+    steps = fh // tile
+
+    def loads(t, slot):
+        first = pl.ds(pl.multiple_of(t * tile, tile), tile)
+        second = pl.ds(pl.multiple_of(fh + t * tile, tile), tile)
+        return [
+            pltpu.make_async_copy(o_gu.at[:, :, :, first], v_w.at[slot, :, :, :, pl.ds(0, tile)], load_sem.at[slot, 0]),
+            pltpu.make_async_copy(
+                o_gu.at[:, :, :, second], v_w.at[slot, :, :, :, pl.ds(tile, tile)], load_sem.at[slot, 1]
+            ),
+        ]
+
+    def stores(t, slot):
+        at = pl.ds(pl.multiple_of(t * tile, tile), tile)
+        return [
+            pltpu.make_async_copy(v_gu.at[slot, :, pl.ds(0, tile)], o_gate.at[:, at], store_sem.at[slot, 0]),
+            pltpu.make_async_copy(v_gu.at[slot, :, pl.ds(tile, tile)], o_up.at[:, at], store_sem.at[slot, 1]),
+        ]
+
+    for copy in loads(0, 0):
+        copy.start()
+    n2_pair.wait_recv()
+    land(down)
+    down = hop(3, d_block, d_piece) if half > 3 else down
+    n2_over.wait_recv()
+    n2_last = give(v_n2.at[1], v_n2.at[3], sib)
+    n2_last.wait_recv()
+    put(v_n2, o_n2)
+
+    def hidden_tile(t, _):
+        slot = t % 2
+        for copy in loads(t, slot):
+            copy.wait()
+
+        @pl.when(t + 1 < steps)
+        def _():
+            for copy in loads(t + 1, 1 - slot):
+                copy.start()
+
+        @pl.when(t >= 2)
+        def _():
+            for copy in stores(t - 2, slot):
+                copy.wait()
+
+        w = v_w[slot].reshape(width, 2 * tile)
+        v_gu[slot] = jnp.dot(v_n2[...].reshape(4 * tokens, width), w, preferred_element_type=F32)
+        for copy in stores(t, slot):
+            copy.start()
+        value, _ = gelu_parts(v_gu[slot, :, 0:tile])
+        v_hidden[:, pl.ds(pl.multiple_of(t * tile, tile), tile)] = (value * v_gu[slot, :, tile:]).astype(BF16)
+        return 0
+
+    lax.fori_loop(0, steps, hidden_tile, 0)
+    put(v_hidden, o_hidden)
+    cot_last.wait_recv()
+    put(v_cot, o_cot)
+    if half > 3:
+        land(down)
+        down = hop(4, d_block, d_piece)
+
+    def pd_store(t, slot):
+        return pltpu.make_async_copy(v_pd.at[slot], o_pd.at[pl.ds(pl.multiple_of(t * BLK, BLK), BLK)], pd_sem.at[slot])
+
+    def down_tile(t, _):
+        slot = t % 2
+
+        @pl.when(t >= 2)
+        def _():
+            pd_store(t - 2, slot).wait()
+
+        left = v_cot[:, :, pl.ds(pl.multiple_of(t * BLK, BLK), BLK)].reshape(4 * tokens, BLK)
+        v_pd[slot] = lax.dot_general(
+            left, v_hidden[...], (((0,), (0,)), ((), ())), preferred_element_type=F32
+        ).astype(BF16)
+        pd_store(t, slot).start()
+        return 0
+
+    lax.fori_loop(0, width // BLK, down_tile, 0)
+    for s in range(5, half + 1):
+        land(down)
+        down = hop(s, d_block, d_piece)
+    for t in (steps - 2, steps - 1):
+        for copy in stores(t, t % 2):
+            copy.wait()
+    for t in (width // BLK - 2, width // BLK - 1):
+        pd_store(t, t % 2).wait()
+    land(down)
+    land([n1_over, o_over])
+    for copy in kept:
+        copy.wait()
+    for copy in every:
+        if copy is not carry:
+            copy.wait_send()
+
+
+def front(n, wx, wy, wo, gs, wg, wu, wd, rows_in, cot, starts):
+    rec, f = wx.shape[1], wg.shape[1]
+    own, own_d, rows_f = wo.shape[0], wx.shape[0], wg.shape[0]
+    rh, fh = rec // 2, f // 2
+    tokens, width = rows_in.shape
+    half = n // 2
+    core = lax.axis_index("dp") % 2
+    row = jnp.arange(4 * n)
+    index = (row // 2) % n * 4 + row // (2 * n) * 2 + row % 2
+    lane_r, lane_d = jnp.arange(rh), jnp.arange(width)
+    spread_r = (lane_r[None] % own == jnp.arange(128)[:, None]).astype(BF16)
+    spread_d = (lane_d[None] % own_d == jnp.arange(128)[:, None]).astype(BF16)
+    pick_r = (index[:, None] - core * 2 * n == lane_r[None] // own).astype(F32)
+    pick_d = (index[:, None] == lane_d[None] // own_d).astype(F32)
+    outs = dict(
+        w_xy=((n, 2, 2, own_d, rec), BF16),
+        w_o=((n, 2, 2, own, width // 2), BF16),
+        gates=((rh, WIDE), BF16),
+        cp=((16, rh), F32),
+        gains=((8, width), F32),
+        w_gu=((n, 2, rows_f, f), BF16),
+        w_d=((n, 2, rows_f, fh), BF16),
+        cot=((4, tokens, width), BF16),
+        starts=((2, tokens, 128), F32),
+        ypre=((2, tokens, rh), F32),
+        u=((2, tokens, rh), BF16),
+        a=((2, tokens, rh), F32),
+        h=((2, tokens, rh), F32),
+        h_in=((2, 8, rh), F32),
+        xb=((2, tokens, rh), BF16),
+        before=((2, 16, rh), BF16),
+        x1=((tokens, width), F32),
+        n2=((4, tokens, width), BF16),
+        n1_t=((n, 2, own_d, 4 * tokens), BF16),
+        o_t=((n, 2, own, 4 * tokens), BF16),
+        hidden=((4 * tokens, fh), BF16),
+        gate=((4 * tokens, fh), F32),
+        up=((4 * tokens, fh), F32),
+        part_d=((width, fh), BF16),
+    )
+    state = (2, tokens, rh)
+    scratch = [
+        ((n, 2, 2, own_d, rec), BF16), ((n, 2, 2, own, width // 2), BF16), ((2, n, 2) + gs.shape, BF16),
+        ((rh, WIDE), BF16), ((2, tokens, width), BF16), ((4, tokens, width), BF16), ((2, tokens, 128), F32),
+        ((16, rh), F32), ((8, width), F32), ((2 * tokens, width), BF16), ((n, 2, 2, own_d, 2 * tokens), BF16),
+        (state, BF16), (state, F32), ((2, 16, rh), BF16), (state, BF16), (state, F32),
+        ((2, tokens, BLK), F32), (state, F32), (state, F32), ((2, 8, rh), F32), (state, BF16), (state, BF16),
+        ((n, 2, 2, own, 2 * tokens), BF16), ((tokens, width // 2), F32), ((tokens, width // 2), F32),
+        ((tokens, width // 2), F32), ((tokens, width), F32), ((4, tokens, width), BF16),
+        ((2, n, 2, rows_f, BLK), BF16), ((4 * tokens, fh), BF16), ((2, 4 * tokens, BLK), F32), ((2, BLK, fh), BF16),
+    ]
+    count = 9 + (3 * n - 1) + n + n + 3 * n + 2 + 12
+    dma = pltpu.SemaphoreType.DMA
+    result = pl.pallas_call(
+        functools.partial(front_kernel, n),
+        out_shape=[jax.ShapeDtypeStruct(shape, kind) for shape, kind in outs.values()],
+        in_specs=[pl.BlockSpec(memory_space=pltpu.VMEM)] * 14,
+        out_specs=[pl.BlockSpec(memory_space=pl.ANY)] * len(outs),
+        scratch_shapes=[pltpu.VMEM(shape, kind) for shape, kind in scratch]
+        + [dma((32,)), dma((count,)), dma((count,)), dma((2, 2)), dma((2, 2)), dma((2,))],
+        compiler_params=pltpu.CompilerParams(
+            collective_id=2, has_side_effects=True, vmem_limit_bytes=60 << 20
+        ),
+        name="front",
+    )(wx, wy, wo, gs, wg, wu, wd, rows_in, cot, starts, spread_r, pick_r, spread_d, pick_d)
+    return dict(zip(outs, result))
+
+
 def nt(left, right):
     return lax.dot_general(left, right, (((1,), (1,)), ((), ())), preferred_element_type=F32)
 
@@ -648,81 +1095,99 @@
     valid = (place < lengths[0]).astype(F32)[:, None]
     cot = grad_out.reshape(tokens, width).astype(F32) * valid
 
-    small = jnp.concatenate(
-        [norm_gain, mlp_gain, conv_w.reshape(-1), conv_b, gate_a_b, gate_i_b, decay_param]
-    )
-    small = jnp.pad(small, (0, PAD * WIDE - small.shape[0])).reshape(PAD, WIDE)
-    gs = jnp.concatenate([jnp.concatenate([gate_a_w, gate_i_w], axis=1), small], axis=0)
-    w_xy, w_o, all_gs, w_gu, d_block, rows_two, cot_all, starts_two = gather_weights(
-        n, w_x, w_y, w_out, gs, w_gate, w_up, w_down.T, rows_own, ring_order(cot.astype(BF16), 1), starts
-    )
-    w_d = lax.all_gather(
-        d_block.reshape(-1, d_block.shape[2]), "dp", axis=0, tiled=True, axis_index_groups=lanes
-    )
-    w_gu = w_gu.reshape(width, w_gate.shape[1])
-    w_xy = w_xy.reshape(width, rec)
-    w_o = w_o.reshape(rec, width // 2)
     def lane_sum(array):
         return lax.psum_scatter(array, "dp", scatter_dimension=0, tiled=True, axis_index_groups=lanes)
 
-    cot_all = cot_all.reshape(4 * tokens, width)
-
-    vectors = all_gs[:, :, :, own:].transpose(1, 0, 2, 3, 4).reshape(2 * dp_size, PAD * WIDE)
-    gain_one = vectors[:, :own_d].reshape(width).astype(F32)
-    gain_two = vectors[:, own_d : 2 * own_d].reshape(width).astype(F32)
-    lines = vectors[:, 2 * own_d : 2 * own_d + (taps + 4) * own].reshape(2 * dp_size, taps + 4, own)
-    lines = lax.dynamic_slice_in_dim(lines, core * dp_size, dp_size, 0)
-    lines = lines.transpose(1, 0, 2).reshape(taps + 4, rh).astype(F32)
-    decay = lines[taps + 3 :]
-    cp = jnp.concatenate(
-        [lines[: taps + 3], jax.nn.softplus(-decay), jax.nn.sigmoid(-decay), jnp.zeros((7, rh), F32)], axis=0
-    )
-    gates = lax.dynamic_slice_in_dim(all_gs[:, :, :, :own], core * half, half, 1)
-    gates = gates.transpose(1, 0, 2, 3, 4).reshape(rh, WIDE)
-
-    n1, xb, ypre = project(rows_two, gain_one[None], w_xy)
-    before = lax.ppermute(xb[:, tokens - (taps - 1) :], "tp", [(0, 1)])
-    halo = jnp.concatenate([jnp.zeros((2, 8 - (taps - 1), rh), F32), before.astype(F32)], axis=1)
-    u, a, h_local, coef = recurrence(xb, halo, gates, cp, starts_two)
-    h_in = lax.ppermute(h_local[:, tokens - 1 :], "tp", [(0, 1)])
-    h = h_local + coef * h_in
-    ybr, _ = gelu_parts(ypre)
-    o = (h * ybr).astype(BF16)
-    o_sib = sibling(o)
-    part_mine, part_theirs = project_out(o, o_sib, w_o)
-    x1 = rows_own.astype(F32) + by_core(part_mine, sibling(part_theirs), 1)
-    rs2 = lax.rsqrt(jnp.mean(x1 * x1, axis=-1, keepdims=True) + EPS)
-    n2 = (x1 * rs2 * gain_two).astype(BF16)
     def plane(array, which):
         return lax.dynamic_index_in_dim(array, which, 2, keepdims=False)
 
     def both(mine, axis):
         return jnp.concatenate([mine, across(mine)], axis)
 
-    n2_x = across(n2)
-
-    def plane_rows(values, rows):
-        grouped = after(values, n2_x).T.reshape(n, 2, 2, rows, 2 * tokens)
-        return plane(grouped, x), plane(grouped, 1 - x)
-
-    o_here, o_send = plane_rows(jnp.concatenate([o, swapped(o_sib)], axis=2).reshape(2 * tokens, rec), own)
-    n1_here, n1_send = plane_rows(n1, own_d)
-    two = jnp.concatenate([n2, n2_x], axis=0)
-    n2_all = jnp.concatenate([two, sibling(two)], axis=0)
-    o_t = jnp.concatenate([o_here, across(o_send)], axis=3).reshape(rh, 4 * tokens)
-    n1_t = jnp.concatenate([n1_here, across(n1_send)], axis=3).reshape(width // 2, 4 * tokens)
-
-    fh = w_d.shape[1]
-    gu = nn(n2_all, w_gu)
-    gate, upv = gu[:, :fh], gu[:, fh:]
-    act, slope = gelu_parts(gate)
-    hidden = (act * upv).astype(BF16)
-
     def tn(left, right):
         return lax.dot_general(left, right, (((0,), (0,)), ((), ())), preferred_element_type=F32)
 
-    part_d = tn(cot_all, hidden).astype(BF16)
+    fh = w_gate.shape[1] // 2
+    cot_ring = ring_order(cot.astype(BF16), 1)
+    if own % 16 == 0 and own_d % 16 == 0:
+        vectors = jnp.concatenate([conv_w, jnp.stack([conv_b, gate_a_b, gate_i_b, decay_param])], axis=0)
+        vectors = jnp.pad(vectors, ((0, 0), (0, WIDE - own)))
+        gains = jnp.pad(jnp.stack([norm_gain, mlp_gain]), ((0, PAD - taps - 6), (0, WIDE - own_d)))
+        gs = jnp.concatenate([jnp.concatenate([gate_a_w, gate_i_w], axis=1), vectors, gains], axis=0)
+        got = front(n, w_x, w_y, w_out, gs, w_gate, w_up, w_down.T, rows_own, cot_ring, starts)
+        w_xy, w_o = got["w_xy"].reshape(width, rec), got["w_o"].reshape(rec, width // 2)
+        w_gu, w_d = got["w_gu"].reshape(width, 2 * fh), got["w_d"].reshape(width, fh)
+        cot_all, n2_all = got["cot"].reshape(4 * tokens, width), got["n2"].reshape(4 * tokens, width)
+        gain_one, gain_two, cp, gates = got["gains"][0], got["gains"][1], got["cp"], got["gates"]
+        starts_two, ypre, u, a, h, xb, x1 = (got[key] for key in ("starts", "ypre", "u", "a", "h", "xb", "x1"))
+        h_in, before = got["h_in"][:, 7:8], got["before"][:, PAD - taps + 1 :]
+        n1_t, o_t = got["n1_t"].reshape(width // 2, 4 * tokens), got["o_t"].reshape(rh, 4 * tokens)
+        hidden, gate, upv, part_d = got["hidden"], got["gate"], got["up"], got["part_d"]
+        rs2 = lax.rsqrt(jnp.mean(x1 * x1, axis=-1, keepdims=True) + EPS)
+    else:
+        small = jnp.concatenate(
+            [norm_gain, mlp_gain, conv_w.reshape(-1), conv_b, gate_a_b, gate_i_b, decay_param]
+        )
+        small = jnp.pad(small, (0, PAD * WIDE - small.shape[0])).reshape(PAD, WIDE)
+        gs = jnp.concatenate([jnp.concatenate([gate_a_w, gate_i_w], axis=1), small], axis=0)
+        w_xy, w_o, all_gs, w_gu, d_block, rows_two, cot_all, starts_two = gather_weights(
+            n, w_x, w_y, w_out, gs, w_gate, w_up, w_down.T, rows_own, cot_ring, starts
+        )
+        w_d = lax.all_gather(
+            d_block.reshape(-1, d_block.shape[2]), "dp", axis=0, tiled=True, axis_index_groups=lanes
+        )
+        w_gu = w_gu.reshape(width, w_gate.shape[1])
+        w_xy = w_xy.reshape(width, rec)
+        w_o = w_o.reshape(rec, width // 2)
+        cot_all = cot_all.reshape(4 * tokens, width)
+
+        vectors = all_gs[:, :, :, own:].transpose(1, 0, 2, 3, 4).reshape(2 * dp_size, PAD * WIDE)
+        gain_one = vectors[:, :own_d].reshape(width).astype(F32)
+        gain_two = vectors[:, own_d : 2 * own_d].reshape(width).astype(F32)
+        lines = vectors[:, 2 * own_d : 2 * own_d + (taps + 4) * own].reshape(2 * dp_size, taps + 4, own)
+        lines = lax.dynamic_slice_in_dim(lines, core * dp_size, dp_size, 0)
+        lines = lines.transpose(1, 0, 2).reshape(taps + 4, rh).astype(F32)
+        decay = lines[taps + 3 :]
+        cp = jnp.concatenate(
+            [lines[: taps + 3], jax.nn.softplus(-decay), jax.nn.sigmoid(-decay), jnp.zeros((7, rh), F32)], axis=0
+        )
+        gates = lax.dynamic_slice_in_dim(all_gs[:, :, :, :own], core * half, half, 1)
+        gates = gates.transpose(1, 0, 2, 3, 4).reshape(rh, WIDE)
+
+        n1, xb, ypre = project(rows_two, gain_one[None], w_xy)
+        before = lax.ppermute(xb[:, tokens - (taps - 1) :], "tp", [(0, 1)])
+        halo = jnp.concatenate([jnp.zeros((2, 8 - (taps - 1), rh), F32), before.astype(F32)], axis=1)
+        u, a, h_local, coef = recurrence(xb, halo, gates, cp, starts_two)
+        h_in = lax.ppermute(h_local[:, tokens - 1 :], "tp", [(0, 1)])
+        h = h_local + coef * h_in
+        ybr, _ = gelu_parts(ypre)
+        o = (h * ybr).astype(BF16)
+        o_sib = sibling(o)
+        part_mine, part_theirs = project_out(o, o_sib, w_o)
+        x1 = rows_own.astype(F32) + by_core(part_mine, sibling(part_theirs), 1)
+        rs2 = lax.rsqrt(jnp.mean(x1 * x1, axis=-1, keepdims=True) + EPS)
+        n2 = (x1 * rs2 * gain_two).astype(BF16)
+        n2_x = across(n2)
+
+        def plane_rows(values, rows):
+            grouped = after(values, n2_x).T.reshape(n, 2, 2, rows, 2 * tokens)
+            return plane(grouped, x), plane(grouped, 1 - x)
+
+        o_here, o_send = plane_rows(jnp.concatenate([o, swapped(o_sib)], axis=2).reshape(2 * tokens, rec), own)
+        n1_here, n1_send = plane_rows(n1, own_d)
+        two = jnp.concatenate([n2, n2_x], axis=0)
+        n2_all = jnp.concatenate([two, sibling(two)], axis=0)
+        o_t = jnp.concatenate([o_here, across(o_send)], axis=3).reshape(rh, 4 * tokens)
+        n1_t = jnp.concatenate([n1_here, across(n1_send)], axis=3).reshape(width // 2, 4 * tokens)
+
+        gu = nn(n2_all, w_gu)
+        gate, upv = gu[:, :fh], gu[:, fh:]
+        act, _ = gelu_parts(gate)
+        hidden = (act * upv).astype(BF16)
+
+        part_d = tn(cot_all, hidden).astype(BF16)
     sum_d = lane_sum(part_d)
+    act, slope = gelu_parts(gate)
     d_hidden = nn(after(cot_all, part_d), w_d)
     d_gu = jnp.concatenate([(d_hidden * upv * slope).astype(BF16), (d_hidden * act).astype(BF16)], axis=1)
 

time: 641 us -> 604 us (0.942)
  Pallas kernels: 335 us -> 419 us
  local copies, waits for them, and re-layouts: 73 us -> 29.6 us
  waiting for transfers between devices: 70.7 us -> 35.8 us
  other arithmetic: 42.5 us -> 23.7 us
  matrix products: 74.5 us -> 57.2 us
  starting transfers between devices: 23 us -> 15.6 us
    pallas_call x4 -> x1, Pallas kernels: 232 us -> 280 us  [front(): pl.pallas_call(functools.partial(front_kernel, n), out_shape=[jax.ShapeDt...]
    pallas_call x1, Pallas kernels: 91 us -> 127 us  [scatter_sums(): pl.pallas_call(functools.partial(scatter_kernel, n), out_shape=[jax.Shape...]
    unnamed x211 -> x108, local copies, waits for them, and re-layouts: 41.6 us -> 12.1 us
    ppermute x10 -> x7, waiting for transfers between devices: 58.5 us -> 30 us  [across(): return lax.ppermute(v, 'tp', [(0, 1), (1, 0)])]
    dot_general x5 -> x4, matrix products: 33.6 us -> 23.4 us  [nn(): return jnp.dot(left, right, preferred_element_type=F32)]
    dot_general x2 -> x1, matrix products: 16.8 us -> 9.94 us  [tn(): lax.dot_general(left, right, (((0,), (0,)), ((), ())), preferred_element_...]
    ppermute x10 -> x7, starting transfers between devices: 14.2 us -> 10.4 us  [across(): return lax.ppermute(v, 'tp', [(0, 1), (1, 0)])]
  transfers between devices with their start and end apart: 29 -> 20, of which waited for: 11 -> 8; matrix products, arithmetic and copies ran while one was open for 23% -> 15% of each run, Pallas kernels for 19% -> 23%
where the time goes in v3:
time: 604 us; the launch traced here: 597 us
  Pallas kernels  419 us (69%)
  matrix products  57.2 us (9%)
  waiting for transfers between devices  35.8 us (6%)
  local copies, waits for them, and re-layouts  29.6 us (5%)
  other arithmetic  23.7 us (4%)
  between operations  16.3 us (3%)
  starting transfers between devices  15.6 us (3%)
    pallas_call x1, Pallas kernels, front(): pl.pallas_call(functools.partial(front_kernel, n), out_shape=[jax.ShapeDt...  280 us
    pallas_call x1, Pallas kernels, scatter_sums(): pl.pallas_call(functools.partial(scatter_kernel, n), out_shape=[jax.Shape...  127 us
    ppermute x7, waiting for transfers between devices, across(): return lax.ppermute(v, 'tp', [(0, 1), (1, 0)])  30 us
    dot_general x4, matrix products, nt(): lax.dot_general(left, right, (((1,), (1,)), ((), ())), preferred_element_...  23.8 us
    dot_general x4, matrix products, nn(): return jnp.dot(left, right, preferred_element_type=F32)  23.4 us
  transfers between devices with their start and end apart: 20, of which 8 were waited for; matrix products, arithmetic and copies ran while one was open for 15% of the time, Pallas kernels for 23%

profile of v3, /device:TPU:0, one launch (start us, length us, event | category | flops | bytes accessed | tf_op | source)
XLA Modules:
  0.0 597.2 jit_solution(13022275943464494519)
XLA Ops:
  8.7 0.8 fusion.41.refs_10_
  9.5 0.9 fusion.36.refs_12_
  10.4 1.3 fusion.34
  11.9 1.2 copy.45
  13.0 0.7 compare_convert_fusion.1.refs_11_
  13.8 0.8 compare_convert_fusion.refs_13_
  16.0 280.2 %front.1 = (bf16[8,2,2,64,2560]{4,3,2,1,0:T(8,128)(2,1)}, bf16[8,2,2,80,1024]{4,3,2,1,0:T(8,128)(2,1)}, bf16[1280,512]{1,0:T(8,128)(2,1)}, f32[16,1280]{1,0:T(8,...) custom-call(bf16[64,2560]{1,0:T(8,128)(2,1)} %refs_0_.1, ...), custom_call_target="tpu_custom_call" | custom-call | tf_op jit(solution)/shard_map/front/pallas_call | solution.py:1017
  296.5 10.4 %fusion.6 = (bf16[512,1536]{1,0:T(8,128)(2,1)S(1)}, bf16[512,1536]{1,0:T(8,128)(2,1)S(1)}) fusion(f32[512,1536]{1,0:T(8,128)} %get-tuple-element.66, f32[512,1536]{1,0:T(8,128)} %get-tuple-element.65, bf16[512,2048]{1,0:T(8,128)(2,1)} %bitcast.147, bf16[2048,1536]{1,0:T(8,128)(2,1)} %bitcast.144), kind=kOutput, calls=%fused_computation.12 | convolution fusion | flops 3239313408 | bytes 17825792 | tf_op jit(solution)/shard_map/dot_general | solution.py:1037
  306.9 6.9 %convolution_convert_fusion.4 = bf16[512,2048]{1,0:T(8,128)(2,1)S(1)} fusion(bf16[2048,3072]{1,0:T(8,128)(2,1)S(1)} %bitcast.142, bf16[512,1536]{1,0:T(8,128)(2,1)S(1)} %get-tuple-element.149, bf16[512,1536]{1,0:T(8,128)(2,1)S(1)} %get-tuple-element.148), kind=kOutput, calls=%fused_computation.15 | convolution fusion | flops 6449790976 | bytes 17825792 | tf_op jit(solution)/shard_map/dot_general | solution.py:1033
  313.9 1.1 collective-permute-start
  316.2 1.1 collective-permute-done
  317.7 0.8 slice.300
  318.5 9.9 %convolution_convert_fusion = bf16[2048,3072]{1,0:T(8,128)(2,1)} fusion(bf16[512,2048]{1,0:T(8,128)(2,1)S(1)} %slice_dynamic-update-slice_fusion.2, bf16[512,3072]{1,0:T(8,128)(2,1)S(1)} %pad_maximum_fusion), kind=kOutput, calls=%fused_computation | convolution fusion | flops 6448742400 | bytes 17825792 | tf_op jit(solution)/shard_map/dot_general | solution.py:1108
  328.6 1.0 slice.240.h_in
  329.6 0.8 slice.270
  330.8 0.9 fusion.80
  331.8 1.6 collective-permute-start.1
  333.4 6.8 %convolution_convert_fusion.5 = bf16[512,2048]{1,0:T(8,128)(2,1)S(1)} fusion(bf16[512,1536]{1,0:T(8,128)(2,1)} %get-tuple-element.83, bf16[2048,1536]{1,0:T(8,128)(2,1)} %bitcast.145), kind=kOutput, calls=%fused_computation.16 | convolution fusion | flops 3222274048 | bytes 9961472 | tf_op jit(solution)/shard_map/dot_general | solution.py:1033
  340.2 1.0 slice.317
  341.2 5.0 collective-permute-done.1
  346.7 1.4 fusion.73
  348.3 1.2 maximum_convert_fusion.1
  349.8 0.9 pad_maximum_fusion.2
  350.7 1.3 collective-permute-start.12
  352.0 4.2 fusion.72
  356.7 0.8 collective-permute-start.7
  357.8 18.5 %collective-permute-done.7 = bf16[128,2048]{1,0:T(8,128)(2,1)S(1)} collective-permute-done((bf16[128,2048]{1,0:T(8,128)(2,1)S(1)}, bf16[128,2048]{1,0:T(8,128)(2,1)S(1)}, u32[]{:S(2)}, u32[]{:S(2)}) %collective-permute-start.7) | collective-permute-done | bytes 524320 | tf_op jit(solution)/shard_map/ppermute | solution.py:1067
  376.8 1.1 copy-done
  378.7 5.3 adjoint.1
  384.0 1.3 collective-permute-start.4
  385.4 2.7 collective-permute-start.11
  388.1 1.6 collective-permute-done.4.inc
  389.7 6.6 %gates_back.1 = (bf16[2,128,1280]{2,1,0:T(8,128)(2,1)S(1)}, f32[1280,512]{1,0:T(8,128)S(1)}, f32[8,1280]{1,0:T(8,128)S(1)}) custom-call(f32[2,128,1280]{2,1,0:T(8,128)S(1)} %get-tuple-element.72.lam_ref, f32[2,128,1280]{2,1,0:T(8,128)S(1)} %get-tuple-element.73.c_ref, f32[2,1,1280]{2,1,0:T(1,128)S(1)} %collective-permute-done.4.inc, ...), custom_call_target="tpu_custom_call" | custom-call | flops 1200000000 | bytes 9000000 | tf_op jit(solution)/shard_map/gates_back/pallas_call | solution.py:565
  396.4 1.3 collective-permute-start.5
  397.7 0.9 fusion.40
  398.8 2.7 collective-permute-start.13
  401.5 2.9 collective-permute-done.5
  404.5 1.3 fusion.7
  405.8 1.2 pad_maximum_fusion.1
  407.0 5.9 fusion.82
  412.9 1.0 slice.328
  414.0 0.9 copy-done.9
  415.6 0.9 fusion.42
  417.2 4.6 convolution_convert_fusion.1
  421.7 1.4 bitcast_add_fusion
  423.3 4.3 convolution_convert_fusion.2
  427.7 3.5 collective-permute-done.9
  431.2 4.1 convolution_convert_fusion.3
  435.3 0.9 fusion.21.c_g
  436.3 1.6 fusion.27
  438.2 1.2 collective-permute-start.15
  439.4 2.9 collective-permute-done.15
  442.6 1.2 constant_dynamic-slice_fusion.9
  443.7 0.9 copy.47
  445.1 2.9 fusion.24
  448.9 1.3 convert_bitcast_fusion
  450.2 126.7 %scatter_sums.1 = (f32[64,2560]{1,0:T(8,128)}, f32[64,2560]{1,0:T(8,128)}, f32[80,2048]{1,0:T(8,128)}, f32[80,512]{1,0:T(8,128)}, f32[8,128]{1,0:T(8,128)}) custom-call(bf16[8,2,64,1280]{3,2,1,0:T(8,128)(2,1)} %bitcast.111, bf16[8,2,64,1280]{3,2,1,0:T(8,128)(2,1)} %bitcast.110, bf16[8,2,80,1024]{3,2,1,0:T(8,128)(2,1)} %bitcast.109, ...), custom_call_target="tpu_custom_call" | custom-call | tf_op jit(solution)/shard_map/scatter_sums/pallas_call | solution.py:290
  578.2 1.5 constant_dynamic-slice_fusion.1
  580.7 1.3 fusion.81
  583.9 1.6 copy.54
  585.7 1.6 copy.53
  587.3 0.8 copy.95
  588.2 0.8 copy.96
  589.0 0.8 copy.97
  (192 shorter events, 15.2 us)
Async XLA Ops:
  7.2 4.7 copy-start.21
  7.2 435.4 %reduce-scatter.3.cloned.1.call-start = ((), (), s32[]{:S(2)}) async-start(), calls=%async_computation.2 | async-start | bytes 7077888 | tf_op jit(solution)/shard_map/reduce_scatter | solution.py:1099
  9.5 3.5 copy-start.32
  9.5 3.5 copy-start.33
  10.4 4.2 copy-start.31
  10.4 4.2 copy-start.34
  10.4 4.2 copy-start.35
  10.4 4.2 copy-start.36
  10.4 4.2 copy-start.37
  10.4 4.2 copy-start.29
  10.4 4.2 copy-start.30
  11.8 4.2 copy-start.22
  296.2 282.0 %reduce-scatter.5.cloned.1.call-start = ((), (), s32[]{:S(2)}) async-start(), calls=%async_computation.3 | async-start | bytes 14155776 | tf_op jit(solution)/shard_map/reduce_scatter | solution.py:1099
  296.5 10.4 %copy-start.38 = (bf16[8,2,128,3072]{3,2,1,0:T(8,128)(2,1)S(1)}, bf16[8,2,128,3072]{3,2,1,0:T(8,128)(2,1)}, u32[]{:S(2)}) copy-start(bf16[8,2,128,3072]{3,2,1,0:T(8,128)(2,1)} %get-tuple-element.67) | copy-start | bytes 37748740
  313.8 1.6 copy-start.14
  313.9 3.4 collective-permute-start
  328.5 1.9 copy-start.6
  328.5 2.0 copy-start.10
  328.5 2.2 copy-start.8
  331.8 14.5 %collective-permute-start.1 = (bf16[128,2048]{1,0:T(8,128)(2,1)}, bf16[128,2048]{1,0:T(8,128)(2,1)S(1)}, u32[]{:S(2)}, u32[]{:S(2)}) collective-permute-start(bf16[128,2048]{1,0:T(8,128)(2,1)} %slice.300), channel_id=1, source_target_pairs={{0,1},{1,0},{2,3},{3,2},{4,5},{5,4},{6,7},{7,6},{8,9},{9,8},{10,11... | collective-permute-start | bytes 1572872 | tf_op jit(solution)/shard_map/ppermute | solution.py:1067
  340.2 6.5 %copy-start.15 = (bf16[512,2048]{1,0:T(8,128)(2,1)}, bf16[512,2048]{1,0:T(8,128)(2,1)S(1)}, u32[]{:S(2)}) copy-start(bf16[512,2048]{1,0:T(8,128)(2,1)S(1)} %convolution_convert_fusion.5) | copy-start | bytes 6291460
  340.2 6.5 %copy-start.17 = (bf16[1,128,2048]{2,1,0:T(8,128)(2,1)S(1)}, bf16[1,128,2048]{2,1,0:T(8,128)(2,1)}, u32[]{:S(2)}) copy-start(bf16[1,128,2048]{2,1,0:T(8,128)(2,1)} %param.20) | copy-start | bytes 1572868
  341.2 15.0 %collective-permute-start.6 = (bf16[256,2048]{1,0:T(8,128)(2,1)}, bf16[256,2048]{1,0:T(8,128)(2,1)S(1)}, u32[]{:S(2)}, u32[]{:S(2)}) collective-permute-start(bf16[256,2048]{1,0:T(8,128)(2,1)} %slice.317), channel_id=1, source_target_pairs={{0,2},{2,0},{4,6},{6,4},{8,10},{10,8},{12,14},{14,12},{16,18},{18,... | collective-permute-start | bytes 3145736 | tf_op jit(solution)/shard_map/ppermute | solution.py:1064
  346.7 1.6 copy-start.23
  348.2 8.0 %copy-start.20 = (bf16[128,1024]{1,0:T(8,128)(2,1)}, bf16[128,1024]{1,0:T(8,128)(2,1)S(1)}, u32[]{:S(2)}) copy-start(bf16[128,1024]{1,0:T(8,128)(2,1)S(1)} %get-tuple-element.165) | copy-start | bytes 786436
  348.2 1.6 collective-permute-start.2
  349.8 6.4 %copy-start.27 = (bf16[128,1024]{1,0:T(8,128)(2,1)}, bf16[128,1024]{1,0:T(8,128)(2,1)S(1)}, u32[]{:S(2)}) copy-start(bf16[128,1024]{1,0:T(8,128)(2,1)S(1)} %collective-permute-done.2) | copy-start | bytes 786436
  350.7 66.5 %collective-permute-start.12 = (bf16[256,1024]{1,0:T(8,128)(2,1)}, bf16[256,1024]{1,0:T(8,128)(2,1)}, u32[]{:S(2)}, u32[]{:S(2)}) collective-permute-start(bf16[256,1024]{1,0:T(8,128)(2,1)} %pad_maximum_fusion.2), channel_id=1, source_target_pairs={{0,1},{1,0},{2,3},{3,2},{4,5},{5,4},{6,7},{7,6},{8,9},{9,8},{10,11... | collective-permute-start | bytes 1572872 | tf_op jit(solution)/shard_map/ppermute | solution.py:1067
  352.0 4.3 copy-start.16
  356.7 19.5 %collective-permute-start.7 = (bf16[128,2048]{1,0:T(8,128)(2,1)S(1)}, bf16[128,2048]{1,0:T(8,128)(2,1)S(1)}, u32[]{:S(2)}, u32[]{:S(2)}) collective-permute-start(bf16[128,2048]{1,0:T(8,128)(2,1)S(1)} %slice.319), channel_id=1, source_target_pairs={{0,1},{1,0},{2,3},{3,2},{4,5},{5,4},{6,7},{7,6},{8,9},{9,8},{10,11... | collective-permute-start | bytes 1572872 | tf_op jit(solution)/shard_map/ppermute | solution.py:1067
  357.7 18.8 %collective-permute-start.3 = (f32[2,128,1280]{2,1,0:T(8,128)S(1)}, f32[2,128,1280]{2,1,0:T(8,128)S(1)}, u32[]{:S(2)}, u32[]{:S(2)}) collective-permute-start(f32[2,128,1280]{2,1,0:T(8,128)S(1)} %bitcast.121), channel_id=1, source_target_pairs={{0,2},{2,0},{4,6},{6,4},{8,10},{10,8},{12,14},{14,12},{16,18},{18,... | collective-permute-start | bytes 3932168 | tf_op jit(solution)/shard_map/ppermute | solution.py:1064
  376.6 1.3 copy-start
  376.6 1.7 copy-start.1
  376.6 2.1 copy-start.2
  378.7 11.0 %copy-start.3 = (bf16[1280,512]{1,0:T(8,128)(2,1)S(1)}, bf16[1280,512]{1,0:T(8,128)(2,1)}, u32[]{:S(2)}) copy-start(bf16[1280,512]{1,0:T(8,128)(2,1)} %get-tuple-element.76.weights) | copy-start | bytes 3932164
  378.7 11.0 %copy-start.4 = (bf16[2,128,1280]{2,1,0:T(8,128)(2,1)S(1)}, bf16[2,128,1280]{2,1,0:T(8,128)(2,1)}, u32[]{:S(2)}) copy-start(bf16[2,128,1280]{2,1,0:T(8,128)(2,1)} %get-tuple-element.75.u_ref) | copy-start | bytes 1966084
  378.7 11.0 %copy-start.5 = (f32[2,128,128]{2,1,0:T(8,128)S(1)}, f32[2,128,128]{2,1,0:T(8,128)}, u32[]{:S(2)}) copy-start(f32[2,128,128]{2,1,0:T(8,128)} %get-tuple-element.77.starts) | copy-start | bytes 393220
  384.0 5.7 collective-permute-start.4
  385.4 11.0 %copy-start.18 = (f32[128,2048]{1,0:T(8,128)}, f32[128,2048]{1,0:T(8,128)S(1)}, u32[]{:S(2)}) copy-start(f32[128,2048]{1,0:T(8,128)S(1)} %slice_dynamic-update-slice_fusion.1) | copy-start | bytes 3145732
  385.4 37.9 %collective-permute-start.11 = (bf16[256,1280]{1,0:T(8,128)(2,1)}, bf16[256,1280]{1,0:T(8,128)(2,1)}, u32[]{:S(2)}, u32[]{:S(2)}) collective-permute-start(bf16[256,1280]{1,0:T(8,128)(2,1)} %bitcast.31), channel_id=1, source_target_pairs={{0,1},{1,0},{2,3},{3,2},{4,5},{5,4},{6,7},{7,6},{8,9},{9,8},{10,11... | collective-permute-start | bytes 1966088 | tf_op jit(solution)/shard_map/ppermute | solution.py:1067
  396.4 8.0 %collective-permute-start.5 = (bf16[2,3,1280]{2,1,0:T(4,128)(2,1)S(1)}, bf16[2,3,1280]{2,1,0:T(4,128)(2,1)S(1)}, u32[]{:S(2)}, u32[]{:S(2)}) collective-permute-start(bf16[2,3,1280]{2,1,0:T(4,128)(2,1)S(1)} %slice.241), channel_id=1, source_target_pairs={{1,0},{3,2},{5,4},{7,6},{9,8},{11,10},{13,12},{15,14},{17,16},{19,... | collective-permute-start | bytes 46088 | tf_op jit(solution)/shard_map/ppermute | solution.py:1220
  398.7 5.7 copy-start.7
  398.8 23.0 %collective-permute-start.13 = (bf16[4,2,80,512]{3,2,0,1:T(8,128)(2,1)}, bf16[4,2,80,512]{3,2,0,1:T(8,128)(2,1)}, u32[]{:S(2)}, u32[]{:S(2)}) collective-permute-start(bf16[4,2,80,512]{3,2,0,1:T(8,128)(2,1)} %fusion.40), channel_id=1, source_target_pairs={{0,1},{1,0},{2,3},{3,2},{4,5},{5,4},{6,7},{7,6},{8,9},{9,8},{10,11... | collective-permute-start | bytes 1966088 | tf_op jit(solution)/shard_map/ppermute | solution.py:1067
  405.7 25.5 %collective-permute-start.9 = (bf16[256,1280]{1,0:T(8,128)(2,1)S(1)}, bf16[256,1280]{1,0:T(8,128)(2,1)}, u32[]{:S(2)}, u32[]{:S(2)}) collective-permute-start(bf16[256,1280]{1,0:T(8,128)(2,1)S(1)} %bitcast.107), channel_id=1, source_target_pairs={{0,1},{1,0},{2,3},{3,2},{4,5},{5,4},{6,7},{7,6},{8,9},{9,8},{10,11... | collective-permute-start | bytes 1966088 | tf_op jit(solution)/shard_map/ppermute | solution.py:1067
  412.9 3.6 copy-start.12
  412.9 2.0 copy-start.9
  412.9 2.7 copy-start.19
  414.0 22.3 %collective-permute-start.8 = (f32[128,2048]{1,0:T(8,128)}, f32[128,2048]{1,0:T(8,128)}, u32[]{:S(2)}, u32[]{:S(2)}) collective-permute-start(f32[128,2048]{1,0:T(8,128)} %slice.328), channel_id=1, source_target_pairs={{0,2},{2,0},{4,6},{6,4},{8,10},{10,8},{12,14},{14,12},{16,18},{18,... | collective-permute-start | bytes 3145736 | tf_op jit(solution)/shard_map/ppermute | solution.py:1064
  421.7 1.6 copy-start.39
  423.2 12.1 %collective-permute-start.14 = (bf16[4,80,512]{2,1,0:T(8,128)(2,1)S(1)}, bf16[4,80,512]{2,1,0:T(8,128)(2,1)S(1)}, u32[]{:S(2)}, u32[]{:S(2)}) collective-permute-start(bf16[4,80,512]{2,1,0:T(8,128)(2,1)S(1)} %get-tuple-element.164), channel_id=1, source_target_pairs={{0,2},{2,0},{4,6},{6,4},{8,10},{10,8},{12,14},{14,12},{16,18},{18,... | collective-permute-start | bytes 983048 | tf_op jit(solution)/shard_map/ppermute | solution.py:1064
  427.7 8.6 %copy-start.11 = (bf16[1,128,2048]{2,1,0:T(8,128)(2,1)S(1)}, bf16[1,128,2048]{2,1,0:T(8,128)(2,1)}, u32[]{:S(2)}) copy-start(bf16[1,128,2048]{2,1,0:T(8,128)(2,1)} %param.19) | copy-start | bytes 1572868
  427.7 8.6 %copy-start.13 = (f32[256,2048]{1,0:T(8,128)S(1)}, f32[256,2048]{1,0:T(8,128)}, u32[]{:S(2)}) copy-start(f32[256,2048]{1,0:T(8,128)} %copy-done.12) | copy-start | bytes 6291460
  438.2 4.2 collective-permute-start.15
  442.5 5.6 collective-permute-start.16
  444.7 4.2 collective-permute-start.10
  578.2 4.3 copy-start.28
  580.1 3.6 collective-permute-start.17
  585.7 1.6 copy-start.26
  585.7 2.5 copy-start.25
  587.3 1.7 copy-start.24
Sparse Core Ops, SparseCore 0:
  296.4 68.0 reduce-scatter.2
  366.7 163.2 reduce-scatter.4

commit v4 on v3

--- a/solution.py
+++ b/solution.py
@@ -2,6 +2,7 @@
 
 import jax
 import jax.numpy as jnp
+import numpy as np
 from jax import lax
 from jax.experimental import pallas as pl
 from jax.experimental.pallas import tpu as pltpu
@@ -629,12 +630,81 @@
         for copy in group:
             copy.wait_recv()
 
+    class Chain:
+        def __init__(self, pieces, arrived=None):
+            self.pieces, self.arrived, self.hop = pieces, arrived, 0
+            self.ways = ((nxt, n - 1), (prv, 1))
+            self.moving = ([], [])
+
+        def start(self, part):
+            self.hop = 1
+            for ref, own_core in self.pieces(pos):
+                if own_core == part:
+                    for way, (device, _) in enumerate(self.ways):
+                        self.moving[way].append(give(ref, ref, device))
+                    if self.arrived:
+                        self.arrived(ref)
+
+        def advance(self):
+            self.hop += 1
+            fresh = ([], [])
+            blocks = [self.pieces((pos + back * (self.hop - 1)) % n) for _, back in self.ways]
+            for i in range(len(blocks[0])):
+                for way, (device, _) in enumerate(self.ways):
+                    ref, own_core = blocks[way][i]
+                    self.moving[way][i].wait_recv()
+                    if self.hop < half or own_core == (way == 0):
+                        fresh[way].append(give(ref, ref, device))
+                    if self.arrived:
+                        self.arrived(ref)
+            self.moving = fresh
+
+        def to_last(self):
+            while self.hop < half:
+                self.advance()
+
+        def finish(self):
+            block = self.pieces((pos + half) % n)
+            for way in (0, 1):
+                refs = [ref for ref, own_core in block if own_core == (way == 0)]
+                for copy, ref in zip(self.moving[way], refs):
+                    copy.wait_recv()
+                    if self.arrived:
+                        self.arrived(ref)
+
     parts = [(wx, v_xy.at[chip, core, x, :, pl.ds(0, rh)]), (wy, v_xy.at[chip, core, x, :, pl.ds(rh, rh)])]
-    pair = [give(half_cols(src, other), slot, sib) for src, slot in parts]
-    pair.append(give(half_cols(wo, other), v_out.at[heads_first(chip, other, n), core, x], sib))
     mine = [stay(half_cols(src, core), slot) for src, slot in parts]
     mine.append(stay(half_cols(wo, core), v_out.at[heads_first(chip, core, n), core, x]))
     mine.append(stay(gs, v_gs.at[core, chip, x]))
+    pair = [give(half_cols(src, other), slot, sib) for src, slot in parts]
+    pair.append(give(half_cols(wo, other), v_out.at[heads_first(chip, other, n), core, x], sib))
+
+    crossed, held = [], []
+
+    def rec_pieces(place):
+        c = chip_at(place, n)
+        at = heads_first(c, core, n)
+        return [
+            (v_xy.at[c, core, x], True), (v_gs.at[core, c, x], True), (v_out.at[at, core, x], True),
+            (v_xy.at[c, other, x], False), (v_out.at[at, other, x], False),
+        ]
+
+    def rec_arrived(ref):
+        if len(ref.shape) == 2 and ref.shape[1] == width // 2:
+            held.append(ref)
+        else:
+            crossed.append(give(ref, ref, over))
+
+    rec_chain = Chain(rec_pieces, rec_arrived)
+    gu = Chain(lambda place: [
+        (o_gu.at[chip_at(place, n), core], True), (o_gu.at[chip_at(place, n), other], False)
+    ])
+    down = Chain(lambda place: [(o_d.at[place, core], True), (o_d.at[place, other], False)])
+    for copy in mine:
+        copy.wait()
+    rec_chain.start(True)
+    land(pair)
+    rec_chain.start(False)
     parts = [
         (wg, o_gu.at[chip, core, :, pl.ds(0, fh)]),
         (wu, o_gu.at[chip, core, :, pl.ds(fh, fh)]),
@@ -644,68 +714,34 @@
     plain = [stay(half_cols(src, core), slot) for src, slot in parts]
     late += [give(rows_in, v_rows.at[1], sib), give(starts, v_starts.at[1], sib), give(cot, v_cot.at[2], sib)]
     plain += [stay(rows_in, v_rows.at[0]), stay(starts, v_starts.at[0]), stay(cot, v_cot.at[0])]
-
-    def rec_block(place):
-        c = chip_at(place, n)
-        return [v_xy.at[c, :, x], v_out.at[heads_first(c, core, n), :, x], v_gs.at[core, c, x]]
-
-    def rec_piece(place, which):
-        c = chip_at(place, n)
-        refs = [v_xy.at[c, which, x], v_out.at[heads_first(c, core, n), which, x]]
-        return refs + ([v_gs.at[core, c, x]] if which == 0 else [])
-
-    def gu_block(place):
-        return [o_gu.at[chip_at(place, n)]]
-
-    def gu_piece(place, which):
-        return [o_gu.at[chip_at(place, n), which]]
-
-    def d_block(place):
-        return [o_d.at[place]]
-
-    def d_piece(place, which):
-        return [o_d.at[place, which]]
-
-    def give_all(group, device):
-        return [give(ref, ref, device) for ref in group]
-
-    def hop(s, block, piece):
-        ahead, behind = (pos + n - (s - 1)) % n, (pos + s - 1) % n
-        if s < half:
-            return give_all(block(ahead), nxt) + give_all(block(behind), prv)
-        return give_all(piece(ahead, 0), nxt) + give_all(piece(behind, 1), prv)
-
-    land(pair)
-    for copy in mine:
-        copy.wait()
-    crossed, moving = give_all(rec_block(pos), over), []
-    for s in range(1, half + 1):
-        land(moving)
-        moving = hop(s, rec_block, rec_piece)
-        if s > 1:
-            crossed += give_all(rec_block((pos + n - (s - 1)) % n), over)
-            crossed += give_all(rec_block((pos + s - 1) % n), over)
+    rec_chain.to_last()
     land(late)
     for copy in plain:
         copy.wait()
-    gu = hop(1, gu_block, gu_piece)
-    land(moving)
-    crossed += give_all(rec_block((pos + half) % n), over)
+    gu.start(True)
+    gu.start(False)
+    rec_chain.finish()
     swap = [give(v_gs.at[core, :, x], v_gs.at[core, :, x], sib)]
     put(v_starts, o_starts)
-    for s in range(2, half + 1):
-        land(gu)
-        gu = hop(s, gu_block, gu_piece)
-    down = hop(1, d_block, d_piece)
+    if half > 3:
+        gu.advance()
     land(crossed)
     swap.append(give(v_gs.at[core, :, 1 - x], v_gs.at[core, :, 1 - x], sib))
+    outs = []
+
+    def cross_held(count):
+        for _ in range(min(count, len(held))):
+            ref = held.pop(0)
+            outs.append(give(ref, ref, over))
+
+    cross_held(4)
     put(v_xy, o_xy)
-    put(v_out, o_out)
     land(swap)
 
     small = v_gs[:, :, :, own : own + PAD, :128].reshape(4 * n * PAD, 128)
     spread = jnp.dot(small, spread_r[...], preferred_element_type=F32).reshape(4 * n, PAD, rh)
-    lines = jnp.sum(spread[:, :8] * pick_r[...][:, None, :], axis=0)
+    heads = pick_r[:, pl.ds(pl.multiple_of(core * rh, 128), rh)]
+    lines = jnp.sum(spread[:, :8] * heads[:, None, :], axis=0)
     decay = lines[7:8]
     e = jnp.exp(-jnp.abs(decay))
     v_cp[0:8, :] = lines
@@ -739,7 +775,10 @@
 
     lax.fori_loop(0, rh // BLK, project_x, 0)
     halo = give(v_xb.at[:, pl.ds(tokens - 16, 16)], v_halo, over)
+    cross_held(4)
     put(v_xb, o_xb)
+    if half > 3:
+        gu.advance()
     lax.fori_loop(0, rh // BLK, project_y, 0)
     put(v_ypre, o_ypre)
     chips_n = BLK // (4 * own_d)
@@ -754,7 +793,6 @@
     halo.wait_recv()
     v_halo[...] = jnp.where(x == 0, jnp.zeros_like(v_halo), v_halo[...])
     put(v_halo, o_before)
-    n1_over = give(v_n1t.at[:, :, 1 - x], o_n1t.at[:, :, :, pl.ds(2 * tokens, 2 * tokens)], over)
     put(v_n1t.at[:, :, x], o_n1t.at[:, :, :, pl.ds(0, 2 * tokens)])
 
     def head(i, _):
@@ -802,7 +840,7 @@
     put(v_a, o_a)
     carry.wait_recv()
     carry.wait_send()
-    cot_over = give(v_cot.at[0], v_cot.at[1], over)
+    cross_held(len(held))
     v_carry[...] = jnp.where(x == 0, jnp.zeros_like(v_carry), v_carry[...])
     put(v_carry, o_hin)
 
@@ -817,10 +855,12 @@
     lax.fori_loop(0, rh // BLK, output, 0)
     o_pair = give(v_o, v_osib, sib)
     put(v_h, o_h)
-    land(gu)
-    land(down)
-    down = hop(2, d_block, d_piece)
+    gu.to_last()
+    down.start(True)
+    down.start(False)
     o_pair.wait_recv()
+    land(outs)
+    put(v_out, o_out)
 
     def project_row(row, ref):
         def tile(i, _):
@@ -840,14 +880,16 @@
     x1_pair.wait_recv()
     at_mine = pl.ds(pl.multiple_of(core * (width // 2), 128), width // 2)
     at_theirs = pl.ds(pl.multiple_of(other * (width // 2), 128), width // 2)
-    v_x1[:, at_mine] = rows_in[:, at_mine].astype(F32) + v_part[...]
-    v_x1[:, at_theirs] = rows_in[:, at_theirs].astype(F32) + v_psib[...]
+    v_x1[:, at_mine] = v_rows[0, :, at_mine].astype(F32) + v_part[...]
+    v_x1[:, at_theirs] = v_rows[0, :, at_theirs].astype(F32) + v_psib[...]
     put(v_x1, o_x1)
     x1 = v_x1[...]
     scale = lax.rsqrt(jnp.mean(x1 * x1, axis=-1, keepdims=True) + EPS)
     v_n2[0] = (x1 * scale * v_gains[1:2, :]).astype(BF16)
     n2_over = give(v_n2.at[0], v_n2.at[1], over)
     n2_pair = give(v_n2.at[0], v_n2.at[2], sib)
+    cot_over = give(v_cot.at[0], v_cot.at[1], over)
+    n1_over = give(v_n1t.at[:, :, 1 - x], o_n1t.at[:, :, :, pl.ds(2 * tokens, 2 * tokens)], over)
 
     chips_o = 640 // (4 * own)
 
@@ -860,8 +902,6 @@
         return 0
 
     lax.fori_loop(0, rh // 640, turn_o, 0)
-    cot_over.wait_recv()
-    cot_last = give(v_cot.at[1], v_cot.at[3], sib)
     o_over = give(v_ot.at[:, :, 1 - x], o_ot.at[:, :, :, pl.ds(2 * tokens, 2 * tokens)], over)
     put(v_ot.at[:, :, x], o_ot.at[:, :, :, pl.ds(0, 2 * tokens)])
 
@@ -885,14 +925,15 @@
             pltpu.make_async_copy(v_gu.at[slot, :, pl.ds(tile, tile)], o_up.at[:, at], store_sem.at[slot, 1]),
         ]
 
+    gu.finish()
     for copy in loads(0, 0):
         copy.start()
     n2_pair.wait_recv()
-    land(down)
-    down = hop(3, d_block, d_piece) if half > 3 else down
     n2_over.wait_recv()
     n2_last = give(v_n2.at[1], v_n2.at[3], sib)
     n2_last.wait_recv()
+    if half > 3:
+        down.advance()
     put(v_n2, o_n2)
 
     def hidden_tile(t, _):
@@ -920,11 +961,12 @@
 
     lax.fori_loop(0, steps, hidden_tile, 0)
     put(v_hidden, o_hidden)
+    cot_over.wait_recv()
+    cot_last = give(v_cot.at[1], v_cot.at[3], sib)
+    if half > 3:
+        down.advance()
     cot_last.wait_recv()
     put(v_cot, o_cot)
-    if half > 3:
-        land(down)
-        down = hop(4, d_block, d_piece)
 
     def pd_store(t, slot):
         return pltpu.make_async_copy(v_pd.at[slot], o_pd.at[pl.ds(pl.multiple_of(t * BLK, BLK), BLK)], pd_sem.at[slot])
@@ -944,15 +986,13 @@
         return 0
 
     lax.fori_loop(0, width // BLK, down_tile, 0)
-    for s in range(5, half + 1):
-        land(down)
-        down = hop(s, d_block, d_piece)
+    down.to_last()
     for t in (steps - 2, steps - 1):
         for copy in stores(t, t % 2):
             copy.wait()
     for t in (width // BLK - 2, width // BLK - 1):
         pd_store(t, t % 2).wait()
-    land(down)
+    down.finish()
     land([n1_over, o_over])
     for copy in kept:
         copy.wait()
@@ -967,14 +1007,13 @@
     rh, fh = rec // 2, f // 2
     tokens, width = rows_in.shape
     half = n // 2
-    core = lax.axis_index("dp") % 2
-    row = jnp.arange(4 * n)
+    row = np.arange(4 * n)
     index = (row // 2) % n * 4 + row // (2 * n) * 2 + row % 2
-    lane_r, lane_d = jnp.arange(rh), jnp.arange(width)
-    spread_r = (lane_r[None] % own == jnp.arange(128)[:, None]).astype(BF16)
-    spread_d = (lane_d[None] % own_d == jnp.arange(128)[:, None]).astype(BF16)
-    pick_r = (index[:, None] - core * 2 * n == lane_r[None] // own).astype(F32)
-    pick_d = (index[:, None] == lane_d[None] // own_d).astype(F32)
+    lane_r, lane_d, short = np.arange(rec), np.arange(width), np.arange(128)[:, None]
+    spread_r = (lane_r[None, :rh] % own == short).astype(jnp.bfloat16)
+    spread_d = (lane_d[None] % own_d == short).astype(jnp.bfloat16)
+    pick_r = (index[:, None] == lane_r[None] // own).astype(np.float32)
+    pick_d = (index[:, None] == lane_d[None] // own_d).astype(np.float32)
     outs = dict(
         w_xy=((n, 2, 2, own_d, rec), BF16),
         w_o=((n, 2, 2, own, width // 2), BF16),
@@ -1012,12 +1051,12 @@
         ((tokens, width // 2), F32), ((tokens, width), F32), ((4, tokens, width), BF16),
         ((2, n, 2, rows_f, BLK), BF16), ((4 * tokens, fh), BF16), ((2, 4 * tokens, BLK), F32), ((2, BLK, fh), BF16),
     ]
-    count = 9 + (3 * n - 1) + n + n + 3 * n + 2 + 12
+    count = 9 + (5 * n - 5) + 2 * (2 * n - 2) + 5 * n + 2 + 12
     dma = pltpu.SemaphoreType.DMA
     result = pl.pallas_call(
         functools.partial(front_kernel, n),
         out_shape=[jax.ShapeDtypeStruct(shape, kind) for shape, kind in outs.values()],
-        in_specs=[pl.BlockSpec(memory_space=pltpu.VMEM)] * 14,
+        in_specs=[pl.BlockSpec(memory_space=pl.ANY)] * 10 + [pl.BlockSpec(memory_space=pltpu.VMEM)] * 4,
         out_specs=[pl.BlockSpec(memory_space=pl.ANY)] * len(outs),
         scratch_shapes=[pltpu.VMEM(shape, kind) for shape, kind in scratch]
         + [dma((32,)), dma((count,)), dma((count,)), dma((2, 2)), dma((2, 2)), dma((2,))],
@@ -1027,6 +1066,38 @@
         name="front",
     )(wx, wy, wo, gs, wg, wu, wd, rows_in, cot, starts, spread_r, pick_r, spread_d, pick_d)
     return dict(zip(outs, result))
+
+
+def finish_kernel(block, theirs, gate_ref, up_ref):
+    core = lax.axis_index("dp") % 2
+    half = gate_ref.shape[1] // 2
+
+    def place(mine, other):
+        for first, values in ((0, (mine, other)), (1, (other, mine))):
+
+            @pl.when(core == first)
+            def _():
+                for i, value in enumerate(values):
+                    at = pl.ds(i * half, half)
+                    gate_ref[:, at] = value[:, :half].astype(F32)
+                    up_ref[:, at] = value[:, half:].astype(F32)
+
+    place(block[core], theirs[...])
+
+
+def finish(block, theirs):
+    _, rows, cols = block.shape
+    tile = 32 if rows % 32 == 0 else rows
+    out = pl.BlockSpec((tile, cols), lambda i: (i, 0))
+    return pl.pallas_call(
+        finish_kernel,
+        grid=(rows // tile,),
+        in_specs=[pl.BlockSpec((2, tile, cols), lambda i: (0, i, 0)), out],
+        out_specs=[out, out],
+        out_shape=[jax.ShapeDtypeStruct((rows, cols), F32)] * 2,
+        compiler_params=pltpu.CompilerParams(vmem_limit_bytes=24 << 20),
+        name="finish",
+    )(block, theirs)
 
 
 def nt(left, right):
@@ -1281,9 +1352,9 @@
         n, after(c_x, grad_down, result, grad_x), c_y, c_out, g_lane.astype(BF16), vec
     )
     sum_vec = sum_vec.reshape(-1)
-    gu_mine, gu_theirs = whole(sum_gu)
-    grad_gate = halves((gu_mine[:, :fh], gu_theirs[:, :fh]))
-    grad_up = halves((gu_mine[:, fh:], gu_theirs[:, fh:]))
+    sum_gu = after(sum_gu, sum_vec).reshape(2, -1, 2 * fh)
+    theirs = lax.dynamic_index_in_dim(sum_gu, 1 - core, 0, keepdims=False)
+    grad_gate, grad_up = finish(sum_gu, sibling(theirs))
     tail = sum_vec[2 * own_d : 2 * own_d + (taps + 4) * own].reshape(taps + 4, own)
     return (
         result,

time: 604 us -> 592 us (0.980)
    pallas_call x1, Pallas kernels: 280 us -> 272 us  [front(): pl.pallas_call(functools.partial(front_kernel, n), out_shape=[jax.ShapeDt...]
  transfers between devices with their start and end apart: 20 -> 20, of which waited for: 8 -> 8; matrix products, arithmetic and copies ran while one was open for 15% -> 16% of each run, Pallas kernels for 23% -> 24%
where the time goes in v4:
time: 592 us; the launch traced here: 585 us
  Pallas kernels  415 us (70%)
  matrix products  57.3 us (10%)
  waiting for transfers between devices  34.9 us (6%)
  local copies, waits for them, and re-layouts  27.3 us (5%)
  other arithmetic  20.1 us (3%)
  between operations  16.3 us (3%)
  starting transfers between devices  14.5 us (2%)
    pallas_call x1, Pallas kernels, front(): pl.pallas_call(functools.partial(front_kernel, n), out_shape=[jax.ShapeDt...  272 us
    pallas_call x1, Pallas kernels, scatter_sums(): pl.pallas_call(functools.partial(scatter_kernel, n), out_shape=[jax.Shape...  129 us
    ppermute x7, waiting for transfers between devices, across(): return lax.ppermute(v, 'tp', [(0, 1), (1, 0)])  29.6 us
    dot_general x4, matrix products, nt(): lax.dot_general(left, right, (((1,), (1,)), ((), ())), preferred_element_...  24 us
    dot_general x4, matrix products, nn(): return jnp.dot(left, right, preferred_element_type=F32)  23.4 us
  transfers between devices with their start and end apart: 20, of which 8 were waited for; matrix products, arithmetic and copies ran while one was open for 16% of the time, Pallas kernels for 24%

profile of v4, /device:TPU:0, one launch (start us, length us, event | category | flops | bytes accessed | tf_op | source)
XLA Modules:
  0.0 584.9 jit_solution(1589736323102903148)
XLA Ops:
  8.1 0.7 fusion.49
  8.7 1.2 fusion.34
  10.1 1.2 copy.45
  11.4 0.6 fusion.42.refs_3_
  12.0 0.7 broadcast_in_dim.12.refs_9_
  12.7 271.8 %front.1 = (bf16[8,2,2,64,2560]{4,3,2,1,0:T(8,128)(2,1)}, bf16[8,2,2,80,1024]{4,3,2,1,0:T(8,128)(2,1)}, bf16[1280,512]{1,0:T(8,128)(2,1)}, f32[16,1280]{1,0:T(8,...) custom-call(bf16[64,2560]{1,0:T(8,128)(2,1)} %refs_0_.1, ...), custom_call_target="tpu_custom_call" | custom-call | tf_op jit(solution)/shard_map/front/pallas_call | solution.py:1056
  284.8 10.4 %fusion.6 = (bf16[512,1536]{1,0:T(8,128)(2,1)S(1)}, bf16[512,1536]{1,0:T(8,128)(2,1)S(1)}) fusion(f32[512,1536]{1,0:T(8,128)} %get-tuple-element.69, f32[512,1536]{1,0:T(8,128)} %get-tuple-element.68, bf16[512,2048]{1,0:T(8,128)(2,1)} %bitcast.146, bf16[2048,1536]{1,0:T(8,128)(2,1)} %bitcast.143), kind=kOutput, calls=%fused_computation.12 | convolution fusion | flops 3239313408 | bytes 17825792 | tf_op jit(solution)/shard_map/dot_general | solution.py:1108
  295.3 6.9 %convolution_convert_fusion.4 = bf16[512,2048]{1,0:T(8,128)(2,1)S(1)} fusion(bf16[2048,3072]{1,0:T(8,128)(2,1)S(1)} %bitcast.141, bf16[512,1536]{1,0:T(8,128)(2,1)S(1)} %get-tuple-element.121, bf16[512,1536]{1,0:T(8,128)(2,1)S(1)} %get-tuple-element.120), kind=kOutput, calls=%fused_computation.15 | convolution fusion | flops 6449790976 | bytes 17825792 | tf_op jit(solution)/shard_map/dot_general | solution.py:1104
  302.4 1.4 copy-done.15
  305.5 0.8 slice.284
  306.3 9.9 %convolution_convert_fusion = bf16[2048,3072]{1,0:T(8,128)(2,1)} fusion(bf16[512,2048]{1,0:T(8,128)(2,1)S(1)} %slice_dynamic-update-slice_fusion.2, bf16[512,3072]{1,0:T(8,128)(2,1)S(1)} %pad_maximum_fusion), kind=kOutput, calls=%fused_computation | convolution fusion | flops 6448742400 | bytes 17825792 | tf_op jit(solution)/shard_map/dot_general | solution.py:1179
  316.3 1.0 slice.228.h_in
  317.4 0.8 slice.258
  318.6 0.9 fusion.59
  319.6 1.6 collective-permute-start.1
  321.1 6.8 %convolution_convert_fusion.5 = bf16[512,2048]{1,0:T(8,128)(2,1)S(1)} fusion(bf16[512,1536]{1,0:T(8,128)(2,1)} %get-tuple-element.86, bf16[2048,1536]{1,0:T(8,128)(2,1)} %bitcast.144), kind=kOutput, calls=%fused_computation.16 | convolution fusion | flops 3222274048 | bytes 9961472 | tf_op jit(solution)/shard_map/dot_general | solution.py:1104
  327.9 1.0 slice.301
  329.0 4.8 collective-permute-done.1
  334.2 1.4 fusion.54
  335.8 1.2 maximum_convert_fusion.1
  337.3 0.9 pad_maximum_fusion.2
  338.2 1.5 collective-permute-start.12
  339.7 4.3 fusion.53
  345.3 18.5 %collective-permute-done.7 = bf16[128,2048]{1,0:T(8,128)(2,1)S(1)} collective-permute-done((bf16[128,2048]{1,0:T(8,128)(2,1)S(1)}, bf16[128,2048]{1,0:T(8,128)(2,1)S(1)}, u32[]{:S(2)}, u32[]{:S(2)}) %collective-permute-start.7) | collective-permute-done | bytes 524320 | tf_op jit(solution)/shard_map/ppermute | solution.py:1138
  364.3 1.1 copy-done
  366.2 5.3 adjoint.1
  371.6 1.3 collective-permute-start.4
  372.9 2.7 collective-permute-start.11
  375.6 1.6 collective-permute-done.4.inc
  377.3 6.6 %gates_back.1 = (bf16[2,128,1280]{2,1,0:T(8,128)(2,1)S(1)}, f32[1280,512]{1,0:T(8,128)S(1)}, f32[8,1280]{1,0:T(8,128)S(1)}) custom-call(f32[2,128,1280]{2,1,0:T(8,128)S(1)} %get-tuple-element.75.lam_ref, f32[2,128,1280]{2,1,0:T(8,128)S(1)} %get-tuple-element.76.c_ref, f32[2,1,1280]{2,1,0:T(1,128)S(1)} %collective-permute-done.4.inc, ...), custom_call_target="tpu_custom_call" | custom-call | flops 1200000000 | bytes 9000000 | tf_op jit(solution)/shard_map/gates_back/pallas_call | solution.py:566
  383.9 1.3 collective-permute-start.5
  385.2 0.9 fusion.37
  386.3 2.7 collective-permute-start.13
  389.0 2.9 collective-permute-done.5
  392.0 1.3 fusion.7
  393.4 1.2 pad_maximum_fusion.1
  394.5 6.0 %fusion.61 = f32[256,2048]{1,0:T(8,128)S(1)} fusion(bf16[256,2560]{1,0:T(8,128)(2,1)S(1)} %bitcast.122, bf16[2048,2560]{1,0:T(8,128)(2,1)} %bitcast.142), kind=kOutput, calls=%fused_computation.166 | convolution fusion | flops 2684354560 | bytes 13893632 | tf_op jit(solution)/shard_map/dot_general | solution.py:1104
  400.6 1.0 slice.312
  401.6 0.9 copy-done.10
  402.6 0.7 copy-done.20
  403.3 0.9 fusion.38
  404.8 4.6 convolution_convert_fusion.1
  409.5 1.4 bitcast_add_fusion
  411.1 4.3 convolution_convert_fusion.2
  415.4 3.4 collective-permute-done.9
  418.7 4.1 convolution_convert_fusion.3
  422.8 0.9 fusion.21.c_g
  423.7 1.6 fusion.27
  425.6 1.3 collective-permute-start.15
  426.9 2.9 collective-permute-done.15
  430.0 1.2 constant_dynamic-slice_fusion.7
  431.2 0.9 copy.47
  432.5 2.9 fusion.24
  435.4 0.6 copy.67
  436.3 1.3 convert_bitcast_fusion
  437.6 128.5 %scatter_sums.1 = (f32[64,2560]{1,0:T(8,128)}, f32[64,2560]{1,0:T(8,128)}, f32[80,2048]{1,0:T(8,128)}, f32[80,512]{1,0:T(8,128)}, f32[8,128]{1,0:T(8,128)}) custom-call(bf16[8,2,64,1280]{3,2,1,0:T(8,128)(2,1)} %bitcast.112, bf16[8,2,64,1280]{3,2,1,0:T(8,128)(2,1)} %bitcast.111, bf16[8,2,80,1024]{3,2,1,0:T(8,128)(2,1)} %bitcast.110, ...), custom_call_target="tpu_custom_call" | custom-call | tf_op jit(solution)/shard_map/scatter_sums/pallas_call | solution.py:291
  566.2 1.3 dynamic-slice_bitcast_fusion
  568.0 0.7 slice.265
  569.4 1.3 fusion.60
  571.2 1.6 fusion.58
  572.8 2.3 finish.1
  575.1 0.8 copy.91
  576.0 0.8 copy.92
  576.8 0.8 copy.93
  (176 shorter events, 10.0 us)
Async XLA Ops:
  7.2 2.9 copy-start.22
  7.2 4.1 copy-start.32
  7.2 4.0 copy-start.33
  7.2 4.0 copy-start.37
  7.2 4.0 copy-start.36
  7.2 4.0 copy-start.35
  7.3 4.0 copy-start.34
  7.3 4.0 copy-start.31
  7.3 4.1 copy-start.29
  7.3 4.1 copy-start.30
  7.3 422.7 %reduce-scatter.3.cloned.1.call-start = ((), (), s32[]{:S(2)}) async-start(), calls=%async_computation.2 | async-start | bytes 7077888 | tf_op jit(solution)/shard_map/reduce_scatter | solution.py:1170
  10.1 2.7 copy-start.23
  284.6 281.6 %reduce-scatter.5.cloned.1.call-start = ((), (), s32[]{:S(2)}) async-start(), calls=%async_computation.3 | async-start | bytes 14155776 | tf_op jit(solution)/shard_map/reduce_scatter | solution.py:1170
  284.8 10.4 %copy-start.38 = (bf16[8,2,128,3072]{3,2,1,0:T(8,128)(2,1)S(1)}, bf16[8,2,128,3072]{3,2,1,0:T(8,128)(2,1)}, u32[]{:S(2)}) copy-start(bf16[8,2,128,3072]{3,2,1,0:T(8,128)(2,1)} %get-tuple-element.70) | copy-start | bytes 37748740
  302.2 1.6 copy-start.15
  302.3 2.7 collective-permute-start
  316.3 1.9 copy-start.7
  316.3 2.0 copy-start.11
  316.3 2.2 copy-start.9
  319.6 14.2 %collective-permute-start.1 = (bf16[128,2048]{1,0:T(8,128)(2,1)}, bf16[128,2048]{1,0:T(8,128)(2,1)S(1)}, u32[]{:S(2)}, u32[]{:S(2)}) collective-permute-start(bf16[128,2048]{1,0:T(8,128)(2,1)} %slice.284), channel_id=1, source_target_pairs={{0,1},{1,0},{2,3},{3,2},{4,5},{5,4},{6,7},{7,6},{8,9},{9,8},{10,11... | collective-permute-start | bytes 1572872 | tf_op jit(solution)/shard_map/ppermute | solution.py:1138
  327.9 6.3 %copy-start.16 = (bf16[512,2048]{1,0:T(8,128)(2,1)}, bf16[512,2048]{1,0:T(8,128)(2,1)S(1)}, u32[]{:S(2)}) copy-start(bf16[512,2048]{1,0:T(8,128)(2,1)S(1)} %convolution_convert_fusion.5) | copy-start | bytes 6291460
  327.9 6.3 %copy-start.18 = (bf16[1,128,2048]{2,1,0:T(8,128)(2,1)S(1)}, bf16[1,128,2048]{2,1,0:T(8,128)(2,1)}, u32[]{:S(2)}) copy-start(bf16[1,128,2048]{2,1,0:T(8,128)(2,1)} %param.24) | copy-start | bytes 1572868
  329.0 15.0 %collective-permute-start.6 = (bf16[256,2048]{1,0:T(8,128)(2,1)}, bf16[256,2048]{1,0:T(8,128)(2,1)S(1)}, u32[]{:S(2)}, u32[]{:S(2)}) collective-permute-start(bf16[256,2048]{1,0:T(8,128)(2,1)} %slice.301), channel_id=1, source_target_pairs={{0,2},{2,0},{4,6},{6,4},{8,10},{10,8},{12,14},{14,12},{16,18},{18,... | collective-permute-start | bytes 3145736 | tf_op jit(solution)/shard_map/ppermute | solution.py:1135
  334.2 1.6 copy-start.24
  335.7 8.3 %copy-start.21 = (bf16[128,1024]{1,0:T(8,128)(2,1)}, bf16[128,1024]{1,0:T(8,128)(2,1)S(1)}, u32[]{:S(2)}) copy-start(bf16[128,1024]{1,0:T(8,128)(2,1)S(1)} %get-tuple-element.131) | copy-start | bytes 786436
  335.7 1.6 collective-permute-start.2
  337.3 6.6 %copy-start.28 = (bf16[128,1024]{1,0:T(8,128)(2,1)}, bf16[128,1024]{1,0:T(8,128)(2,1)S(1)}, u32[]{:S(2)}) copy-start(bf16[128,1024]{1,0:T(8,128)(2,1)S(1)} %collective-permute-done.2) | copy-start | bytes 786436
  338.2 66.6 %collective-permute-start.12 = (bf16[256,1024]{1,0:T(8,128)(2,1)}, bf16[256,1024]{1,0:T(8,128)(2,1)}, u32[]{:S(2)}, u32[]{:S(2)}) collective-permute-start(bf16[256,1024]{1,0:T(8,128)(2,1)} %pad_maximum_fusion.2), channel_id=1, source_target_pairs={{0,1},{1,0},{2,3},{3,2},{4,5},{5,4},{6,7},{7,6},{8,9},{9,8},{10,11... | collective-permute-start | bytes 1572872 | tf_op jit(solution)/shard_map/ppermute | solution.py:1138
  339.7 4.3 copy-start.17
  344.5 19.3 %collective-permute-start.7 = (bf16[128,2048]{1,0:T(8,128)(2,1)S(1)}, bf16[128,2048]{1,0:T(8,128)(2,1)S(1)}, u32[]{:S(2)}, u32[]{:S(2)}) collective-permute-start(bf16[128,2048]{1,0:T(8,128)(2,1)S(1)} %slice.303), channel_id=1, source_target_pairs={{0,1},{1,0},{2,3},{3,2},{4,5},{5,4},{6,7},{7,6},{8,9},{9,8},{10,11... | collective-permute-start | bytes 1572872 | tf_op jit(solution)/shard_map/ppermute | solution.py:1138
  345.2 18.8 %collective-permute-start.3 = (f32[2,128,1280]{2,1,0:T(8,128)S(1)}, f32[2,128,1280]{2,1,0:T(8,128)S(1)}, u32[]{:S(2)}, u32[]{:S(2)}) collective-permute-start(f32[2,128,1280]{2,1,0:T(8,128)S(1)} %bitcast.121), channel_id=1, source_target_pairs={{0,2},{2,0},{4,6},{6,4},{8,10},{10,8},{12,14},{14,12},{16,18},{18,... | collective-permute-start | bytes 3932168 | tf_op jit(solution)/shard_map/ppermute | solution.py:1135
  364.1 1.3 copy-start
  364.1 1.7 copy-start.2
  364.2 2.1 copy-start.3
  366.2 11.0 %copy-start.4 = (bf16[1280,512]{1,0:T(8,128)(2,1)S(1)}, bf16[1280,512]{1,0:T(8,128)(2,1)}, u32[]{:S(2)}) copy-start(bf16[1280,512]{1,0:T(8,128)(2,1)} %get-tuple-element.79.weights) | copy-start | bytes 3932164
  366.2 11.0 %copy-start.5 = (bf16[2,128,1280]{2,1,0:T(8,128)(2,1)S(1)}, bf16[2,128,1280]{2,1,0:T(8,128)(2,1)}, u32[]{:S(2)}) copy-start(bf16[2,128,1280]{2,1,0:T(8,128)(2,1)} %get-tuple-element.78.u_ref) | copy-start | bytes 1966084
  366.2 11.0 %copy-start.6 = (f32[2,128,128]{2,1,0:T(8,128)S(1)}, f32[2,128,128]{2,1,0:T(8,128)}, u32[]{:S(2)}) copy-start(f32[2,128,128]{2,1,0:T(8,128)} %get-tuple-element.80.starts) | copy-start | bytes 393220
  371.6 5.7 collective-permute-start.4
  372.9 11.0 %copy-start.19 = (f32[128,2048]{1,0:T(8,128)}, f32[128,2048]{1,0:T(8,128)S(1)}, u32[]{:S(2)}) copy-start(f32[128,2048]{1,0:T(8,128)S(1)} %slice_dynamic-update-slice_fusion.1) | copy-start | bytes 3145732
  372.9 38.1 %collective-permute-start.11 = (bf16[256,1280]{1,0:T(8,128)(2,1)}, bf16[256,1280]{1,0:T(8,128)(2,1)}, u32[]{:S(2)}, u32[]{:S(2)}) collective-permute-start(bf16[256,1280]{1,0:T(8,128)(2,1)} %bitcast.31), channel_id=1, source_target_pairs={{0,1},{1,0},{2,3},{3,2},{4,5},{5,4},{6,7},{7,6},{8,9},{9,8},{10,11... | collective-permute-start | bytes 1966088 | tf_op jit(solution)/shard_map/ppermute | solution.py:1138
  383.9 8.0 %collective-permute-start.5 = (bf16[2,3,1280]{2,1,0:T(4,128)(2,1)S(1)}, bf16[2,3,1280]{2,1,0:T(4,128)(2,1)S(1)}, u32[]{:S(2)}, u32[]{:S(2)}) collective-permute-start(bf16[2,3,1280]{2,1,0:T(4,128)(2,1)S(1)} %slice.229), channel_id=1, source_target_pairs={{1,0},{3,2},{5,4},{7,6},{9,8},{11,10},{13,12},{15,14},{17,16},{19,... | collective-permute-start | bytes 46088 | tf_op jit(solution)/shard_map/ppermute | solution.py:1291
  386.3 5.7 copy-start.8
  386.3 23.1 %collective-permute-start.13 = (bf16[4,2,80,512]{3,2,0,1:T(8,128)(2,1)}, bf16[4,2,80,512]{3,2,0,1:T(8,128)(2,1)}, u32[]{:S(2)}, u32[]{:S(2)}) collective-permute-start(bf16[4,2,80,512]{3,2,0,1:T(8,128)(2,1)} %fusion.37), channel_id=1, source_target_pairs={{0,1},{1,0},{2,3},{3,2},{4,5},{5,4},{6,7},{7,6},{8,9},{9,8},{10,11... | collective-permute-start | bytes 1966088 | tf_op jit(solution)/shard_map/ppermute | solution.py:1138
  393.3 25.4 %collective-permute-start.9 = (bf16[256,1280]{1,0:T(8,128)(2,1)S(1)}, bf16[256,1280]{1,0:T(8,128)(2,1)}, u32[]{:S(2)}, u32[]{:S(2)}) collective-permute-start(bf16[256,1280]{1,0:T(8,128)(2,1)S(1)} %bitcast.108), channel_id=1, source_target_pairs={{0,1},{1,0},{2,3},{3,2},{4,5},{5,4},{6,7},{7,6},{8,9},{9,8},{10,11... | collective-permute-start | bytes 1966088 | tf_op jit(solution)/shard_map/ppermute | solution.py:1138
  400.6 3.6 copy-start.13
  400.6 2.0 copy-start.10
  400.6 2.7 copy-start.20
  401.6 22.1 %collective-permute-start.8 = (f32[128,2048]{1,0:T(8,128)}, f32[128,2048]{1,0:T(8,128)}, u32[]{:S(2)}, u32[]{:S(2)}) collective-permute-start(f32[128,2048]{1,0:T(8,128)} %slice.312), channel_id=1, source_target_pairs={{0,2},{2,0},{4,6},{6,4},{8,10},{10,8},{12,14},{14,12},{16,18},{18,... | collective-permute-start | bytes 3145736 | tf_op jit(solution)/shard_map/ppermute | solution.py:1135
  409.5 1.6 copy-start.39
  411.0 11.8 %collective-permute-start.14 = (bf16[4,80,512]{2,1,0:T(8,128)(2,1)S(1)}, bf16[4,80,512]{2,1,0:T(8,128)(2,1)S(1)}, u32[]{:S(2)}, u32[]{:S(2)}) collective-permute-start(bf16[4,80,512]{2,1,0:T(8,128)(2,1)S(1)} %get-tuple-element.130), channel_id=1, source_target_pairs={{0,2},{2,0},{4,6},{6,4},{8,10},{10,8},{12,14},{14,12},{16,18},{18,... | collective-permute-start | bytes 983048 | tf_op jit(solution)/shard_map/ppermute | solution.py:1135
  415.4 8.4 %copy-start.12 = (bf16[1,128,2048]{2,1,0:T(8,128)(2,1)S(1)}, bf16[1,128,2048]{2,1,0:T(8,128)(2,1)}, u32[]{:S(2)}) copy-start(bf16[1,128,2048]{2,1,0:T(8,128)(2,1)} %param.23) | copy-start | bytes 1572868
  415.4 8.4 %copy-start.14 = (f32[256,2048]{1,0:T(8,128)S(1)}, f32[256,2048]{1,0:T(8,128)}, u32[]{:S(2)}) copy-start(f32[256,2048]{1,0:T(8,128)} %copy-done.13) | copy-start | bytes 6291460
  425.6 4.2 collective-permute-start.15
  429.9 5.5 collective-permute-start.16
  432.1 4.2 collective-permute-start.10
  566.2 6.7 %copy-start.1 = (bf16[256,3072]{1,0:T(8,128)(2,1)S(1)}, bf16[256,3072]{1,0:T(8,128)(2,1)}, u32[]{:S(2)}) copy-start(bf16[256,3072]{1,0:T(8,128)(2,1)} %reduce-scatter.5.cloned.1.call-done) | copy-start | bytes 4718596
  567.5 5.4 collective-permute-start.17
  568.8 6.3 %copy-start.27 = (f32[64,2560]{1,0:T(8,128)S(1)}, f32[64,2560]{1,0:T(8,128)}, u32[]{:S(2)}) copy-start(f32[64,2560]{1,0:T(8,128)} %get-tuple-element.171) | copy-start | bytes 1966084
  568.8 7.2 %copy-start.26 = (f32[64,2560]{1,0:T(8,128)S(1)}, f32[64,2560]{1,0:T(8,128)}, u32[]{:S(2)}) copy-start(f32[64,2560]{1,0:T(8,128)} %get-tuple-element.172) | copy-start | bytes 1966084
  572.8 4.0 copy-start.25
Sparse Core Ops, SparseCore 0:
  284.7 68.9 reduce-scatter.2
  356.0 164.6 reduce-scatter.4

commit v5 on v4

--- a/solution.py
+++ b/solution.py
@@ -1068,36 +1068,55 @@
     return dict(zip(outs, result))
 
 
-def finish_kernel(block, theirs, gate_ref, up_ref):
+def finish_kernel(
+    sums, x_sum, y_sum, out_sum, gates, vec,
+    gate_ref, up_ref, x_ref, y_ref, out_ref, a_ref, i_ref, taps_ref, *lines,
+):
     core = lax.axis_index("dp") % 2
     half = gate_ref.shape[1] // 2
-
-    def place(mine, other):
-        for first, values in ((0, (mine, other)), (1, (other, mine))):
-
-            @pl.when(core == first)
-            def _():
-                for i, value in enumerate(values):
-                    at = pl.ds(i * half, half)
-                    gate_ref[:, at] = value[:, :half].astype(F32)
-                    up_ref[:, at] = value[:, half:].astype(F32)
-
-    place(block[core], theirs[...])
-
-
-def finish(block, theirs):
-    _, rows, cols = block.shape
-    tile = 32 if rows % 32 == 0 else rows
-    out = pl.BlockSpec((tile, cols), lambda i: (i, 0))
+    for first in (0, 1):
+
+        @pl.when(core == first)
+        def _():
+            for i in (0, 1):
+                start = (i != first) * 2 * half
+                at = pl.ds(i * half, half)
+                gate_ref[:, at] = sums[:, start : start + half].astype(F32)
+                up_ref[:, at] = sums[:, start + half : start + 2 * half].astype(F32)
+
+    x_ref[...] = x_sum[...]
+    y_ref[...] = y_sum[...]
+    out_ref[...] = out_sum[...]
+    a_ref[...] = gates[:, :BLK]
+    i_ref[...] = gates[:, BLK:]
+    taps, own = taps_ref.shape
+    taps_ref[...] = vec[0:taps, 0:own]
+    for k, ref in enumerate(lines):
+        ref[...] = vec[taps + k : taps + k + 1, 0 : ref.shape[1]]
+
+
+def finish(sums, x_sum, y_sum, out_sum, gates, vec, taps):
+    rows, cols = sums.shape
+    own, own_d = out_sum.shape[0], x_sum.shape[0]
+    steps = 2 if rows % 16 == 0 and own % 16 == 0 and own_d % 16 == 0 else 1
+
+    def tiled(shape):
+        return pl.BlockSpec((shape[0] // steps, shape[1]), lambda i: (i, 0))
+
+    def fixed(shape):
+        return pl.BlockSpec(shape, lambda i: (0, 0))
+
+    big = [(rows, cols // 2)] * 2 + [x_sum.shape, y_sum.shape, out_sum.shape] + [(own, BLK)] * 2
+    small = [(taps, own)] + [(1, own)] * 4 + [(1, own_d)] * 2
     return pl.pallas_call(
         finish_kernel,
-        grid=(rows // tile,),
-        in_specs=[pl.BlockSpec((2, tile, cols), lambda i: (0, i, 0)), out],
-        out_specs=[out, out],
-        out_shape=[jax.ShapeDtypeStruct((rows, cols), F32)] * 2,
-        compiler_params=pltpu.CompilerParams(vmem_limit_bytes=24 << 20),
+        grid=(steps,),
+        in_specs=[tiled(v.shape) for v in (sums, x_sum, y_sum, out_sum, gates)] + [fixed(vec.shape)],
+        out_specs=[tiled(shape) for shape in big] + [fixed(shape) for shape in small],
+        out_shape=[jax.ShapeDtypeStruct(shape, F32) for shape in big + small],
+        compiler_params=pltpu.CompilerParams(vmem_limit_bytes=60 << 20),
         name="finish",
-    )(block, theirs)
+    )(sums, x_sum, y_sum, out_sum, gates, vec)
 
 
 def nt(left, right):
@@ -1268,7 +1287,11 @@
     d_n2_pair = pair_sum(nt(d_gu, w_gu).astype(BF16))
     d_n2_send = d_n2_pair[tokens:]
     d_n2 = d_n2_pair[:tokens].astype(F32) + across(d_n2_send).astype(F32)
-    part_gu = tn(ring_order(n2_all, 1), after(d_gu, d_n2_send)).astype(BF16)
+    n2_rows = ring_order(after(n2_all, d_n2_send), 1).reshape(4 * tokens, n, 2, width // dp_size)
+    n2_rows = plane(n2_rows, core).reshape(4 * tokens, width // 2)
+    d_gu_sib = sibling(d_gu)
+    d_gu_sib = jnp.concatenate([d_gu_sib[2 * tokens :], d_gu_sib[: 2 * tokens]], axis=0)
+    part_gu = tn(n2_rows, after(jnp.concatenate([d_gu, d_gu_sib], axis=1), d_n2_send)).astype(BF16)
     sum_gu = lane_sum(part_gu)
     ff_pair = pair_sum(nt(after(hidden, part_gu), w_d).astype(BF16))
     ff_out = ff_pair[:tokens].astype(F32) + across(ff_pair[tokens:]).astype(F32)
@@ -1327,16 +1350,15 @@
 
     lines_back = jnp.concatenate([d_taps, d_bias, sums[:3]], axis=0)
     lines_back = lines_back.reshape(taps + 4, half, 2, 2, own).transpose(1, 2, 3, 0, 4)
-    lines_back = placed(lines_back.reshape(half, 2, 2, (taps + 4) * own))
-    gains = jnp.concatenate([d_gain_one.reshape(n, 2, 2, own_d), d_gain_two.reshape(n, 2, 2, own_d)], axis=3)
-    vec = jnp.concatenate([gains, lines_back], axis=3)
-    vec = jnp.pad(vec, ((0, 0), (0, 0), (0, 0), (0, -vec.shape[3] % 128)))
+    lines_back = placed(jnp.pad(lines_back, ((0, 0),) * 4 + ((0, 128 - own),)))
+    gains = jnp.stack([d_gain_one.reshape(n, 2, 2, own_d), d_gain_two.reshape(n, 2, 2, own_d)], axis=3)
+    gains = jnp.pad(gains, ((0, 0),) * 3 + ((0, PAD - taps - 6), (0, 128 - own_d)))
+    vec = jnp.concatenate([lines_back, gains], axis=3)
     vec = plane(vec, x) + across(plane(vec, 1 - x))
     vec = lax.dynamic_index_in_dim(vec, core, 1, keepdims=False) + sibling(
         lax.dynamic_index_in_dim(vec, 1 - core, 1, keepdims=False)
     )
 
-    vec = jnp.pad(vec, ((0, 0), (0, -vec.shape[1] % 1024))).reshape(n, -1, 128)
     def whole(block):
         rows = block.shape[0] // 2
         block = block.reshape(2, rows, block.shape[1])
@@ -1348,29 +1370,27 @@
         return by_core(pair[0], pair[1], 1).astype(F32)
 
     grad_down = halves(whole(sum_d)).T
-    grad_w_x, grad_w_y, grad_w_out, sum_gates, sum_vec = scatter_sums(
+    x_sum, y_sum, out_sum, sum_gates, sum_vec = scatter_sums(
         n, after(c_x, grad_down, result, grad_x), c_y, c_out, g_lane.astype(BF16), vec
     )
-    sum_vec = sum_vec.reshape(-1)
-    sum_gu = after(sum_gu, sum_vec).reshape(2, -1, 2 * fh)
-    theirs = lax.dynamic_index_in_dim(sum_gu, 1 - core, 0, keepdims=False)
-    grad_gate, grad_up = finish(sum_gu, sibling(theirs))
-    tail = sum_vec[2 * own_d : 2 * own_d + (taps + 4) * own].reshape(taps + 4, own)
+    done = finish(after(sum_gu, sum_vec), x_sum, y_sum, out_sum, sum_gates, sum_vec, taps)
+    grad_gate, grad_up, grad_w_x, grad_w_y, grad_w_out, grad_a_w, grad_i_w, grad_taps = done[:8]
+    grad_bias, grad_a_b, grad_i_b, grad_decay, grad_gain_one, grad_gain_two = (v.reshape(-1) for v in done[8:])
     return (
         result,
         grad_x.reshape(1, tokens, width),
-        sum_vec[:own_d],
+        grad_gain_one,
         grad_w_x,
         grad_w_y,
-        tail[:taps],
-        tail[taps],
-        sum_gates[:, :BLK],
-        tail[taps + 1],
-        sum_gates[:, BLK:],
-        tail[taps + 2],
-        tail[taps + 3],
+        grad_taps,
+        grad_bias,
+        grad_a_w,
+        grad_a_b,
+        grad_i_w,
+        grad_i_b,
+        grad_decay,
         grad_w_out,
-        sum_vec[own_d : 2 * own_d],
+        grad_gain_two,
         grad_gate,
         grad_up,
         grad_down,

time: 592 us -> 585 us (0.988)
  Pallas kernels: 415 us -> 394 us
  other arithmetic: 20.1 us -> 36.9 us
    pallas_call x1, Pallas kernels: 129 us -> 106 us  [scatter_sums(): pl.pallas_call(functools.partial(scatter_kernel, n), out_shape=[jax.Shape...]
    concatenate x1 -> x2, other arithmetic: 0.11 us -> 12.3 us  [the longest x1 12 us: body(): jnp.concatenate([d_gu, d_gu_sib], axis=1)]
  transfers between devices with their start and end apart: 20 -> 20, of which waited for: 8 -> 7; matrix products, arithmetic and copies ran while one was open for 16% -> 18% of each run, Pallas kernels for 24% -> 20%
where the time goes in v5:
time: 585 us; the launch traced here: 578 us
  Pallas kernels  394 us (67%)
  matrix products  54.3 us (9%)
  other arithmetic  36.9 us (6%)
  waiting for transfers between devices  33.2 us (6%)
  local copies, waits for them, and re-layouts  28 us (5%)
  between operations  16.1 us (3%)
  starting transfers between devices  15.3 us (3%)
    pallas_call x1, Pallas kernels, front(): pl.pallas_call(functools.partial(front_kernel, n), out_shape=[jax.ShapeDt...  272 us
    pallas_call x1, Pallas kernels, scatter_sums(): pl.pallas_call(functools.partial(scatter_kernel, n), out_shape=[jax.Shape...  106 us
    ppermute x7, waiting for transfers between devices, across(): return lax.ppermute(v, 'tp', [(0, 1), (1, 0)])  30.3 us
    dot_general x4, matrix products, nt(): lax.dot_general(left, right, (((1,), (1,)), ((), ())), preferred_element_...  23.3 us
    dot_general x4, matrix products, nn(): return jnp.dot(left, right, preferred_element_type=F32)  21 us
    concatenate x1, other arithmetic, body(): jnp.concatenate([d_gu, d_gu_sib], axis=1)  12 us
  transfers between devices with their start and end apart: 20, of which 7 were waited for; matrix products, arithmetic and copies ran while one was open for 18% of the time, Pallas kernels for 20%

profile of v5, /device:TPU:0, one launch (start us, length us, event | category | flops | bytes accessed | tf_op | source)
XLA Modules:
  0.0 577.5 jit_solution(14206209387953124684)
XLA Ops:
  8.1 0.7 fusion.51
  8.7 1.2 fusion.34
  10.1 1.2 copy.54
  11.4 0.6 fusion.44.refs_3_
  12.0 0.7 broadcast_in_dim.12.refs_9_
  12.7 271.8 %front.1 = (bf16[8,2,2,64,2560]{4,3,2,1,0:T(8,128)(2,1)}, bf16[8,2,2,80,1024]{4,3,2,1,0:T(8,128)(2,1)}, bf16[1280,512]{1,0:T(8,128)(2,1)}, f32[16,1280]{1,0:T(8,...) custom-call(bf16[64,2560]{1,0:T(8,128)(2,1)} %refs_0_.1, ...), custom_call_target="tpu_custom_call" | custom-call | tf_op jit(solution)/shard_map/front/pallas_call | solution.py:1056
  284.8 1.6 copy-done.39
  286.4 9.6 %fusion.6 = (bf16[512,1536]{1,0:T(8,128)(2,1)S(1)}, bf16[512,1536]{1,0:T(8,128)(2,1)S(1)}) fusion(f32[512,1536]{1,0:T(8,128)S(1)} %copy-done.39, f32[512,1536]{1,0:T(8,128)} %get-tuple-element.81, bf16[512,2048]{1,0:T(8,128)(2,1)} %bitcast.124, bf16[2048,1536]{1,0:T(8,128)(2,1)} %bitcast.121), kind=kOutput, calls=%fused_computation.13 | convolution fusion | flops 3239313408 | bytes 17825792 | tf_op jit(solution)/shard_map/dot_general | solution.py:1127
  296.1 6.9 %convolution_convert_fusion.4 = bf16[512,2048]{1,0:T(8,128)(2,1)S(1)} fusion(bf16[2048,3072]{1,0:T(8,128)(2,1)S(1)} %bitcast.119, bf16[512,1536]{1,0:T(8,128)(2,1)S(1)} %get-tuple-element.147, bf16[512,1536]{1,0:T(8,128)(2,1)S(1)} %get-tuple-element.146), kind=kOutput, calls=%fused_computation.16 | convolution fusion | flops 6449790976 | bytes 17825792 | tf_op jit(solution)/shard_map/dot_general | solution.py:1123
  303.3 2.1 pad_maximum_fusion
  306.0 1.6 add_convert_fusion.1
  307.6 0.8 slice.251
  308.5 2.9 copy.55
  311.7 2.2 fusion.58
  314.5 12.0 %maximum_maximum_fusion = bf16[512,6144]{1,0:T(8,128)(2,1)S(1)} fusion(bf16[256,3072]{1,0:T(8,128)(2,1)S(1)} %get-tuple-element.149, bf16[256,3072]{1,0:T(8,128)(2,1)S(1)} %get-tuple-element.148, bf16[512,1536]{1,0:T(8,128)(2,1)S(1)} %copy-done.15, bf16[512,1536]{1,0:T(8,128)(2,1)S(1)} %copy-done.13), kind=kLoop, calls=%fused_computation.1 | loop fusion | flops 25165824 | bytes 12582912 | tf_op jit(solution)/shard_map/concatenate | solution.py:1294
  326.6 10.0 %convolution_convert_fusion = bf16[1024,6144]{1,0:T(8,128)(2,1)} fusion(bf16[512,1024]{0,1:T(8,128)(2,1)S(1)} %bitcast.102, bf16[512,6144]{1,0:T(8,128)(2,1)S(1)} %maximum_maximum_fusion), kind=kOutput, calls=%fused_computation | convolution fusion | flops 6448742400 | bytes 19922944 | tf_op jit(solution)/shard_map/dot_general | solution.py:1198
  336.6 1.2 copy-done.8
  338.0 1.5 collective-permute-start.1
  339.5 0.9 fusion.61
  340.5 11.8 %collective-permute-done.1 = bf16[128,2048]{1,0:T(8,128)(2,1)S(1)} collective-permute-done((bf16[128,2048]{1,0:T(8,128)(2,1)}, bf16[128,2048]{1,0:T(8,128)(2,1)S(1)}, u32[]{:S(2)}, u32[]{:S(2)}) %collective-permute-start.1) | collective-permute-done | bytes 524320 | tf_op jit(solution)/shard_map/ppermute | solution.py:1157
  352.6 1.4 fusion.56
  354.2 1.5 collective-permute-done.2
  355.7 4.1 fusion.55
  359.9 1.2 fusion.59
  361.2 0.9 slice.203.h_in
  362.2 0.8 slice.235
  363.3 1.2 maximum_convert_fusion.1
  364.6 0.8 pad_maximum_fusion.2
  365.4 1.5 collective-permute-start.13
  366.9 1.4 fusion.60
  368.5 1.1 copy-done
  370.4 5.3 adjoint.1
  375.7 1.3 collective-permute-start.4
  377.0 2.7 collective-permute-start.12
  379.8 6.4 %convolution_convert_fusion.5 = bf16[512,2048]{1,0:T(8,128)(2,1)S(1)} fusion(bf16[512,1536]{1,0:T(8,128)(2,1)S(1)} %copy-done.40, bf16[2048,1536]{1,0:T(8,128)(2,1)} %bitcast.122), kind=kOutput, calls=%fused_computation.17 | convolution fusion | flops 3222274048 | bytes 9961472 | tf_op jit(solution)/shard_map/dot_general | solution.py:1123
  386.2 1.1 slice.270
  387.9 0.6 copy-done.3
  388.9 6.6 %gates_back.1 = (bf16[2,128,1280]{2,1,0:T(8,128)(2,1)S(1)}, f32[1280,512]{1,0:T(8,128)S(1)}, f32[8,1280]{1,0:T(8,128)S(1)}) custom-call(f32[2,128,1280]{2,1,0:T(8,128)S(1)} %get-tuple-element.88.lam_ref, f32[2,128,1280]{2,1,0:T(8,128)S(1)} %get-tuple-element.89.c_ref, f32[2,1,1280]{2,1,0:T(1,128)S(1)} %collective-permute-done.4.inc, ...), custom_call_target="tpu_custom_call" | custom-call | flops 1200000000 | bytes 9000000 | tf_op jit(solution)/shard_map/gates_back/pallas_call | solution.py:566
  395.5 1.3 collective-permute-start.5
  396.8 0.9 fusion.37
  397.9 2.7 collective-permute-start.14
  400.6 0.8 collective-permute-done.5
  401.5 1.3 fusion.7
  403.6 1.2 pad_maximum_fusion.1
  404.8 5.8 %fusion.62 = f32[256,2048]{1,0:T(8,128)S(1)} fusion(bf16[256,2560]{1,0:T(8,128)(2,1)S(1)} %bitcast.101, bf16[2048,2560]{1,0:T(8,128)(2,1)} %bitcast.120), kind=kOutput, calls=%fused_computation.169 | convolution fusion | flops 2684354560 | bytes 13893632 | tf_op jit(solution)/shard_map/dot_general | solution.py:1123
  411.0 0.8 copy-done.23
  412.1 0.8 copy-done.41
  412.9 4.1 convolution_convert_fusion.1
  416.9 1.4 bitcast_add_fusion
  418.5 4.3 convolution_convert_fusion.2
  422.8 6.5 %collective-permute-done.10 = bf16[256,1280]{1,0:T(8,128)(2,1)S(1)} collective-permute-done((bf16[256,1280]{1,0:T(8,128)(2,1)S(1)}, bf16[256,1280]{1,0:T(8,128)(2,1)S(1)}, u32[]{:S(2)}, u32[]{:S(2)}) %collective-permute-start.10) | collective-permute-done | bytes 655392 | tf_op jit(solution)/shard_map/ppermute | solution.py:1157
  429.3 3.0 convolution_convert_fusion.3
  432.3 0.9 fusion.21.c_g
  433.2 1.7 add_convert_fusion
  435.0 1.6 collective-permute-start.8
  438.6 12.1 %collective-permute-done.16 = f32[8,2,16,128]{3,2,0,1:T(8,128)S(1)} collective-permute-done((f32[8,2,16,128]{3,2,0,1:T(8,128)S(1)}, f32[8,2,16,128]{3,2,0,1:T(8,128)S(1)}, u32[]{:S(2)}, u32[]{:S(2)}) %collective-permute-start.16) | collective-permute-done | bytes 131104 | tf_op jit(solution)/shard_map/ppermute | solution.py:1157
  450.8 2.9 fusion.24
  453.8 0.6 bitcast_add_fusion.2.c_v
  454.4 1.2 convert_add_fusion
  455.8 1.3 constant_dynamic-slice_fusion.3
  457.8 0.9 fusion.38
  459.1 1.3 convert_bitcast_fusion
  460.4 105.8 %scatter_sums.1 = (f32[64,2560]{1,0:T(8,128)}, f32[64,2560]{1,0:T(8,128)}, f32[80,2048]{1,0:T(8,128)}, f32[80,512]{1,0:T(8,128)}, f32[16,128]{1,0:T(8,128)}) custom-call(bf16[8,2,64,1280]{3,2,1,0:T(8,128)(2,1)} %bitcast.98, bf16[8,2,64,1280]{3,2,1,0:T(8,128)(2,1)} %bitcast.97, bf16[8,2,80,1024]{3,2,1,0:T(8,128)(2,1)} %bitcast.96, ...), custom_call_target="tpu_custom_call" | custom-call | tf_op jit(solution)/shard_map/scatter_sums/pallas_call | solution.py:291
  566.2 4.3 finish.1
  (177 shorter events, 10.4 us)
Async XLA Ops:
  7.2 2.9 copy-start.24
  7.2 4.1 copy-start.32
  7.2 4.0 copy-start.33
  7.2 4.0 copy-start.37
  7.2 4.0 copy-start.36
  7.2 4.0 copy-start.35
  7.3 4.0 copy-start.34
  7.3 4.0 copy-start.31
  7.3 4.1 copy-start.29
  7.3 4.1 copy-start.30
  7.3 448.5 %reduce-scatter.5.cloned.1.call-start = ((), (), s32[]{:S(2)}) async-start(), calls=%async_computation.3 | async-start | bytes 7077888 | tf_op jit(solution)/shard_map/reduce_scatter | solution.py:1189
  10.1 2.7 copy-start.25
  284.6 1.9 copy-start.39
  284.6 281.6 %reduce-scatter.3.cloned.1.call-start = ((), (), s32[]{:S(2)}) async-start(), calls=%async_computation.2 | async-start | bytes 14155776 | tf_op jit(solution)/shard_map/reduce_scatter | solution.py:1189
  286.4 9.7 %copy-start.38 = (bf16[8,2,128,3072]{3,2,1,0:T(8,128)(2,1)S(1)}, bf16[8,2,128,3072]{3,2,1,0:T(8,128)(2,1)}, u32[]{:S(2)}) copy-start(bf16[8,2,128,3072]{3,2,1,0:T(8,128)(2,1)} %get-tuple-element.83) | copy-start | bytes 37748740
  296.1 7.2 %copy-start.12 = (bf16[512,1536]{1,0:T(8,128)(2,1)}, bf16[512,1536]{1,0:T(8,128)(2,1)S(1)}, u32[]{:S(2)}) copy-start(bf16[512,1536]{1,0:T(8,128)(2,1)S(1)} %get-tuple-element.146) | copy-start | bytes 4718596
  296.1 7.2 %copy-start.14 = (bf16[512,1536]{1,0:T(8,128)(2,1)}, bf16[512,1536]{1,0:T(8,128)(2,1)S(1)}, u32[]{:S(2)}) copy-start(bf16[512,1536]{1,0:T(8,128)(2,1)S(1)} %get-tuple-element.147) | copy-start | bytes 4718596
  303.2 2.9 collective-permute-start
  305.4 6.3 %collective-permute-start.6 = (bf16[512,3072]{1,0:T(8,128)(2,1)}, bf16[512,3072]{1,0:T(8,128)(2,1)}, u32[]{:S(2)}, u32[]{:S(2)}) collective-permute-start(bf16[512,3072]{1,0:T(8,128)(2,1)} %pad_maximum_fusion), channel_id=1, source_target_pairs={{0,2},{2,0},{4,6},{6,4},{8,10},{10,8},{12,14},{14,12},{16,18},{18,... | collective-permute-start | bytes 9437192 | tf_op jit(solution)/shard_map/ppermute | solution.py:1154
  311.6 2.4 copy-start.13
  311.6 2.9 copy-start.15
  336.6 1.3 copy-start.8
  336.6 16.0 %copy-start.21 = (bf16[1,128,2048]{2,1,0:T(8,128)(2,1)S(1)}, bf16[1,128,2048]{2,1,0:T(8,128)(2,1)}, u32[]{:S(2)}) copy-start(bf16[1,128,2048]{2,1,0:T(8,128)(2,1)} %param.24) | copy-start | bytes 1572868
  338.0 14.3 %collective-permute-start.1 = (bf16[128,2048]{1,0:T(8,128)(2,1)}, bf16[128,2048]{1,0:T(8,128)(2,1)S(1)}, u32[]{:S(2)}, u32[]{:S(2)}) collective-permute-start(bf16[128,2048]{1,0:T(8,128)(2,1)} %slice.251), channel_id=1, source_target_pairs={{0,1},{1,0},{2,3},{3,2},{4,5},{5,4},{6,7},{7,6},{8,9},{9,8},{10,11... | collective-permute-start | bytes 1572872 | tf_op jit(solution)/shard_map/ppermute | solution.py:1157
  354.1 10.5 %copy-start.22 = (bf16[128,1024]{1,0:T(8,128)(2,1)}, bf16[128,1024]{1,0:T(8,128)(2,1)S(1)}, u32[]{:S(2)}) copy-start(bf16[128,1024]{1,0:T(8,128)(2,1)S(1)} %get-tuple-element.159) | copy-start | bytes 786436
  354.1 1.6 collective-permute-start.2
  355.7 8.9 %copy-start.27 = (bf16[128,1024]{1,0:T(8,128)(2,1)}, bf16[128,1024]{1,0:T(8,128)(2,1)S(1)}, u32[]{:S(2)}) copy-start(bf16[128,1024]{1,0:T(8,128)(2,1)S(1)} %collective-permute-done.2) | copy-start | bytes 786436
  359.8 3.2 copy-start.6
  359.9 3.2 copy-start.10
  359.9 3.4 copy-start.26
  361.1 5.8 %collective-permute-start.3 = (f32[2,128,1280]{2,1,0:T(8,128)}, f32[2,128,1280]{2,1,0:T(8,128)}, u32[]{:S(2)}, u32[]{:S(2)}) collective-permute-start(f32[2,128,1280]{2,1,0:T(8,128)} %bitcast.17), channel_id=1, source_target_pairs={{0,2},{2,0},{4,6},{6,4},{8,10},{10,8},{12,14},{14,12},{16,18},{18,... | collective-permute-start | bytes 3932168 | tf_op jit(solution)/shard_map/ppermute | solution.py:1154
  365.4 45.5 %collective-permute-start.13 = (bf16[256,1024]{1,0:T(8,128)(2,1)}, bf16[256,1024]{1,0:T(8,128)(2,1)}, u32[]{:S(2)}, u32[]{:S(2)}) collective-permute-start(bf16[256,1024]{1,0:T(8,128)(2,1)} %pad_maximum_fusion.2), channel_id=1, source_target_pairs={{0,1},{1,0},{2,3},{3,2},{4,5},{5,4},{6,7},{7,6},{8,9},{9,8},{10,11... | collective-permute-start | bytes 1572872 | tf_op jit(solution)/shard_map/ppermute | solution.py:1157
  368.3 1.3 copy-start
  368.3 1.7 copy-start.1
  368.3 2.1 copy-start.2
  370.4 9.3 %copy-start.40 = (bf16[512,1536]{1,0:T(8,128)(2,1)S(1)}, bf16[512,1536]{1,0:T(8,128)(2,1)}, u32[]{:S(2)}) copy-start(bf16[512,1536]{1,0:T(8,128)(2,1)} %get-tuple-element.100) | copy-start | bytes 4718596
  375.7 11.6 %collective-permute-start.4 = (f32[2,1,1280]{2,1,0:T(1,128)S(1)}, f32[2,1,1280]{2,1,0:T(1,128)S(1)}, u32[]{:S(2)}, u32[]{:S(2)}) collective-permute-start(f32[2,1,1280]{2,1,0:T(1,128)S(1)} %slice_multiply_fusion.7), channel_id=1, source_target_pairs={{1,0},{3,2},{5,4},{7,6},{9,8},{11,10},{13,12},{15,14},{17,16},{19,... | collective-permute-start | bytes 30728 | tf_op jit(solution)/shard_map/ppermute | solution.py:1312
  377.0 41.5 %collective-permute-start.12 = (bf16[256,1280]{1,0:T(8,128)(2,1)}, bf16[256,1280]{1,0:T(8,128)(2,1)}, u32[]{:S(2)}, u32[]{:S(2)}) collective-permute-start(bf16[256,1280]{1,0:T(8,128)(2,1)} %bitcast.33), channel_id=1, source_target_pairs={{0,1},{1,0},{2,3},{3,2},{4,5},{5,4},{6,7},{7,6},{8,9},{9,8},{10,11... | collective-permute-start | bytes 1966088 | tf_op jit(solution)/shard_map/ppermute | solution.py:1157
  386.2 1.7 copy-start.19
  386.2 2.3 copy-start.3
  386.2 2.6 copy-start.4
  386.2 2.6 copy-start.5
  387.3 45.9 %collective-permute-start.7 = (bf16[256,2048]{1,0:T(8,128)(2,1)}, bf16[256,2048]{1,0:T(8,128)(2,1)}, u32[]{:S(2)}, u32[]{:S(2)}) collective-permute-start(bf16[256,2048]{1,0:T(8,128)(2,1)} %slice.270), channel_id=1, source_target_pairs={{0,2},{2,0},{4,6},{6,4},{8,10},{10,8},{12,14},{14,12},{16,18},{18,... | collective-permute-start | bytes 3145736 | tf_op jit(solution)/shard_map/ppermute | solution.py:1154
  395.5 5.9 %collective-permute-start.5 = (bf16[2,3,1280]{2,1,0:T(4,128)(2,1)S(1)}, bf16[2,3,1280]{2,1,0:T(4,128)(2,1)S(1)}, u32[]{:S(2)}, u32[]{:S(2)}) collective-permute-start(bf16[2,3,1280]{2,1,0:T(4,128)(2,1)S(1)} %slice.204), channel_id=1, source_target_pairs={{1,0},{3,2},{5,4},{7,6},{9,8},{11,10},{13,12},{15,14},{17,16},{19,... | collective-permute-start | bytes 46088 | tf_op jit(solution)/shard_map/ppermute | solution.py:1314
  397.9 3.6 copy-start.7
  397.9 19.0 %collective-permute-start.14 = (bf16[4,2,80,512]{3,2,0,1:T(8,128)(2,1)}, bf16[4,2,80,512]{3,2,0,1:T(8,128)(2,1)}, u32[]{:S(2)}, u32[]{:S(2)}) collective-permute-start(bf16[4,2,80,512]{3,2,0,1:T(8,128)(2,1)} %fusion.37), channel_id=1, source_target_pairs={{0,1},{1,0},{2,3},{3,2},{4,5},{5,4},{6,7},{7,6},{8,9},{9,8},{10,11... | collective-permute-start | bytes 1966088 | tf_op jit(solution)/shard_map/ppermute | solution.py:1157
  403.2 26.1 %collective-permute-start.10 = (bf16[256,1280]{1,0:T(8,128)(2,1)S(1)}, bf16[256,1280]{1,0:T(8,128)(2,1)S(1)}, u32[]{:S(2)}, u32[]{:S(2)}) collective-permute-start(bf16[256,1280]{1,0:T(8,128)(2,1)S(1)} %bitcast.94), channel_id=1, source_target_pairs={{0,1},{1,0},{2,3},{3,2},{4,5},{5,4},{6,7},{7,6},{8,9},{9,8},{10,11... | collective-permute-start | bytes 1966088 | tf_op jit(solution)/shard_map/ppermute | solution.py:1157
  410.6 25.9 %copy-start.16 = (f32[256,2048]{1,0:T(8,128)}, f32[256,2048]{1,0:T(8,128)S(1)}, u32[]{:S(2)}) copy-start(f32[256,2048]{1,0:T(8,128)S(1)} %fusion.62) | copy-start | bytes 6291460
  410.6 1.1 copy-start.23
  410.7 1.4 copy-start.28
  410.7 2.2 copy-start.41
  410.9 25.6 %collective-permute-start.9 = (f32[128,2048]{1,0:T(8,128)S(1)}, f32[128,2048]{1,0:T(8,128)S(1)}, u32[]{:S(2)}, u32[]{:S(2)}) collective-permute-start(f32[128,2048]{1,0:T(8,128)S(1)} %slice.281), channel_id=1, source_target_pairs={{0,2},{2,0},{4,6},{6,4},{8,10},{10,8},{12,14},{14,12},{16,18},{18,... | collective-permute-start | bytes 3145736 | tf_op jit(solution)/shard_map/ppermute | solution.py:1154
  416.9 1.6 copy-start.42
  418.4 13.9 %collective-permute-start.15 = (bf16[4,80,512]{2,1,0:T(8,128)(2,1)S(1)}, bf16[4,80,512]{2,1,0:T(8,128)(2,1)S(1)}, u32[]{:S(2)}, u32[]{:S(2)}) collective-permute-start(bf16[4,80,512]{2,1,0:T(8,128)(2,1)S(1)} %get-tuple-element.158), channel_id=1, source_target_pairs={{0,2},{2,0},{4,6},{6,4},{8,10},{10,8},{12,14},{14,12},{16,18},{18,... | collective-permute-start | bytes 983048 | tf_op jit(solution)/shard_map/ppermute | solution.py:1154
  422.8 10.4 %copy-start.20 = (bf16[512,2048]{1,0:T(8,128)(2,1)S(1)}, bf16[512,2048]{1,0:T(8,128)(2,1)}, u32[]{:S(2)}) copy-start(bf16[512,2048]{1,0:T(8,128)(2,1)} %copy-done.19) | copy-start | bytes 6291460
  433.2 3.3 copy-start.11
  435.0 19.4 %collective-permute-start.8 = (bf16[128,2048]{1,0:T(8,128)(2,1)S(1)}, bf16[128,2048]{1,0:T(8,128)(2,1)}, u32[]{:S(2)}, u32[]{:S(2)}) collective-permute-start(bf16[128,2048]{1,0:T(8,128)(2,1)S(1)} %slice.272), channel_id=1, source_target_pairs={{0,1},{1,0},{2,3},{3,2},{4,5},{5,4},{6,7},{7,6},{8,9},{9,8},{10,11... | collective-permute-start | bytes 1572872 | tf_op jit(solution)/shard_map/ppermute | solution.py:1157
  436.5 1.0 copy-start.17
  437.5 13.3 %copy-start.18 = (f32[128,2048]{1,0:T(8,128)S(1)}, f32[128,2048]{1,0:T(8,128)}, u32[]{:S(2)}) copy-start(f32[128,2048]{1,0:T(8,128)} %copy-done.17) | copy-start | bytes 3145732
  438.0 12.7 %collective-permute-start.16 = (f32[8,2,16,128]{3,2,0,1:T(8,128)S(1)}, f32[8,2,16,128]{3,2,0,1:T(8,128)S(1)}, u32[]{:S(2)}, u32[]{:S(2)}) collective-permute-start(f32[8,2,16,128]{3,2,0,1:T(8,128)S(1)} %bitcast.107), channel_id=1, source_target_pairs={{0,1},{1,0},{2,3},{3,2},{4,5},{5,4},{6,7},{7,6},{8,9},{9,8},{10,11... | collective-permute-start | bytes 393224 | tf_op jit(solution)/shard_map/ppermute | solution.py:1157
  450.7 3.0 collective-permute-start.17
  455.6 2.2 copy-start.9
  457.3 1.9 collective-permute-start.11
Sparse Core Ops, SparseCore 0:
  284.7 68.9 reduce-scatter.4
  356.0 141.7 reduce-scatter.2

commit v6 on v5

--- a/solution.py
+++ b/solution.py
@@ -258,21 +258,17 @@
         width = ref.shape[1] // 2
         return pl.ds(pl.multiple_of(core * width, 128), width)
 
-    results = ((g_out, s_out), (g_y, s_y), (g_x, s_x))
-    for part in (0, 1):
-        sums = [total(3 * part + i) for i in range(3)]
-
-        @pl.when(core == part)
-        def _():
-            for value, (ref, _) in zip(sums, results):
-                ref[:, cols(ref)] = value
-
-        @pl.when(core != part)
-        def _():
-            for value, (_, ref) in zip(sums, results):
-                ref[...] = value
-
-    final = [copies.send(src, ref.at[:, cols(ref)], sib) for ref, src in results]
+    final = []
+    for i, (ref, handed) in enumerate(((g_out, s_out), (g_y, s_y), (g_x, s_x))):
+        sums = [total(3 * part + i) for part in (0, 1)]
+        for part in (0, 1):
+
+            @pl.when(core == part)
+            def _():
+                ref[:, cols(ref)] = sums[part]
+                handed[...] = sums[1 - part]
+
+        final.append(copies.send(handed, ref.at[:, cols(ref)], sib))
     g_gates[...] = total(6)
     g_vec[...] = total(7)
     for copy in final:
@@ -592,11 +588,11 @@
 
 def front_kernel(n, *refs):
     (
-        wx, wy, wo, gs, wg, wu, wd, rows_in, cot, starts, spread_r, pick_r, spread_d, pick_d,
+        wx, wy, wo, gs, wg, wu, wd, rows_in, grad, lengths, resets, spread_r, pick_r, spread_d, pick_d,
         o_xy, o_out, o_gates, o_cp, o_gains, o_gu, o_d, o_cot, o_starts, o_ypre, o_u, o_a, o_h, o_hin, o_xb, o_before,
         o_x1, o_n2, o_n1t, o_ot, o_hidden, o_gate, o_up, o_pd,
         v_xy, v_out, v_gs, v_gates, v_rows, v_cot, v_starts, v_cp, v_gains, v_n1, v_n1t, v_xb, v_ypre, v_halo, v_u, v_a,
-        v_b, v_h, v_c, v_carry, v_o, v_osib, v_ot, v_part, v_theirs, v_psib, v_x1, v_n2, v_w, v_hidden, v_gu, v_pd,
+        v_b, v_h, v_c, v_carry, v_o, v_osib, v_ot, v_part, v_theirs, v_psib, v_x1, v_n2, v_w, v_hidden, v_gu, v_pd, v_wd,
         local_sem, send_sem, recv_sem, load_sem, store_sem, pd_sem,
     ) = refs
     dp, x = lax.axis_index("dp"), lax.axis_index("tp")
@@ -608,7 +604,6 @@
     prv = (chip_at((pos + n - 1) % n, n) * 2 + core, x)
     sib = (chip * 2 + other, x)
     over = (dp, 1 - x)
-    greet([nxt, prv, sib, over])
     copies = Copies(local_sem, send_sem, recv_sem)
     send, stay = copies.send, copies.stay
     tokens, width = rows_in.shape
@@ -616,6 +611,7 @@
     rh = rec // 2
     own, own_d = wo.shape[0], wx.shape[0]
     fh = wg.shape[1] // 2
+    own_f = wg.shape[0]
     kept, every = [], []
 
     def put(src, dst):
@@ -676,6 +672,7 @@
     mine = [stay(half_cols(src, core), slot) for src, slot in parts]
     mine.append(stay(half_cols(wo, core), v_out.at[heads_first(chip, core, n), core, x]))
     mine.append(stay(gs, v_gs.at[core, chip, x]))
+    greet([nxt, prv, sib, over])
     pair = [give(half_cols(src, other), slot, sib) for src, slot in parts]
     pair.append(give(half_cols(wo, other), v_out.at[heads_first(chip, other, n), core, x], sib))
 
@@ -684,13 +681,15 @@
     def rec_pieces(place):
         c = chip_at(place, n)
         at = heads_first(c, core, n)
+        rows = (own + PAD) // 2
         return [
-            (v_xy.at[c, core, x], True), (v_gs.at[core, c, x], True), (v_out.at[at, core, x], True),
-            (v_xy.at[c, other, x], False), (v_out.at[at, other, x], False),
+            (v_xy.at[c, core, x], True), (v_gs.at[core, c, x, pl.ds(0, rows)], True), (v_out.at[at, core, x], True),
+            (v_xy.at[c, other, x], False), (v_gs.at[core, c, x, pl.ds(rows, rows)], False),
+            (v_out.at[at, other, x], False),
         ]
 
     def rec_arrived(ref):
-        if len(ref.shape) == 2 and ref.shape[1] == width // 2:
+        if ref.shape[1] == width // 2:
             held.append(ref)
         else:
             crossed.append(give(ref, ref, over))
@@ -705,15 +704,25 @@
     rec_chain.start(True)
     land(pair)
     rec_chain.start(False)
-    parts = [
-        (wg, o_gu.at[chip, core, :, pl.ds(0, fh)]),
-        (wu, o_gu.at[chip, core, :, pl.ds(fh, fh)]),
-        (wd, o_d.at[pos, core]),
-    ]
+    parts = [(wg, o_gu.at[chip, core, :, pl.ds(0, fh)]), (wu, o_gu.at[chip, core, :, pl.ds(fh, fh)])]
     late = [give(half_cols(src, other), slot, sib) for src, slot in parts]
     plain = [stay(half_cols(src, core), slot) for src, slot in parts]
-    late += [give(rows_in, v_rows.at[1], sib), give(starts, v_starts.at[1], sib), give(cot, v_cot.at[2], sib)]
-    plain += [stay(rows_in, v_rows.at[0]), stay(starts, v_starts.at[0]), stay(cot, v_cot.at[0])]
+    late += [give(wd.at[pl.ds(pl.multiple_of(other * fh, 128), fh)], v_wd.at[1], sib), give(rows_in, v_rows.at[1], sib)]
+    plain += [stay(wd.at[pl.ds(pl.multiple_of(core * fh, 128), fh)], v_wd.at[0]), stay(rows_in, v_rows.at[0])]
+    cotangent = stay(grad, v_n2.at[0])
+
+    lane = lax.broadcasted_iota(jnp.int32, (1, tokens), 1) + x * tokens
+    begins = jnp.where((resets[...] > 0) | (lane == 0), 1.0, 0.0)
+    v_starts[0] = jnp.broadcast_to(begins, (tokens, tokens)).T
+    late.append(give(v_starts.at[0], v_starts.at[1], sib))
+    valid = lax.broadcasted_iota(jnp.int32, (tokens, 1), 0) + x * tokens < lengths[0]
+    valid = jnp.where(valid, 1.0, 0.0)
+    cotangent.wait()
+    size = width // n
+    for i in range(n):
+        from_chip = chip_at(i, n) * size
+        v_cot[0, :, i * size : (i + 1) * size] = (v_n2[0, :, from_chip : from_chip + size].astype(F32) * valid).astype(BF16)
+    late.append(give(v_cot.at[0], v_cot.at[2], sib))
     rec_chain.to_last()
     land(late)
     for copy in plain:
@@ -721,6 +730,11 @@
     gu.start(True)
     gu.start(False)
     rec_chain.finish()
+    for i in range(fh // 128):
+        at = pl.ds(i * 128, 128)
+        for which in (0, 1):
+            v_pd[which, 0:own_f, at] = v_wd[which, at, :].astype(F32).T.astype(BF16)
+    turned = [stay(v_pd.at[which, pl.ds(0, own_f)], o_d.at[pos, place]) for which, place in ((0, core), (1, other))]
     swap = [give(v_gs.at[core, :, x], v_gs.at[core, :, x], sib)]
     put(v_starts, o_starts)
     if half > 3:
@@ -856,6 +870,8 @@
     o_pair = give(v_o, v_osib, sib)
     put(v_h, o_h)
     gu.to_last()
+    for copy in turned:
+        copy.wait()
     down.start(True)
     down.start(False)
     o_pair.wait_recv()
@@ -1001,7 +1017,7 @@
             copy.wait_send()
 
 
-def front(n, wx, wy, wo, gs, wg, wu, wd, rows_in, cot, starts):
+def front(n, wx, wy, wo, gs, wg, wu, wd, rows_in, grad, lengths, resets):
     rec, f = wx.shape[1], wg.shape[1]
     own, own_d, rows_f = wo.shape[0], wx.shape[0], wg.shape[0]
     rh, fh = rec // 2, f // 2
@@ -1049,14 +1065,16 @@
         ((2, tokens, BLK), F32), (state, F32), (state, F32), ((2, 8, rh), F32), (state, BF16), (state, BF16),
         ((n, 2, 2, own, 2 * tokens), BF16), ((tokens, width // 2), F32), ((tokens, width // 2), F32),
         ((tokens, width // 2), F32), ((tokens, width), F32), ((4, tokens, width), BF16),
-        ((2, n, 2, rows_f, BLK), BF16), ((4 * tokens, fh), BF16), ((2, 4 * tokens, BLK), F32), ((2, BLK, fh), BF16),
+        ((2, n, 2, rows_f, BLK), BF16), ((4 * tokens, fh), BF16), ((2, 4 * tokens, BLK), F32), ((2, BLK, fh), BF16), ((2, fh, own_d * 2), BF16),
     ]
-    count = 9 + (5 * n - 5) + 2 * (2 * n - 2) + 5 * n + 2 + 12
+    count = 9 + (6 * n - 6) + 2 * (2 * n - 2) + 6 * n + 2 + 12
     dma = pltpu.SemaphoreType.DMA
     result = pl.pallas_call(
         functools.partial(front_kernel, n),
         out_shape=[jax.ShapeDtypeStruct(shape, kind) for shape, kind in outs.values()],
-        in_specs=[pl.BlockSpec(memory_space=pl.ANY)] * 10 + [pl.BlockSpec(memory_space=pltpu.VMEM)] * 4,
+        in_specs=[pl.BlockSpec(memory_space=pl.ANY)] * 9
+        + [pl.BlockSpec(memory_space=pltpu.SMEM)]
+        + [pl.BlockSpec(memory_space=pltpu.VMEM)] * 5,
         out_specs=[pl.BlockSpec(memory_space=pl.ANY)] * len(outs),
         scratch_shapes=[pltpu.VMEM(shape, kind) for shape, kind in scratch]
         + [dma((32,)), dma((count,)), dma((count,)), dma((2, 2)), dma((2, 2)), dma((2,))],
@@ -1064,7 +1082,7 @@
             collective_id=2, has_side_effects=True, vmem_limit_bytes=60 << 20
         ),
         name="front",
-    )(wx, wy, wo, gs, wg, wu, wd, rows_in, cot, starts, spread_r, pick_r, spread_d, pick_d)
+    )(wx, wy, wo, gs, wg, wu, wd, rows_in, grad, lengths, resets, spread_r, pick_r, spread_d, pick_d)
     return dict(zip(outs, result))
 
 
@@ -1198,13 +1216,14 @@
         return lax.dot_general(left, right, (((0,), (0,)), ((), ())), preferred_element_type=F32)
 
     fh = w_gate.shape[1] // 2
-    cot_ring = ring_order(cot.astype(BF16), 1)
     if own % 16 == 0 and own_d % 16 == 0:
         vectors = jnp.concatenate([conv_w, jnp.stack([conv_b, gate_a_b, gate_i_b, decay_param])], axis=0)
         vectors = jnp.pad(vectors, ((0, 0), (0, WIDE - own)))
         gains = jnp.pad(jnp.stack([norm_gain, mlp_gain]), ((0, PAD - taps - 6), (0, WIDE - own_d)))
         gs = jnp.concatenate([jnp.concatenate([gate_a_w, gate_i_w], axis=1), vectors, gains], axis=0)
-        got = front(n, w_x, w_y, w_out, gs, w_gate, w_up, w_down.T, rows_own, cot_ring, starts)
+        got = front(
+            n, w_x, w_y, w_out, gs, w_gate, w_up, w_down, rows_own, grad_out.reshape(tokens, width), lengths, resets
+        )
         w_xy, w_o = got["w_xy"].reshape(width, rec), got["w_o"].reshape(rec, width // 2)
         w_gu, w_d = got["w_gu"].reshape(width, 2 * fh), got["w_d"].reshape(width, fh)
         cot_all, n2_all = got["cot"].reshape(4 * tokens, width), got["n2"].reshape(4 * tokens, width)
@@ -1221,7 +1240,7 @@
         small = jnp.pad(small, (0, PAD * WIDE - small.shape[0])).reshape(PAD, WIDE)
         gs = jnp.concatenate([jnp.concatenate([gate_a_w, gate_i_w], axis=1), small], axis=0)
         w_xy, w_o, all_gs, w_gu, d_block, rows_two, cot_all, starts_two = gather_weights(
-            n, w_x, w_y, w_out, gs, w_gate, w_up, w_down.T, rows_own, cot_ring, starts
+            n, w_x, w_y, w_out, gs, w_gate, w_up, w_down.T, rows_own, ring_order(cot.astype(BF16), 1), starts
         )
         w_d = lax.all_gather(
             d_block.reshape(-1, d_block.shape[2]), "dp", axis=0, tiled=True, axis_index_groups=lanes

time: 585 us -> 581 us (level)
  no operation moved by 1% of the time
where the time goes in v6:
time: 581 us; the launch traced here: 574 us
  Pallas kernels  392 us (67%)
  matrix products  54.4 us (9%)
  other arithmetic  36.6 us (6%)
  waiting for transfers between devices  32.9 us (6%)
  local copies, waits for them, and re-layouts  26.7 us (5%)
  between operations  15.8 us (3%)
  starting transfers between devices  15.4 us (3%)
    pallas_call x1, Pallas kernels, front(): pl.pallas_call(functools.partial(front_kernel, n), out_shape=[jax.ShapeDt...  271 us
    pallas_call x1, Pallas kernels, scatter_sums(): pl.pallas_call(functools.partial(scatter_kernel, n), out_shape=[jax.Shape...  105 us
    ppermute x7, waiting for transfers between devices, across(): return lax.ppermute(v, 'tp', [(0, 1), (1, 0)])  30.1 us
    dot_general x4, matrix products, nt(): lax.dot_general(left, right, (((1,), (1,)), ((), ())), preferred_element_...  23.3 us
    dot_general x4, matrix products, nn(): return jnp.dot(left, right, preferred_element_type=F32)  21.1 us
    concatenate x1, other arithmetic, body(): jnp.concatenate([d_gu, d_gu_sib], axis=1)  12 us
  transfers between devices with their start and end apart: 20, of which 7 were waited for; matrix products, arithmetic and copies ran while one was open for 18% of the time, Pallas kernels for 20%

profile of v6, /device:TPU:0, one launch (start us, length us, event | category | flops | bytes accessed | tf_op | source)
XLA Modules:
  0.0 573.8 jit_solution(7797612859297553332)
XLA Ops:
  7.9 0.7 fusion.47
  8.6 0.7 concatenate.90
  9.3 1.4 fusion.41.refs_3_
  10.8 270.8 %front.1 = (bf16[8,2,2,64,2560]{4,3,2,1,0:T(8,128)(2,1)}, bf16[8,2,2,80,1024]{4,3,2,1,0:T(8,128)(2,1)}, bf16[1280,512]{1,0:T(8,128)(2,1)}, f32[16,1280]{1,0:T(8,...) custom-call(bf16[64,2560]{1,0:T(8,128)(2,1)} %refs_0_.1, ...), custom_call_target="tpu_custom_call" | custom-call | tf_op jit(solution)/shard_map/front/pallas_call | solution.py:1072
  281.8 1.6 copy-done.29
  283.4 9.7 %fusion.6 = (bf16[512,1536]{1,0:T(8,128)(2,1)S(1)}, bf16[512,1536]{1,0:T(8,128)(2,1)S(1)}) fusion(f32[512,1536]{1,0:T(8,128)S(1)} %copy-done.29, f32[512,1536]{1,0:T(8,128)} %get-tuple-element.81, bf16[512,2048]{1,0:T(8,128)(2,1)} %bitcast.117, bf16[2048,1536]{1,0:T(8,128)(2,1)} %bitcast.114), kind=kOutput, calls=%fused_computation.13 | convolution fusion | flops 3239313408 | bytes 17825792 | tf_op jit(solution)/shard_map/dot_general | solution.py:1145
  293.2 6.9 %convolution_convert_fusion.4 = bf16[512,2048]{1,0:T(8,128)(2,1)S(1)} fusion(bf16[2048,3072]{1,0:T(8,128)(2,1)S(1)} %bitcast.112, bf16[512,1536]{1,0:T(8,128)(2,1)S(1)} %get-tuple-element.147, bf16[512,1536]{1,0:T(8,128)(2,1)S(1)} %get-tuple-element.146), kind=kOutput, calls=%fused_computation.16 | convolution fusion | flops 6449790976 | bytes 17825792 | tf_op jit(solution)/shard_map/dot_general | solution.py:1141
  300.3 2.1 pad_maximum_fusion
  303.1 1.6 add_convert_fusion.1
  304.7 0.8 slice.214
  305.5 2.9 copy.52
  308.8 2.3 fusion.53
  311.6 12.0 %maximum_maximum_fusion = bf16[512,6144]{1,0:T(8,128)(2,1)S(1)} fusion(bf16[256,3072]{1,0:T(8,128)(2,1)S(1)} %get-tuple-element.149, bf16[256,3072]{1,0:T(8,128)(2,1)S(1)} %get-tuple-element.148, bf16[512,1536]{1,0:T(8,128)(2,1)S(1)} %copy-done.15, bf16[512,1536]{1,0:T(8,128)(2,1)S(1)} %copy-done.13), kind=kLoop, calls=%fused_computation.1 | loop fusion | flops 25165824 | bytes 12582912 | tf_op jit(solution)/shard_map/concatenate | solution.py:1313
  323.7 10.0 %convolution_convert_fusion = bf16[1024,6144]{1,0:T(8,128)(2,1)} fusion(bf16[512,1024]{0,1:T(8,128)(2,1)S(1)} %bitcast.95, bf16[512,6144]{1,0:T(8,128)(2,1)S(1)} %maximum_maximum_fusion), kind=kOutput, calls=%fused_computation | convolution fusion | flops 6448742400 | bytes 19922944 | tf_op jit(solution)/shard_map/dot_general | solution.py:1216
  333.8 1.2 copy-done.8
  335.1 1.6 collective-permute-start.1
  336.7 0.9 fusion.56
  337.6 11.6 %collective-permute-done.1 = bf16[128,2048]{1,0:T(8,128)(2,1)S(1)} collective-permute-done((bf16[128,2048]{1,0:T(8,128)(2,1)S(1)}, bf16[128,2048]{1,0:T(8,128)(2,1)S(1)}, u32[]{:S(2)}, u32[]{:S(2)}) %collective-permute-start.1) | collective-permute-done | bytes 524320 | tf_op jit(solution)/shard_map/ppermute | solution.py:1175
  349.6 1.4 fusion.52
  351.2 1.5 collective-permute-done.2
  352.7 4.1 fusion.51
  356.8 1.2 fusion.54
  358.2 0.9 slice.173.h_in
  359.1 0.8 slice.205
  360.3 1.2 maximum_convert_fusion.1
  361.6 0.8 pad_maximum_fusion.2
  362.4 1.5 collective-permute-start.13
  363.9 1.4 fusion.55
  365.5 1.1 copy-done
  367.5 5.3 adjoint.1
  372.8 1.3 collective-permute-start.4
  374.1 2.7 collective-permute-start.12
  376.8 6.4 %convolution_convert_fusion.5 = bf16[512,2048]{1,0:T(8,128)(2,1)S(1)} fusion(bf16[512,1536]{1,0:T(8,128)(2,1)S(1)} %copy-done.30, bf16[2048,1536]{1,0:T(8,128)(2,1)} %bitcast.115), kind=kOutput, calls=%fused_computation.17 | convolution fusion | flops 3222274048 | bytes 9961472 | tf_op jit(solution)/shard_map/dot_general | solution.py:1141
  383.3 1.1 slice.233
  384.9 0.7 copy-done.3
  385.9 6.6 %gates_back.1 = (bf16[2,128,1280]{2,1,0:T(8,128)(2,1)S(1)}, f32[1280,512]{1,0:T(8,128)S(1)}, f32[8,1280]{1,0:T(8,128)S(1)}) custom-call(f32[2,128,1280]{2,1,0:T(8,128)S(1)} %get-tuple-element.88.lam_ref, f32[2,128,1280]{2,1,0:T(8,128)S(1)} %get-tuple-element.89.c_ref, f32[2,1,1280]{2,1,0:T(1,128)S(1)} %collective-permute-done.4.inc, ...), custom_call_target="tpu_custom_call" | custom-call | flops 1200000000 | bytes 9000000 | tf_op jit(solution)/shard_map/gates_back/pallas_call | solution.py:562
  392.6 1.3 collective-permute-start.5
  393.9 0.9 fusion.34
  395.0 2.7 collective-permute-start.14
  397.7 0.8 collective-permute-done.5
  398.6 1.3 fusion.7
  400.7 1.2 pad_maximum_fusion.1
  401.9 5.8 %fusion.57 = f32[256,2048]{1,0:T(8,128)S(1)} fusion(bf16[256,2560]{1,0:T(8,128)(2,1)S(1)} %bitcast.94, bf16[2048,2560]{1,0:T(8,128)(2,1)} %bitcast.113), kind=kOutput, calls=%fused_computation.156 | convolution fusion | flops 2684354560 | bytes 13893632 | tf_op jit(solution)/shard_map/dot_general | solution.py:1141
  408.1 0.8 copy-done.23
  409.2 0.8 copy-done.31
  410.0 4.1 convolution_convert_fusion.1
  414.0 1.4 bitcast_add_fusion
  415.6 4.3 convolution_convert_fusion.2
  419.9 6.4 %collective-permute-done.10 = bf16[256,1280]{1,0:T(8,128)(2,1)S(1)} collective-permute-done((bf16[256,1280]{1,0:T(8,128)(2,1)S(1)}, bf16[256,1280]{1,0:T(8,128)(2,1)S(1)}, u32[]{:S(2)}, u32[]{:S(2)}) %collective-permute-start.10) | collective-permute-done | bytes 655392 | tf_op jit(solution)/shard_map/ppermute | solution.py:1175
  426.3 3.0 convolution_convert_fusion.3
  429.3 0.9 fusion.21.c_g
  430.3 1.7 add_convert_fusion
  432.0 1.6 collective-permute-start.8
  434.0 0.6 copy-done.17
  435.1 0.6 collective-permute-start.16
  435.6 12.1 %collective-permute-done.16 = f32[8,2,16,128]{3,2,0,1:T(8,128)S(1)} collective-permute-done((f32[8,2,16,128]{3,2,0,1:T(8,128)S(1)}, f32[8,2,16,128]{3,2,0,1:T(8,128)S(1)}, u32[]{:S(2)}, u32[]{:S(2)}) %collective-permute-start.16) | collective-permute-done | bytes 131104 | tf_op jit(solution)/shard_map/ppermute | solution.py:1175
  447.9 2.9 fusion.24
  450.8 0.6 bitcast_add_fusion.2.c_v
  451.4 1.2 convert_add_fusion
  452.8 1.3 constant_dynamic-slice_fusion.3
  454.8 0.9 fusion.35
  456.1 1.3 convert_bitcast_fusion
  457.4 104.9 %scatter_sums.1 = (f32[64,2560]{1,0:T(8,128)}, f32[64,2560]{1,0:T(8,128)}, f32[80,2048]{1,0:T(8,128)}, f32[80,512]{1,0:T(8,128)}, f32[16,128]{1,0:T(8,128)}) custom-call(bf16[8,2,64,1280]{3,2,1,0:T(8,128)(2,1)} %bitcast.90, bf16[8,2,64,1280]{3,2,1,0:T(8,128)(2,1)} %bitcast.89, bf16[8,2,80,1024]{3,2,1,0:T(8,128)(2,1)} %bitcast.88, ...), custom_call_target="tpu_custom_call" | custom-call | tf_op jit(solution)/shard_map/scatter_sums/pallas_call | solution.py:287
  562.4 4.4 finish.1
  (146 shorter events, 9.1 us)
Async XLA Ops:
  7.2 445.6 %reduce-scatter.5.cloned.1.call-start = ((), (), s32[]{:S(2)}) async-start(), calls=%async_computation.3 | async-start | bytes 7077888 | tf_op jit(solution)/shard_map/reduce_scatter | solution.py:1207
  281.5 1.9 copy-start.29
  281.6 280.8 %reduce-scatter.3.cloned.1.call-start = ((), (), s32[]{:S(2)}) async-start(), calls=%async_computation.2 | async-start | bytes 14155776 | tf_op jit(solution)/shard_map/reduce_scatter | solution.py:1207
  283.4 9.8 %copy-start.28 = (bf16[8,2,128,3072]{3,2,1,0:T(8,128)(2,1)S(1)}, bf16[8,2,128,3072]{3,2,1,0:T(8,128)(2,1)}, u32[]{:S(2)}) copy-start(bf16[8,2,128,3072]{3,2,1,0:T(8,128)(2,1)} %get-tuple-element.83) | copy-start | bytes 37748740
  293.2 7.2 %copy-start.12 = (bf16[512,1536]{1,0:T(8,128)(2,1)}, bf16[512,1536]{1,0:T(8,128)(2,1)S(1)}, u32[]{:S(2)}) copy-start(bf16[512,1536]{1,0:T(8,128)(2,1)S(1)} %get-tuple-element.146) | copy-start | bytes 4718596
  293.2 7.2 %copy-start.14 = (bf16[512,1536]{1,0:T(8,128)(2,1)}, bf16[512,1536]{1,0:T(8,128)(2,1)S(1)}, u32[]{:S(2)}) copy-start(bf16[512,1536]{1,0:T(8,128)(2,1)S(1)} %get-tuple-element.147) | copy-start | bytes 4718596
  300.2 2.9 collective-permute-start
  302.4 6.3 %collective-permute-start.6 = (bf16[512,3072]{1,0:T(8,128)(2,1)}, bf16[512,3072]{1,0:T(8,128)(2,1)}, u32[]{:S(2)}, u32[]{:S(2)}) collective-permute-start(bf16[512,3072]{1,0:T(8,128)(2,1)} %pad_maximum_fusion), channel_id=1, source_target_pairs={{0,2},{2,0},{4,6},{6,4},{8,10},{10,8},{12,14},{14,12},{16,18},{18,... | collective-permute-start | bytes 9437192 | tf_op jit(solution)/shard_map/ppermute | solution.py:1172
  308.7 2.4 copy-start.13
  308.7 2.9 copy-start.15
  333.7 1.2 copy-start.8
  333.7 1.4 copy-start.25
  333.8 15.8 %copy-start.21 = (bf16[1,128,2048]{2,1,0:T(8,128)(2,1)S(1)}, bf16[1,128,2048]{2,1,0:T(8,128)(2,1)}, u32[]{:S(2)}) copy-start(bf16[1,128,2048]{2,1,0:T(8,128)(2,1)} %param.24) | copy-start | bytes 1572868
  335.1 14.1 %collective-permute-start.1 = (bf16[128,2048]{1,0:T(8,128)(2,1)S(1)}, bf16[128,2048]{1,0:T(8,128)(2,1)S(1)}, u32[]{:S(2)}, u32[]{:S(2)}) collective-permute-start(bf16[128,2048]{1,0:T(8,128)(2,1)S(1)} %copy-done.25), channel_id=1, source_target_pairs={{0,1},{1,0},{2,3},{3,2},{4,5},{5,4},{6,7},{7,6},{8,9},{9,8},{10,11... | collective-permute-start | bytes 1572872 | tf_op jit(solution)/shard_map/ppermute | solution.py:1175
  351.1 10.5 %copy-start.22 = (bf16[128,1024]{1,0:T(8,128)(2,1)}, bf16[128,1024]{1,0:T(8,128)(2,1)S(1)}, u32[]{:S(2)}) copy-start(bf16[128,1024]{1,0:T(8,128)(2,1)S(1)} %get-tuple-element.159) | copy-start | bytes 786436
  351.1 1.6 collective-permute-start.2
  352.7 8.9 %copy-start.26 = (bf16[128,1024]{1,0:T(8,128)(2,1)}, bf16[128,1024]{1,0:T(8,128)(2,1)S(1)}, u32[]{:S(2)}) copy-start(bf16[128,1024]{1,0:T(8,128)(2,1)S(1)} %collective-permute-done.2) | copy-start | bytes 786436
  356.8 3.1 copy-start.6
  356.8 3.2 copy-start.10
  356.8 3.4 copy-start.24
  358.1 5.9 %collective-permute-start.3 = (f32[2,128,1280]{2,1,0:T(8,128)}, f32[2,128,1280]{2,1,0:T(8,128)}, u32[]{:S(2)}, u32[]{:S(2)}) collective-permute-start(f32[2,128,1280]{2,1,0:T(8,128)} %bitcast.15), channel_id=1, source_target_pairs={{0,2},{2,0},{4,6},{6,4},{8,10},{10,8},{12,14},{14,12},{16,18},{18,... | collective-permute-start | bytes 3932168 | tf_op jit(solution)/shard_map/ppermute | solution.py:1172
  362.4 45.6 %collective-permute-start.13 = (bf16[256,1024]{1,0:T(8,128)(2,1)}, bf16[256,1024]{1,0:T(8,128)(2,1)}, u32[]{:S(2)}, u32[]{:S(2)}) collective-permute-start(bf16[256,1024]{1,0:T(8,128)(2,1)} %pad_maximum_fusion.2), channel_id=1, source_target_pairs={{0,1},{1,0},{2,3},{3,2},{4,5},{5,4},{6,7},{7,6},{8,9},{9,8},{10,11... | collective-permute-start | bytes 1572872 | tf_op jit(solution)/shard_map/ppermute | solution.py:1175
  365.3 1.3 copy-start
  365.3 1.7 copy-start.1
  365.3 2.2 copy-start.2
  367.5 9.3 %copy-start.30 = (bf16[512,1536]{1,0:T(8,128)(2,1)S(1)}, bf16[512,1536]{1,0:T(8,128)(2,1)}, u32[]{:S(2)}) copy-start(bf16[512,1536]{1,0:T(8,128)(2,1)} %get-tuple-element.100) | copy-start | bytes 4718596
  372.8 11.6 %collective-permute-start.4 = (f32[2,1,1280]{2,1,0:T(1,128)S(1)}, f32[2,1,1280]{2,1,0:T(1,128)S(1)}, u32[]{:S(2)}, u32[]{:S(2)}) collective-permute-start(f32[2,1,1280]{2,1,0:T(1,128)S(1)} %slice_multiply_fusion.7), channel_id=1, source_target_pairs={{1,0},{3,2},{5,4},{7,6},{9,8},{11,10},{13,12},{15,14},{17,16},{19,... | collective-permute-start | bytes 30728 | tf_op jit(solution)/shard_map/ppermute | solution.py:1331
  374.1 41.5 %collective-permute-start.12 = (bf16[256,1280]{1,0:T(8,128)(2,1)}, bf16[256,1280]{1,0:T(8,128)(2,1)}, u32[]{:S(2)}, u32[]{:S(2)}) collective-permute-start(bf16[256,1280]{1,0:T(8,128)(2,1)} %bitcast.31), channel_id=1, source_target_pairs={{0,1},{1,0},{2,3},{3,2},{4,5},{5,4},{6,7},{7,6},{8,9},{9,8},{10,11... | collective-permute-start | bytes 1966088 | tf_op jit(solution)/shard_map/ppermute | solution.py:1175
  383.3 1.7 copy-start.19
  383.3 2.3 copy-start.3
  383.3 2.6 copy-start.4
  383.3 2.6 copy-start.5
  384.4 45.9 %collective-permute-start.7 = (bf16[256,2048]{1,0:T(8,128)(2,1)}, bf16[256,2048]{1,0:T(8,128)(2,1)}, u32[]{:S(2)}, u32[]{:S(2)}) collective-permute-start(bf16[256,2048]{1,0:T(8,128)(2,1)} %slice.233), channel_id=1, source_target_pairs={{0,2},{2,0},{4,6},{6,4},{8,10},{10,8},{12,14},{14,12},{16,18},{18,... | collective-permute-start | bytes 3145736 | tf_op jit(solution)/shard_map/ppermute | solution.py:1172
  392.6 5.9 %collective-permute-start.5 = (bf16[2,3,1280]{2,1,0:T(4,128)(2,1)S(1)}, bf16[2,3,1280]{2,1,0:T(4,128)(2,1)S(1)}, u32[]{:S(2)}, u32[]{:S(2)}) collective-permute-start(bf16[2,3,1280]{2,1,0:T(4,128)(2,1)S(1)} %slice.174), channel_id=1, source_target_pairs={{1,0},{3,2},{5,4},{7,6},{9,8},{11,10},{13,12},{15,14},{17,16},{19,... | collective-permute-start | bytes 46088 | tf_op jit(solution)/shard_map/ppermute | solution.py:1333
  394.9 3.6 copy-start.7
  395.0 19.1 %collective-permute-start.14 = (bf16[4,2,80,512]{3,2,0,1:T(8,128)(2,1)}, bf16[4,2,80,512]{3,2,0,1:T(8,128)(2,1)}, u32[]{:S(2)}, u32[]{:S(2)}) collective-permute-start(bf16[4,2,80,512]{3,2,0,1:T(8,128)(2,1)} %fusion.34), channel_id=1, source_target_pairs={{0,1},{1,0},{2,3},{3,2},{4,5},{5,4},{6,7},{7,6},{8,9},{9,8},{10,11... | collective-permute-start | bytes 1966088 | tf_op jit(solution)/shard_map/ppermute | solution.py:1175
  400.3 26.1 %collective-permute-start.10 = (bf16[256,1280]{1,0:T(8,128)(2,1)S(1)}, bf16[256,1280]{1,0:T(8,128)(2,1)S(1)}, u32[]{:S(2)}, u32[]{:S(2)}) collective-permute-start(bf16[256,1280]{1,0:T(8,128)(2,1)S(1)} %bitcast.86), channel_id=1, source_target_pairs={{0,1},{1,0},{2,3},{3,2},{4,5},{5,4},{6,7},{7,6},{8,9},{9,8},{10,11... | collective-permute-start | bytes 1966088 | tf_op jit(solution)/shard_map/ppermute | solution.py:1175
  407.7 25.9 %copy-start.16 = (f32[256,2048]{1,0:T(8,128)}, f32[256,2048]{1,0:T(8,128)S(1)}, u32[]{:S(2)}) copy-start(f32[256,2048]{1,0:T(8,128)S(1)} %fusion.57) | copy-start | bytes 6291460
  407.7 1.1 copy-start.23
  407.8 1.4 copy-start.27
  407.8 2.2 copy-start.31
  408.0 25.6 %collective-permute-start.9 = (f32[128,2048]{1,0:T(8,128)S(1)}, f32[128,2048]{1,0:T(8,128)S(1)}, u32[]{:S(2)}, u32[]{:S(2)}) collective-permute-start(f32[128,2048]{1,0:T(8,128)S(1)} %slice.244), channel_id=1, source_target_pairs={{0,2},{2,0},{4,6},{6,4},{8,10},{10,8},{12,14},{14,12},{16,18},{18,... | collective-permute-start | bytes 3145736 | tf_op jit(solution)/shard_map/ppermute | solution.py:1172
  414.0 1.6 copy-start.32
  415.5 13.8 %collective-permute-start.15 = (bf16[4,80,512]{2,1,0:T(8,128)(2,1)S(1)}, bf16[4,80,512]{2,1,0:T(8,128)(2,1)S(1)}, u32[]{:S(2)}, u32[]{:S(2)}) collective-permute-start(bf16[4,80,512]{2,1,0:T(8,128)(2,1)S(1)} %get-tuple-element.158), channel_id=1, source_target_pairs={{0,2},{2,0},{4,6},{6,4},{8,10},{10,8},{12,14},{14,12},{16,18},{18,... | collective-permute-start | bytes 983048 | tf_op jit(solution)/shard_map/ppermute | solution.py:1172
  419.9 10.4 %copy-start.20 = (bf16[512,2048]{1,0:T(8,128)(2,1)S(1)}, bf16[512,2048]{1,0:T(8,128)(2,1)}, u32[]{:S(2)}) copy-start(bf16[512,2048]{1,0:T(8,128)(2,1)} %copy-done.19) | copy-start | bytes 6291460
  430.3 3.4 copy-start.11
  432.0 19.4 %collective-permute-start.8 = (bf16[128,2048]{1,0:T(8,128)(2,1)S(1)}, bf16[128,2048]{1,0:T(8,128)(2,1)}, u32[]{:S(2)}, u32[]{:S(2)}) collective-permute-start(bf16[128,2048]{1,0:T(8,128)(2,1)S(1)} %slice.235), channel_id=1, source_target_pairs={{0,1},{1,0},{2,3},{3,2},{4,5},{5,4},{6,7},{7,6},{8,9},{9,8},{10,11... | collective-permute-start | bytes 1572872 | tf_op jit(solution)/shard_map/ppermute | solution.py:1175
  433.6 1.0 copy-start.17
  434.6 13.3 %copy-start.18 = (f32[128,2048]{1,0:T(8,128)S(1)}, f32[128,2048]{1,0:T(8,128)}, u32[]{:S(2)}) copy-start(f32[128,2048]{1,0:T(8,128)} %copy-done.17) | copy-start | bytes 3145732
  435.1 12.7 %collective-permute-start.16 = (f32[8,2,16,128]{3,2,0,1:T(8,128)S(1)}, f32[8,2,16,128]{3,2,0,1:T(8,128)S(1)}, u32[]{:S(2)}, u32[]{:S(2)}) collective-permute-start(f32[8,2,16,128]{3,2,0,1:T(8,128)S(1)} %bitcast.100), channel_id=1, source_target_pairs={{0,1},{1,0},{2,3},{3,2},{4,5},{5,4},{6,7},{7,6},{8,9},{9,8},{10,11... | collective-permute-start | bytes 393224 | tf_op jit(solution)/shard_map/ppermute | solution.py:1175
  447.8 3.0 collective-permute-start.17
  452.6 2.2 copy-start.9
  454.3 1.9 collective-permute-start.11
Sparse Core Ops, SparseCore 0:
  281.7 68.5 reduce-scatter.4
  352.6 142.0 reduce-scatter.2

commit v7 on v6

--- a/solution.py
+++ b/solution.py
@@ -1086,6 +1086,200 @@
     return dict(zip(outs, result))
 
 
+def ff_back_kernel(n, *refs):
+    (
+        part_d, cot, w_d, gate, up, n2, w_gu,
+        g_d, d_n2, o_part,
+        v_pd, v_cot, v_n2, v_wd, v_gate, v_up, v_dgu, v_sib, v_wgu, v_dn2, v_pair, v_plane, v_part, r_d, handed,
+        local_sem, send_sem, recv_sem, down_sem, up_sem, part_sem,
+    ) = refs
+    dp, x = lax.axis_index("dp"), lax.axis_index("tp")
+    chip, core = dp // 2, dp % 2
+    pos = place_of(chip, n)
+    half = n // 2
+    nxt = (chip_at((pos + 1) % n, n) * 2 + core, x)
+    prv = (chip_at((pos + n - 1) % n, n) * 2 + core, x)
+    sib = (dp + 1 - 2 * core, x)
+    over = (dp, 1 - x)
+    copies = Copies(local_sem, send_sem, recv_sem)
+    send, stay = copies.send, copies.stay
+    rows, fh = v_pd.shape[2], v_pd.shape[3]
+    count, width = v_cot.shape
+    tokens = count // 4
+    products = stay(part_d, v_pd)
+    rest = [stay(cot, v_cot), stay(n2, v_n2)]
+    greet([nxt, prv, sib, over])
+
+    chains = [(part, way) for part in (0, 1) for way in (0, 1)]
+    coming, sent, left = {}, [], {}
+
+    def forward():
+        for part, way in chains:
+            first = half if way == part else half - 1
+            k = left.get((part, way), first)
+            if k == 0:
+                continue
+            device, sign = ((nxt, 1), (prv, n - 1))[way]
+            source = (part_d if k == first else v_pd).at[(pos + sign * k) % n, part]
+            if k < first:
+                coming[part, way].wait_recv()
+                got = r_d.at[part, way, k]
+                got[...] = (got[...].astype(F32) + source[...].astype(F32)).astype(BF16)
+                source = got
+            copy = send(source, r_d.at[part, way, k - 1], device)
+            coming[part, way] = copy
+            sent.append(copy)
+            left[part, way] = k - 1
+
+    forward()
+
+    def down_loads(t, slot):
+        at = pl.ds(pl.multiple_of(t * BLK, BLK), BLK)
+        pairs = ((w_d, v_wd), (gate, v_gate), (up, v_up))
+        return [
+            pltpu.make_async_copy(src.at[:, at], dst.at[slot], down_sem.at[slot, i])
+            for i, (src, dst) in enumerate(pairs)
+        ]
+
+    steps = fh // BLK
+    for copy in down_loads(0, 0):
+        copy.start()
+    for copy in rest + [products]:
+        copy.wait()
+
+    def cotangent_tile(t, _):
+        slot = t % 2
+        for copy in down_loads(t, slot):
+            copy.wait()
+
+        @pl.when(t + 1 < steps)
+        def _():
+            for copy in down_loads(t + 1, 1 - slot):
+                copy.start()
+
+        d_hidden = jnp.dot(v_cot[...], v_wd[slot], preferred_element_type=F32)
+        act, slope = gelu_parts(v_gate[slot])
+        v_dgu[:, pl.ds(pl.multiple_of(t * BLK, BLK), BLK)] = (d_hidden * v_up[slot] * slope).astype(BF16)
+        v_dgu[:, pl.ds(pl.multiple_of(fh + t * BLK, BLK), BLK)] = (d_hidden * act).astype(BF16)
+        return 0
+
+    def up_loads(t, slot):
+        at = pl.ds(pl.multiple_of(t * BLK, BLK), BLK)
+        return pltpu.make_async_copy(w_gu.at[at], v_wgu.at[slot], up_sem.at[slot])
+
+    up_loads(0, 0).start()
+    lax.fori_loop(0, steps, cotangent_tile, 0)
+    swap = [
+        send(v_dgu.at[pl.ds(0, 2 * tokens)], v_sib.at[pl.ds(2 * tokens, 2 * tokens)], sib),
+        send(v_dgu.at[pl.ds(2 * tokens, 2 * tokens)], v_sib.at[pl.ds(0, 2 * tokens)], sib),
+    ]
+
+    def norm_tile(t, _):
+        slot = t % 2
+        up_loads(t, slot).wait()
+
+        @pl.when(t + 1 < width // BLK)
+        def _():
+            up_loads(t + 1, 1 - slot).start()
+
+        product = nt(v_dgu[...], v_wgu[slot]).astype(BF16)
+        v_dn2[:, :, pl.ds(pl.multiple_of(t * BLK, BLK), BLK)] = product.reshape(4, tokens, BLK)
+        return 0
+
+    lax.fori_loop(0, width // BLK // 2, norm_tile, 0)
+    forward()
+    lax.fori_loop(width // BLK // 2, width // BLK, norm_tile, 0)
+    pair = send(v_dn2.at[pl.ds(2, 2)], v_pair, sib)
+    for copy in swap:
+        copy.wait_recv()
+
+    def part_store(i, slot):
+        return pltpu.make_async_copy(
+            v_part.at[slot], o_part.at[pl.ds(pl.multiple_of(i * rows, 8), rows)], part_sem.at[slot]
+        )
+
+    def part_tile(i, _):
+        slot = i % 2
+
+        @pl.when(i >= 2)
+        def _():
+            part_store(i - 2, slot).wait()
+
+        at = pl.ds(pl.multiple_of(chip_at(i, n) * 2 * rows + core * rows, 128), rows)
+        columns = v_n2[:, at]
+        for j, ref in enumerate((v_dgu, v_sib)):
+            product = lax.dot_general(columns, ref[...], (((0,), (0,)), ((), ())), preferred_element_type=F32)
+            v_part[slot, :, 2 * fh * j : 2 * fh * (j + 1)] = product.astype(BF16)
+        part_store(i, slot).start()
+        return 0
+
+    lax.fori_loop(0, n // 4, part_tile, 0)
+    pair.wait_recv()
+    for i in (1, 0):
+        v_pair[i] = (v_dn2[i].astype(F32) + v_pair[i].astype(F32)).astype(BF16)
+        if i == 1:
+            plane = send(v_pair.at[1], v_plane, over)
+    lax.fori_loop(n // 4, n // 2, part_tile, 0)
+    forward()
+    lax.fori_loop(n // 2, n, part_tile, 0)
+    plane.wait_recv()
+    d_n2[...] = v_pair[0].astype(F32) + v_plane[...].astype(F32)
+    while any(left.values()):
+        forward()
+    for i in (n - 2, n - 1):
+        part_store(i, i % 2).wait()
+
+    at = pl.ds(pl.multiple_of(core * fh, 128), fh)
+    totals = []
+    for part in (0, 1):
+        for way in (0, 1):
+            coming[part, way].wait_recv()
+        totals.append(v_pd[pos, part].astype(F32) + r_d[part, 0, 0].astype(F32) + r_d[part, 1, 0].astype(F32))
+    for part in (0, 1):
+
+        @pl.when(core == part)
+        def _():
+            g_d[:, at] = totals[part]
+            handed[...] = totals[1 - part]
+
+    last = send(handed, g_d.at[:, at], sib)
+    last.wait_recv()
+    for copy in sent + swap + [pair, plane, last]:
+        copy.wait_send()
+
+
+def ff_back(n, part_d, cot, w_d, gate, up, n2, w_gu):
+    width, fh = part_d.shape
+    count = cot.shape[0]
+    tokens = count // 4
+    rows = width // (2 * n)
+    half = n // 2
+    dma = pltpu.SemaphoreType.DMA
+    scratch = [
+        ((n, 2, rows, fh), BF16), ((count, width), BF16), ((count, width), BF16), ((2, width, BLK), BF16),
+        ((2, count, BLK), F32), ((2, count, BLK), F32), ((count, 2 * fh), BF16), ((count, 2 * fh), BF16),
+        ((2, BLK, 2 * fh), BF16), ((4, tokens, width), BF16), ((2, tokens, width), BF16), ((tokens, width), BF16),
+        ((2, rows, 4 * fh), BF16), ((2, 2, half, rows, fh), BF16), ((rows, fh), F32),
+    ]
+    copies = 2 * (2 * half - 1) + 5
+    return pl.pallas_call(
+        functools.partial(ff_back_kernel, n),
+        out_shape=[
+            jax.ShapeDtypeStruct((rows, 2 * fh), F32),
+            jax.ShapeDtypeStruct((tokens, width), F32),
+            jax.ShapeDtypeStruct((n * rows, 4 * fh), BF16),
+        ],
+        in_specs=[pl.BlockSpec(memory_space=pl.ANY)] * 7,
+        out_specs=[pl.BlockSpec(memory_space=pltpu.VMEM)] * 2 + [pl.BlockSpec(memory_space=pl.ANY)],
+        scratch_shapes=[pltpu.VMEM(shape, kind) for shape, kind in scratch]
+        + [dma((3,)), dma((copies,)), dma((copies,)), dma((2, 3)), dma((2,)), dma((2,))],
+        compiler_params=pltpu.CompilerParams(
+            collective_id=3, has_side_effects=True, vmem_limit_bytes=60 << 20
+        ),
+        name="ff_back",
+    )(part_d.reshape(n, 2, rows, fh), cot, w_d, gate, up, n2, w_gu)
+
+
 def finish_kernel(
     sums, x_sum, y_sum, out_sum, gates, vec,
     gate_ref, up_ref, x_ref, y_ref, out_ref, a_ref, i_ref, taps_ref, *lines,
@@ -1295,22 +1489,26 @@
         hidden = (act * upv).astype(BF16)
 
         part_d = tn(cot_all, hidden).astype(BF16)
-    sum_d = lane_sum(part_d)
-    act, slope = gelu_parts(gate)
-    d_hidden = nn(after(cot_all, part_d), w_d)
-    d_gu = jnp.concatenate([(d_hidden * upv * slope).astype(BF16), (d_hidden * act).astype(BF16)], axis=1)
-
     def pair_sum(partial):
         return (partial[: 2 * tokens].astype(F32) + sibling(partial[2 * tokens :]).astype(F32)).astype(BF16)
 
-    d_n2_pair = pair_sum(nt(d_gu, w_gu).astype(BF16))
-    d_n2_send = d_n2_pair[tokens:]
-    d_n2 = d_n2_pair[:tokens].astype(F32) + across(d_n2_send).astype(F32)
-    n2_rows = ring_order(after(n2_all, d_n2_send), 1).reshape(4 * tokens, n, 2, width // dp_size)
-    n2_rows = plane(n2_rows, core).reshape(4 * tokens, width // 2)
-    d_gu_sib = sibling(d_gu)
-    d_gu_sib = jnp.concatenate([d_gu_sib[2 * tokens :], d_gu_sib[: 2 * tokens]], axis=0)
-    part_gu = tn(n2_rows, after(jnp.concatenate([d_gu, d_gu_sib], axis=1), d_n2_send)).astype(BF16)
+    if own % 16 == 0 and own_d % 16 == 0:
+        grad_d, d_n2, part_gu = ff_back(n, part_d, cot_all, w_d, gate, upv, n2_all, w_gu)
+    else:
+        sum_d = lane_sum(part_d)
+        act, slope = gelu_parts(gate)
+        d_hidden = nn(after(cot_all, part_d), w_d)
+        d_gu = jnp.concatenate([(d_hidden * upv * slope).astype(BF16), (d_hidden * act).astype(BF16)], axis=1)
+
+        d_n2_pair = pair_sum(nt(d_gu, w_gu).astype(BF16))
+        d_n2_send = d_n2_pair[tokens:]
+        d_n2 = d_n2_pair[:tokens].astype(F32) + across(d_n2_send).astype(F32)
+        n2_rows = ring_order(after(n2_all, d_n2_send), 1).reshape(4 * tokens, n, 2, width // dp_size)
+        n2_rows = plane(n2_rows, core).reshape(4 * tokens, width // 2)
+        d_gu_sib = sibling(d_gu)
+        d_gu_sib = jnp.concatenate([d_gu_sib[2 * tokens :], d_gu_sib[: 2 * tokens]], axis=0)
+        part_gu = tn(n2_rows, after(jnp.concatenate([d_gu, d_gu_sib], axis=1), d_n2_send)).astype(BF16)
+        grad_d = None
     sum_gu = lane_sum(part_gu)
     ff_pair = pair_sum(nt(after(hidden, part_gu), w_d).astype(BF16))
     ff_out = ff_pair[:tokens].astype(F32) + across(ff_pair[tokens:]).astype(F32)
@@ -1388,7 +1586,7 @@
     def halves(pair):
         return by_core(pair[0], pair[1], 1).astype(F32)
 
-    grad_down = halves(whole(sum_d)).T
+    grad_down = (halves(whole(sum_d)) if grad_d is None else grad_d).T
     x_sum, y_sum, out_sum, sum_gates, sum_vec = scatter_sums(
         n, after(c_x, grad_down, result, grad_x), c_y, c_out, g_lane.astype(BF16), vec
     )

time: 581 us -> 571 us (0.983)
  Pallas kernels: 392 us -> 447 us
  matrix products: 54.4 us -> 26.7 us
  other arithmetic: 36.6 us -> 19.5 us
  local copies, waits for them, and re-layouts: 26.7 us -> 18.2 us
    pallas_call x0 -> x1, Pallas kernels: none -> 66.9 us  [ff_back(): pl.pallas_call(functools.partial(ff_back_kernel, n), out_shape=[jax.Shape...]
    concatenate x2 -> x0, other arithmetic: 14.1 us -> none  [the longest x1 12 us: body(): jnp.concatenate([d_gu, d_gu_sib], axis=1)]
    pallas_call x1, Pallas kernels: 105 us -> 93.3 us  [scatter_sums(): pl.pallas_call(functools.partial(scatter_kernel, n), out_shape=[jax.Shape...]
    dot_general x1 -> x0, matrix products: 10 us -> none  [tn(): lax.dot_general(left, right, (((0,), (0,)), ((), ())), preferred_element_...]
    dot_general x4 -> x3, matrix products: 21.1 us -> 11.4 us  [nn(): return jnp.dot(left, right, preferred_element_type=F32)]
    dot_general x4 -> x3, matrix products: 23.3 us -> 15.3 us  [nt(): lax.dot_general(left, right, (((1,), (1,)), ((), ())), preferred_element_...]
    ppermute x7 -> x6, waiting for transfers between devices: 30.1 us -> 24.7 us  [across(): return lax.ppermute(v, 'tp', [(0, 1), (1, 0)])]
  transfers between devices with their start and end apart: 20 -> 15, of which waited for: 7 -> 5; matrix products, arithmetic and copies ran while one was open for 18% -> 9% of each run, Pallas kernels for 20% -> 18%
where the time goes in v7:
time: 571 us; the launch traced here: 569 us
  Pallas kernels  447 us (78%)
  waiting for transfers between devices  29 us (5%)
  matrix products  26.7 us (5%)
  other arithmetic  19.5 us (3%)
  local copies, waits for them, and re-layouts  18.2 us (3%)
  between operations  15.4 us (3%)
  starting transfers between devices  12.9 us (2%)
    pallas_call x1, Pallas kernels, front(): pl.pallas_call(functools.partial(front_kernel, n), out_shape=[jax.ShapeDt...  271 us
    pallas_call x1, Pallas kernels, scatter_sums(): pl.pallas_call(functools.partial(scatter_kernel, n), out_shape=[jax.Shape...  93.3 us
    pallas_call x1, Pallas kernels, ff_back(): pl.pallas_call(functools.partial(ff_back_kernel, n), out_shape=[jax.Shape...  66.9 us
    ppermute x6, waiting for transfers between devices, across(): return lax.ppermute(v, 'tp', [(0, 1), (1, 0)])  24.7 us
    dot_general x3, matrix products, nt(): lax.dot_general(left, right, (((1,), (1,)), ((), ())), preferred_element_...  15.3 us
  transfers between devices with their start and end apart: 15, of which 5 were waited for; matrix products, arithmetic and copies ran while one was open for 9% of the time, Pallas kernels for 18%

profile of v7, /device:TPU:0, one launch (start us, length us, event | category | flops | bytes accessed | tf_op | source)
XLA Modules:
  0.0 568.9 jit_solution(10257742491538507277)
XLA Ops:
  7.9 0.7 fusion.39
  8.6 0.7 concatenate.70
  9.3 1.4 fusion.33.refs_3_
  10.8 270.8 %front.1 = (bf16[8,2,2,64,2560]{4,3,2,1,0:T(8,128)(2,1)}, bf16[8,2,2,80,1024]{4,3,2,1,0:T(8,128)(2,1)}, bf16[1280,512]{1,0:T(8,128)(2,1)}, f32[16,1280]{1,0:T(8,...) custom-call(bf16[64,2560]{1,0:T(8,128)(2,1)} %refs_0_.1, ...), custom_call_target="tpu_custom_call" | custom-call | tf_op jit(solution)/shard_map/front/pallas_call | solution.py:1072
  281.5 66.9 %ff_back.1 = (f32[128,3072]{1,0:T(8,128)}, f32[128,2048]{1,0:T(8,128)}, bf16[1024,6144]{1,0:T(8,128)(2,1)}) custom-call(bf16[8,2,128,1536]{3,2,1,0:T(8,128)(2,1)} %bitcast.78, bf16[512,2048]{1,0:T(8,128)(2,1)} %bitcast.85, bf16[2048,1536]{1,0:T(8,128)(2,1)} %bitcast.76, f32[512,1536]{1,0:T(8,128)} %get-tuple-element.80.refs_3_, ...), custom_call_target="tpu_custom_call" | custom-call | tf_op jit(solution)/shard_map/ff_back/pallas_call | solution.py:1265
  348.5 1.1 copy-done.8
  349.7 0.2 multiply_reduce_fusion.2
  349.8 0.9 fusion.47
  350.8 0.3 multiply_reduce_fusion
  351.1 1.4 fusion.44
  352.5 0.5 collective-permute-start
  353.0 1.2 copy-done.12
  354.1 5.5 convolution_convert_fusion.3
  359.6 1.0 slice.166
  360.7 0.4 collective-permute-start.4
  361.2 0.9 slice.128.h_in
  362.1 0.8 slice.151
  362.9 3.1 copy.44
  366.0 0.7 slice_reduce_fusion.4
  366.6 0.2 fusion.15
  366.8 0.5 multiply_multiply_fusion
  367.4 2.3 maximum_convert_fusion.1
  369.7 0.9 pad_maximum_fusion.1
  370.5 1.5 collective-permute-start.9
  372.0 4.0 fusion.43
  376.1 1.6 add_convert_fusion
  377.7 0.6 collective-permute-start.5
  378.4 0.2 fusion.45
  378.6 17.3 %collective-permute-done.5 = bf16[128,2048]{1,0:T(8,128)(2,1)S(1)} collective-permute-done((bf16[128,2048]{1,0:T(8,128)(2,1)S(1)}, bf16[128,2048]{1,0:T(8,128)(2,1)S(1)}, u32[]{:S(2)}, u32[]{:S(2)}) %collective-permute-start.5) | collective-permute-done | bytes 524320 | tf_op jit(solution)/shard_map/ppermute | solution.py:1369
  396.4 1.2 copy-done
  397.6 0.4 copy-done.1
  398.1 0.4 copy-done.2
  398.5 5.3 adjoint.1
  403.8 1.3 collective-permute-start.2
  405.1 2.7 collective-permute-start.8
  407.8 1.7 collective-permute-done.2.inc
  409.5 6.6 %gates_back.1 = (bf16[2,128,1280]{2,1,0:T(8,128)(2,1)S(1)}, f32[1280,512]{1,0:T(8,128)S(1)}, f32[8,1280]{1,0:T(8,128)S(1)}) custom-call(f32[2,128,1280]{2,1,0:T(8,128)S(1)} %get-tuple-element.89.lam_ref, f32[2,128,1280]{2,1,0:T(8,128)S(1)} %get-tuple-element.90.c_ref, f32[2,1,1280]{2,1,0:T(1,128)S(1)} %collective-permute-done.2.inc, ...), custom_call_target="tpu_custom_call" | custom-call | flops 1200000000 | bytes 9000000 | tf_op jit(solution)/shard_map/gates_back/pallas_call | solution.py:562
  416.2 1.6 collective-permute-start.3
  417.7 0.9 fusion.26
  418.8 2.7 collective-permute-start.10
  421.5 2.6 collective-permute-done.3
  424.3 1.3 fusion
  426.0 1.2 pad_maximum_fusion
  427.2 5.7 %fusion.48 = f32[256,2048]{1,0:T(8,128)S(1)} fusion(bf16[256,2560]{1,0:T(8,128)(2,1)S(1)} %bitcast.90, bf16[2048,2560]{1,0:T(8,128)(2,1)} %bitcast.104), kind=kOutput, calls=%fused_computation.126 | convolution fusion | flops 2684354560 | bytes 13893632 | tf_op jit(solution)/shard_map/dot_general | solution.py:1335
  433.2 1.8 copy-done.9
  435.0 0.4 copy-done.20
  435.3 0.9 fusion.27
  436.4 0.6 copy-done.30
  437.0 4.1 convolution_convert_fusion
  441.1 1.4 bitcast_add_fusion
  442.7 4.3 convolution_convert_fusion.1
  447.0 3.6 collective-permute-done.7
  450.7 3.0 convolution_convert_fusion.2
  453.7 0.9 fusion.14.c_g
  454.6 0.2 copy-done.11
  454.8 0.4 fusion.20
  455.1 0.5 copy-done.14
  455.7 0.3 fusion.31
  456.0 1.3 collective-permute-start.12
  457.3 3.8 collective-permute-done.12
  461.3 2.6 fusion.17
  463.8 0.6 bitcast_add_fusion.2.c_v
  464.4 93.3 %scatter_sums.1 = (f32[64,2560]{1,0:T(8,128)}, f32[64,2560]{1,0:T(8,128)}, f32[80,2048]{1,0:T(8,128)}, f32[80,512]{1,0:T(8,128)}, f32[16,128]{1,0:T(8,128)}) custom-call(bf16[8,2,64,1280]{3,2,1,0:T(8,128)(2,1)} %bitcast.84, bf16[8,2,64,1280]{3,2,1,0:T(8,128)(2,1)} %bitcast.83, bf16[8,2,80,1024]{3,2,1,0:T(8,128)(2,1)} %bitcast.82, ...), custom_call_target="tpu_custom_call" | custom-call | tf_op jit(solution)/shard_map/scatter_sums/pallas_call | solution.py:287
  557.8 4.3 finish.1
  (113 shorter events, 2.3 us)
Async XLA Ops:
  7.2 550.6 %reduce-scatter.2.cloned.1.call-start = ((), (), s32[]{:S(2)}) async-start(), calls=%async_computation.1 | async-start | bytes 14155776 | tf_op jit(solution)/shard_map/reduce_scatter | solution.py:1401
  348.4 1.2 copy-start.8
  348.5 2.3 copy-start.16
  349.7 1.4 copy-start.18
  350.8 3.3 copy-start.12
  352.5 19.5 %copy-start.21 = (bf16[128,1024]{1,0:T(8,128)(2,1)}, bf16[128,1024]{1,0:T(8,128)(2,1)S(1)}, u32[]{:S(2)}) copy-start(bf16[128,1024]{1,0:T(8,128)(2,1)S(1)} %get-tuple-element.170) | copy-start | bytes 786436
  352.5 17.2 %collective-permute-start = (bf16[128,1024]{1,0:T(8,128)(2,1)S(1)}, bf16[128,1024]{1,0:T(8,128)(2,1)S(1)}, u32[]{:S(2)}, u32[]{:S(2)}) collective-permute-start(bf16[128,1024]{1,0:T(8,128)(2,1)S(1)} %get-tuple-element.171), channel_id=1, source_target_pairs={{0,2},{2,0},{4,6},{6,4},{8,10},{10,8},{12,14},{14,12},{16,18},{18,... | collective-permute-start | bytes 786440 | tf_op jit(solution)/shard_map/ppermute | solution.py:1366
  360.7 15.4 %collective-permute-start.4 = (bf16[256,2048]{1,0:T(8,128)(2,1)}, bf16[256,2048]{1,0:T(8,128)(2,1)}, u32[]{:S(2)}, u32[]{:S(2)}) collective-permute-start(bf16[256,2048]{1,0:T(8,128)(2,1)} %slice.166), channel_id=1, source_target_pairs={{0,2},{2,0},{4,6},{6,4},{8,10},{10,8},{12,14},{14,12},{16,18},{18,... | collective-permute-start | bytes 3145736 | tf_op jit(solution)/shard_map/ppermute | solution.py:1366
  362.9 3.1 copy-start.6
  362.9 3.8 copy-start.10
  369.7 6.4 %copy-start.23 = (bf16[128,1024]{1,0:T(8,128)(2,1)}, bf16[128,1024]{1,0:T(8,128)(2,1)S(1)}, u32[]{:S(2)}) copy-start(bf16[128,1024]{1,0:T(8,128)(2,1)S(1)} %collective-permute-done) | copy-start | bytes 786436
  370.5 65.8 %collective-permute-start.9 = (bf16[256,1024]{1,0:T(8,128)(2,1)}, bf16[256,1024]{1,0:T(8,128)(2,1)}, u32[]{:S(2)}, u32[]{:S(2)}) collective-permute-start(bf16[256,1024]{1,0:T(8,128)(2,1)} %pad_maximum_fusion.1), channel_id=1, source_target_pairs={{0,1},{1,0},{2,3},{3,2},{4,5},{5,4},{6,7},{7,6},{8,9},{9,8},{10,11... | collective-permute-start | bytes 1572872 | tf_op jit(solution)/shard_map/ppermute | solution.py:1369
  377.7 18.2 %collective-permute-start.5 = (bf16[128,2048]{1,0:T(8,128)(2,1)S(1)}, bf16[128,2048]{1,0:T(8,128)(2,1)S(1)}, u32[]{:S(2)}, u32[]{:S(2)}) collective-permute-start(bf16[128,2048]{1,0:T(8,128)(2,1)S(1)} %slice.168), channel_id=1, source_target_pairs={{0,1},{1,0},{2,3},{3,2},{4,5},{5,4},{6,7},{7,6},{8,9},{9,8},{10,11... | collective-permute-start | bytes 1572872 | tf_op jit(solution)/shard_map/ppermute | solution.py:1369
  378.6 17.6 %collective-permute-start.1 = (f32[2,128,1280]{2,1,0:T(8,128)S(1)}, f32[2,128,1280]{2,1,0:T(8,128)S(1)}, u32[]{:S(2)}, u32[]{:S(2)}) collective-permute-start(f32[2,128,1280]{2,1,0:T(8,128)S(1)} %bitcast.89), channel_id=1, source_target_pairs={{0,2},{2,0},{4,6},{6,4},{8,10},{10,8},{12,14},{14,12},{16,18},{18,... | collective-permute-start | bytes 3932168 | tf_op jit(solution)/shard_map/ppermute | solution.py:1366
  396.3 1.4 copy-start
  396.3 1.8 copy-start.1
  396.3 2.2 copy-start.2
  398.5 11.0 %copy-start.3 = (bf16[1280,512]{1,0:T(8,128)(2,1)S(1)}, bf16[1280,512]{1,0:T(8,128)(2,1)}, u32[]{:S(2)}) copy-start(bf16[1280,512]{1,0:T(8,128)(2,1)} %get-tuple-element.93.weights) | copy-start | bytes 3932164
  398.5 11.0 %copy-start.4 = (bf16[2,128,1280]{2,1,0:T(8,128)(2,1)S(1)}, bf16[2,128,1280]{2,1,0:T(8,128)(2,1)}, u32[]{:S(2)}) copy-start(bf16[2,128,1280]{2,1,0:T(8,128)(2,1)} %get-tuple-element.92.u_ref) | copy-start | bytes 1966084
  398.5 11.0 %copy-start.5 = (f32[2,128,128]{2,1,0:T(8,128)S(1)}, f32[2,128,128]{2,1,0:T(8,128)}, u32[]{:S(2)}) copy-start(f32[2,128,128]{2,1,0:T(8,128)} %get-tuple-element.94.starts) | copy-start | bytes 393220
  403.8 5.7 %collective-permute-start.2 = (f32[2,1,1280]{2,1,0:T(1,128)S(1)}, f32[2,1,1280]{2,1,0:T(1,128)S(1)}, u32[]{:S(2)}, u32[]{:S(2)}) collective-permute-start(f32[2,1,1280]{2,1,0:T(1,128)S(1)} %slice_multiply_fusion.7), channel_id=1, source_target_pairs={{1,0},{3,2},{5,4},{7,6},{9,8},{11,10},{13,12},{15,14},{17,16},{19,... | collective-permute-start | bytes 30728 | tf_op jit(solution)/shard_map/ppermute | solution.py:1529
  405.1 11.0 %copy-start.19 = (f32[128,2048]{1,0:T(8,128)}, f32[128,2048]{1,0:T(8,128)S(1)}, u32[]{:S(2)}) copy-start(f32[128,2048]{1,0:T(8,128)S(1)} %slice_dynamic-update-slice_fusion) | copy-start | bytes 3145732
  405.1 37.5 %collective-permute-start.8 = (bf16[256,1280]{1,0:T(8,128)(2,1)}, bf16[256,1280]{1,0:T(8,128)(2,1)}, u32[]{:S(2)}, u32[]{:S(2)}) collective-permute-start(bf16[256,1280]{1,0:T(8,128)(2,1)} %bitcast.27), channel_id=1, source_target_pairs={{0,1},{1,0},{2,3},{3,2},{4,5},{5,4},{6,7},{7,6},{8,9},{9,8},{10,11... | collective-permute-start | bytes 1966088 | tf_op jit(solution)/shard_map/ppermute | solution.py:1369
  416.2 8.0 %collective-permute-start.3 = (bf16[2,3,1280]{2,1,0:T(4,128)(2,1)S(1)}, bf16[2,3,1280]{2,1,0:T(4,128)(2,1)S(1)}, u32[]{:S(2)}, u32[]{:S(2)}) collective-permute-start(bf16[2,3,1280]{2,1,0:T(4,128)(2,1)S(1)} %slice.129), channel_id=1, source_target_pairs={{1,0},{3,2},{5,4},{7,6},{9,8},{11,10},{13,12},{15,14},{17,16},{19,... | collective-permute-start | bytes 46088 | tf_op jit(solution)/shard_map/ppermute | solution.py:1531
  418.7 5.6 copy-start.25
  418.7 5.6 copy-start.26
  418.7 5.6 copy-start.27
  418.8 5.5 copy-start.7
  418.8 22.3 %collective-permute-start.10 = (bf16[4,2,80,512]{3,2,0,1:T(8,128)(2,1)}, bf16[4,2,80,512]{3,2,0,1:T(8,128)(2,1)}, u32[]{:S(2)}, u32[]{:S(2)}) collective-permute-start(bf16[4,2,80,512]{3,2,0,1:T(8,128)(2,1)} %fusion.26), channel_id=1, source_target_pairs={{0,1},{1,0},{2,3},{3,2},{4,5},{5,4},{6,7},{7,6},{8,9},{9,8},{10,11... | collective-permute-start | bytes 1966088 | tf_op jit(solution)/shard_map/ppermute | solution.py:1369
  426.0 24.7 %collective-permute-start.7 = (bf16[256,1280]{1,0:T(8,128)(2,1)S(1)}, bf16[256,1280]{1,0:T(8,128)(2,1)S(1)}, u32[]{:S(2)}, u32[]{:S(2)}) collective-permute-start(bf16[256,1280]{1,0:T(8,128)(2,1)S(1)} %bitcast.80), channel_id=1, source_target_pairs={{0,1},{1,0},{2,3},{3,2},{4,5},{5,4},{6,7},{7,6},{8,9},{9,8},{10,11... | collective-permute-start | bytes 1966088 | tf_op jit(solution)/shard_map/ppermute | solution.py:1369
  433.0 21.6 %copy-start.13 = (f32[256,2048]{1,0:T(8,128)}, f32[256,2048]{1,0:T(8,128)S(1)}, u32[]{:S(2)}) copy-start(f32[256,2048]{1,0:T(8,128)S(1)} %fusion.48) | copy-start | bytes 6291460
  433.0 2.0 copy-start.9
  433.0 2.3 copy-start.20
  433.1 21.5 %collective-permute-start.6 = (f32[128,2048]{1,0:T(8,128)S(1)}, f32[128,2048]{1,0:T(8,128)S(1)}, u32[]{:S(2)}, u32[]{:S(2)}) collective-permute-start(f32[128,2048]{1,0:T(8,128)S(1)} %slice.177), channel_id=1, source_target_pairs={{0,2},{2,0},{4,6},{6,4},{8,10},{10,8},{12,14},{14,12},{16,18},{18,... | collective-permute-start | bytes 3145736 | tf_op jit(solution)/shard_map/ppermute | solution.py:1366
  435.3 1.0 copy-start.22
  435.3 1.1 copy-start.24
  435.3 1.7 copy-start.30
  441.1 1.6 copy-start.31
  442.6 11.1 %collective-permute-start.11 = (bf16[4,80,512]{2,1,0:T(8,128)(2,1)S(1)}, bf16[4,80,512]{2,1,0:T(8,128)(2,1)S(1)}, u32[]{:S(2)}, u32[]{:S(2)}) collective-permute-start(bf16[4,80,512]{2,1,0:T(8,128)(2,1)S(1)} %get-tuple-element.169), channel_id=1, source_target_pairs={{0,2},{2,0},{4,6},{6,4},{8,10},{10,8},{12,14},{14,12},{16,18},{18,... | collective-permute-start | bytes 983048 | tf_op jit(solution)/shard_map/ppermute | solution.py:1366
  447.0 7.6 %copy-start.28 = (f32[128]{0:T(128)S(1)}, f32[128]{0:T(128)}, u32[]{:S(2)}) copy-start(f32[128]{0:T(128)} %get-tuple-element.177) | copy-start | bytes 1540
  453.6 1.1 copy-start.11
  454.6 1.0 copy-start.14
  454.8 6.5 %copy-start.17 = (f32[128,2048]{1,0:T(8,128)S(1)}, f32[128,2048]{1,0:T(8,128)}, u32[]{:S(2)}) copy-start(f32[128,2048]{1,0:T(8,128)} %get-tuple-element.162) | copy-start | bytes 3145732
  455.6 5.7 copy-start.29
  455.6 5.7 copy-start.15
  456.0 5.0 collective-permute-start.12
  461.1 2.7 collective-permute-start.13
Sparse Core Ops, SparseCore 0:
  348.6 129.9 reduce-scatter.1

commit v8 on v7

--- a/solution.py
+++ b/solution.py
@@ -202,10 +202,10 @@
 
 def scatter_kernel(
     n,
-    c_x, c_y, c_out, c_g, c_v,
+    h_x, h_y, h_out, h_g, h_v,
     g_x, g_y, g_out, g_gates, g_vec,
-    r_x, r_y, r_out, r_g, r_v, s_x, s_y, s_out,
-    send_sem, recv_sem,
+    r_x, r_y, r_out, r_g, r_v, s_x, s_y, s_out, c_x, c_y, c_out, c_g, c_v,
+    send_sem, recv_sem, local_sem,
 ):
     dp, x = lax.axis_index("dp"), lax.axis_index("tp")
     chip, core = dp // 2, dp % 2
@@ -214,31 +214,38 @@
     nxt = (chip_at((pos + 1) % n, n) * 2 + core, x)
     prv = (chip_at((pos + n - 1) % n, n) * 2 + core, x)
     sib = (dp + 1 - 2 * core, x)
+    copies = Copies(local_sem, send_sem, recv_sem)
+    loads = [
+        copies.stay(src, dst) for src, dst in ((h_out, c_out), (h_y, c_y), (h_x, c_x), (h_g, c_g), (h_v, c_v))
+    ]
     greet([nxt, prv, sib])
-    copies = Copies(None, send_sem, recv_sem)
 
     pieces = []
     for part in (0, 1):
-        for terms, slots, first in ((c_out, r_out, core), (c_y, r_y, 0), (c_x, r_x, 0)):
+        for far_terms, terms, slots, first in ((h_out, c_out, r_out, core), (h_y, c_y, r_y, 0), (h_x, c_x, r_x, 0)):
             pieces.append((
                 lambda c, terms=terms, part=part, first=first: terms.at[heads_first(c, first, n), part],
                 lambda w, k, slots=slots, part=part: slots.at[part, w, k],
                 part,
+                lambda c, terms=far_terms, part=part, first=first: terms.at[heads_first(c, first, n), part],
             ))
-    pieces.append((lambda c: c_g.at[c], lambda w, k: r_g.at[w, k], 0))
-    pieces.append((lambda c: c_v.at[c], lambda w, k: r_v.at[w, k], 1))
+    pieces.append((lambda c: c_g.at[c], lambda w, k: r_g.at[w, k], 0, lambda c: h_g.at[c]))
+    pieces.append((lambda c: c_v.at[c], lambda w, k: r_v.at[w, k], 1, lambda c: h_v.at[c]))
 
     def add(a, b):
         return a[...].astype(F32) + b[...].astype(F32)
 
     sent, coming = [], {}
     for k in range(half, -1, -1):
-        for i, (term, slot, far) in enumerate(pieces):
+        if k == half - 1:
+            for copy in loads:
+                copy.wait()
+        for i, (term, slot, far, raw) in enumerate(pieces):
             for way, (device, sign) in enumerate(((nxt, 1), (prv, n - 1))):
                 first = half if way == far else half - 1
                 if k > first or k == 0:
                     continue
-                source = term(chip_at((pos + sign * k) % n, n))
+                source = (raw if k == half else term)(chip_at((pos + sign * k) % n, n))
                 if k < first:
                     coming[i, way].wait_recv()
                     got = slot(way, k)
@@ -249,7 +256,7 @@
                 sent.append(copy)
 
     def total(i):
-        term, slot, _ = pieces[i]
+        term, slot = pieces[i][:2]
         for way in (0, 1):
             coming[i, way].wait_recv()
         return add(term(chip), slot(0, 0)) + slot(1, 0)[...].astype(F32)
@@ -293,7 +300,7 @@
             jax.ShapeDtypeStruct(c_g.shape[1:], F32),
             jax.ShapeDtypeStruct(c_v.shape[1:], F32),
         ],
-        in_specs=[vmem] * 5,
+        in_specs=[pl.BlockSpec(memory_space=pl.ANY)] * 5,
         out_specs=[vmem] * 5,
         scratch_shapes=[
             pltpu.VMEM((2, 2, half, rows_d, rhalf), BF16),
@@ -304,7 +311,10 @@
             pltpu.VMEM((rows_d, rhalf), F32),
             pltpu.VMEM((rows_d, rhalf), F32),
             pltpu.VMEM((rows_r, dhalf), F32),
-            dma((count,)), dma((count,)),
+        ]
+        + [pltpu.VMEM(v.shape, v.dtype) for v in (c_x, c_y, c_out, c_g, c_v)]
+        + [
+            dma((count,)), dma((count,)), dma((5,)),
         ],
         compiler_params=pltpu.CompilerParams(
             collective_id=1, has_side_effects=True, vmem_limit_bytes=56 << 20
@@ -1510,8 +1520,6 @@
         part_gu = tn(n2_rows, after(jnp.concatenate([d_gu, d_gu_sib], axis=1), d_n2_send)).astype(BF16)
         grad_d = None
     sum_gu = lane_sum(part_gu)
-    ff_pair = pair_sum(nt(after(hidden, part_gu), w_d).astype(BF16))
-    ff_out = ff_pair[:tokens].astype(F32) + across(ff_pair[tokens:]).astype(F32)
 
     q2 = gain_two * d_n2
     d_gain_two = jnp.sum(d_n2 * x1 * rs2, axis=0)
@@ -1526,6 +1534,8 @@
 
     d_ypre, lam_local, coef_back = adjoint(do, h, ypre, a)
     d_ypre_x = both(d_ypre.reshape(2 * tokens, rh), 0)
+    ff_pair = pair_sum(nt(after(hidden, part_gu, d_ypre), w_d).astype(BF16))
+    ff_out = ff_pair[:tokens].astype(F32) + across(ff_pair[tokens:]).astype(F32)
     inc = lax.ppermute(a[:, :1] * lam_local[:, :1], "tp", [(1, 0)])
     du, d_gates, sums = gates_back(lam_local, coef_back, inc, h, h_in, u, gates, cp, starts_two)
     du_next = lax.ppermute(du[:, : taps - 1], "tp", [(1, 0)])

time: 571 us -> 571 us (level)
  Pallas kernels: 447 us -> 454 us
  waiting for transfers between devices: 29 us -> 23 us
    pallas_call x1, Pallas kernels: 93.3 us -> 100 us  [scatter_sums(): pl.pallas_call(functools.partial(scatter_kernel, n), out_shape=[jax.Shape...]
  transfers between devices with their start and end apart: 15 -> 15, of which waited for: 5 -> 4; matrix products, arithmetic and copies ran while one was open for 9% -> 9% of each run, Pallas kernels for 18% -> 20%
where the time goes in v8:
time: 571 us; the launch traced here: 569 us
  Pallas kernels  454 us (80%)
  matrix products  25.2 us (4%)
  waiting for transfers between devices  23 us (4%)
  other arithmetic  19.3 us (3%)
  local copies, waits for them, and re-layouts  19.1 us (3%)
  between operations  15.4 us (3%)
  starting transfers between devices  13 us (2%)
    pallas_call x1, Pallas kernels, front(): pl.pallas_call(functools.partial(front_kernel, n), out_shape=[jax.ShapeDt...  271 us
    pallas_call x1, Pallas kernels, scatter_sums(): pl.pallas_call(functools.partial(scatter_kernel, n), out_shape=[jax.Shape...  100 us
    pallas_call x1, Pallas kernels, ff_back(): pl.pallas_call(functools.partial(ff_back_kernel, n), out_shape=[jax.Shape...  66.9 us
    ppermute x6, waiting for transfers between devices, across(): return lax.ppermute(v, 'tp', [(0, 1), (1, 0)])  19.1 us
    dot_general x3, matrix products, nt(): lax.dot_general(left, right, (((1,), (1,)), ((), ())), preferred_element_...  13.8 us
  transfers between devices with their start and end apart: 15, of which 4 were waited for; matrix products, arithmetic and copies ran while one was open for 9% of the time, Pallas kernels for 20%

profile of v8, /device:TPU:0, one launch (start us, length us, event | category | flops | bytes accessed | tf_op | source)
XLA Modules:
  0.0 569.0 jit_solution(15764059103100593608)
XLA Ops:
  7.9 0.7 fusion.39
  8.6 0.7 concatenate.70
  9.3 1.4 fusion.33.refs_3_
  10.8 270.8 %front.1 = (bf16[8,2,2,64,2560]{4,3,2,1,0:T(8,128)(2,1)}, bf16[8,2,2,80,1024]{4,3,2,1,0:T(8,128)(2,1)}, bf16[1280,512]{1,0:T(8,128)(2,1)}, f32[16,1280]{1,0:T(8,...) custom-call(bf16[64,2560]{1,0:T(8,128)(2,1)} %refs_0_.1, ...), custom_call_target="tpu_custom_call" | custom-call | tf_op jit(solution)/shard_map/front/pallas_call | solution.py:1082
  281.5 66.9 %ff_back.1 = (f32[128,3072]{1,0:T(8,128)}, f32[128,2048]{1,0:T(8,128)}, bf16[1024,6144]{1,0:T(8,128)(2,1)}) custom-call(bf16[8,2,128,1536]{3,2,1,0:T(8,128)(2,1)} %bitcast.78, bf16[512,2048]{1,0:T(8,128)(2,1)} %bitcast.85, bf16[2048,1536]{1,0:T(8,128)(2,1)} %bitcast.76, f32[512,1536]{1,0:T(8,128)} %get-tuple-element.80.refs_3_, ...), custom_call_target="tpu_custom_call" | custom-call | tf_op jit(solution)/shard_map/ff_back/pallas_call | solution.py:1275
  348.5 1.1 copy-done.8
  349.7 0.2 multiply_reduce_fusion.2
  349.8 0.9 fusion.47
  350.8 0.3 multiply_reduce_fusion
  351.1 1.3 fusion.44
  352.5 0.5 collective-permute-start
  352.9 1.2 collective-permute-done
  354.2 1.6 fusion.43
  355.8 1.2 fusion.45
  357.0 0.5 collective-permute-start.1
  357.6 0.9 slice.128.h_in
  358.5 0.8 slice.151
  359.3 3.1 copy.44
  362.5 0.2 fusion.15
  362.7 1.2 maximum_convert_fusion.1
  363.9 0.8 pad_maximum_fusion.1
  364.8 1.4 collective-permute-start.9
  366.1 1.4 fusion.46
  367.6 0.1 maximum_add_fusion.do
  367.8 1.1 copy-done
  368.9 0.4 copy-done.1
  369.3 0.4 copy-done.2
  369.7 5.3 adjoint.1
  375.0 1.3 collective-permute-start.2
  376.3 6.5 %convolution_convert_fusion.3 = bf16[512,2048]{1,0:T(8,128)(2,1)S(1)} fusion(bf16[512,1536]{1,0:T(8,128)(2,1)S(1)} %copy-done.25, bf16[2048,1536]{1,0:T(8,128)(2,1)} %bitcast.77), kind=kOutput, calls=%fused_computation.3 | convolution fusion | flops 3222274048 | bytes 9961472 | tf_op jit(solution)/shard_map/dot_general | solution.py:1345
  382.8 2.7 collective-permute-start.8
  385.5 1.0 slice.166
  386.6 6.7 %gates_back.1 = (bf16[2,128,1280]{2,1,0:T(8,128)(2,1)S(1)}, f32[1280,512]{1,0:T(8,128)S(1)}, f32[8,1280]{1,0:T(8,128)S(1)}) custom-call(f32[2,128,1280]{2,1,0:T(8,128)S(1)} %get-tuple-element.89.lam_ref, f32[2,128,1280]{2,1,0:T(8,128)S(1)} %get-tuple-element.90.c_ref, f32[2,1,1280]{2,1,0:T(1,128)S(1)} %collective-permute-done.2.inc, ...), custom_call_target="tpu_custom_call" | custom-call | flops 1200000000 | bytes 9000000 | tf_op jit(solution)/shard_map/gates_back/pallas_call | solution.py:572
  393.3 1.6 collective-permute-start.3
  394.9 0.9 fusion.26
  395.8 0.1 concatenate.88
  395.9 2.7 collective-permute-start.10
  398.6 2.7 collective-permute-done.3
  401.4 1.3 fusion
  403.2 1.2 pad_maximum_fusion
  404.4 5.8 %fusion.48 = f32[256,2048]{1,0:T(8,128)S(1)} fusion(bf16[256,2560]{1,0:T(8,128)(2,1)S(1)} %bitcast.89, bf16[2048,2560]{1,0:T(8,128)(2,1)} %bitcast.103), kind=kOutput, calls=%fused_computation.126 | convolution fusion | flops 2684354560 | bytes 13893632 | tf_op jit(solution)/shard_map/dot_general | solution.py:1345
  410.5 0.8 copy-done.20
  411.3 0.3 copy-done.23
  411.6 0.8 copy-done.26
  412.4 4.0 convolution_convert_fusion
  416.4 1.4 bitcast_add_fusion
  418.0 4.3 convolution_convert_fusion.1
  422.3 6.5 %collective-permute-done.7 = bf16[256,1280]{1,0:T(8,128)(2,1)S(1)} collective-permute-done((bf16[256,1280]{1,0:T(8,128)(2,1)S(1)}, bf16[256,1280]{1,0:T(8,128)(2,1)S(1)}, u32[]{:S(2)}, u32[]{:S(2)}) %collective-permute-start.7) | collective-permute-done | bytes 655392 | tf_op jit(solution)/shard_map/ppermute | solution.py:1379
  428.7 3.0 convolution_convert_fusion.2
  431.8 0.9 fusion.14.h_g
  432.7 1.7 add_convert_fusion
  434.4 1.4 collective-permute-start.5
  435.8 0.4 fusion.20
  436.2 0.6 copy-done.13
  436.9 0.3 fusion.31
  437.2 0.8 collective-permute-start.12
  438.0 12.7 %collective-permute-done.12 = f32[8,2,16,128]{3,2,0,1:T(8,128)S(1)} collective-permute-done((f32[8,2,16,128]{3,2,0,1:T(8,128)S(1)}, f32[8,2,16,128]{3,2,0,1:T(8,128)S(1)}, u32[]{:S(2)}, u32[]{:S(2)}) %collective-permute-start.12) | collective-permute-done | bytes 131104 | tf_op jit(solution)/shard_map/ppermute | solution.py:1379
  450.9 3.0 fusion.17
  453.8 0.6 bitcast_add_fusion.2.h_v
  454.5 1.2 convert_add_fusion
  455.8 1.1 copy-done.9
  456.9 0.9 fusion.27
  457.8 100.0 %scatter_sums.1 = (f32[64,2560]{1,0:T(8,128)}, f32[64,2560]{1,0:T(8,128)}, f32[80,2048]{1,0:T(8,128)}, f32[80,512]{1,0:T(8,128)}, f32[16,128]{1,0:T(8,128)}) custom-call(bf16[8,2,64,1280]{3,2,1,0:T(8,128)(2,1)} %bitcast.84, bf16[8,2,64,1280]{3,2,1,0:T(8,128)(2,1)} %bitcast.83, bf16[8,2,80,1024]{3,2,1,0:T(8,128)(2,1)} %bitcast.82, ...), custom_call_target="tpu_custom_call" | custom-call | tf_op jit(solution)/shard_map/scatter_sums/pallas_call | solution.py:294
  557.8 4.3 finish.1
  (105 shorter events, 1.9 us)
Async XLA Ops:
  7.2 550.6 %reduce-scatter.2.cloned.1.call-start = ((), (), s32[]{:S(2)}) async-start(), calls=%async_computation.1 | async-start | bytes 14155776 | tf_op jit(solution)/shard_map/reduce_scatter | solution.py:1411
  348.4 1.2 copy-start.8
  348.5 2.3 copy-start.15
  349.7 1.4 copy-start.18
  351.1 3.1 copy-start.24
  352.5 11.5 %copy-start.19 = (bf16[128,1024]{1,0:T(8,128)(2,1)}, bf16[128,1024]{1,0:T(8,128)(2,1)S(1)}, u32[]{:S(2)}) copy-start(bf16[128,1024]{1,0:T(8,128)(2,1)S(1)} %get-tuple-element.170) | copy-start | bytes 786436
  352.5 1.6 collective-permute-start
  354.1 9.8 %copy-start.22 = (bf16[128,1024]{1,0:T(8,128)(2,1)}, bf16[128,1024]{1,0:T(8,128)(2,1)S(1)}, u32[]{:S(2)}) copy-start(bf16[128,1024]{1,0:T(8,128)(2,1)S(1)} %collective-permute-done) | copy-start | bytes 786436
  357.0 9.1 %collective-permute-start.1 = (f32[2,128,1280]{2,1,0:T(8,128)}, f32[2,128,1280]{2,1,0:T(8,128)}, u32[]{:S(2)}, u32[]{:S(2)}) collective-permute-start(f32[2,128,1280]{2,1,0:T(8,128)} %bitcast.17), channel_id=1, source_target_pairs={{0,2},{2,0},{4,6},{6,4},{8,10},{10,8},{12,14},{14,12},{16,18},{18,... | collective-permute-start | bytes 3932168 | tf_op jit(solution)/shard_map/ppermute | solution.py:1376
  359.3 3.2 copy-start.6
  359.3 3.2 copy-start.10
  359.3 3.4 copy-start.21
  364.8 45.7 %collective-permute-start.9 = (bf16[256,1024]{1,0:T(8,128)(2,1)}, bf16[256,1024]{1,0:T(8,128)(2,1)}, u32[]{:S(2)}, u32[]{:S(2)}) collective-permute-start(bf16[256,1024]{1,0:T(8,128)(2,1)} %pad_maximum_fusion.1), channel_id=1, source_target_pairs={{0,1},{1,0},{2,3},{3,2},{4,5},{5,4},{6,7},{7,6},{8,9},{9,8},{10,11... | collective-permute-start | bytes 1572872 | tf_op jit(solution)/shard_map/ppermute | solution.py:1379
  367.6 1.3 copy-start
  367.6 1.7 copy-start.1
  367.6 2.1 copy-start.2
  369.7 6.6 %copy-start.25 = (bf16[512,1536]{1,0:T(8,128)(2,1)S(1)}, bf16[512,1536]{1,0:T(8,128)(2,1)}, u32[]{:S(2)}) copy-start(bf16[512,1536]{1,0:T(8,128)(2,1)} %get-tuple-element.100) | copy-start | bytes 4718596
  375.0 11.6 %collective-permute-start.2 = (f32[2,1,1280]{2,1,0:T(1,128)S(1)}, f32[2,1,1280]{2,1,0:T(1,128)S(1)}, u32[]{:S(2)}, u32[]{:S(2)}) collective-permute-start(f32[2,1,1280]{2,1,0:T(1,128)S(1)} %slice_multiply_fusion.7), channel_id=1, source_target_pairs={{1,0},{3,2},{5,4},{7,6},{9,8},{11,10},{13,12},{15,14},{17,16},{19,... | collective-permute-start | bytes 30728 | tf_op jit(solution)/shard_map/ppermute | solution.py:1539
  382.8 3.8 copy-start.16
  382.8 3.8 copy-start.3
  382.8 3.8 copy-start.4
  382.8 3.8 copy-start.5
  382.8 35.1 %collective-permute-start.8 = (bf16[256,1280]{1,0:T(8,128)(2,1)}, bf16[256,1280]{1,0:T(8,128)(2,1)}, u32[]{:S(2)}, u32[]{:S(2)}) collective-permute-start(bf16[256,1280]{1,0:T(8,128)(2,1)} %bitcast.27), channel_id=1, source_target_pairs={{0,1},{1,0},{2,3},{3,2},{4,5},{5,4},{6,7},{7,6},{8,9},{9,8},{10,11... | collective-permute-start | bytes 1966088 | tf_op jit(solution)/shard_map/ppermute | solution.py:1379
  386.6 46.1 %collective-permute-start.4 = (bf16[256,2048]{1,0:T(8,128)(2,1)}, bf16[256,2048]{1,0:T(8,128)(2,1)}, u32[]{:S(2)}, u32[]{:S(2)}) collective-permute-start(bf16[256,2048]{1,0:T(8,128)(2,1)} %slice.166), channel_id=1, source_target_pairs={{0,2},{2,0},{4,6},{6,4},{8,10},{10,8},{12,14},{14,12},{16,18},{18,... | collective-permute-start | bytes 3145736 | tf_op jit(solution)/shard_map/ppermute | solution.py:1376
  393.3 8.0 %collective-permute-start.3 = (bf16[2,3,1280]{2,1,0:T(4,128)(2,1)S(1)}, bf16[2,3,1280]{2,1,0:T(4,128)(2,1)S(1)}, u32[]{:S(2)}, u32[]{:S(2)}) collective-permute-start(bf16[2,3,1280]{2,1,0:T(4,128)(2,1)S(1)} %slice.129), channel_id=1, source_target_pairs={{1,0},{3,2},{5,4},{7,6},{9,8},{11,10},{13,12},{15,14},{17,16},{19,... | collective-permute-start | bytes 46088 | tf_op jit(solution)/shard_map/ppermute | solution.py:1541
  395.9 5.5 copy-start.7
  395.9 20.5 %collective-permute-start.10 = (bf16[4,2,80,512]{3,2,0,1:T(8,128)(2,1)}, bf16[4,2,80,512]{3,2,0,1:T(8,128)(2,1)}, u32[]{:S(2)}, u32[]{:S(2)}) collective-permute-start(bf16[4,2,80,512]{3,2,0,1:T(8,128)(2,1)} %fusion.26), channel_id=1, source_target_pairs={{0,1},{1,0},{2,3},{3,2},{4,5},{5,4},{6,7},{7,6},{8,9},{9,8},{10,11... | collective-permute-start | bytes 1966088 | tf_op jit(solution)/shard_map/ppermute | solution.py:1379
  403.1 25.6 %collective-permute-start.7 = (bf16[256,1280]{1,0:T(8,128)(2,1)S(1)}, bf16[256,1280]{1,0:T(8,128)(2,1)S(1)}, u32[]{:S(2)}, u32[]{:S(2)}) collective-permute-start(bf16[256,1280]{1,0:T(8,128)(2,1)S(1)} %bitcast.80), channel_id=1, source_target_pairs={{0,1},{1,0},{2,3},{3,2},{4,5},{5,4},{6,7},{7,6},{8,9},{9,8},{10,11... | collective-permute-start | bytes 1966088 | tf_op jit(solution)/shard_map/ppermute | solution.py:1379
  410.1 25.7 %copy-start.12 = (f32[256,2048]{1,0:T(8,128)}, f32[256,2048]{1,0:T(8,128)S(1)}, u32[]{:S(2)}) copy-start(f32[256,2048]{1,0:T(8,128)S(1)} %fusion.48) | copy-start | bytes 6291460
  410.1 1.1 copy-start.20
  410.2 1.4 copy-start.23
  410.2 2.2 copy-start.26
  410.5 25.3 %collective-permute-start.6 = (f32[128,2048]{1,0:T(8,128)S(1)}, f32[128,2048]{1,0:T(8,128)S(1)}, u32[]{:S(2)}, u32[]{:S(2)}) collective-permute-start(f32[128,2048]{1,0:T(8,128)S(1)} %slice.177), channel_id=1, source_target_pairs={{0,2},{2,0},{4,6},{6,4},{8,10},{10,8},{12,14},{14,12},{16,18},{18,... | collective-permute-start | bytes 3145736 | tf_op jit(solution)/shard_map/ppermute | solution.py:1376
  416.4 1.5 copy-start.27
  417.9 13.9 %collective-permute-start.11 = (bf16[4,80,512]{2,1,0:T(8,128)(2,1)S(1)}, bf16[4,80,512]{2,1,0:T(8,128)(2,1)S(1)}, u32[]{:S(2)}, u32[]{:S(2)}) collective-permute-start(bf16[4,80,512]{2,1,0:T(8,128)(2,1)S(1)} %get-tuple-element.169), channel_id=1, source_target_pairs={{0,2},{2,0},{4,6},{6,4},{8,10},{10,8},{12,14},{14,12},{16,18},{18,... | collective-permute-start | bytes 983048 | tf_op jit(solution)/shard_map/ppermute | solution.py:1376
  428.7 4.0 copy-start.17
  432.7 3.1 copy-start.11
  434.4 20.0 %collective-permute-start.5 = (bf16[128,2048]{1,0:T(8,128)(2,1)S(1)}, bf16[128,2048]{1,0:T(8,128)(2,1)}, u32[]{:S(2)}, u32[]{:S(2)}) collective-permute-start(bf16[128,2048]{1,0:T(8,128)(2,1)S(1)} %slice.168), channel_id=1, source_target_pairs={{0,1},{1,0},{2,3},{3,2},{4,5},{5,4},{6,7},{7,6},{8,9},{9,8},{10,11... | collective-permute-start | bytes 1572872 | tf_op jit(solution)/shard_map/ppermute | solution.py:1379
  435.8 1.0 copy-start.13
  436.8 14.1 %copy-start.14 = (f32[128,2048]{1,0:T(8,128)S(1)}, f32[128,2048]{1,0:T(8,128)}, u32[]{:S(2)}) copy-start(f32[128,2048]{1,0:T(8,128)} %copy-done.13) | copy-start | bytes 3145732
  437.2 13.5 %collective-permute-start.12 = (f32[8,2,16,128]{3,2,0,1:T(8,128)S(1)}, f32[8,2,16,128]{3,2,0,1:T(8,128)S(1)}, u32[]{:S(2)}, u32[]{:S(2)}) collective-permute-start(f32[8,2,16,128]{3,2,0,1:T(8,128)S(1)} %bitcast.91), channel_id=1, source_target_pairs={{0,1},{1,0},{2,3},{3,2},{4,5},{5,4},{6,7},{7,6},{8,9},{9,8},{10,11... | collective-permute-start | bytes 393224 | tf_op jit(solution)/shard_map/ppermute | solution.py:1379
  450.8 3.1 collective-permute-start.13
  455.6 1.3 copy-start.9
Sparse Core Ops, SparseCore 0:
  348.6 139.9 reduce-scatter.1
